TPU v7x, 32 devices: a whole 2x2x4 slice. The times are simulated.
32 devices in a mesh: ctx: 8 (over y, x, core), tp: 4 (over z).
Axes of the slice: x: 2, y: 2, z: 4, core: 2. Of those that a mesh axis runs over, the one named last changes fastest.
Arguments:
- tokens: bfloat16 [6144, 2048], P('ctx', 'tp'), may hold values from -6 to 6
- segment_ids: int32 [6144], P('ctx'), may hold values from 0 to 6143, as said below
- in_weight: bfloat16 [2048, 3, 2048], P(None, None, 'tp'), may hold values from -0.125 to 0.125
- out_weight: bfloat16 [2048, 2048], P('tp'), may hold values from -2 to 2
- gate_up_weight: bfloat16 [2048, 2, 8192], P(None, None, 'tp'), may hold values from -0.125 to 0.125
- down_weight: bfloat16 [8192, 2048], P('tp'), may hold values from -0.0625 to 0.0625
- cotangent: bfloat16 [6144, 2048], P('ctx', 'tp'), may hold values from -6 to 6
Outputs:
- layer_out: bfloat16 [6144, 2048], P('ctx', 'tp')
- tokens_grad: float32 [6144, 2048], P('ctx', 'tp')
- in_weight_grad: float32 [2048, 3, 2048], P(None, None, 'tp')
- out_weight_grad: float32 [2048, 2048], P('tp')
- gate_up_weight_grad: float32 [2048, 2, 8192], P(None, None, 'tp')
- down_weight_grad: float32 [8192, 2048], P('tp')
Inputs may be any that keep to these rules, and one draw needn't show every extreme that they name: `segment_ids`: document numbers never fall along the sequence; the first token's number is 0 and the last token's is 6143.
All inputs are finite; a program needn't handle non-finite values.
Results may differ from a plain program's by a relative error of at most 0.024.
Values may be sent and summed in bfloat16 or wider, within the bound.
A program may use at most 256 MiB of HBM per device.

v0:
```python
from functools import partial
import math

import jax
import jax.numpy as jnp
from jax import lax
from jax.sharding import PartitionSpec as P

HD = 128


EPS = 1e-05
NEG = -1e30


def row_sums(first, second):
    return lax.psum((first, second), "tp")


def normalize(local, width):
    total, squares = row_sums(jnp.sum(local, axis=1), jnp.sum(local * local, axis=1))
    center = total / width
    inverse = lax.rsqrt(squares / width - center * center + EPS)
    return ((local - center[:, None]) * inverse[:, None], inverse)


def norm_back(grad, normed, inverse, width):
    total, inner = row_sums(jnp.sum(grad, axis=1), jnp.sum(grad * normed, axis=1))
    return inverse[:, None] * (grad - total[:, None] / width - normed * (inner[:, None] / width))


def normed_rows(local):
    return lax.all_gather(local, "tp", axis=1, tiled=True)


def grad_rows(local):
    return lax.all_gather(local, "tp", axis=1, tiled=True)


def feature_sums(partial_sum):
    return lax.psum_scatter(
        partial_sum.astype(jnp.bfloat16), "tp", scatter_dimension=1, tiled=True
    ).astype(jnp.float32)


def rope_tables(places, head):
    half = head // 2
    freq = 10000.0 ** (-jnp.arange(half, dtype=jnp.float32) * 2.0 / head)
    angle = places.astype(jnp.float32)[:, None] * freq[None, :]
    angle = jnp.concatenate([angle, angle], axis=1)[:, None, :]
    return (jnp.cos(angle), jnp.sin(angle))


def rotate(values, cosine, sine):
    half = values.shape[-1] // 2
    swapped = jnp.concatenate([-values[..., half:], values[..., :half]], axis=-1)
    return values * cosine + swapped * sine


def rotate_back(grad, cosine, sine):
    half = grad.shape[-1] // 2
    moved = grad * sine
    return grad * cosine + jnp.concatenate([moved[..., half:], -moved[..., :half]], axis=-1)


def guarded(step_fn, last_place, first_seg):

    def checked(carry, piece, start):
        live = (start <= last_place) & (piece[2][piece[2].shape[0] - 1] >= first_seg)
        return lax.cond(
            live, lambda state: step_fn(state, piece, start), lambda state: state, carry
        )

    return checked


def by_blocks(step_fn, size, carry, piece, start):
    count = piece[0].shape[0]
    block = math.gcd(count, size)
    number = count // block
    stacked = tuple((member.reshape((number, block) + member.shape[1:]) for member in piece))

    def turn(state, item):
        members, index = item
        return (step_fn(state, members, index * block), None)

    result = lax.scan(turn, carry, (stacked, jnp.arange(number, dtype=jnp.int32)))
    return result[0]


def masked_scores(query, key, query_place, query_seg, key_seg, start, scale):
    count = key.shape[0]
    key_place = start + jnp.arange(count, dtype=jnp.int32)
    allowed = (
        (query_seg[:, None] == key_seg[None, :]) & (query_place[:, None] >= key_place[None, :])
    )[None]
    scores = jnp.einsum("qhd,khd->hqk", query, key, preferred_element_type=jnp.float32) * scale
    return (jnp.where(allowed, scores, NEG), allowed)


def forward_step(query, query_place, query_seg, scale):

    def step_fn(carry, piece, start):
        highest, total, accum = carry
        key, value, key_seg = piece
        scores, allowed = masked_scores(query, key, query_place, query_seg, key_seg, start, scale)
        new_high = jnp.maximum(highest, jnp.max(scores, axis=2))
        decay = jnp.exp(highest - new_high)
        weights = jnp.where(allowed, jnp.exp(scores - new_high[:, :, None]), 0.0)
        total = total * decay + jnp.sum(weights, axis=2)
        accum = accum * decay[:, :, None] + jnp.einsum(
            "hqk,khd->hqd", weights.astype(jnp.bfloat16), value, preferred_element_type=jnp.float32
        )
        return (new_high, total, accum)

    return step_fn


def backward_step(query, query_place, query_seg, scale, log_total, delta, grad_mixed):

    def step_fn(carry, piece, start):
        grad_query, grad_pairs = carry
        key, value, key_seg = piece
        count = key.shape[0]
        scores, allowed = masked_scores(query, key, query_place, query_seg, key_seg, start, scale)
        probs = jnp.where(allowed, jnp.exp(scores - log_total[:, :, None]), 0.0)
        grad_probs = jnp.einsum(
            "qhd,khd->hqk", grad_mixed, value, preferred_element_type=jnp.float32
        )
        grad_scores = (probs * (grad_probs - delta[:, :, None])).astype(jnp.bfloat16)
        grad_query = grad_query + jnp.einsum(
            "hqk,khd->qhd", grad_scores, key, preferred_element_type=jnp.float32
        )
        grad_key = jnp.einsum(
            "hqk,qhd->khd", grad_scores, query, preferred_element_type=jnp.float32
        )
        grad_value = jnp.einsum(
            "hqk,qhd->khd",
            probs.astype(jnp.bfloat16),
            grad_mixed,
            preferred_element_type=jnp.float32,
        )
        previous = lax.dynamic_slice_in_dim(grad_pairs, start, count, 0)
        grad_pairs = lax.dynamic_update_slice_in_dim(
            grad_pairs, previous + jnp.stack([grad_key, grad_value], axis=1), start, 0
        )
        return (grad_query, grad_pairs)

    return step_fn


def per_device(tokens, segment_ids, in_weight, out_weight, gate_up_weight, down_weight, cotangent):
    rows = tokens.shape[0]
    width = in_weight.shape[0]
    heads_local = in_weight.shape[2] // HD
    hidden_local = down_weight.shape[0]
    cycle_size = lax.axis_size("ctx")
    scale = HD ** (-0.5)
    size = rows * max(1, 512 // rows)
    places = lax.axis_index("ctx") * rows + jnp.arange(rows, dtype=jnp.int32)
    last_place = places[rows - 1]
    first_seg = segment_ids[0]
    cosine, sine = rope_tables(places, HD)
    resid = tokens.astype(jnp.float32)
    normed1, inverse1 = normalize(resid, width)
    inner1 = normed_rows(normed1.astype(jnp.bfloat16))
    projected = jnp.dot(inner1, in_weight.reshape(width, -1), preferred_element_type=jnp.float32)
    projected = projected.reshape(rows, 3, heads_local, HD)
    query = rotate(projected[:, 0], cosine, sine).astype(jnp.bfloat16)
    key = rotate(projected[:, 1], cosine, sine).astype(jnp.bfloat16)
    value = projected[:, 2].astype(jnp.bfloat16)
    start_state = (
        jnp.full((heads_local, rows), NEG, jnp.float32),
        jnp.zeros((heads_local, rows), jnp.float32),
        jnp.zeros((heads_local, rows, HD), jnp.float32),
    )
    forward_fn = guarded(forward_step(query, places, segment_ids, scale), last_place, first_seg)
    attend_fn = partial(by_blocks, forward_fn, size)
    highest, total, accum = attend_fn(
        start_state,
        (
            lax.all_gather(key, "ctx", axis=0, tiled=True),
            lax.all_gather(value, "ctx", axis=0, tiled=True),
            lax.all_gather(segment_ids, "ctx", axis=0, tiled=True),
        ),
        jnp.int32(0),
    )
    log_total = highest + jnp.log(total)
    mixed_raw = jnp.transpose(accum / total[:, :, None], (1, 0, 2))
    mixed = mixed_raw.astype(jnp.bfloat16).reshape(rows, heads_local * HD)
    resid1 = resid + feature_sums(jnp.dot(mixed, out_weight, preferred_element_type=jnp.float32))
    normed2, inverse2 = normalize(resid1, width)
    inner2 = normed_rows(normed2.astype(jnp.bfloat16))
    gate_up = jnp.dot(inner2, gate_up_weight.reshape(width, -1), preferred_element_type=jnp.float32)
    gate = gate_up[:, :hidden_local]
    up = gate_up[:, hidden_local:]
    sigma = jax.nn.sigmoid(gate)
    active = gate * sigma
    hidden = (active * up).astype(jnp.bfloat16)
    branch = feature_sums(jnp.dot(hidden, down_weight, preferred_element_type=jnp.float32))
    layer_out = (resid1 + branch).astype(jnp.bfloat16)
    grad_full = grad_rows(cotangent)
    down_grad = jnp.einsum("tf,td->fd", hidden, grad_full, preferred_element_type=jnp.float32)
    grad_hidden = jnp.einsum(
        "td,fd->tf", grad_full, down_weight, preferred_element_type=jnp.float32
    )
    grad_gate = grad_hidden * up * sigma * (1.0 + gate * (1.0 - sigma))
    grad_gate_up = jnp.concatenate([grad_gate, grad_hidden * active], axis=1).astype(jnp.bfloat16)
    gate_up_grad = jnp.einsum(
        "td,tf->df", inner2, grad_gate_up, preferred_element_type=jnp.float32
    ).reshape(gate_up_weight.shape)
    grad_normed2 = feature_sums(
        jnp.einsum(
            "tf,df->td",
            grad_gate_up,
            gate_up_weight.reshape(width, -1),
            preferred_element_type=jnp.float32,
        )
    )
    resid1_grad = cotangent.astype(jnp.float32) + norm_back(grad_normed2, normed2, inverse2, width)
    branch_full = grad_rows(resid1_grad.astype(jnp.bfloat16))
    out_grad = jnp.einsum("tk,td->kd", mixed, branch_full, preferred_element_type=jnp.float32)
    grad_mixed = jnp.einsum(
        "td,kd->tk", branch_full, out_weight, preferred_element_type=jnp.float32
    )
    grad_mixed = grad_mixed.astype(jnp.bfloat16).reshape(rows, heads_local, HD)
    delta = jnp.transpose(jnp.sum(grad_mixed.astype(jnp.float32) * mixed_raw, axis=2))
    back_state = (
        jnp.zeros((rows, heads_local, HD), jnp.float32),
        jnp.zeros((rows * cycle_size, 2, heads_local, HD), jnp.float32),
    )
    backward_fn = guarded(
        backward_step(query, places, segment_ids, scale, log_total, delta, grad_mixed),
        last_place,
        first_seg,
    )
    back_fn = partial(by_blocks, backward_fn, size)
    grad_query, grad_pairs = back_fn(
        back_state,
        (
            lax.all_gather(key, "ctx", axis=0, tiled=True),
            lax.all_gather(value, "ctx", axis=0, tiled=True),
            lax.all_gather(segment_ids, "ctx", axis=0, tiled=True),
        ),
        jnp.int32(0),
    )
    own_pairs = lax.psum_scatter(
        grad_pairs.astype(jnp.bfloat16), "ctx", scatter_dimension=0, tiled=True
    ).astype(jnp.float32)
    grad_projected = (
        jnp.stack(
            [
                rotate_back(grad_query * scale, cosine, sine),
                rotate_back(own_pairs[:, 0] * scale, cosine, sine),
                own_pairs[:, 1],
            ],
            axis=1,
        )
        .astype(jnp.bfloat16)
        .reshape(rows, -1)
    )
    in_grad = jnp.einsum(
        "td,tk->dk", inner1, grad_projected, preferred_element_type=jnp.float32
    ).reshape(in_weight.shape)
    grad_normed1 = feature_sums(
        jnp.einsum(
            "tk,dk->td",
            grad_projected,
            in_weight.reshape(width, -1),
            preferred_element_type=jnp.float32,
        )
    )
    tokens_grad = resid1_grad + norm_back(grad_normed1, normed1, inverse1, width)
    in_grad, out_grad, gate_up_grad, down_grad = (
        lax.psum(in_grad.astype(jnp.bfloat16), "ctx").astype(jnp.float32),
        lax.psum(out_grad.astype(jnp.bfloat16), "ctx").astype(jnp.float32),
        lax.psum(gate_up_grad.astype(jnp.bfloat16), "ctx").astype(jnp.float32),
        lax.psum(down_grad.astype(jnp.bfloat16), "ctx").astype(jnp.float32),
    )
    return (layer_out, tokens_grad, in_grad, out_grad, gate_up_grad, down_grad)


def solution(mesh):
    placed = (
        P("ctx", "tp"),
        P("ctx"),
        P(None, None, "tp"),
        P("tp", None),
        P(None, None, "tp"),
        P("tp", None),
        P("ctx", "tp"),
    )
    return jax.shard_map(
        per_device,
        mesh=mesh,
        in_specs=placed,
        out_specs=(
            P("ctx", "tp"),
            P("ctx", "tp"),
            P(None, None, "tp"),
            P("tp", None),
            P(None, None, "tp"),
            P("tp", None),
        ),
        check_vma=False,
    )
```

profile of v0, /device:TPU:0, one launch (start us, length us, event | category | flops | bytes accessed | tf_op | source)
XLA Modules:
  0.0 1800.4 jit_solution(15519750821491032273)
XLA Ops:
  8.8 13.7 all-reduce.3
  36.2 50.5 %all-gather.9.cloned.1.call-done = bf16[768,2048]{1,0:T(8,128)(2,1)} async-done(((bf16[768,512]{1,0:T(8,128)(2,1)}), bf16[768,2048]{1,0:T(8,128)(2,1)}) %all-gather.9.cloned.1.call-update) | async-done | bytes 3145744 | tf_op jit(solution)/shard_map/all_gather | solution.py:33
  113.0 30.1 %all-gather.11.cloned.1.call-done = bf16[6144,4,128]{0,2,1:T(8,128)(2,1)} async-done(((bf16[768,4,128]{0,2,1:T(8,128)(2,1)}), bf16[6144,4,128]{0,2,1:T(8,128)(2,1)}) %all-gather.11.cloned.1.call-update) | async-done | bytes 6291472 | tf_op jit(solution)/shard_map/all_gather | solution.py:182
  160.2 30.8 %all-gather.19.cloned.1.call-done = bf16[6144,1,4,128]{0,3,2,1:T(8,128)(2,1)} async-done(((bf16[768,1,4,128]{0,3,2,1:T(8,128)(2,1)}), bf16[6144,1,4,128]{0,3,2,1:T(8,128)(2,1)}) %all-gather.19.cloned.1.call-update) | async-done | bytes 6291472 | tf_op jit(solution)/shard_map/all_gather | solution.py:183
  208.8 42.7 %while.28 = (s32[]{:T(128)}, f32[4,768]{1,0:T(4,128)S(1)}, f32[4,768]{1,0:T(4,128)S(1)}, f32[4,768,128]{2,1,0:T(8,128)}, s32[8]{0:T(128)S(1)}, /*index=5*/s32[]{...) while((s32[]{:T(128)}, f32[4,768]{1,0:T(4,128)S(1)}, ...), condition=%wide.region_9.10_spmd.clone, body=%wide.region_4.9_spmd.clone.sunk | while | flops 1241193984 | bytes 48993744 | solution.py:87
  212.5 12.5 conditional.6
  260.6 147.6 %reduce-scatter.6.cloned.1.call-done = bf16[768,512]{1,0:T(8,128)(2,1)} async-done(((bf16[768,2048]{1,0:T(8,128)(2,1)}), bf16[768,512]{1,0:T(8,128)(2,1)}) %reduce-scatter.6.cloned.1.call-update) | async-done | bytes 786448 | tf_op jit(solution)/shard_map/reduce_scatter | solution.py:41
  409.9 10.6 all-reduce.2
  423.8 17.5 copy.65
  441.3 43.8 %all-gather.13.cloned.1.call-done = bf16[768,2048]{1,0:T(8,128)(2,1)} async-done(((bf16[768,512]{1,0:T(8,128)(2,1)}), bf16[768,2048]{1,0:T(8,128)(2,1)}) %all-gather.13.cloned.1.call-update) | async-done | bytes 3145744 | tf_op jit(solution)/shard_map/all_gather | solution.py:33
  485.2 20.3 %fusion.80 = f32[768,4096]{1,0:T(8,128)} fusion(bf16[768,2048]{1,0:T(8,128)(2,1)} %all-gather.13.cloned.1.call-done, bf16[2048,4096]{1,0:T(8,128)(2,1)} %bitcast.165), kind=kOutput, calls=%fused_computation.150 | convolution fusion | flops 12884901888 | bytes 32505856 | tf_op jit(solution)/shard_map/dot_general | solution.py:194
  505.5 43.3 %all-gather.15.cloned.1.call-done = bf16[768,2048]{1,0:T(8,128)(2,1)} async-done(((bf16[768,512]{1,0:T(8,128)(2,1)}), bf16[768,2048]{1,0:T(8,128)(2,1)}) %all-gather.15.cloned.1.call-update) | async-done | bytes 3145744 | tf_op jit(solution)/shard_map/all_gather | solution.py:37
  548.8 17.2 multiply_convert_fusion.1
  566.0 19.9 %fusion.48 = bf16[768,2048]{1,0:T(8,128)(2,1)} fusion(bf16[2048,4096]{1,0:T(8,128)(2,1)} %bitcast.166, bf16[768,2048]{1,0:T(8,128)(2,1)} %get-tuple-element.607, bf16[768,2048]{1,0:T(8,128)(2,1)} %get-tuple-element.606), kind=kOutput, calls=%fused_computation.69 | convolution fusion | flops 12899057664 | bytes 26214400 | tf_op jit(solution)/shard_map/tf,df->td/dot_general | solution.py:213
  586.0 59.0 %reduce-scatter.10.cloned.1.call-done = bf16[768,512]{1,0:T(8,128)(2,1)} async-done(((bf16[768,2048]{1,0:T(8,128)(2,1)}), bf16[768,512]{1,0:T(8,128)(2,1)}) %reduce-scatter.10.cloned.1.call-update) | async-done | bytes 786448 | tf_op jit(solution)/shard_map/reduce_scatter | solution.py:41
  647.4 10.6 all-reduce.1
  661.6 61.9 %all-gather.17.cloned.1.call-done = bf16[768,2048]{1,0:T(8,128)(2,1)} async-done(((bf16[768,512]{1,0:T(8,128)(2,1)}), bf16[768,2048]{1,0:T(8,128)(2,1)}) %all-gather.17.cloned.1.call-update) | async-done | bytes 3145744 | tf_op jit(solution)/shard_map/all_gather | solution.py:37
  731.1 10.9 broadcast_in_dim.93
  742.0 70.7 %while.29 = (s32[]{:T(128)}, f32[768,4,128]{2,0,1:T(8,128)S(1)}, f32[6144,2,4,128]{3,0,2,1:T(8,128)}, s32[8]{0:T(128)S(1)}, s32[]{:T(128)}, /*index=5*/s32[8,768...) while((s32[]{:T(128)}, f32[768,4,128]{2,0,1:T(8,128)S(1)}, ...), condition=%wide.region_25.26_spmd.clone, body=%wide.region_22.25_spmd.clone.sunk | while | flops 3051947520 | bytes 103295016 | solution.py:87
  746.1 40.4 %conditional.7 = ((f32[768,4,128]{2,0,1:T(8,128)S(1)}, f32[6144,2,4,128]{3,0,2,1:T(8,128)})) conditional(s32[]{:T(128)} %convert_element_type.294, (f32[768,4,128]{2,0,1:T(8,128)S(1)}, f32[6144,2,4,128]{3,0,2,1:T(8,128)}) %tuple.106, (s32[768]{0:T(1024)S(1)}, s32[1,768]{1,0:T(1,128)S(1)}, s32[]{:T(128)}, s32[]{:T(128)}, ...), branch_computations={%region_23.23_spmd, %region_24.24_spmd} | conditional | flops 3051947520 | bytes 103285416 | solution.py:70
  775.2 11.2 dynamic_update_slice.4
  812.8 19.2 %copy.55 = bf16[6144,2,4,128]{0,3,2,1:T(8,128)(2,1)} copy(f32[6144,2,4,128]{3,0,2,1:T(8,128)} %get-tuple-element.364) | data formatting | bytes 37748736 | tf_op jit(solution)/shard_map/while | solution.py:87
  833.8 371.1 %reduce-scatter.12.cloned.1.call-done = bf16[768,2,4,128]{0,3,2,1:T(8,128)(2,1)} async-done(((bf16[6144,2,4,128]{0,3,2,1:T(8,128)(2,1)}), bf16[768,2,4,128]{0,3,2,1:T(8,128)(2,1)}) %reduce-scatter.12.cloned.1.call-update) | async-done | bytes 1572880 | tf_op jit(solution)/shard_map/reduce_scatter | solution.py:247
  1218.7 11.9 convolution_convert_fusion.3
  1230.9 20.3 %convolution_convert_fusion = bf16[2048,4096]{1,0:T(8,128)(2,1)} fusion(bf16[768,2048]{1,0:T(8,128)(2,1)} %all-gather.13.cloned.1.call-done, bf16[768,2048]{1,0:T(8,128)(2,1)} %get-tuple-element.607, bf16[768,2048]{1,0:T(8,128)(2,1)} %get-tuple-element.606), kind=kOutput, calls=%fused_computation.56 | convolution fusion | flops 12905873408 | bytes 26214400 | tf_op jit(solution)/shard_map/td,tf->df/dot_general | solution.py:209
  1251.3 27.8 %convert_element_type.171 = bf16[2048,2,2048]{2,1,0:T(2,128)(2,1)} reshape(bf16[2048,4096]{1,0:T(8,128)(2,1)} %convolution_convert_fusion) | data formatting | bytes 33554432 | tf_op jit(solution)/shard_map/convert_element_type | solution.py:277
  1279.1 11.5 convolution_convert_fusion.1
  1304.3 12.7 all-reduce
  1317.1 25.1 %reduce-scatter.8.cloned.1.call-done = bf16[768,512]{1,0:T(8,128)(2,1)} async-done(((bf16[768,2048]{1,0:T(8,128)(2,1)}), bf16[768,512]{1,0:T(8,128)(2,1)}) %reduce-scatter.8.cloned.1.call-update) | async-done | bytes 786448 | tf_op jit(solution)/shard_map/reduce_scatter | solution.py:41
  1345.9 402.0 %all-reduce.7.cloned.1.call-done = (bf16[2048,3,512]{2,0,1:T(8,128)(2,1)}, bf16[512,2048]{1,0:T(8,128)(2,1)}, bf16[2048,2,2048]{2,1,0:T(2,128)(2,1)}, bf16[2048,2048]{1,0:T(8,128)(2,1)}) async-done(((bf16[2048,3,512]{2,0,1:T(8,128)(2,1)}, bf16[512,2048]{1,0:T(8,128)(2,1)}, bf16[2048,2,2048]{2,1,0:T(2,128)(2,1)}, bf16[2048,2048]{1,0:T(8,128)(2,1)}), (bf16[2048,3,512]{2,0,1:T(8,128)(2,1)}, ...) | async-done | bytes 33554448 | tf_op jit(solution)/shard_map/psum | solution.py:275
  1760.0 21.5 %convert_element_type.172 = f32[2048,2,2048]{2,1,0:T(2,128)} convert(bf16[2048,2,2048]{2,1,0:T(2,128)(2,1)} %get-tuple-element.596) | non-fusion elementwise | flops 8388608 | bytes 50331648 | tf_op jit(solution)/shard_map/convert_element_type | solution.py:277
  1781.4 11.8 convert_element_type.174
  (260 shorter events, 209.6 us)
Async XLA Ops:
  7.2 249.8 %copy-start = (bf16[512,2048]{1,0:T(8,128)(2,1)S(1)}, bf16[512,2048]{1,0:T(8,128)(2,1)}, u32[]{:S(2)}) copy-start(bf16[512,2048]{1,0:T(8,128)(2,1)} %param.18) | copy-start | bytes 6291460
  7.2 79.5 %all-gather.9.cloned.1.call-start = ((), (), s32[]{:S(2)}) async-start(), calls=%async_computation.5 | async-start | bytes 3932160 | tf_op jit(solution)/shard_map/all_gather | solution.py:33
  22.5 11.3 copy-start.24
  22.5 11.3 copy-start.26
  24.9 118.3 %all-gather.11.cloned.1.call-start = ((), (), s32[]{:S(2)}) async-start(), calls=%async_computation.6 | async-start | bytes 7077888 | tf_op jit(solution)/shard_map/all_gather | solution.py:182
  98.9 92.1 %all-gather.19.cloned.1.call-start = ((), (), s32[]{:S(2)}) async-start(), calls=%async_computation.15 | async-start | bytes 7077888 | tf_op jit(solution)/shard_map/all_gather | solution.py:183
  101.3 306.8 %reduce-scatter.6.cloned.1.call-start = ((), (), s32[]{:S(2)}) async-start(), calls=%async_computation.7 | async-start | bytes 3932160 | tf_op jit(solution)/shard_map/reduce_scatter | solution.py:41
  260.5 224.7 %all-gather.13.cloned.1.call-start = ((), (), s32[]{:S(2)}) async-start(), calls=%async_computation.8 | async-start | bytes 3932160 | tf_op jit(solution)/shard_map/all_gather | solution.py:33
  420.5 237.5 %copy-start.20 = (f32[768]{0:T(1024)}, f32[768]{0:T(1024)S(1)}, u32[]{:S(2)}) copy-start(f32[768]{0:T(1024)S(1)} %get-tuple-element.629) | copy-start | bytes 9220
  420.5 237.5 %copy-start.22 = (f32[768]{0:T(1024)}, f32[768]{0:T(1024)S(1)}, u32[]{:S(2)}) copy-start(f32[768]{0:T(1024)S(1)} %get-tuple-element.630) | copy-start | bytes 9220
  423.1 125.6 %all-gather.15.cloned.1.call-start = ((), (), s32[]{:S(2)}) async-start(), calls=%async_computation.10 | async-start | bytes 3932160 | tf_op jit(solution)/shard_map/all_gather | solution.py:37
  423.7 221.3 %reduce-scatter.10.cloned.1.call-start = ((), (), s32[]{:S(2)}) async-start(), calls=%async_computation.11 | async-start | bytes 3932160 | tf_op jit(solution)/shard_map/reduce_scatter | solution.py:41
  585.9 137.6 %all-gather.17.cloned.1.call-start = ((), (), s32[]{:S(2)}) async-start(), calls=%async_computation.12 | async-start | bytes 3932160 | tf_op jit(solution)/shard_map/all_gather | solution.py:37
  658.0 70.6 %copy-start.28 = (f32[768]{0:T(1024)}, f32[768]{0:T(1024)S(1)}, u32[]{:S(2)}) copy-start(f32[768]{0:T(1024)S(1)} %broadcast_multiply_fusion.6) | copy-start | bytes 9220
  658.1 70.5 %copy-start.30 = (f32[768]{0:T(1024)}, f32[768]{0:T(1024)S(1)}, u32[]{:S(2)}) copy-start(f32[768]{0:T(1024)S(1)} %broadcast_multiply_fusion.7) | copy-start | bytes 9220
  661.6 543.4 %reduce-scatter.12.cloned.1.call-start = ((), (), s32[]{:S(2)}) async-start(), calls=%async_computation.13 | async-start | bytes 14155776 | tf_op jit(solution)/shard_map/reduce_scatter | solution.py:247
  752.4 11.7 slice-start
  753.0 11.2 slice-start.1
  832.0 469.3 %reduce-scatter.14.cloned.1.call-start = ((), (), s32[]{:S(2)}) async-start(), calls=%async_computation.14 | async-start | bytes 3932160 | tf_op jit(solution)/shard_map/reduce_scatter | solution.py:41
  833.8 372.8 %copy-start.4 = (f32[768,4,128]{0,2,1:T(8,128)S(1)}, f32[768,4,128]{0,2,1:T(8,128)}, u32[]{:S(2)}) copy-start(f32[768,4,128]{0,2,1:T(8,128)} %copy.53) | copy-start | bytes 4718596
  833.8 372.8 %copy-start.15 = (f32[768,128]{0,1:T(8,128)S(1)}, f32[768,128]{0,1:T(8,128)}, u32[]{:S(2)}) copy-start(f32[768,128]{0,1:T(8,128)} %get-tuple-element.626) | copy-start | bytes 1179652
  1218.7 123.6 %reduce-scatter.8.cloned.1.call-start = ((), (), s32[]{:S(2)}) async-start(), calls=%async_computation.9 | async-start | bytes 3932160 | tf_op jit(solution)/shard_map/reduce_scatter | solution.py:41
  1230.7 517.2 %all-reduce.7.cloned.1.call-start = ((), (), s32[]{:S(2)}) async-start(), calls=%async_computation.16 | async-start | bytes 67108864 | tf_op jit(solution)/shard_map/psum | solution.py:275
  1279.1 11.5 copy-start.10
  1279.1 11.5 copy-start.18
  1301.2 41.0 %copy-start.3 = (bf16[768,512]{1,0:T(8,128)(2,1)S(1)}, bf16[768,512]{1,0:T(8,128)(2,1)}, u32[]{:S(2)}) copy-start(bf16[768,512]{1,0:T(8,128)(2,1)} %reduce-scatter.6.cloned.1.call-done) | copy-start | bytes 2359300
  1301.2 41.0 %copy-start.6 = (bf16[768,512]{1,0:T(8,128)(2,1)S(1)}, bf16[768,512]{1,0:T(8,128)(2,1)}, u32[]{:S(2)}) copy-start(bf16[768,512]{1,0:T(8,128)(2,1)} %param.21) | copy-start | bytes 2359300
  1301.2 41.0 %copy-start.21 = (f32[768]{0:T(1024)S(1)}, f32[768]{0:T(1024)}, u32[]{:S(2)}) copy-start(f32[768]{0:T(1024)} %copy-done.20) | copy-start | bytes 9220
  1301.2 41.0 %copy-start.23 = (f32[768]{0:T(1024)S(1)}, f32[768]{0:T(1024)}, u32[]{:S(2)}) copy-start(f32[768]{0:T(1024)} %copy-done.22) | copy-start | bytes 9220
  1301.2 41.0 %copy-start.29 = (f32[768]{0:T(1024)S(1)}, f32[768]{0:T(1024)}, u32[]{:S(2)}) copy-start(f32[768]{0:T(1024)} %copy-done.28) | copy-start | bytes 9220
  1301.2 41.0 %copy-start.31 = (f32[768]{0:T(1024)S(1)}, f32[768]{0:T(1024)}, u32[]{:S(2)}) copy-start(f32[768]{0:T(1024)} %copy-done.30) | copy-start | bytes 9220
  1781.4 11.8 copy-start.1
  (19 other events, 57.5 us)
Sparse Core Ops, SparseCore 0:
  25.0 61.6 all-gather.8
  99.0 44.0 all-gather.10
  145.6 45.3 all-gather.18
  260.6 147.4 reduce-scatter.5
  423.3 61.8 all-gather.12
  486.6 62.1 all-gather.14
  586.1 58.9 reduce-scatter.9
  661.7 61.8 all-gather.16
  832.1 372.7 reduce-scatter.11
  1218.8 60.2 reduce-scatter.13
  1281.4 60.8 reduce-scatter.7
  1347.0 400.8 all-reduce.6
where the time goes:
time: 1810 us; the launch traced here: 1800 us
  waiting for transfers between devices  1270 us (70%)
  local copies, waits for them, and re-layouts  171 us (9%)
  matrix products  167 us (9%)
  other arithmetic  82.3 us (5%)
  blocking collectives  56.6 us (3%)
  loops' own time  41.7 us (2%)
    psum x1, waiting for transfers between devices, per_device(): lax.psum(in_grad.astype(jnp.bfloat16), 'ctx').astype(jnp.float32)  402 us
    reduce_scatter x1, waiting for transfers between devices, per_device(): lax.psum_scatter(grad_pairs.astype(jnp.bfloat16), 'ctx', scatter_dimensio...  371 us
    reduce_scatter x4, waiting for transfers between devices, feature_sums(): lax.psum_scatter(partial_sum.astype(jnp.bfloat16), 'tp', scatter_dimensio...  232 us
    all_gather x2, waiting for transfers between devices, grad_rows(): return lax.all_gather(local, 'tp', axis=1, tiled=True)  105 us
    all_gather x2, waiting for transfers between devices, normed_rows(): return lax.all_gather(local, 'tp', axis=1, tiled=True)  94.3 us
    unnamed x74, local copies, waits for them, and re-layouts  69.7 us
    psum x4, blocking collectives, row_sums(): return lax.psum((first, second), 'tp')  47.7 us
    another operation x2, loops' own time, by_blocks(): lax.scan(turn, carry, (stacked, jnp.arange(number, dtype=jnp.int32)))  41.3 us
  transfers between devices with their start and end apart: 12, of which 11 were waited for; matrix products, arithmetic and copies ran while one was open for 9% of the time, Pallas kernels for 0%

commit v1 on v0

v1 whole, which is shorter than its diff:
```python
import functools

import jax
import jax.numpy as jnp
from jax import lax
from jax.experimental import pallas as pl
from jax.experimental.pallas import tpu as pltpu
from jax.sharding import PartitionSpec as P

HD = 128
EPS = 1e-05
NEG = -1e30
SCALE = HD ** (-0.5)
LOG2E = 1.4426950408889634
C2 = SCALE * LOG2E
F32 = jnp.float32
BF16 = jnp.bfloat16
NT = (((1,), (1,)), ((), ()))
TN = (((0,), (0,)), ((), ()))


def params(mib, **more):
    return pltpu.CompilerParams(vmem_limit_bytes=mib << 20, **more)


def cost(flops, nbytes, trans=0):
    return pl.CostEstimate(flops=int(flops), bytes_accessed=int(nbytes), transcendentals=int(trans))


def rope_tables(places):
    half = HD // 2
    freq = 10000.0 ** (-jnp.arange(half, dtype=F32) * 2.0 / HD)
    angle = places.astype(F32)[:, None] * freq[None, :]
    cosine, sine = jnp.cos(angle), jnp.sin(angle)
    return jnp.concatenate([cosine, cosine], axis=1), jnp.concatenate([-sine, sine], axis=1)


def project_kernel(heads, tok_ref, w_ref, cos_ref, sin_ref, inner_ref, stat_ref, q_ref, kv_ref):
    x = tok_ref[...].astype(F32)
    center = x - jnp.mean(x, axis=1, keepdims=True)
    inverse = lax.rsqrt(jnp.mean(center * center, axis=1, keepdims=True) + EPS)
    inner = (center * inverse).astype(BF16)
    inner_ref[...] = inner
    stat_ref[...] = jnp.concatenate(
        [jnp.mean(x, axis=1, keepdims=True), inverse], axis=1
    )
    cosine, sine = cos_ref[...], sin_ref[...]
    span = heads * HD
    for part in range(3):
        out = jnp.dot(inner, w_ref[part], preferred_element_type=F32)
        if part == 2:
            kv_ref[:, span:] = out.astype(BF16)
            continue
        for h in range(heads):
            piece = out[:, h * HD : (h + 1) * HD]
            turned = (piece * cosine + pltpu.roll(piece, HD // 2, 1) * sine).astype(BF16)
            if part == 0:
                q_ref[:, h * HD : (h + 1) * HD] = turned
            else:
                kv_ref[:, h * HD : (h + 1) * HD] = turned


def project(tok_full, weight, cosine, sine, heads):
    rows, width = tok_full.shape
    span = heads * HD
    block = 256
    row = lambda n: pl.BlockSpec((block, n), lambda i: (i, 0))
    return pl.pallas_call(
        functools.partial(project_kernel, heads),
        grid=(rows // block,),
        in_specs=[
            row(width),
            pl.BlockSpec((3, width, span), lambda i: (0, 0, 0)),
            row(HD),
            row(HD),
        ],
        out_specs=[row(width), row(2), row(span), row(2 * span)],
        out_shape=[
            jax.ShapeDtypeStruct((rows, width), BF16),
            jax.ShapeDtypeStruct((rows, 2), F32),
            jax.ShapeDtypeStruct((rows, span), BF16),
            jax.ShapeDtypeStruct((rows, 2 * span), BF16),
        ],
        compiler_params=params(56),
        cost_estimate=cost(6 * rows * width * span, 6 * width * span + 6 * rows * width),
        name="project",
    )(tok_full, weight, cosine, sine)


def masked(scores, j, me, rows, begin):
    key_place = lax.broadcasted_iota(jnp.int32, scores.shape, 0) + j * rows
    query_place = lax.broadcasted_iota(jnp.int32, scores.shape, 1) + me * rows
    return jnp.where((key_place <= query_place) & (key_place >= begin), scores, NEG)


def attend_kernel(
    heads, info, q_ref, k_ref, v_ref, begin_ref, raw_ref, mixed_ref, lse_ref,
    high_ref, total_ref, acc_ref, s_ref,
):
    me, first, clear = info[0], info[1], info[2]
    j = pl.program_id(0)
    rows = q_ref.shape[0]

    @pl.when(j == 0)
    def _():
        high_ref[...] = jnp.full_like(high_ref, NEG)
        total_ref[...] = jnp.zeros_like(total_ref)
        acc_ref[...] = jnp.zeros_like(acc_ref)

    def block(hide):
        def score(h):
            hs = slice(h * HD, (h + 1) * HD)
            s = lax.dot_general(k_ref[:, hs], q_ref[:, hs], NT, preferred_element_type=F32)
            if hide:
                s = masked(s, j, me, rows, begin_ref[...])
            s_ref[h % 2] = s

        def spread(h):
            hs = slice(h * HD, (h + 1) * HD)
            s = s_ref[h % 2]
            old = high_ref[h : h + 1, :]
            new = jnp.maximum(old, jnp.max(s, axis=0, keepdims=True))
            high_ref[h : h + 1, :] = new
            p = jnp.exp2(s * C2 - new * C2)
            decay = jnp.exp2((old - new) * C2)
            total_ref[h : h + 1, :] = total_ref[h : h + 1, :] * decay + jnp.sum(
                p, axis=0, keepdims=True
            )
            acc_ref[h] = acc_ref[h] * decay + lax.dot_general(
                v_ref[:, hs], p.astype(BF16), TN, preferred_element_type=F32
            )

        score(0)
        for h in range(heads):
            if h + 1 < heads:
                score(h + 1)
            spread(h)

    @pl.when((j >= clear) & (j < me))
    def _():
        block(False)

    @pl.when(((j >= first) & (j < clear) & (j < me)) | (j == me))
    def _():
        block(True)

    @pl.when(j == me)
    def _():
        for h in range(heads):
            hs = slice(h * HD, (h + 1) * HD)
            out = (acc_ref[h] / total_ref[h : h + 1, :]).T
            raw_ref[:, hs] = out
            mixed_ref[:, hs] = out.astype(BF16)
        lse_ref[...] = high_ref[...] * C2 + jnp.log2(total_ref[...])


def attend(info, query, pairs, begin, heads):
    rows = query.shape[0]
    total = pairs.shape[0]
    span = heads * HD
    full = lambda shape: pl.BlockSpec(shape, lambda j, s: (0, 0))
    key = pl.BlockSpec((rows, span), lambda j, s: (jnp.clip(j, s[1], s[0]), 0))
    value = pl.BlockSpec((rows, span), lambda j, s: (jnp.clip(j, s[1], s[0]), 1))
    return pl.pallas_call(
        functools.partial(attend_kernel, heads),
        grid_spec=pltpu.PrefetchScalarGridSpec(
            num_scalar_prefetch=1,
            grid=(total // rows,),
            in_specs=[full((rows, span)), key, value, full((1, rows))],
            out_specs=[full((rows, span)), full((rows, span)), full((heads, rows))],
            scratch_shapes=[
                pltpu.VMEM((heads, rows), F32),
                pltpu.VMEM((heads, rows), F32),
                pltpu.VMEM((heads, HD, rows), F32),
                pltpu.VMEM((2, rows, rows), F32),
            ],
        ),
        out_shape=[
            jax.ShapeDtypeStruct((rows, span), F32),
            jax.ShapeDtypeStruct((rows, span), BF16),
            jax.ShapeDtypeStruct((heads, rows), F32),
        ],
        compiler_params=params(56),
        cost_estimate=cost(4 * rows * total * span, 4 * total * span, rows * total * heads),
        name="attend",
    )(info, query, pairs, pairs, begin)


def attend_back_kernel(
    heads, info, q_ref, do_ref, raw_ref, lse_ref, k_ref, v_ref, begin_ref,
    dq_ref, dpair_ref, acc_ref, delta_ref, s_ref, g_ref,
):
    me, first, clear = info[0], info[1], info[2]
    j = pl.program_id(0)
    rows = q_ref.shape[0]
    span = heads * HD

    @pl.when(j == 0)
    def _():
        acc_ref[...] = jnp.zeros_like(acc_ref)
        for h in range(heads):
            hs = slice(h * HD, (h + 1) * HD)
            both = do_ref[:, hs].astype(F32) * raw_ref[:, hs]
            delta_ref[h : h + 1, :] = jnp.sum(both.T, axis=0, keepdims=True)

    def block(hide):
        def score(h):
            hs = slice(h * HD, (h + 1) * HD)
            s = lax.dot_general(k_ref[:, hs], q_ref[:, hs], NT, preferred_element_type=F32)
            if hide:
                s = masked(s, j, me, rows, begin_ref[...])
            s_ref[h % 2] = s
            g_ref[h % 2] = lax.dot_general(
                v_ref[:, hs], do_ref[:, hs], NT, preferred_element_type=F32
            )

        def spread(h):
            hs = slice(h * HD, (h + 1) * HD)
            p = jnp.exp2(s_ref[h % 2] * C2 - lse_ref[h : h + 1, :])
            ds = (p * (g_ref[h % 2] - delta_ref[h : h + 1, :])).astype(BF16)
            dv = jnp.dot(p.astype(BF16), do_ref[:, hs], preferred_element_type=F32)
            dk = jnp.dot(ds, q_ref[:, hs], preferred_element_type=F32)
            dpair_ref[:, hs] = (dk * SCALE).astype(BF16)
            dpair_ref[:, span + h * HD : span + (h + 1) * HD] = dv.astype(BF16)
            acc_ref[h] = acc_ref[h] + lax.dot_general(
                k_ref[:, hs], ds, TN, preferred_element_type=F32
            )

        score(0)
        for h in range(heads):
            if h + 1 < heads:
                score(h + 1)
            spread(h)

    @pl.when((j >= clear) & (j < me))
    def _():
        block(False)

    @pl.when(((j >= first) & (j < clear) & (j < me)) | (j == me))
    def _():
        block(True)

    @pl.when((j < first) | (j > me))
    def _():
        dpair_ref[...] = jnp.zeros_like(dpair_ref)

    @pl.when(j == me)
    def _():
        for h in range(heads):
            dq_ref[:, h * HD : (h + 1) * HD] = (acc_ref[h] * SCALE).T


def attend_back(info, query, grad_mixed, raw, lse, pairs, begin, heads):
    rows = query.shape[0]
    total = pairs.shape[0]
    span = heads * HD
    full = lambda shape: pl.BlockSpec(shape, lambda j, s: (0, 0))
    key = pl.BlockSpec((rows, span), lambda j, s: (jnp.clip(j, s[1], s[0]), 0))
    value = pl.BlockSpec((rows, span), lambda j, s: (jnp.clip(j, s[1], s[0]), 1))
    wide = full((rows, span))
    return pl.pallas_call(
        functools.partial(attend_back_kernel, heads),
        grid_spec=pltpu.PrefetchScalarGridSpec(
            num_scalar_prefetch=1,
            grid=(total // rows,),
            in_specs=[wide, wide, wide, full((heads, rows)), key, value, full((1, rows))],
            out_specs=[wide, pl.BlockSpec((rows, 2 * span), lambda j, s: (j, 0))],
            scratch_shapes=[
                pltpu.VMEM((heads, HD, rows), F32),
                pltpu.VMEM((heads, rows), F32),
                pltpu.VMEM((2, rows, rows), F32),
                pltpu.VMEM((2, rows, rows), F32),
            ],
        ),
        out_shape=[
            jax.ShapeDtypeStruct((rows, span), F32),
            jax.ShapeDtypeStruct((total, 2 * span), BF16),
        ],
        compiler_params=params(58),
        cost_estimate=cost(10 * rows * total * span, 8 * total * span, rows * total * heads),
        name="attend_back",
    )(info, query, grad_mixed, raw, lse, pairs, pairs, begin)


def merge_kernel(mixed_ref, w_ref, tok_ref, resid_ref, stat_ref, inner_ref):
    out = jnp.dot(mixed_ref[...], w_ref[...], preferred_element_type=F32)
    x = tok_ref[...].astype(F32) + out
    resid_ref[...] = x
    mean = jnp.mean(x, axis=1, keepdims=True)
    center = x - mean
    inverse = lax.rsqrt(jnp.mean(center * center, axis=1, keepdims=True) + EPS)
    stat_ref[...] = jnp.concatenate([mean, inverse], axis=1)
    inner_ref[...] = (center * inverse).astype(BF16)


def merge(mixed_full, weight, tok_full):
    rows, width = tok_full.shape
    block = 256
    row = lambda n: pl.BlockSpec((block, n), lambda i: (i, 0))
    return pl.pallas_call(
        merge_kernel,
        grid=(rows // block,),
        in_specs=[row(width), pl.BlockSpec((width, width), lambda i: (0, 0)), row(width)],
        out_specs=[row(width), row(2), row(width)],
        out_shape=[
            jax.ShapeDtypeStruct((rows, width), F32),
            jax.ShapeDtypeStruct((rows, 2), F32),
            jax.ShapeDtypeStruct((rows, width), BF16),
        ],
        compiler_params=params(56),
        cost_estimate=cost(2 * rows * width * width, 2 * width * width + 10 * rows * width),
        name="merge",
    )(mixed_full, weight, tok_full)


def unproject_kernel(
    heads, dq_ref, dpair_ref, cos_ref, sin_ref, tok_ref, stat_ref, w_ref,
    dproj_ref, part_ref, sums_ref,
):
    cosine, sine = cos_ref[...], sin_ref[...]
    span = heads * HD

    def back(piece):
        return piece * cosine - pltpu.roll(piece, HD // 2, 1) * sine

    for h in range(heads):
        hs = slice(h * HD, (h + 1) * HD)
        dproj_ref[:, hs] = back(dq_ref[:, hs]).astype(BF16)
        dproj_ref[:, span + h * HD : span + (h + 1) * HD] = back(
            dpair_ref[:, hs].astype(F32)
        ).astype(BF16)
    dproj_ref[:, 2 * span :] = dpair_ref[:, span:]
    total = None
    for part in range(3):
        term = lax.dot_general(
            dproj_ref[:, part * span : (part + 1) * span], w_ref[part], NT,
            preferred_element_type=F32,
        )
        total = term if total is None else total + term
    part_ref[...] = total.astype(BF16)
    normed = (tok_ref[...].astype(F32) - stat_ref[:, 0:1]) * stat_ref[:, 1:2]
    sums_ref[...] = jnp.concatenate(
        [
            jnp.sum(total, axis=1, keepdims=True),
            jnp.sum(total * normed, axis=1, keepdims=True),
        ],
        axis=1,
    )


def unproject(dq, own_pairs, cosine, sine, tok_full, stat, weight, heads):
    rows, width = tok_full.shape
    span = heads * HD
    block = 256
    row = lambda n: pl.BlockSpec((block, n), lambda i: (i, 0))
    return pl.pallas_call(
        functools.partial(unproject_kernel, heads),
        grid=(rows // block,),
        in_specs=[
            row(span), row(2 * span), row(HD), row(HD), row(width), row(2),
            pl.BlockSpec((3, width, span), lambda i: (0, 0, 0)),
        ],
        out_specs=[row(3 * span), row(width), row(2)],
        out_shape=[
            jax.ShapeDtypeStruct((rows, 3 * span), BF16),
            jax.ShapeDtypeStruct((rows, width), BF16),
            jax.ShapeDtypeStruct((rows, 2), F32),
        ],
        compiler_params=params(56),
        cost_estimate=cost(6 * rows * width * span, 6 * width * span + 6 * rows * width),
        name="unproject",
    )(dq, own_pairs, cosine, sine, tok_full, stat, weight)


def per_device(tokens, segment_ids, in_weight, out_weight, gate_up_weight, down_weight, cotangent):
    rows, shard = tokens.shape
    width = in_weight.shape[0]
    span = in_weight.shape[2]
    heads = span // HD
    hidden_local = down_weight.shape[0]
    me = lax.axis_index("ctx")
    tp_at = lax.axis_index("tp")

    def own(whole):
        return lax.dynamic_slice_in_dim(whole, tp_at * shard, shard, axis=1)

    def gather(local, axis=1):
        return lax.all_gather(local, "tp", axis=axis, tiled=True)

    places = me * rows + jnp.arange(rows, dtype=jnp.int32)
    cosine, sine = rope_tables(places)
    in_w = jnp.transpose(in_weight, (1, 0, 2))
    gate_w, up_w = lax.optimization_barrier((gate_up_weight[:, 0, :], gate_up_weight[:, 1, :]))

    all_seg = lax.all_gather(segment_ids, "ctx", axis=0, tiled=True)
    before = jnp.sum((all_seg < segment_ids[0]).astype(jnp.int32))
    own_begin = me * rows + jnp.sum(
        (segment_ids[None, :] < segment_ids[:, None]).astype(jnp.int32), axis=1
    )
    begin = jnp.where(segment_ids == segment_ids[0], before, own_begin).astype(jnp.int32)
    last = jnp.max(begin)
    info = jnp.stack([me, before // rows, (last + rows - 1) // rows]).astype(jnp.int32)
    begin = begin[None, :]

    tok_full = gather(tokens)
    inner1, stat1, query, pairs = project(tok_full, in_w, cosine, sine, heads)
    all_pairs = lax.all_gather(pairs, "ctx", axis=0, tiled=True)
    out_full = gather(out_weight, 0)
    cot_full = gather(cotangent)
    raw, mixed, lse = attend(info, query, all_pairs, begin, heads)
    resid1, stat2, inner2 = merge(gather(mixed), out_full, tok_full)

    gate = jnp.dot(inner2, gate_w, preferred_element_type=F32)
    up = jnp.dot(inner2, up_w, preferred_element_type=F32)
    sigma = jax.nn.sigmoid(gate)
    active = gate * sigma
    hidden = (active * up).astype(BF16)
    branch = jnp.dot(hidden, down_weight, preferred_element_type=F32).astype(BF16)
    branch = lax.psum_scatter(branch, "tp", scatter_dimension=1, tiled=True)
    layer_out = (own(resid1) + branch.astype(F32)).astype(BF16)

    grad_hidden = lax.dot_general(cot_full, down_weight, NT, preferred_element_type=F32)
    grad_gate = (grad_hidden * up * sigma * (1.0 + gate * (1.0 - sigma))).astype(BF16)
    grad_up = (grad_hidden * active).astype(BF16)
    grad_normed2 = lax.dot_general(
        grad_gate, gate_w, NT, preferred_element_type=F32
    ) + lax.dot_general(grad_up, up_w, NT, preferred_element_type=F32)
    grad_normed2 = lax.psum(grad_normed2.astype(BF16), "tp").astype(F32)

    down_grad = lax.dot_general(hidden, cot_full, TN, preferred_element_type=F32)
    gate_grad = lax.dot_general(inner2, grad_gate, TN, preferred_element_type=F32)
    up_grad = lax.dot_general(inner2, grad_up, TN, preferred_element_type=F32)
    down_grad, gate_grad, up_grad = lax.optimization_barrier(
        lax.psum(
            lax.optimization_barrier(
                (down_grad.astype(BF16), gate_grad.astype(BF16), up_grad.astype(BF16))
            ),
            "ctx",
        )
    )

    normed2 = (resid1 - stat2[:, 0:1]) * stat2[:, 1:2]
    mean_g = jnp.mean(grad_normed2, axis=1, keepdims=True)
    mean_gn = jnp.mean(grad_normed2 * normed2, axis=1, keepdims=True)
    resid1_grad = cot_full.astype(F32) + stat2[:, 1:2] * (
        grad_normed2 - mean_g - normed2 * mean_gn
    )
    branch_grad = resid1_grad.astype(BF16)
    grad_mixed = lax.dot_general(
        branch_grad, out_weight, NT, preferred_element_type=F32
    ).astype(BF16)
    out_grad = lax.dot_general(mixed, branch_grad, TN, preferred_element_type=F32).astype(BF16)

    dq, dpairs = attend_back(info, query, grad_mixed, raw, lse, all_pairs, begin, heads)
    own_pairs = lax.psum_scatter(dpairs, "ctx", scatter_dimension=0, tiled=True)
    dproj, part, sums = unproject(dq, own_pairs, cosine, sine, tok_full, stat1, in_w, heads)
    grad_normed1 = lax.psum_scatter(part, "tp", scatter_dimension=1, tiled=True).astype(F32)
    sums = lax.psum(sums, "tp") / width
    in_grad = jnp.stack(
        [
            lax.dot_general(
                inner1, dproj[:, i * span : (i + 1) * span], TN, preferred_element_type=F32
            ).astype(BF16)
            for i in range(3)
        ]
    )
    in_grad, out_grad, down_grad = lax.optimization_barrier((in_grad, out_grad, down_grad))
    in_grad, out_grad = lax.psum((in_grad, out_grad), "ctx")

    normed1 = (tokens.astype(F32) - stat1[:, 0:1]) * stat1[:, 1:2]
    tokens_grad = own(resid1_grad) + stat1[:, 1:2] * (
        grad_normed1 - sums[:, 0:1] - normed1 * sums[:, 1:2]
    )
    return (
        layer_out,
        tokens_grad,
        jnp.transpose(in_grad, (1, 0, 2)).astype(F32),
        out_grad.astype(F32),
        jnp.stack([gate_grad.astype(F32), up_grad.astype(F32)], axis=1),
        down_grad.astype(F32),
    )


def solution(mesh):
    placed = (
        P("ctx", "tp"),
        P("ctx"),
        P(None, None, "tp"),
        P("tp", None),
        P(None, None, "tp"),
        P("tp", None),
        P("ctx", "tp"),
    )
    return jax.shard_map(
        per_device,
        mesh=mesh,
        in_specs=placed,
        out_specs=(
            P("ctx", "tp"),
            P("ctx", "tp"),
            P(None, None, "tp"),
            P("tp", None),
            P(None, None, "tp"),
            P("tp", None),
        ),
        check_vma=False,
    )
```

time: 1810 us -> 1290 us (0.71)
  waiting for transfers between devices: 1270 us -> 867 us
  Pallas kernels: 0 us -> 61.4 us
  local copies, waits for them, and re-layouts: 171 us -> 110 us
  matrix products: 167 us -> 119 us
  loops' own time: 41.7 us -> 0 us
  blocking collectives: 56.6 us -> 36.1 us
    reduce_scatter x5 -> x3, waiting for transfers between devices: 603 us -> 188 us  [the longest x1 97 us: per_device(): own_pairs = lax.psum_scatter(dpairs, 'ctx', scatter_dimension=0, tiled=True)]
    pallas_call x0 -> x5, Pallas kernels: none -> 61.4 us  [the longest x1 16.4 us: attend_back(): pl.pallas_call(functools.partial(attend_back_kernel, heads), grid_spec=pl...]
    dot_general x19 -> x14, matrix products: 167 us -> 119 us  [the longest x1 17.7 us: per_device(): lax.dot_general(cot_full, down_weight, NT, preferred_element_type=F32)]
    another operation x18 -> x0, loops' own time: 41.7 us -> none  [the longest x2 41.3 us: by_blocks(): lax.scan(turn, carry, (stacked, jnp.arange(number, dtype=jnp.int32)))]
    all_gather x6 -> x5, waiting for transfers between devices: 260 us -> 297 us  [the longest x4 231 us: gather(): return lax.all_gather(local, 'tp', axis=axis, tiled=True)]
    convert_element_type x11 -> x4, other arithmetic: 58.9 us -> 26.6 us  [the longest x1 11.8 us: per_device(): down_grad.astype(F32)]
    convert_element_type x1 -> x0, local copies, waits for them, and re-layouts: 27.8 us -> none  [per_device(): gate_up_grad.astype(jnp.bfloat16)]
    while x3 -> x0, local copies, waits for them, and re-layouts: 23.8 us -> none  [by_blocks(): lax.scan(turn, carry, (stacked, jnp.arange(number, dtype=jnp.int32)))]
  transfers between devices with their start and end apart: 12 -> 11, of which waited for: 11 -> 11; matrix products, arithmetic and copies ran while one was open for 9% -> 19% of each run, Pallas kernels for 0% -> 4%
where the time goes in v1:
time: 1290 us; the launch traced here: 1280 us
  waiting for transfers between devices  867 us (67%)
  matrix products  119 us (9%)
  local copies, waits for them, and re-layouts  110 us (9%)
  other arithmetic  70.3 us (5%)
  Pallas kernels  61.4 us (5%)
  blocking collectives  36.1 us (3%)
  between operations  16.9 us (1%)
    psum x1, waiting for transfers between devices, per_device(): lax.psum(lax.optimization_barrier((down_grad.astype(BF16), gate_grad.asty...  265 us
    all_gather x4, waiting for transfers between devices, gather(): return lax.all_gather(local, 'tp', axis=axis, tiled=True)  231 us
    psum x1, waiting for transfers between devices, per_device(): grad_normed2 = lax.psum(grad_normed2.astype(BF16), 'tp').astype(F32)  97.8 us
    reduce_scatter x1, waiting for transfers between devices, per_device(): own_pairs = lax.psum_scatter(dpairs, 'ctx', scatter_dimension=0, tiled=True)  97 us
    all_gather x1, waiting for transfers between devices, per_device(): all_pairs = lax.all_gather(pairs, 'ctx', axis=0, tiled=True)  66.1 us
    unnamed x40, local copies, waits for them, and re-layouts  57 us
    reduce_scatter x1, waiting for transfers between devices, per_device(): lax.psum_scatter(part, 'tp', scatter_dimension=1, tiled=True).astype(F32)  50.7 us
    reduce_scatter x1, waiting for transfers between devices, per_device(): branch = lax.psum_scatter(branch, 'tp', scatter_dimension=1, tiled=True)  39.9 us
  transfers between devices with their start and end apart: 11, of which 11 were waited for; matrix products, arithmetic and copies ran while one was open for 19% of the time, Pallas kernels for 4%

profile of v1, /device:TPU:0, one launch (start us, length us, event | category | flops | bytes accessed | tf_op | source)
XLA Modules:
  0.0 1282.1 jit_solution(9932513973594317313)
XLA Ops:
  9.8 10.5 all-gather
  28.7 47.0 %all-gather.7.cloned.1.call-done.tok_ref = bf16[768,2048]{1,0:T(8,128)(2,1)} async-done(((bf16[768,512]{1,0:T(8,128)(2,1)}), bf16[768,2048]{1,0:T(8,128)(2,1)}) %all-gather.7.cloned.1.call-update) | async-done | bytes 3145744 | tf_op jit(solution)/shard_map/all_gather | solution.py:388
  75.8 11.2 project.1
  91.8 66.1 %all-gather.9.cloned.1.call-done.k_ref.v_ref = bf16[6144,1024]{1,0:T(8,128)(2,1)} async-done(((bf16[768,1024]{1,0:T(8,128)(2,1)}), bf16[6144,1024]{1,0:T(8,128)(2,1)}) %all-gather.9.cloned.1.call-update) | async-done | bytes 12582928 | tf_op jit(solution)/shard_map/all_gather | solution.py:407
  167.4 32.0 %fusion.20 = (bf16[2048,1,2048]{2,1,0:T(2,128)(2,1)S(1)}, bf16[2048,1,2048]{2,1,0:T(2,128)(2,1)}) fusion(bf16[2048,2,2048]{2,1,0:T(2,128)(2,1)} %param.11), kind=kLoop, calls=%fused_computation.60 | loop fusion | bytes 33554432 | tf_op jit(solution)/shard_map/slice | solution.py:393
  199.3 18.5 %copy_bitcast_fusion = (bf16[2048,2048]{1,0:T(8,128)(2,1)}, bf16[2048,2048]{1,0:T(8,128)(2,1)}) fusion(bf16[2048,1,2048]{2,1,0:T(2,128)(2,1)S(1)} %get-tuple-element.97, bf16[2048,1,2048]{2,1,0:T(2,128)(2,1)} %get-tuple-element.98), kind=kLoop, calls=%fused_computation.4 | loop fusion | bytes 33554432 | tf_op jit(solution)/shard_map/squeeze | solution.py:393
  217.8 91.4 %all-gather.13.cloned.1.call-done.w_ref = bf16[2048,2048]{1,0:T(8,128)(2,1)} async-done(((bf16[512,2048]{1,0:T(8,128)(2,1)}), bf16[2048,2048]{1,0:T(8,128)(2,1)}) %all-gather.13.cloned.1.call-update) | async-done | bytes 8388624 | tf_op jit(solution)/shard_map/all_gather | solution.py:388
  309.2 63.1 %all-gather.11.cloned.1.call-done.mixed_ref = bf16[768,2048]{1,0:T(8,128)(2,1)} async-done(((bf16[768,512]{1,0:T(8,128)(2,1)}), bf16[768,2048]{1,0:T(8,128)(2,1)}) %all-gather.11.cloned.1.call-update) | async-done | bytes 3145744 | tf_op jit(solution)/shard_map/all_gather | solution.py:388
  372.4 13.8 %merge.1 = (f32[768,2048]{1,0:T(8,128)}, f32[768,2]{1,0:T(8,128)}, bf16[768,2048]{1,0:T(8,128)(2,1)}) custom-call(bf16[768,2048]{1,0:T(8,128)(2,1)} %all-gather.11.cloned.1.call-done.mixed_ref, bf16[2048,2048]{1,0:T(8,128)(2,1)} %all-gather.13.cloned.1.call-done.w_ref, bf16[768,2048]{1,0:T(8,128)(2,1)} %all-gather.7.cloned.1.call-done.tok_ref), custom_call_target="tpu_custom_call" | custom-call | flops 6442450944 | bytes 24117248 | tf_op jit(solution)/shard_map/merge/pallas_call | solution.py:300
  386.2 11.8 fusion.21
  398.1 8.6 fusion.22
  406.6 29.4 %all-gather.15.cloned.1.call-done = bf16[768,2048]{1,0:T(8,128)(2,1)} async-done(((bf16[768,512]{1,0:T(8,128)(2,1)}), bf16[768,2048]{1,0:T(8,128)(2,1)}) %all-gather.15.cloned.1.call-update) | async-done | bytes 3145744 | tf_op jit(solution)/shard_map/all_gather | solution.py:388
  436.0 17.7 %multiply_convert_fusion = (bf16[768,2048]{1,0:T(8,128)(2,1)}, bf16[768,2048]{1,0:T(8,128)(2,1)}, bf16[768,2048]{1,0:T(8,128)(2,1)}) fusion(f32[768,2048]{1,0:T(8,128)} %fusion.21, f32[768,2048]{1,0:T(8,128)} %fusion.22, bf16[768,2048]{1,0:T(8,128)(2,1)} %all-gather.15.cloned.1.call-done, bf16[2048,2048]{1,0:T(8,128)(2,1)} %param.12), kind=kOutput, calls=%fused_computation.16 | convolution fusion | flops 6466043904 | bytes 33554432 | tf_op jit(solution)/shard_map/dot_general | solution.py:422
  453.7 11.9 fusion.23
  465.6 9.0 convolution_convert_fusion.1
  474.6 11.1 add_convert_fusion
  485.8 11.5 convolution_convert_fusion
  497.3 9.1 convolution_convert_fusion.2
  507.8 97.8 %all-reduce.6.cloned.1.call-done = bf16[768,2048]{1,0:T(8,128)(2,1)} async-done(((bf16[768,2048]{1,0:T(8,128)(2,1)}), bf16[768,2048]{1,0:T(8,128)(2,1)}) %all-reduce.6.cloned.1.call-update) | async-done | bytes 3145744 | tf_op jit(solution)/shard_map/psum | solution.py:428
  618.2 16.4 %attend_back.1 = (f32[768,512]{1,0:T(8,128)}, bf16[6144,1024]{1,0:T(8,128)(2,1)}) custom-call(s32[3]{0:T(128)} %pad_add_fusion.info, bf16[768,512]{1,0:T(8,128)(2,1)} %get-tuple-element.32.q_ref, bf16[768,512]{1,0:T(8,128)(2,1)} %fusion.11.do_ref, f32[768,512]{1,0:T(8,128)} %get-tuple-element.41.raw_ref, f32[4,768]{1,0:T(4,128)} %get-tuple-element.42.lse_ref, ...), custom_call_target="tpu_custom_call" | custom-call | flops 24159191040 | bytes 25165824 | tf_op jit(solution)/shard_map/attend_back/pallas_call | solution.py:261
  634.7 12.3 convolution_convert_fusion.3
  653.2 264.8 %all-reduce.10.cloned.1.call-done = (bf16[2048,2048]{1,0:T(8,128)(2,1)}, bf16[2048,2048]{1,0:T(8,128)(2,1)}, bf16[2048,2048]{1,0:T(8,128)(2,1)}) async-done(((bf16[2048,2048]{1,0:T(8,128)(2,1)}, bf16[2048,2048]{1,0:T(8,128)(2,1)}, bf16[2048,2048]{1,0:T(8,128)(2,1)}), (bf16[2048,2048]{1,0:T(8,128)(2,1)}, bf16[2048,2048]{1,0:T(8,128)(2,1)}, bf16[2048,2048]{1,0:T(8,128)(2,1)})) %all-reduce.10.cloned.1.call-update) | async-done | bytes 25165840 | tf_op jit(solution)/shard_map/psum | solution.py:434
  918.0 97.0 %reduce-scatter.6.cloned.1.call-done.dpair_ref = bf16[768,1024]{1,0:T(8,128)(2,1)} async-done(((bf16[6144,1024]{1,0:T(8,128)(2,1)}), bf16[768,1024]{1,0:T(8,128)(2,1)}) %reduce-scatter.6.cloned.1.call-update) | async-done | bytes 1572880 | tf_op jit(solution)/shard_map/reduce_scatter | solution.py:455
  1015.0 11.4 unproject.1
  1037.7 39.9 %reduce-scatter.4.cloned.1.call-done = bf16[768,512]{1,0:T(8,128)(2,1)} async-done(((bf16[768,2048]{1,0:T(8,128)(2,1)}), bf16[768,512]{1,0:T(8,128)(2,1)}) %reduce-scatter.4.cloned.1.call-update) | async-done | bytes 786448 | tf_op jit(solution)/shard_map/reduce_scatter | solution.py:419
  1080.4 18.6 %maximum_convert_fusion = f32[2048,2,2048]{2,0,1:T(8,128)} fusion(bf16[2048,1,2048]{2,0,1:T(8,128)(2,1)} %bitcast.43, bf16[2048,1,2048]{2,0,1:T(8,128)(2,1)} %bitcast.42), kind=kLoop, calls=%fused_computation | loop fusion | flops 16777216 | bytes 50331648 | tf_op jit(solution)/shard_map/stack | solution.py:479
  1099.1 55.0 %copy.22 = f32[2048,2,2048]{2,1,0:T(2,128)} copy(f32[2048,2,2048]{2,0,1:T(8,128)} %maximum_convert_fusion) | data formatting | bytes 67108864
  1154.1 11.8 convert_element_type.113
  1165.9 25.6 %psum.50 = f32[768,2]{1,0:T(8,128)S(1)} all-reduce(f32[768,2]{1,0:T(8,128)S(1)} %copy-done.9), channel_id=1, replica_groups=mesh['ctx'=8,'tp'=4] {'tp'}, use_global_device_ids=true, to_apply=%region_9.10 | all-reduce | flops 1536 | bytes 12288 | tf_op jit(solution)/shard_map/psum | solution.py:458
  1192.0 17.3 %all-reduce.8.cloned.1.call-done = (bf16[2048,3,512]{2,0,1:T(8,128)(2,1)}, bf16[512,2048]{1,0:T(8,128)(2,1)}) async-done(((bf16[2048,3,512]{2,0,1:T(8,128)(2,1)}, bf16[512,2048]{1,0:T(8,128)(2,1)}), (bf16[2048,3,512]{2,0,1:T(8,128)(2,1)}, bf16[512,2048]{1,0:T(8,128)(2,1)})) %all-reduce.8.cloned.1.call-update) | async-done | bytes 8388624 | tf_op jit(solution)/shard_map/psum | solution.py:468
  1209.2 9.5 convert_element_type.111
  1221.3 50.7 %reduce-scatter.8.cloned.1.call-done = bf16[768,512]{1,0:T(8,128)(2,1)} async-done(((bf16[768,2048]{1,0:T(8,128)(2,1)}), bf16[768,512]{1,0:T(8,128)(2,1)}) %reduce-scatter.8.cloned.1.call-update) | async-done | bytes 786448 | tf_op jit(solution)/shard_map/reduce_scatter | solution.py:457
  (91 shorter events, 63.2 us)
Async XLA Ops:
  7.2 68.6 %all-gather.7.cloned.1.call-start = ((), (), s32[]{:S(2)}) async-start(), calls=%async_computation.3 | async-start | bytes 3932160 | tf_op jit(solution)/shard_map/all_gather | solution.py:388
  7.9 150.1 %all-gather.9.cloned.1.call-start = ((), (), s32[]{:S(2)}) async-start(), calls=%async_computation.4 | async-start | bytes 14155776 | tf_op jit(solution)/shard_map/all_gather | solution.py:407
  87.0 222.2 %all-gather.13.cloned.1.call-start = ((), (), s32[]{:S(2)}) async-start(), calls=%async_computation.6 | async-start | bytes 10485760 | tf_op jit(solution)/shard_map/all_gather | solution.py:388
  87.8 284.6 %all-gather.11.cloned.1.call-start = ((), (), s32[]{:S(2)}) async-start(), calls=%async_computation.5 | async-start | bytes 3932160 | tf_op jit(solution)/shard_map/all_gather | solution.py:388
  166.5 269.5 %all-gather.15.cloned.1.call-start = ((), (), s32[]{:S(2)}) async-start(), calls=%async_computation.8 | async-start | bytes 3932160 | tf_op jit(solution)/shard_map/all_gather | solution.py:388
  167.1 438.5 %all-reduce.6.cloned.1.call-start = ((), (), s32[]{:S(2)}) async-start(), calls=%async_computation.9 | async-start | bytes 6291456 | tf_op jit(solution)/shard_map/psum | solution.py:428
  372.4 25.7 %slice-start = ((s8[8388608]{0:T(1024)(128)(4,1)}), s8[4194304]{0:T(1024)(128)(4,1)S(1)}, s32[]{:S(2)}) async-start(s8[8388608]{0:T(1024)(128)(4,1)} %bitcast.44), calls=%async_computation.14 | async-start | bytes 8388608
  386.2 11.9 slice-start.1
  386.2 11.9 copy-start.12
  436.0 38.6 %slice-start.2 = ((s8[8388608]{0:T(1024)(128)(4,1)}), s8[4194304]{0:T(1024)(128)(4,1)S(1)}, s32[]{:S(2)}) async-start(s8[8388608]{0:T(1024)(128)(4,1)} %bitcast.46), calls=%async_computation.16 | async-start | bytes 8388608
  453.7 11.9 copy-start.14
  453.7 20.9 %slice-start.3 = ((s8[8388608]{0:T(1024)(128)(4,1)}), s8[4194304]{0:T(1024)(128)(4,1)S(1)}, s32[]{:S(2)}) async-start(s8[8388608]{0:T(1024)(128)(4,1)} %bitcast.46), calls=%async_computation.17 | async-start | bytes 8388608
  485.7 11.6 copy-start.3
  485.7 432.2 %all-reduce.10.cloned.1.call-start = ((), (), s32[]{:S(2)}) async-start(), calls=%async_computation.13 | async-start | bytes 50331648 | tf_op jit(solution)/shard_map/psum | solution.py:434
  485.8 11.5 copy-start.13
  506.4 1.0 copy-start.7
  506.4 508.5 %reduce-scatter.6.cloned.1.call-start = ((), (), s32[]{:S(2)}) async-start(), calls=%async_computation.10 | async-start | bytes 14155776 | tf_op jit(solution)/shard_map/reduce_scatter | solution.py:455
  605.6 5.1 copy-start
  610.7 4.5 copy-start.5
  615.2 3.0 copy-start.1
  634.6 12.4 copy-start.8
  634.6 443.0 %reduce-scatter.4.cloned.1.call-start = ((), (), s32[]{:S(2)}) async-start(), calls=%async_computation.7 | async-start | bytes 3932160 | tf_op jit(solution)/shard_map/reduce_scatter | solution.py:419
  647.0 562.3 %all-reduce.8.cloned.1.call-start = ((), (), s32[]{:S(2)}) async-start(), calls=%async_computation.12 | async-start | bytes 16777216 | tf_op jit(solution)/shard_map/psum | solution.py:468
  1015.0 11.4 copy-start.11
  1026.4 3.1 copy-start.10
  1036.3 1.0 copy-start.6
  1036.4 235.7 %reduce-scatter.8.cloned.1.call-start = ((), (), s32[]{:S(2)}) async-start(), calls=%async_computation.11 | async-start | bytes 3932160 | tf_op jit(solution)/shard_map/reduce_scatter | solution.py:457
  1154.1 11.8 copy-start.9
  1209.2 9.5 copy-start.4
  1218.8 53.3 %copy-start.2 = (bf16[768,512]{1,0:T(8,128)(2,1)S(1)}, bf16[768,512]{1,0:T(8,128)(2,1)}, u32[]{:S(2)}) copy-start(bf16[768,512]{1,0:T(8,128)(2,1)} %param.7) | copy-start | bytes 2359300
Sparse Core Ops, SparseCore 0:
  9.6 66.1 all-gather.6
  87.1 70.8 all-gather.8
  159.6 149.6 all-gather.12
  310.7 61.6 all-gather.10
  373.8 62.1 all-gather.14
  485.8 119.7 all-reduce.5
  610.4 307.5 all-reduce.9
  922.4 92.4 reduce-scatter.5
  1017.4 60.2 reduce-scatter.3
  1082.3 126.9 all-reduce.7
  1211.6 60.4 reduce-scatter.7

commit v2 on v1

--- a/solution.py
+++ b/solution.py
@@ -17,6 +17,8 @@
 BF16 = jnp.bfloat16
 NT = (((1,), (1,)), ((), ()))
 TN = (((0,), (0,)), ((), ()))
+MESH = pl.DeviceIdType.MESH
+BLOCK = 512
 
 
 def params(mib, **more):
@@ -186,22 +188,17 @@
     )(info, query, pairs, pairs, begin)
 
 
-def attend_back_kernel(
-    heads, info, q_ref, do_ref, raw_ref, lse_ref, k_ref, v_ref, begin_ref,
-    dq_ref, dpair_ref, acc_ref, delta_ref, s_ref, g_ref,
+def query_grad_kernel(
+    heads, info, q_ref, do_ref, lse_ref, delta_ref, k_ref, v_ref, begin_ref,
+    dq_ref, acc_ref, s_ref, g_ref,
 ):
     me, first, clear = info[0], info[1], info[2]
     j = pl.program_id(0)
     rows = q_ref.shape[0]
-    span = heads * HD
 
     @pl.when(j == 0)
     def _():
         acc_ref[...] = jnp.zeros_like(acc_ref)
-        for h in range(heads):
-            hs = slice(h * HD, (h + 1) * HD)
-            both = do_ref[:, hs].astype(F32) * raw_ref[:, hs]
-            delta_ref[h : h + 1, :] = jnp.sum(both.T, axis=0, keepdims=True)
 
     def block(hide):
         def score(h):
@@ -218,10 +215,6 @@
             hs = slice(h * HD, (h + 1) * HD)
             p = jnp.exp2(s_ref[h % 2] * C2 - lse_ref[h : h + 1, :])
             ds = (p * (g_ref[h % 2] - delta_ref[h : h + 1, :])).astype(BF16)
-            dv = jnp.dot(p.astype(BF16), do_ref[:, hs], preferred_element_type=F32)
-            dk = jnp.dot(ds, q_ref[:, hs], preferred_element_type=F32)
-            dpair_ref[:, hs] = (dk * SCALE).astype(BF16)
-            dpair_ref[:, span + h * HD : span + (h + 1) * HD] = dv.astype(BF16)
             acc_ref[h] = acc_ref[h] + lax.dot_general(
                 k_ref[:, hs], ds, TN, preferred_element_type=F32
             )
@@ -240,17 +233,13 @@
     def _():
         block(True)
 
-    @pl.when((j < first) | (j > me))
-    def _():
-        dpair_ref[...] = jnp.zeros_like(dpair_ref)
-
     @pl.when(j == me)
     def _():
         for h in range(heads):
             dq_ref[:, h * HD : (h + 1) * HD] = (acc_ref[h] * SCALE).T
 
 
-def attend_back(info, query, grad_mixed, raw, lse, pairs, begin, heads):
+def query_grad(info, query, grad_mixed, lse, delta, pairs, begin, heads):
     rows = query.shape[0]
     total = pairs.shape[0]
     span = heads * HD
@@ -258,28 +247,160 @@
     key = pl.BlockSpec((rows, span), lambda j, s: (jnp.clip(j, s[1], s[0]), 0))
     value = pl.BlockSpec((rows, span), lambda j, s: (jnp.clip(j, s[1], s[0]), 1))
     wide = full((rows, span))
-    return pl.pallas_call(
-        functools.partial(attend_back_kernel, heads),
+    thin = full((heads, rows))
+    return pl.pallas_call(
+        functools.partial(query_grad_kernel, heads),
         grid_spec=pltpu.PrefetchScalarGridSpec(
             num_scalar_prefetch=1,
             grid=(total // rows,),
-            in_specs=[wide, wide, wide, full((heads, rows)), key, value, full((1, rows))],
-            out_specs=[wide, pl.BlockSpec((rows, 2 * span), lambda j, s: (j, 0))],
+            in_specs=[wide, wide, thin, thin, key, value, full((1, rows))],
+            out_specs=wide,
             scratch_shapes=[
                 pltpu.VMEM((heads, HD, rows), F32),
-                pltpu.VMEM((heads, rows), F32),
                 pltpu.VMEM((2, rows, rows), F32),
                 pltpu.VMEM((2, rows, rows), F32),
             ],
         ),
+        out_shape=jax.ShapeDtypeStruct((rows, span), F32),
+        compiler_params=params(58),
+        cost_estimate=cost(6 * rows * total * span, 4 * total * span, rows * total * heads),
+        name="query_grad",
+    )(info, query, grad_mixed, lse, delta, pairs, pairs, begin)
+
+
+def key_grad_kernel(
+    heads, info, k_ref, v_ref, q_ref, g_ref, begin_ref, dk_ref, dv_ref,
+    rows_ref, s_ref, p_ref,
+):
+    me, last, clear = info[0], info[1], info[2]
+    j = pl.program_id(0)
+    rows = k_ref.shape[0]
+    span = heads * HD
+
+    @pl.when(j == me)
+    def _():
+        dk_ref[...] = jnp.zeros_like(dk_ref)
+        dv_ref[...] = jnp.zeros_like(dv_ref)
+
+    def block(hide):
+        coded = g_ref[:, span:].astype(F32).T
+        for n in range(2 * heads):
+            rows_ref[n : n + 1, :] = (
+                coded[3 * n : 3 * n + 1] + coded[3 * n + 1 : 3 * n + 2] + coded[3 * n + 2 : 3 * n + 3]
+            )
+
+        def score(h):
+            hs = slice(h * HD, (h + 1) * HD)
+            s = lax.dot_general(k_ref[:, hs], q_ref[:, hs], NT, preferred_element_type=F32)
+            if hide:
+                key_place = lax.broadcasted_iota(jnp.int32, s.shape, 0) + me * rows
+                query_place = lax.broadcasted_iota(jnp.int32, s.shape, 1) + j * rows
+                s = jnp.where(
+                    (key_place <= query_place) & (key_place >= begin_ref[...]), s, NEG
+                )
+            s_ref[h % 2] = s
+            p_ref[h % 2] = lax.dot_general(
+                v_ref[:, hs], g_ref[:, hs], NT, preferred_element_type=F32
+            )
+
+        def spread(h):
+            hs = slice(h * HD, (h + 1) * HD)
+            p = jnp.exp2(s_ref[h % 2] * C2 - rows_ref[h : h + 1, :])
+            ds = (p * (p_ref[h % 2] - rows_ref[heads + h : heads + h + 1, :])).astype(BF16)
+            dv_ref[:, hs] += jnp.dot(p.astype(BF16), g_ref[:, hs], preferred_element_type=F32)
+            dk_ref[:, hs] += jnp.dot(ds, q_ref[:, hs], preferred_element_type=F32)
+
+        score(0)
+        for h in range(heads):
+            if h + 1 < heads:
+                score(h + 1)
+            spread(h)
+
+    @pl.when((j > me) & (j <= clear))
+    def _():
+        block(False)
+
+    @pl.when((j == me) | ((j > me) & (j > clear) & (j <= last)))
+    def _():
+        block(True)
+
+    @pl.when(j == pl.num_programs(0) - 1)
+    def _():
+        dk_ref[...] = dk_ref[...] * SCALE
+
+
+def key_grad(info, pairs, all_query, all_grad, all_begin, heads):
+    rows = pairs.shape[0]
+    total = all_query.shape[0]
+    span = heads * HD
+    full = lambda shape, at=0: pl.BlockSpec(shape, lambda j, s: (0, at))
+    near = lambda j, s: (jnp.clip(j, s[0], s[1]), 0)
+    wide = full((rows, span))
+    return pl.pallas_call(
+        functools.partial(key_grad_kernel, heads),
+        grid_spec=pltpu.PrefetchScalarGridSpec(
+            num_scalar_prefetch=1,
+            grid=(total // rows,),
+            in_specs=[
+                wide, full((rows, span), 1),
+                pl.BlockSpec((rows, span), near),
+                pl.BlockSpec((rows, span + HD), near),
+                pl.BlockSpec((1, rows), lambda j, s: (0, jnp.clip(j, s[0], s[1]))),
+            ],
+            out_specs=[wide, wide],
+            scratch_shapes=[
+                pltpu.VMEM((2 * heads, rows), F32),
+                pltpu.VMEM((2, rows, rows), F32),
+                pltpu.VMEM((2, rows, rows), F32),
+            ],
+        ),
+        out_shape=[jax.ShapeDtypeStruct((rows, span), F32)] * 2,
+        compiler_params=params(58),
+        cost_estimate=cost(8 * rows * total * span, 4 * total * span, rows * total * heads),
+        name="key_grad",
+    )(info, pairs, pairs, all_query, all_grad, all_begin)
+
+
+def mixed_grad_kernel(heads, branch_ref, w_ref, raw_ref, lse_ref, out_ref, delta_ref):
+    span = heads * HD
+    low = lax.dot_general(
+        branch_ref[...], w_ref[...], NT, preferred_element_type=F32
+    ).astype(BF16)
+    out_ref[:, :span] = low
+    count = low.shape[0]
+    both = low.astype(F32) * raw_ref[...]
+    for h in range(heads):
+        delta_ref[h : h + 1, :] = jnp.sum(both[:, h * HD : (h + 1) * HD].T, axis=0, keepdims=True)
+    lines = []
+    for n in range(2 * heads):
+        value = lse_ref[n : n + 1, :] if n < heads else delta_ref[n - heads : n - heads + 1, :]
+        for _ in range(3):
+            piece = value.astype(BF16).astype(F32)
+            lines.append(piece)
+            value = value - piece
+    lines.append(jnp.zeros((HD - len(lines), count), F32))
+    out_ref[:, span:] = jnp.concatenate(lines, axis=0).T.astype(BF16)
+
+
+def mixed_grad(branch, weight, raw, lse, heads):
+    rows, width = branch.shape
+    span = heads * HD
+    block = 256
+    row = lambda n: pl.BlockSpec((block, n), lambda i: (i, 0))
+    line = pl.BlockSpec((heads, block), lambda i: (0, i))
+    return pl.pallas_call(
+        functools.partial(mixed_grad_kernel, heads),
+        grid=(rows // block,),
+        in_specs=[row(width), pl.BlockSpec((span, width), lambda i: (0, 0)), row(span), line],
+        out_specs=[row(span + HD), line],
         out_shape=[
-            jax.ShapeDtypeStruct((rows, span), F32),
-            jax.ShapeDtypeStruct((total, 2 * span), BF16),
-        ],
-        compiler_params=params(58),
-        cost_estimate=cost(10 * rows * total * span, 8 * total * span, rows * total * heads),
-        name="attend_back",
-    )(info, query, grad_mixed, raw, lse, pairs, pairs, begin)
+            jax.ShapeDtypeStruct((rows, span + HD), BF16),
+            jax.ShapeDtypeStruct((heads, rows), F32),
+        ],
+        compiler_params=params(56),
+        cost_estimate=cost(2 * rows * width * span, 2 * width * span + 4 * rows * width),
+        name="mixed_grad",
+    )(branch, weight, raw, lse)
 
 
 def merge_kernel(mixed_ref, w_ref, tok_ref, resid_ref, stat_ref, inner_ref):
@@ -313,8 +434,221 @@
     )(mixed_full, weight, tok_full)
 
 
+def feed_kernel(inner_ref, cot_ref, w_ref, down_ref, hidden_ref, dgu_ref):
+    block = down_ref.shape[0]
+    both = jnp.dot(inner_ref[...], w_ref[...], preferred_element_type=F32)
+    grad = lax.dot_general(cot_ref[...], down_ref[...], NT, preferred_element_type=F32)
+    gate, up = both[:, :block], both[:, block:]
+    sigma = 1.0 / (1.0 + jnp.exp(-gate))
+    active = gate * sigma
+    hidden_ref[...] = (active * up).astype(BF16)
+    dgu_ref[:, :block] = (grad * up * sigma * (1.0 + gate * (1.0 - sigma))).astype(BF16)
+    dgu_ref[:, block:] = (grad * active).astype(BF16)
+
+
+def feed(inner, cot, weight, down, block):
+    rows, width = inner.shape
+    units = down.shape[0]
+    whole = pl.BlockSpec((rows, width), lambda j: (0, 0))
+    return pl.pallas_call(
+        feed_kernel,
+        grid=(units // block,),
+        in_specs=[
+            whole, whole,
+            pl.BlockSpec((width, 2 * block), lambda j: (0, j)),
+            pl.BlockSpec((block, width), lambda j: (j, 0)),
+        ],
+        out_specs=[
+            pl.BlockSpec((rows, block), lambda j: (0, j)),
+            pl.BlockSpec((rows, 2 * block), lambda j: (0, j)),
+        ],
+        out_shape=[
+            jax.ShapeDtypeStruct((rows, units), BF16),
+            jax.ShapeDtypeStruct((rows, 2 * units), BF16),
+        ],
+        compiler_params=params(56),
+        cost_estimate=cost(
+            6 * rows * width * units, 6 * width * units + 4 * rows * width, rows * units
+        ),
+        name="feed",
+    )(inner, cot, weight, down)
+
+
+def weave_kernel(block, sum_ref, out_ref):
+    for j in range(sum_ref.shape[1] // (2 * block)):
+        for k in range(2):
+            at = (2 * j + k) * block
+            out_ref[:, k, j * block : (j + 1) * block] = sum_ref[:, at : at + block].astype(F32)
+
+
+def weave(summed, block):
+    width, both = summed.shape
+    rows = 256
+    return pl.pallas_call(
+        functools.partial(weave_kernel, block),
+        grid=(width // rows,),
+        in_specs=[pl.BlockSpec((rows, both), lambda i: (i, 0))],
+        out_specs=pl.BlockSpec((rows, 2, both // 2), lambda i: (i, 0, 0)),
+        out_shape=jax.ShapeDtypeStruct((width, 2, both // 2), F32),
+        compiler_params=params(56),
+        cost_estimate=cost(width * both, 6 * width * both),
+        name="weave",
+    )(summed)
+
+
+def line_barrier(at, n):
+    barrier = pltpu.get_barrier_semaphore()
+
+    @pl.when(at > 0)
+    def _():
+        pl.semaphore_signal(barrier, inc=1, device_id={"tp": at - 1}, device_id_type=MESH)
+
+    @pl.when(at < n - 1)
+    def _():
+        pl.semaphore_signal(barrier, inc=1, device_id={"tp": at + 1}, device_id_type=MESH)
+
+    pl.semaphore_wait(barrier, jnp.where((at > 0) & (at < n - 1), 2, 1))
+
+
+def sum_rows(n, sub, part_ref, out_ref, row_fn, from_left, from_right, send, recv):
+    at = lax.axis_index("tp")
+    chunks = part_ref.shape[0] // sub
+    middle = (n // 2 - 1, n // 2)
+
+    def link(kind, right, src, dst, c):
+        which = (kind * 2 + (1 if right else 0), c)
+        return pltpu.make_async_remote_copy(
+            src_ref=src.at[pl.ds(c * sub, sub)],
+            dst_ref=dst.at[pl.ds(c * sub, sub)],
+            send_sem=send.at[which],
+            recv_sem=recv.at[which],
+            device_id={"tp": at + 1 if right else at - 1},
+            device_id_type=MESH,
+        )
+
+    def came(right):
+        return from_left if right else from_right
+
+    def first(right, c):
+        return link(0, right, part_ref, came(right), c)
+
+    def onward(right, c):
+        return link(0, right, came(right), came(right), c)
+
+    def hand(right, c):
+        return link(1, right, out_ref, out_ref, c)
+
+    def reduce_step(c):
+        owner = middle[c % 2]
+        rows = slice(c * sub, (c + 1) * sub)
+        for right in (True, False):
+            edge = 0 if right else n - 1
+            held = came(right)
+
+            @pl.when(at == edge)
+            def _():
+                first(right, c).start()
+
+            @pl.when(((at < owner) if right else (at > owner)) & (at != edge))
+            def _():
+                copy = onward(right, c)
+                copy.wait_recv()
+                held[rows, :] = (
+                    held[rows, :].astype(F32) + part_ref[rows, :].astype(F32)
+                ).astype(BF16)
+                copy.start()
+
+    def final_step(c):
+        owner = middle[c % 2]
+        rows = slice(c * sub, (c + 1) * sub)
+
+        @pl.when(at == owner)
+        def _():
+            total = part_ref[rows, :].astype(F32)
+            onward(True, c).wait_recv()
+            total = total + from_left[rows, :].astype(F32)
+            onward(False, c).wait_recv()
+            total = total + from_right[rows, :].astype(F32)
+            row_fn(total, rows)
+            hand(True, c).start()
+            hand(False, c).start()
+
+    def hand_step(c):
+        owner = middle[c % 2]
+        for right in (True, False):
+            edge = n - 1 if right else 0
+
+            @pl.when((at > owner) if right else (at < owner))
+            def _():
+                copy = hand(right, c)
+                copy.wait_recv()
+
+                @pl.when(at != edge)
+                def _():
+                    copy.start()
+
+    for c in range(chunks + 4):
+        if c < chunks:
+            reduce_step(c)
+        if 2 <= c < chunks + 2:
+            final_step(c - 2)
+        if c >= 4:
+            hand_step(c - 4)
+    for c in range(chunks):
+        owner = middle[c % 2]
+
+        @pl.when(at < owner)
+        def _():
+            first(True, c).wait_send()
+
+        @pl.when(at > owner)
+        def _():
+            first(False, c).wait_send()
+
+        @pl.when((at >= owner) & (at < n - 1))
+        def _():
+            hand(True, c).wait_send()
+
+        @pl.when((at <= owner) & (at > 0))
+        def _():
+            hand(False, c).wait_send()
+
+
+def norm_back_kernel(
+    n, sub, part_ref, cot_ref, resid_ref, stat_ref, out_ref, from_left, from_right, send, recv
+):
+    line_barrier(lax.axis_index("tp"), n)
+
+    def row_fn(total, rows):
+        inverse = stat_ref[rows, 1:2]
+        normed = (resid_ref[rows, :] - stat_ref[rows, 0:1]) * inverse
+        mean = jnp.mean(total, axis=1, keepdims=True)
+        inner = jnp.mean(total * normed, axis=1, keepdims=True)
+        out = cot_ref[rows, :].astype(F32) + inverse * (total - mean - normed * inner)
+        out_ref[rows, :] = out.astype(BF16)
+
+    sum_rows(n, sub, part_ref, out_ref, row_fn, from_left, from_right, send, recv)
+
+
+def norm_back(part, cot, resid, stat, n):
+    rows, width = part.shape
+    sub = 48
+    vmem = pl.BlockSpec(memory_space=pltpu.VMEM)
+    return pl.pallas_call(
+        functools.partial(norm_back_kernel, n, sub),
+        in_specs=[vmem] * 4,
+        out_specs=vmem,
+        out_shape=jax.ShapeDtypeStruct((rows, width), BF16),
+        scratch_shapes=[pltpu.VMEM((rows, width), BF16)] * 2
+        + [pltpu.SemaphoreType.DMA((4, rows // sub))] * 2,
+        compiler_params=params(56, collective_id=1, has_side_effects=True),
+        cost_estimate=cost(100e9, 12 * rows * width),
+        name="norm_back",
+    )(part, cot, resid, stat)
+
+
 def unproject_kernel(
-    heads, dq_ref, dpair_ref, cos_ref, sin_ref, tok_ref, stat_ref, w_ref,
+    heads, dq_ref, dk_ref, dv_ref, cos_ref, sin_ref, tok_ref, stat_ref, w_ref,
     dproj_ref, part_ref, sums_ref,
 ):
     cosine, sine = cos_ref[...], sin_ref[...]
@@ -326,10 +660,8 @@
     for h in range(heads):
         hs = slice(h * HD, (h + 1) * HD)
         dproj_ref[:, hs] = back(dq_ref[:, hs]).astype(BF16)
-        dproj_ref[:, span + h * HD : span + (h + 1) * HD] = back(
-            dpair_ref[:, hs].astype(F32)
-        ).astype(BF16)
-    dproj_ref[:, 2 * span :] = dpair_ref[:, span:]
+        dproj_ref[:, span + h * HD : span + (h + 1) * HD] = back(dk_ref[:, hs]).astype(BF16)
+    dproj_ref[:, 2 * span :] = dv_ref[...].astype(BF16)
     total = None
     for part in range(3):
         term = lax.dot_general(
@@ -348,7 +680,7 @@
     )
 
 
-def unproject(dq, own_pairs, cosine, sine, tok_full, stat, weight, heads):
+def unproject(dq, dk, dv, cosine, sine, tok_full, stat, weight, heads):
     rows, width = tok_full.shape
     span = heads * HD
     block = 256
@@ -357,7 +689,7 @@
         functools.partial(unproject_kernel, heads),
         grid=(rows // block,),
         in_specs=[
-            row(span), row(2 * span), row(HD), row(HD), row(width), row(2),
+            row(span), row(span), row(span), row(HD), row(HD), row(width), row(2),
             pl.BlockSpec((3, width, span), lambda i: (0, 0, 0)),
         ],
         out_specs=[row(3 * span), row(width), row(2)],
@@ -369,7 +701,7 @@
         compiler_params=params(56),
         cost_estimate=cost(6 * rows * width * span, 6 * width * span + 6 * rows * width),
         name="unproject",
-    )(dq, own_pairs, cosine, sine, tok_full, stat, weight)
+    )(dq, dk, dv, cosine, sine, tok_full, stat, weight)
 
 
 def per_device(tokens, segment_ids, in_weight, out_weight, gate_up_weight, down_weight, cotangent):
@@ -390,70 +722,61 @@
     places = me * rows + jnp.arange(rows, dtype=jnp.int32)
     cosine, sine = rope_tables(places)
     in_w = jnp.transpose(in_weight, (1, 0, 2))
-    gate_w, up_w = lax.optimization_barrier((gate_up_weight[:, 0, :], gate_up_weight[:, 1, :]))
+    gu_w = jnp.transpose(
+        gate_up_weight.reshape(width, 2, hidden_local // BLOCK, BLOCK), (0, 2, 1, 3)
+    )
+    gu_w = lax.optimization_barrier(gu_w.reshape(width, 2 * hidden_local))
 
     all_seg = lax.all_gather(segment_ids, "ctx", axis=0, tiled=True)
-    before = jnp.sum((all_seg < segment_ids[0]).astype(jnp.int32))
-    own_begin = me * rows + jnp.sum(
-        (segment_ids[None, :] < segment_ids[:, None]).astype(jnp.int32), axis=1
-    )
-    begin = jnp.where(segment_ids == segment_ids[0], before, own_begin).astype(jnp.int32)
-    last = jnp.max(begin)
-    info = jnp.stack([me, before // rows, (last + rows - 1) // rows]).astype(jnp.int32)
-    begin = begin[None, :]
+    count = all_seg.shape[0]
+    every = jnp.arange(count, dtype=jnp.int32)
+    opens = jnp.concatenate([jnp.ones((1,), jnp.bool_), all_seg[1:] != all_seg[:-1]])
+    all_begin = lax.cummax(jnp.where(opens, every, 0))
+    begin = lax.dynamic_slice_in_dim(all_begin, me * rows, rows, 0)
+    blocks = all_begin.reshape(count // rows, rows)
+    key_info = jnp.stack(
+        [me, blocks[me, 0] // rows, (blocks[me, rows - 1] + rows - 1) // rows]
+    ).astype(jnp.int32)
+    query_info = jnp.stack(
+        [
+            me,
+            jnp.sum((blocks[:, 0] < (me + 1) * rows).astype(jnp.int32)) - 1,
+            jnp.sum((blocks[:, rows - 1] <= me * rows).astype(jnp.int32)) - 1,
+        ]
+    ).astype(jnp.int32)
+    begin, all_begin = begin[None, :], all_begin[None, :]
 
     tok_full = gather(tokens)
     inner1, stat1, query, pairs = project(tok_full, in_w, cosine, sine, heads)
     all_pairs = lax.all_gather(pairs, "ctx", axis=0, tiled=True)
-    out_full = gather(out_weight, 0)
+    share = width // lax.axis_size("ctx")
+    out_full = gather(lax.dynamic_slice_in_dim(out_weight, me * share, share, axis=1), 0)
+    out_full = lax.all_gather(out_full, "ctx", axis=1, tiled=True)
+    all_query = lax.all_gather(query, "ctx", axis=0, tiled=True)
     cot_full = gather(cotangent)
-    raw, mixed, lse = attend(info, query, all_pairs, begin, heads)
+    raw, mixed, lse = attend(key_info, query, all_pairs, begin, heads)
     resid1, stat2, inner2 = merge(gather(mixed), out_full, tok_full)
 
-    gate = jnp.dot(inner2, gate_w, preferred_element_type=F32)
-    up = jnp.dot(inner2, up_w, preferred_element_type=F32)
-    sigma = jax.nn.sigmoid(gate)
-    active = gate * sigma
-    hidden = (active * up).astype(BF16)
+    hidden, grad_gu = feed(inner2, cot_full, gu_w, down_weight, BLOCK)
+    grad_part = lax.dot_general(grad_gu, gu_w, NT, preferred_element_type=F32).astype(BF16)
+    down_grad = lax.dot_general(hidden, cot_full, TN, preferred_element_type=F32)
+    gu_grad = lax.dot_general(inner2, grad_gu, TN, preferred_element_type=F32)
+    grad_part, down_grad, gu_grad = lax.optimization_barrier(
+        (grad_part, down_grad.astype(BF16), gu_grad.astype(BF16))
+    )
+    down_grad, gu_grad = lax.optimization_barrier(lax.psum((down_grad, gu_grad), "ctx"))
+    branch_grad = norm_back(grad_part, cot_full, resid1, stat2, lax.axis_size("tp"))
+
     branch = jnp.dot(hidden, down_weight, preferred_element_type=F32).astype(BF16)
     branch = lax.psum_scatter(branch, "tp", scatter_dimension=1, tiled=True)
     layer_out = (own(resid1) + branch.astype(F32)).astype(BF16)
 
-    grad_hidden = lax.dot_general(cot_full, down_weight, NT, preferred_element_type=F32)
-    grad_gate = (grad_hidden * up * sigma * (1.0 + gate * (1.0 - sigma))).astype(BF16)
-    grad_up = (grad_hidden * active).astype(BF16)
-    grad_normed2 = lax.dot_general(
-        grad_gate, gate_w, NT, preferred_element_type=F32
-    ) + lax.dot_general(grad_up, up_w, NT, preferred_element_type=F32)
-    grad_normed2 = lax.psum(grad_normed2.astype(BF16), "tp").astype(F32)
-
-    down_grad = lax.dot_general(hidden, cot_full, TN, preferred_element_type=F32)
-    gate_grad = lax.dot_general(inner2, grad_gate, TN, preferred_element_type=F32)
-    up_grad = lax.dot_general(inner2, grad_up, TN, preferred_element_type=F32)
-    down_grad, gate_grad, up_grad = lax.optimization_barrier(
-        lax.psum(
-            lax.optimization_barrier(
-                (down_grad.astype(BF16), gate_grad.astype(BF16), up_grad.astype(BF16))
-            ),
-            "ctx",
-        )
-    )
-
-    normed2 = (resid1 - stat2[:, 0:1]) * stat2[:, 1:2]
-    mean_g = jnp.mean(grad_normed2, axis=1, keepdims=True)
-    mean_gn = jnp.mean(grad_normed2 * normed2, axis=1, keepdims=True)
-    resid1_grad = cot_full.astype(F32) + stat2[:, 1:2] * (
-        grad_normed2 - mean_g - normed2 * mean_gn
-    )
-    branch_grad = resid1_grad.astype(BF16)
-    grad_mixed = lax.dot_general(
-        branch_grad, out_weight, NT, preferred_element_type=F32
-    ).astype(BF16)
     out_grad = lax.dot_general(mixed, branch_grad, TN, preferred_element_type=F32).astype(BF16)
-
-    dq, dpairs = attend_back(info, query, grad_mixed, raw, lse, all_pairs, begin, heads)
-    own_pairs = lax.psum_scatter(dpairs, "ctx", scatter_dimension=0, tiled=True)
-    dproj, part, sums = unproject(dq, own_pairs, cosine, sine, tok_full, stat1, in_w, heads)
+    grad_mixed, delta = mixed_grad(branch_grad, out_weight, raw, lse, heads)
+    all_grad = lax.all_gather(grad_mixed, "ctx", axis=0, tiled=True)
+    dq = query_grad(key_info, query, grad_mixed, lse, delta, all_pairs, begin, heads)
+    dk, dv = key_grad(query_info, pairs, all_query, all_grad, all_begin, heads)
+    dproj, part, sums = unproject(dq, dk, dv, cosine, sine, tok_full, stat1, in_w, heads)
     grad_normed1 = lax.psum_scatter(part, "tp", scatter_dimension=1, tiled=True).astype(F32)
     sums = lax.psum(sums, "tp") / width
     in_grad = jnp.stack(
@@ -464,11 +787,13 @@
             for i in range(3)
         ]
     )
-    in_grad, out_grad, down_grad = lax.optimization_barrier((in_grad, out_grad, down_grad))
+    in_grad, out_grad, down_grad, gu_grad = lax.optimization_barrier(
+        (in_grad, out_grad, down_grad, gu_grad)
+    )
     in_grad, out_grad = lax.psum((in_grad, out_grad), "ctx")
 
     normed1 = (tokens.astype(F32) - stat1[:, 0:1]) * stat1[:, 1:2]
-    tokens_grad = own(resid1_grad) + stat1[:, 1:2] * (
+    tokens_grad = own(branch_grad).astype(F32) + stat1[:, 1:2] * (
         grad_normed1 - sums[:, 0:1] - normed1 * sums[:, 1:2]
     )
     return (
@@ -476,7 +801,7 @@
         tokens_grad,
         jnp.transpose(in_grad, (1, 0, 2)).astype(F32),
         out_grad.astype(F32),
-        jnp.stack([gate_grad.astype(F32), up_grad.astype(F32)], axis=1),
+        weave(gu_grad, BLOCK),
         down_grad.astype(F32),
     )
 

time: 1290 us -> 1120 us (0.87)
  waiting for transfers between devices: 867 us -> 653 us
  Pallas kernels: 61.4 us -> 268 us
  local copies, waits for them, and re-layouts: 110 us -> 32.4 us
  matrix products: 119 us -> 69.7 us
  other arithmetic: 70.3 us -> 40 us
    pallas_call x1 -> x6, Pallas kernels: 16.4 us -> 222 us  [the longest x1 111 us: norm_back(): pl.pallas_call(functools.partial(norm_back_kernel, n, sub), in_specs=[vme...]
    psum x2 -> x1, waiting for transfers between devices: 363 us -> 160 us  [per_device(): lax.psum((down_grad, gu_grad), 'ctx')]
    all_gather x0 -> x3, waiting for transfers between devices: none -> 123 us  [the longest x1 54.3 us: per_device(): all_grad = lax.all_gather(grad_mixed, 'ctx', axis=0, tiled=True)]
    reduce_scatter x1 -> x0, waiting for transfers between devices: 97 us -> none  [per_device(): own_pairs = lax.psum_scatter(dpairs, 'ctx', scatter_dimension=0, tiled=True)]
    unnamed x40 -> x31, local copies, waits for them, and re-layouts: 57 us -> 0.46 us
    dot_general x8 -> x2, matrix products: 84.6 us -> 39.3 us  [the longest x1 19.9 us: per_device(): lax.dot_general(grad_gu, gu_w, NT, preferred_element_type=F32).astype(BF16)]
    psum x1, waiting for transfers between devices: 17.3 us -> 61.8 us  [per_device(): in_grad, out_grad = lax.psum((in_grad, out_grad), 'ctx')]
    reduce_scatter x1, waiting for transfers between devices: 39.9 us -> 0.02 us  [per_device(): branch = lax.psum_scatter(branch, 'tp', scatter_dimension=1, tiled=True)]
  transfers between devices with their start and end apart: 11 -> 12, of which waited for: 11 -> 11; matrix products, arithmetic and copies ran while one was open for 19% -> 8% of each run, Pallas kernels for 4% -> 22%
where the time goes in v2:
time: 1120 us
  waiting for transfers between devices  653 us (58%)
  Pallas kernels  268 us (24%)
  matrix products  69.7 us (6%)
  other arithmetic  40 us (4%)
  blocking collectives  36.5 us (3%)
  local copies, waits for them, and re-layouts  32.4 us (3%)
  between operations  18.6 us (2%)
    all_gather x4, waiting for transfers between devices, gather(): return lax.all_gather(local, 'tp', axis=axis, tiled=True)  196 us
    psum x1, waiting for transfers between devices, per_device(): lax.psum((down_grad, gu_grad), 'ctx')  160 us
    pallas_call x1, Pallas kernels, norm_back(): pl.pallas_call(functools.partial(norm_back_kernel, n, sub), in_specs=[vme...  111 us
    psum x1, waiting for transfers between devices, per_device(): in_grad, out_grad = lax.psum((in_grad, out_grad), 'ctx')  61.8 us
    all_gather x1, waiting for transfers between devices, per_device(): all_pairs = lax.all_gather(pairs, 'ctx', axis=0, tiled=True)  58.9 us
    all_gather x1, waiting for transfers between devices, per_device(): all_grad = lax.all_gather(grad_mixed, 'ctx', axis=0, tiled=True)  54.3 us
    reduce_scatter x1, waiting for transfers between devices, per_device(): lax.psum_scatter(part, 'tp', scatter_dimension=1, tiled=True).astype(F32)  50.6 us
    all_gather x1, waiting for transfers between devices, per_device(): all_query = lax.all_gather(query, 'ctx', axis=0, tiled=True)  48.3 us
  transfers between devices with their start and end apart: 12, of which 11 were waited for; matrix products, arithmetic and copies ran while one was open for 8% of the time, Pallas kernels for 22%

profile of v2, /device:TPU:0, one launch (start us, length us, event | category | flops | bytes accessed | tf_op | source)
XLA Modules:
  0.0 1118.5 jit_solution(344952954441165757)
XLA Ops:
  12.4 63.4 %all-gather.10.cloned.1.call-done.tok_ref = bf16[768,2048]{1,0:T(8,128)(2,1)} async-done(((bf16[768,512]{1,0:T(8,128)(2,1)}), bf16[768,2048]{1,0:T(8,128)(2,1)}) %all-gather.10.cloned.1.call-update) | async-done | bytes 3145744 | tf_op jit(solution)/shard_map/all_gather | solution.py:720
  75.8 11.2 %project.1 = (bf16[768,2048]{1,0:T(8,128)(2,1)}, f32[768,2]{1,0:T(8,128)}, bf16[768,512]{1,0:T(8,128)(2,1)}, bf16[768,1024]{1,0:T(8,128)(2,1)}) custom-call(bf16[768,2048]{1,0:T(8,128)(2,1)} %all-gather.10.cloned.1.call-done.tok_ref, bf16[3,2048,512]{2,1,0:T(8,128)(2,1)} %bitcast.47, f32[768,128]{1,0:T(8,128)} %get-tuple-element.77.cos_ref, ...), custom_call_target="tpu_custom_call" | custom-call | flops 4831838208 | bytes 15728640 | tf_op jit(solution)/shard_map/project/pallas_call | solution.py:70
  87.1 17.5 %all-gather.16.cloned.1.call-done = bf16[2048,256]{1,0:T(8,128)(2,1)} async-done(((bf16[512,256]{1,0:T(8,128)(2,1)}), bf16[2048,256]{1,0:T(8,128)(2,1)}) %all-gather.16.cloned.1.call-update) | async-done | bytes 1048592 | tf_op jit(solution)/shard_map/all_gather | solution.py:720
  104.6 9.5 all-gather
  119.8 58.9 %all-gather.12.cloned.1.call-done.k_ref.v_ref = bf16[6144,1024]{1,0:T(8,128)(2,1)} async-done(((bf16[768,1024]{1,0:T(8,128)(2,1)}), bf16[6144,1024]{1,0:T(8,128)(2,1)}) %all-gather.12.cloned.1.call-update) | async-done | bytes 12582928 | tf_op jit(solution)/shard_map/all_gather | solution.py:751
  178.7 8.5 attend.1
  188.1 27.9 %reshape.110.w_ref = bf16[2048,4096]{1,0:T(8,128)(2,1)} reshape(bf16[2048,4,2,512]{3,2,1,0:T(2,128)(2,1)} %bitcast.44) | data formatting | bytes 33554432 | tf_op jit(solution)/shard_map/reshape | solution.py:728
  215.9 20.5 %all-gather.18.cloned.1.call-done.w_ref = bf16[2048,2048]{1,0:T(8,128)(2,1)} async-done(((bf16[2048,256]{1,0:T(8,128)(2,1)}), bf16[2048,2048]{1,0:T(8,128)(2,1)}) %all-gather.18.cloned.1.call-update) | async-done | bytes 8388624 | tf_op jit(solution)/shard_map/all_gather | solution.py:754
  236.4 64.9 %all-gather.14.cloned.1.call-done.mixed_ref = bf16[768,2048]{1,0:T(8,128)(2,1)} async-done(((bf16[768,512]{1,0:T(8,128)(2,1)}), bf16[768,2048]{1,0:T(8,128)(2,1)}) %all-gather.14.cloned.1.call-update) | async-done | bytes 3145744 | tf_op jit(solution)/shard_map/all_gather | solution.py:720
  301.3 13.7 %merge.1 = (f32[768,2048]{1,0:T(8,128)}, f32[768,2]{1,0:T(8,128)}, bf16[768,2048]{1,0:T(8,128)(2,1)}) custom-call(bf16[768,2048]{1,0:T(8,128)(2,1)} %all-gather.14.cloned.1.call-done.mixed_ref, bf16[2048,2048]{1,0:T(8,128)(2,1)} %all-gather.18.cloned.1.call-done.w_ref, bf16[768,2048]{1,0:T(8,128)(2,1)} %all-gather.10.cloned.1.call-done.tok_ref), custom_call_target="tpu_custom_call" | custom-call | flops 6442450944 | bytes 24117248 | tf_op jit(solution)/shard_map/merge/pallas_call | solution.py:421
  315.0 49.9 %all-gather.20.cloned.1.call-done.cot_ref = bf16[768,2048]{1,0:T(8,128)(2,1)} async-done(((bf16[768,512]{1,0:T(8,128)(2,1)}), bf16[768,2048]{1,0:T(8,128)(2,1)}) %all-gather.20.cloned.1.call-update) | async-done | bytes 3145744 | tf_op jit(solution)/shard_map/all_gather | solution.py:720
  364.9 26.9 %feed.1 = (bf16[768,2048]{1,0:T(8,128)(2,1)}, bf16[768,4096]{1,0:T(8,128)(2,1)}) custom-call(bf16[768,2048]{1,0:T(8,128)(2,1)} %get-tuple-element.38.inner_ref, bf16[768,2048]{1,0:T(8,128)(2,1)} %all-gather.20.cloned.1.call-done.cot_ref, bf16[2048,4096]{1,0:T(8,128)(2,1)} %reshape.110.w_ref, bf16[2048,2048]{1,0:T(8,128)(2,1)} %down_ref.1), custom_call_target="tpu_custom_call" | custom-call | flops 19327352832 | bytes 31457280 | tf_op jit(solution)/shard_map/feed/pallas_call | solution.py:453
  391.8 19.9 %convolution_convert_fusion.2.part_ref = bf16[768,2048]{1,0:T(8,128)(2,1)} fusion(bf16[768,4096]{1,0:T(8,128)(2,1)} %get-tuple-element.40, bf16[2048,4096]{1,0:T(8,128)(2,1)} %reshape.110.w_ref), kind=kOutput, calls=%fused_computation.3 | convolution fusion | flops 12886474752 | bytes 26214400 | tf_op jit(solution)/shard_map/dot_general | solution.py:761
  411.7 19.4 %convolution_convert_fusion = bf16[2048,4096]{1,0:T(8,128)(2,1)} fusion(bf16[768,2048]{1,0:T(8,128)(2,1)S(1)} %copy-done.12, bf16[768,4096]{1,0:T(8,128)(2,1)} %get-tuple-element.40), kind=kOutput, calls=%fused_computation | convolution fusion | flops 12893290496 | bytes 26214400 | tf_op jit(solution)/shard_map/dot_general | solution.py:763
  431.2 9.1 convolution_convert_fusion.1
  441.0 110.7 %norm_back.1.branch_ref = bf16[768,2048]{1,0:T(8,128)(2,1)} custom-call(bf16[768,2048]{1,0:T(8,128)(2,1)} %convolution_convert_fusion.2.part_ref, bf16[768,2048]{1,0:T(8,128)(2,1)} %all-gather.20.cloned.1.call-done.cot_ref, f32[768,2048]{1,0:T(8,128)} %get-tuple-element.37.resid_ref, f32[768,2]{1,0:T(8,128)} %get-tuple-element.42.stat_ref), custom_call_target="tpu_custom_call" | custom-call | flops 99999997952 | bytes 18874368 | tf_op jit(solution)/shard_map/norm_back/pallas_call | solution.py:637
  551.8 6.8 mixed_grad.1
  558.7 10.2 convolution_convert_fusion.3
  573.2 4.3 convolution_convert_fusion.4
  577.5 9.1 query_grad.1.dq_ref
  586.6 160.3 %all-reduce.7.cloned.1.call-done = (bf16[2048,2048]{1,0:T(8,128)(2,1)}, bf16[2048,4096]{1,0:T(8,128)(2,1)}) async-done(((bf16[2048,2048]{1,0:T(8,128)(2,1)}, bf16[2048,4096]{1,0:T(8,128)(2,1)}), (bf16[2048,2048]{1,0:T(8,128)(2,1)}, bf16[2048,4096]{1,0:T(8,128)(2,1)})) %all-reduce.7.cloned.1.call-update) | async-done | bytes 25165840 | tf_op jit(solution)/shard_map/psum | solution.py:767
  746.9 48.3 %all-gather.22.cloned.1.call-done.q_ref = bf16[6144,512]{1,0:T(8,128)(2,1)} async-done(((bf16[768,512]{1,0:T(8,128)(2,1)}), bf16[6144,512]{1,0:T(8,128)(2,1)}) %all-gather.22.cloned.1.call-update) | async-done | bytes 6291472 | tf_op jit(solution)/shard_map/all_gather | solution.py:755
  795.1 54.3 %all-gather.24.cloned.1.call-done.g_ref = bf16[6144,640]{1,0:T(8,128)(2,1)} async-done(((bf16[768,640]{1,0:T(8,128)(2,1)}), bf16[6144,640]{1,0:T(8,128)(2,1)}) %all-gather.24.cloned.1.call-update) | async-done | bytes 7864336 | tf_op jit(solution)/shard_map/all_gather | solution.py:776
  849.4 47.8 %key_grad.1 = (f32[768,512]{1,0:T(8,128)}, f32[768,512]{1,0:T(8,128)}) custom-call(s32[3]{0:T(128)} %pad_add_fusion.1.info, bf16[768,1024]{1,0:T(8,128)(2,1)} %get-tuple-element.35.k_ref.v_ref, bf16[768,1024]{1,0:T(8,128)(2,1)} %get-tuple-element.35.k_ref.v_ref, bf16[6144,512]{1,0:T(8,128)(2,1)} %all-gather.22.cloned.1.call-done.q_ref, ...), custom_call_target="tpu_custom_call" | custom-call | flops 19327352832 | bytes 12582912 | tf_op jit(solution)/shard_map/key_grad/pallas_call | solution.py:339
  897.2 12.4 %unproject.1 = (bf16[768,1536]{1,0:T(8,128)(2,1)}, bf16[768,2048]{1,0:T(8,128)(2,1)}, f32[768,2]{1,0:T(8,128)}) custom-call(f32[768,512]{1,0:T(8,128)} %query_grad.1.dq_ref, f32[768,512]{1,0:T(8,128)} %get-tuple-element.48.dk_ref, f32[768,512]{1,0:T(8,128)} %get-tuple-element.49.dv_ref, f32[768,128]{1,0:T(8,128)} %get-tuple-element.77.cos_ref, ...), custom_call_target="tpu_custom_call" | custom-call | flops 4831838208 | bytes 15728640 | tf_op jit(solution)/shard_map/unproject/pallas_call | solution.py:688
  923.8 12.0 %convert_element_type.85 = f32[2048,2048]{1,0:T(8,128)} convert(bf16[2048,2048]{1,0:T(8,128)(2,1)} %get-tuple-element.61) | non-fusion elementwise | flops 4194304 | bytes 25165824 | tf_op jit(solution)/shard_map/convert_element_type | solution.py:805
  935.8 20.8 %weave.1 = f32[2048,2,2048]{2,1,0:T(2,128)} custom-call(bf16[2048,4096]{1,0:T(8,128)(2,1)} %get-tuple-element.60.sum_ref), custom_call_target="tpu_custom_call" | custom-call | flops 8388608 | bytes 50331648 | tf_op jit(solution)/shard_map/weave/pallas_call | solution.py:487
  956.5 26.9 %psum.35 = f32[768,2]{1,0:T(8,128)S(1)} all-reduce(f32[768,2]{1,0:T(8,128)} %get-tuple-element.51), channel_id=1, replica_groups=mesh['ctx'=8,'tp'=4] {'tp'}, use_global_device_ids=true, to_apply=%region_6.7 | all-reduce | flops 1536 | bytes 12288 | tf_op jit(solution)/shard_map/psum | solution.py:781
  983.9 61.8 %all-reduce.5.cloned.1.call-done = (bf16[2048,3,512]{2,0,1:T(8,128)(2,1)}, bf16[512,2048]{1,0:T(8,128)(2,1)}) async-done(((bf16[2048,3,512]{2,0,1:T(8,128)(2,1)}, bf16[512,2048]{1,0:T(8,128)(2,1)}), (bf16[2048,3,512]{2,0,1:T(8,128)(2,1)}, bf16[512,2048]{1,0:T(8,128)(2,1)})) %all-reduce.5.cloned.1.call-update) | async-done | bytes 8388624 | tf_op jit(solution)/shard_map/psum | solution.py:793
  1045.7 9.5 convert_element_type.83
  1057.7 50.6 %reduce-scatter.5.cloned.1.call-done = bf16[768,512]{1,0:T(8,128)(2,1)} async-done(((bf16[768,2048]{1,0:T(8,128)(2,1)}), bf16[768,512]{1,0:T(8,128)(2,1)}) %reduce-scatter.5.cloned.1.call-update) | async-done | bytes 786448 | tf_op jit(solution)/shard_map/reduce_scatter | solution.py:780
  1108.3 3.1 multiply_add_fusion
  (88 shorter events, 29.9 us)
Async XLA Ops:
  7.2 68.6 %all-gather.10.cloned.1.call-start = ((), (), s32[]{:S(2)}) async-start(), calls=%async_computation.2 | async-start | bytes 3932160 | tf_op jit(solution)/shard_map/all_gather | solution.py:720
  7.9 96.7 %all-gather.16.cloned.1.call-start = ((), (), s32[]{:S(2)}) async-start(), calls=%async_computation.5 | async-start | bytes 1310720 | tf_op jit(solution)/shard_map/all_gather | solution.py:720
  9.7 169.0 %all-gather.12.cloned.1.call-start = ((), (), s32[]{:S(2)}) async-start(), calls=%async_computation.3 | async-start | bytes 14155776 | tf_op jit(solution)/shard_map/all_gather | solution.py:751
  75.8 28.9 %copy-start.8 = (s32[768]{0:T(1024)S(1)}, s32[768]{0:T(1024)}, u32[]{:S(2)}) copy-start(s32[768]{0:T(1024)} %param.8) | copy-start | bytes 9220
  87.0 149.4 %all-gather.18.cloned.1.call-start = ((), (), s32[]{:S(2)}) async-start(), calls=%async_computation.6 | async-start | bytes 9437184 | tf_op jit(solution)/shard_map/all_gather | solution.py:754
  104.6 196.7 %all-gather.14.cloned.1.call-start = ((), (), s32[]{:S(2)}) async-start(), calls=%async_computation.4 | async-start | bytes 3932160 | tf_op jit(solution)/shard_map/all_gather | solution.py:720
  114.6 72.6 %copy-start.3 = (s32[48,128]{1,0:T(8,128)}, s32[48,128]{1,0:T(8,128)S(1)}, u32[]{:S(2)}) copy-start(s32[48,128]{1,0:T(8,128)S(1)} %reduce-window.9) | copy-start | bytes 73732
  114.9 72.3 %copy-start.6 = (s32[48]{0:T(128)}, s32[48]{0:T(128)S(1)}, u32[]{:S(2)}) copy-start(s32[48]{0:T(128)S(1)} %slice_reduce_fusion.4) | copy-start | bytes 580
  115.2 72.1 %copy-start.5 = (s32[8,768]{1,0:T(8,128)}, s32[8,768]{1,0:T(8,128)S(1)}, u32[]{:S(2)}) copy-start(s32[8,768]{1,0:T(8,128)S(1)} %bitcast_maximum_fusion) | copy-start | bytes 73732
  187.3 177.7 %all-gather.20.cloned.1.call-start = ((), (), s32[]{:S(2)}) async-start(), calls=%async_computation.7 | async-start | bytes 3932160 | tf_op jit(solution)/shard_map/all_gather | solution.py:720
  187.8 559.0 %all-reduce.7.cloned.1.call-start = ((), (), s32[]{:S(2)}) async-start(), calls=%async_computation.13 | async-start | bytes 50331648 | tf_op jit(solution)/shard_map/psum | solution.py:767
  391.8 19.9 %copy-start.12 = (bf16[768,2048]{1,0:T(8,128)(2,1)S(1)}, bf16[768,2048]{1,0:T(8,128)(2,1)}, u32[]{:S(2)}) copy-start(bf16[768,2048]{1,0:T(8,128)(2,1)} %get-tuple-element.38.inner_ref) | copy-start | bytes 9437188
  411.7 19.4 %copy-start.9 = (bf16[768,2048]{1,0:T(8,128)(2,1)S(1)}, bf16[768,2048]{1,0:T(8,128)(2,1)}, u32[]{:S(2)}) copy-start(bf16[768,2048]{1,0:T(8,128)(2,1)} %all-gather.20.cloned.1.call-done.cot_ref) | copy-start | bytes 9437188
  411.7 19.4 %copy-start.13 = (bf16[768,2048]{1,0:T(8,128)(2,1)S(1)}, bf16[768,2048]{1,0:T(8,128)(2,1)}, u32[]{:S(2)}) copy-start(bf16[768,2048]{1,0:T(8,128)(2,1)} %get-tuple-element.39) | copy-start | bytes 9437188
  440.2 354.9 %all-gather.22.cloned.1.call-start = ((), (), s32[]{:S(2)}) async-start(), calls=%async_computation.9 | async-start | bytes 7077888 | tf_op jit(solution)/shard_map/all_gather | solution.py:755
  441.0 408.4 %all-gather.24.cloned.1.call-start = ((), (), s32[]{:S(2)}) async-start(), calls=%async_computation.10 | async-start | bytes 8847360 | tf_op jit(solution)/shard_map/all_gather | solution.py:776
  551.7 6.9 copy-start.14
  558.6 362.4 %reduce-scatter.3.cloned.1.call-start = ((), (), s32[]{:S(2)}) async-start(), calls=%async_computation.8 | async-start | bytes 3932160 | tf_op jit(solution)/shard_map/reduce_scatter | solution.py:771
  568.9 3.6 copy-start.4
  568.9 3.6 copy-start.7
  568.9 4.3 copy-start
  568.9 476.7 %all-reduce.5.cloned.1.call-start = ((), (), s32[]{:S(2)}) async-start(), calls=%async_computation.12 | async-start | bytes 16777216 | tf_op jit(solution)/shard_map/psum | solution.py:793
  897.2 12.4 %copy-start.11 = (bf16[768,2048]{1,0:T(8,128)(2,1)S(1)}, bf16[768,2048]{1,0:T(8,128)(2,1)}, u32[]{:S(2)}) copy-start(bf16[768,2048]{1,0:T(8,128)(2,1)} %get-tuple-element.52) | copy-start | bytes 9437188
  909.6 3.1 copy-start.10
  919.5 1.0 copy-start.2
  919.5 188.8 %reduce-scatter.5.cloned.1.call-start = ((), (), s32[]{:S(2)}) async-start(), calls=%async_computation.11 | async-start | bytes 3932160 | tf_op jit(solution)/shard_map/reduce_scatter | solution.py:780
  1045.7 9.5 copy-start.1
Sparse Core Ops, SparseCore 0:
  9.6 66.1 all-gather.9
  77.9 26.6 all-gather.15
  107.0 71.6 all-gather.11
  180.4 55.9 all-gather.17
  237.8 63.4 all-gather.13
  302.7 62.1 all-gather.19
  440.4 306.4 all-reduce.6
  749.5 45.6 all-gather.21
  797.2 52.1 all-gather.23
  851.7 60.2 reduce-scatter.2
  919.7 125.9 all-reduce.4
  1047.8 60.4 reduce-scatter.4

commit v3 on v2

--- a/solution.py
+++ b/solution.py
@@ -188,6 +188,393 @@
     )(info, query, pairs, pairs, begin)
 
 
+CUBE = 8
+CUBE_SENDS = 10
+
+
+class Cube:
+    def __init__(self, buf, send, recv):
+        me = lax.axis_index("ctx")
+        flip = (1 - 2 * (me % 2), 2 - 4 * ((me // 2) % 2), 4 - 8 * (me // 4))
+        self.me, self.flip, self.buf, self.send, self.recv = me, flip, buf, send, recv
+        self.rows = buf.shape[0] // CUBE
+
+    def copy(self, n):
+        core, x, y = self.flip
+        half = self.rows // 2
+        block, part, target = (
+            (0, None, core),
+            (0, 0, x), (0, 1, x), (0, 1, y), (0, 0, y),
+            (x, 0, y), (y, 1, x),
+            (x, None, core), (y, None, core), (x + y, None, core),
+        )[n]
+        start = (self.me + block) * self.rows
+        size = self.rows
+        if part is not None:
+            start, size = start + part * half, half
+        place = self.buf.at[pl.ds(pl.multiple_of(start, 16), size)]
+        return pltpu.make_async_remote_copy(
+            src_ref=place, dst_ref=place, send_sem=self.send.at[n], recv_sem=self.recv.at[n],
+            device_id={"ctx": self.me + target}, device_id_type=MESH,
+        )
+
+    def arrived(self, n):
+        self.copy(n).wait_recv()
+
+    def start(self, *which):
+        for n in which:
+            self.copy(n).start()
+
+    def signal(self, barrier):
+        for target in self.flip:
+            pl.semaphore_signal(
+                barrier, inc=1, device_id={"ctx": self.me + target}, device_id_type=MESH
+            )
+
+    def block(self, step):
+        core, x, y = self.flip
+        on = lambda *steps: sum((step == n).astype(jnp.int32) for n in steps)
+        return self.me + on(1, 4, 5, 7) * core + on(2, 4, 6, 7) * x + on(3, 5, 6, 7) * y
+
+    def advance(self, step):
+        @pl.when(step == 0)
+        def _():
+            self.start(0, 1, 3, 2, 4)
+
+        @pl.when(step == 1)
+        def _():
+            self.arrived(0)
+
+        @pl.when(step == 2)
+        def _():
+            self.arrived(1)
+            self.start(5)
+            self.arrived(3)
+            self.start(6)
+            self.arrived(2)
+            self.start(7)
+
+        @pl.when(step == 3)
+        def _():
+            self.arrived(4)
+            self.start(8)
+
+        @pl.when(step == 4)
+        def _():
+            self.arrived(7)
+
+        @pl.when(step == 5)
+        def _():
+            self.arrived(8)
+
+        @pl.when(step == 6)
+        def _():
+            self.arrived(5)
+            self.arrived(6)
+            self.start(9)
+
+        @pl.when(step == 7)
+        def _():
+            self.arrived(9)
+
+    def finish(self):
+        for n in range(CUBE_SENDS):
+            self.copy(n).wait_send()
+
+
+def hidden_scores(scores, key_block, query_block, rows, begin):
+    key_place = lax.broadcasted_iota(jnp.int32, scores.shape, 0) + key_block * rows
+    query_place = lax.broadcasted_iota(jnp.int32, scores.shape, 1) + query_block * rows
+    return jnp.where((key_place <= query_place) & (key_place >= begin), scores, NEG)
+
+
+def attend_far_kernel(
+    heads, n, q_ref, own_ref, begin_ref, cot_ref,
+    raw_ref, mixed_ref, lse_ref, pair_ref, full_ref,
+    high_ref, total_ref, acc_ref, s_ref, send, recv, zsend, zrecv,
+):
+    rows = q_ref.shape[0]
+    span = heads * HD
+    shard = cot_ref.shape[1]
+    at = lax.axis_index("tp")
+    cube = Cube(pair_ref, send, recv)
+    me = cube.me
+    barrier = pltpu.get_barrier_semaphore()
+    cube.signal(barrier)
+
+    @pl.when(at > 0)
+    def _():
+        pl.semaphore_signal(barrier, inc=1, device_id={"tp": at - 1}, device_id_type=MESH)
+
+    @pl.when(at < n - 1)
+    def _():
+        pl.semaphore_signal(barrier, inc=1, device_id={"tp": at + 1}, device_id_type=MESH)
+
+    pair_ref[pl.ds(pl.multiple_of(me * rows, 16), rows), :] = own_ref[...]
+    full_ref[:, pl.ds(pl.multiple_of(at * shard, 128), shard)] = cot_ref[...]
+    high_ref[...] = jnp.full_like(high_ref, NEG)
+    total_ref[...] = jnp.zeros_like(total_ref)
+    acc_ref[...] = jnp.zeros_like(acc_ref)
+    pl.semaphore_wait(barrier, jnp.where((at > 0) & (at < n - 1), 5, 4))
+
+    def pass_on(right, s, k):
+        place = full_ref.at[:, pl.ds(pl.multiple_of(s * shard, 128), shard)]
+        which = (1 if right else 0, k)
+        return pltpu.make_async_remote_copy(
+            src_ref=place, dst_ref=place, send_sem=zsend.at[which], recv_sem=zrecv.at[which],
+            device_id={"tp": at + 1 if right else at - 1}, device_id_type=MESH,
+        )
+
+    def line_step(k):
+        @pl.when(at >= k)
+        def _():
+            if k > 0:
+                pass_on(True, at - k, k - 1).wait_recv()
+
+            @pl.when(at < n - 1)
+            def _():
+                pass_on(True, at - k, k).start()
+
+        @pl.when(at + k < n)
+        def _():
+            if k > 0:
+                pass_on(False, at + k, k - 1).wait_recv()
+
+            @pl.when(at > 0)
+            def _():
+                pass_on(False, at + k, k).start()
+
+    def turn(step, carry):
+        cube.advance(step)
+        for k in range(n):
+            @pl.when(step == min(k * 2, CUBE - 1 - (n - 1 - k)) if n <= CUBE else k)
+            def _():
+                line_step(k)
+        block = cube.block(step)
+
+        @pl.when(block <= me)
+        def _():
+            place = pl.ds(pl.multiple_of(block * rows, 16), rows)
+
+            def score(h):
+                hs = slice(h * HD, (h + 1) * HD)
+                s = lax.dot_general(
+                    pair_ref[place, hs], q_ref[:, hs], NT, preferred_element_type=F32
+                )
+                s_ref[h % 2] = hidden_scores(s, block, me, rows, begin_ref[...])
+
+            def spread(h):
+                s = s_ref[h % 2]
+                old = high_ref[h : h + 1, :]
+                new = jnp.maximum(old, jnp.max(s, axis=0, keepdims=True))
+                high_ref[h : h + 1, :] = new
+                p = jnp.exp2(s * C2 - new * C2)
+                decay = jnp.exp2((old - new) * C2)
+                total_ref[h : h + 1, :] = total_ref[h : h + 1, :] * decay + jnp.sum(
+                    p, axis=0, keepdims=True
+                )
+                acc_ref[h] = acc_ref[h] * decay + lax.dot_general(
+                    pair_ref[place, span + h * HD : span + (h + 1) * HD], p.astype(BF16), TN,
+                    preferred_element_type=F32,
+                )
+
+            score(0)
+            for h in range(heads):
+                if h + 1 < heads:
+                    score(h + 1)
+                spread(h)
+
+        return carry
+
+    lax.fori_loop(0, CUBE, turn, 0)
+    for h in range(heads):
+        hs = slice(h * HD, (h + 1) * HD)
+        out = (acc_ref[h] / total_ref[h : h + 1, :]).T
+        raw_ref[:, hs] = out
+        mixed_ref[:, hs] = out.astype(BF16)
+    lse_ref[...] = high_ref[...] * C2 + jnp.log2(total_ref[...])
+    cube.finish()
+    for k in range(n):
+        @pl.when((at >= k) & (at < n - 1))
+        def _():
+            pass_on(True, at - k, k).wait_send()
+
+        @pl.when((at + k < n) & (at > 0))
+        def _():
+            pass_on(False, at + k, k).wait_send()
+
+
+def attend_far(query, pairs, begin, cot, heads, n):
+    rows = query.shape[0]
+    span = heads * HD
+    vmem = pl.BlockSpec(memory_space=pltpu.VMEM)
+    return pl.pallas_call(
+        functools.partial(attend_far_kernel, heads, n),
+        in_specs=[vmem] * 4,
+        out_specs=[vmem] * 5,
+        out_shape=[
+            jax.ShapeDtypeStruct((rows, span), F32),
+            jax.ShapeDtypeStruct((rows, span), BF16),
+            jax.ShapeDtypeStruct((heads, rows), F32),
+            jax.ShapeDtypeStruct((CUBE * rows, 2 * span), BF16),
+            jax.ShapeDtypeStruct((rows, n * cot.shape[1]), BF16),
+        ],
+        scratch_shapes=[
+            pltpu.VMEM((heads, rows), F32),
+            pltpu.VMEM((heads, rows), F32),
+            pltpu.VMEM((heads, HD, rows), F32),
+            pltpu.VMEM((2, rows, rows), F32),
+            pltpu.SemaphoreType.DMA((CUBE_SENDS,)),
+            pltpu.SemaphoreType.DMA((CUBE_SENDS,)),
+            pltpu.SemaphoreType.DMA((2, n)),
+            pltpu.SemaphoreType.DMA((2, n)),
+        ],
+        compiler_params=params(58, collective_id=2, has_side_effects=True),
+        cost_estimate=cost(1e6, 1e6),
+        name="attend_far",
+    )(query, pairs, begin, cot)
+
+
+def attend_back_far_kernel(
+    heads, n, g_ref, q_ref, pair_ref, begin_ref, part_ref,
+    dq_ref, dk_ref, dv_ref, layer_ref,
+    all_ref, acc_ref, rows_ref, s_ref, p_ref, land_ref, send, recv, zsend, zrecv,
+):
+    rows = g_ref.shape[0]
+    span = heads * HD
+    shard = layer_ref.shape[1]
+    at = lax.axis_index("tp")
+    cube = Cube(all_ref, send, recv)
+    me = cube.me
+    barrier = pltpu.get_barrier_semaphore()
+    cube.signal(barrier)
+    for o in range(1, n):
+        pl.semaphore_signal(
+            barrier, inc=1, device_id={"tp": lax.rem(at + o, n)}, device_id_type=MESH
+        )
+    all_ref[pl.ds(pl.multiple_of(me * rows, 16), rows), :] = g_ref[...]
+    acc_ref[...] = jnp.zeros_like(acc_ref)
+    dk_ref[...] = jnp.zeros_like(dk_ref)
+    dv_ref[...] = jnp.zeros_like(dv_ref)
+    pl.semaphore_wait(barrier, 3 + n - 1)
+
+    def term(o):
+        target = lax.rem(at + o, n)
+        return pltpu.make_async_remote_copy(
+            src_ref=part_ref.at[:, pl.ds(pl.multiple_of(target * shard, 128), shard)],
+            dst_ref=land_ref.at[o - 1],
+            send_sem=zsend.at[o - 1], recv_sem=zrecv.at[o - 1],
+            device_id={"tp": target}, device_id_type=MESH,
+        )
+
+    own = pl.ds(pl.multiple_of(me * rows, 16), rows)
+
+    def turn(step, carry):
+        cube.advance(step)
+
+        @pl.when(step == 0)
+        def _():
+            for o in range(1, n):
+                term(o).start()
+
+        block = cube.block(step)
+        place = pl.ds(pl.multiple_of(block * rows, 16), rows)
+
+        def scores(h, key_block, key_place, query_block, query_place):
+            hs = slice(h * HD, (h + 1) * HD)
+            vs = slice(span + h * HD, span + (h + 1) * HD)
+            s = lax.dot_general(
+                pair_ref[key_place, hs], q_ref[query_place, hs], NT, preferred_element_type=F32
+            )
+            begin = begin_ref[pl.ds(query_block, 1), :]
+            s_ref[h % 2] = hidden_scores(s, key_block, query_block, rows, begin)
+            p_ref[h % 2] = lax.dot_general(
+                pair_ref[key_place, vs], all_ref[query_place, hs], NT, preferred_element_type=F32
+            )
+
+        def read_rows(query_place):
+            coded = all_ref[query_place, span:].astype(F32).T
+            for k in range(2 * heads):
+                rows_ref[k : k + 1, :] = (
+                    coded[3 * k : 3 * k + 1]
+                    + coded[3 * k + 1 : 3 * k + 2]
+                    + coded[3 * k + 2 : 3 * k + 3]
+                )
+
+        def weights(h):
+            p = jnp.exp2(s_ref[h % 2] * C2 - rows_ref[h : h + 1, :])
+            ds = p * (p_ref[h % 2] - rows_ref[heads + h : heads + h + 1, :])
+            return p.astype(BF16), ds.astype(BF16)
+
+        @pl.when(block <= me)
+        def _():
+            read_rows(own)
+            scores(0, block, place, me, own)
+            for h in range(heads):
+                if h + 1 < heads:
+                    scores(h + 1, block, place, me, own)
+                _, ds = weights(h)
+                acc_ref[h] = acc_ref[h] + lax.dot_general(
+                    pair_ref[place, h * HD : (h + 1) * HD], ds, TN, preferred_element_type=F32
+                )
+
+        @pl.when(block >= me)
+        def _():
+            read_rows(place)
+            scores(0, me, own, block, place)
+            for h in range(heads):
+                hs = slice(h * HD, (h + 1) * HD)
+                if h + 1 < heads:
+                    scores(h + 1, me, own, block, place)
+                p, ds = weights(h)
+                dv_ref[:, hs] += jnp.dot(p, all_ref[place, hs], preferred_element_type=F32)
+                dk_ref[:, hs] += jnp.dot(ds, q_ref[place, hs], preferred_element_type=F32)
+
+        return carry
+
+    lax.fori_loop(0, CUBE, turn, 0)
+    for h in range(heads):
+        dq_ref[:, h * HD : (h + 1) * HD] = (acc_ref[h] * SCALE).T
+    dk_ref[...] = dk_ref[...] * SCALE
+    total = part_ref[:, pl.ds(pl.multiple_of(at * shard, 128), shard)].astype(F32)
+    for o in range(1, n):
+        term(o).wait_recv()
+        total = total + land_ref[o - 1].astype(F32)
+    layer_ref[...] = total.astype(BF16)
+    cube.finish()
+    for o in range(1, n):
+        term(o).wait_send()
+
+
+def attend_back_far(grad, all_query, all_pairs, all_begin, part, heads, n):
+    rows = grad.shape[0]
+    span = heads * HD
+    shard = part.shape[1] // n
+    vmem = pl.BlockSpec(memory_space=pltpu.VMEM)
+    wide = jax.ShapeDtypeStruct((rows, span), F32)
+    return pl.pallas_call(
+        functools.partial(attend_back_far_kernel, heads, n),
+        in_specs=[vmem] * 5,
+        out_specs=[vmem] * 4,
+        out_shape=[wide, wide, wide, jax.ShapeDtypeStruct((rows, shard), BF16)],
+        scratch_shapes=[
+            pltpu.VMEM((CUBE * rows, span + HD), BF16),
+            pltpu.VMEM((heads, HD, rows), F32),
+            pltpu.VMEM((2 * heads, rows), F32),
+            pltpu.VMEM((2, rows, rows), F32),
+            pltpu.VMEM((2, rows, rows), F32),
+            pltpu.VMEM((n - 1, rows, shard), BF16),
+            pltpu.SemaphoreType.DMA((CUBE_SENDS,)),
+            pltpu.SemaphoreType.DMA((CUBE_SENDS,)),
+            pltpu.SemaphoreType.DMA((n - 1,)),
+            pltpu.SemaphoreType.DMA((n - 1,)),
+        ],
+        compiler_params=params(60, collective_id=3, has_side_effects=True),
+        cost_estimate=cost(1e6, 1e6),
+        name="attend_back_far",
+    )(grad, all_query, all_pairs, all_begin, part)
+
+
 def query_grad_kernel(
     heads, info, q_ref, do_ref, lse_ref, delta_ref, k_ref, v_ref, begin_ref,
     dq_ref, acc_ref, s_ref, g_ref,
@@ -403,37 +790,6 @@
     )(branch, weight, raw, lse)
 
 
-def merge_kernel(mixed_ref, w_ref, tok_ref, resid_ref, stat_ref, inner_ref):
-    out = jnp.dot(mixed_ref[...], w_ref[...], preferred_element_type=F32)
-    x = tok_ref[...].astype(F32) + out
-    resid_ref[...] = x
-    mean = jnp.mean(x, axis=1, keepdims=True)
-    center = x - mean
-    inverse = lax.rsqrt(jnp.mean(center * center, axis=1, keepdims=True) + EPS)
-    stat_ref[...] = jnp.concatenate([mean, inverse], axis=1)
-    inner_ref[...] = (center * inverse).astype(BF16)
-
-
-def merge(mixed_full, weight, tok_full):
-    rows, width = tok_full.shape
-    block = 256
-    row = lambda n: pl.BlockSpec((block, n), lambda i: (i, 0))
-    return pl.pallas_call(
-        merge_kernel,
-        grid=(rows // block,),
-        in_specs=[row(width), pl.BlockSpec((width, width), lambda i: (0, 0)), row(width)],
-        out_specs=[row(width), row(2), row(width)],
-        out_shape=[
-            jax.ShapeDtypeStruct((rows, width), F32),
-            jax.ShapeDtypeStruct((rows, 2), F32),
-            jax.ShapeDtypeStruct((rows, width), BF16),
-        ],
-        compiler_params=params(56),
-        cost_estimate=cost(2 * rows * width * width, 2 * width * width + 10 * rows * width),
-        name="merge",
-    )(mixed_full, weight, tok_full)
-
-
 def feed_kernel(inner_ref, cot_ref, w_ref, down_ref, hidden_ref, dgu_ref):
     block = down_ref.shape[0]
     both = jnp.dot(inner_ref[...], w_ref[...], preferred_element_type=F32)
@@ -614,6 +970,46 @@
             hand(False, c).wait_send()
 
 
+def merge_kernel(
+    n, sub, part_ref, tok_ref, inner_ref, resid_ref, stat_ref, from_left, from_right, send, recv
+):
+    line_barrier(lax.axis_index("tp"), n)
+    resid_ref[...] = jnp.zeros_like(resid_ref)
+    stat_ref[...] = jnp.zeros_like(stat_ref)
+
+    def row_fn(total, rows):
+        x = tok_ref[rows, :].astype(F32) + total
+        mean = jnp.mean(x, axis=1, keepdims=True)
+        center = x - mean
+        inverse = lax.rsqrt(jnp.mean(center * center, axis=1, keepdims=True) + EPS)
+        resid_ref[rows, :] = x
+        stat_ref[rows, :] = jnp.concatenate([mean, inverse], axis=1)
+        inner_ref[rows, :] = (center * inverse).astype(BF16)
+
+    sum_rows(n, sub, part_ref, inner_ref, row_fn, from_left, from_right, send, recv)
+
+
+def merge(part, tok_full, n):
+    rows, width = part.shape
+    sub = 48
+    vmem = pl.BlockSpec(memory_space=pltpu.VMEM)
+    return pl.pallas_call(
+        functools.partial(merge_kernel, n, sub),
+        in_specs=[vmem] * 2,
+        out_specs=[vmem] * 3,
+        out_shape=[
+            jax.ShapeDtypeStruct((rows, width), BF16),
+            jax.ShapeDtypeStruct((rows, width), F32),
+            jax.ShapeDtypeStruct((rows, 2), F32),
+        ],
+        scratch_shapes=[pltpu.VMEM((rows, width), BF16)] * 2
+        + [pltpu.SemaphoreType.DMA((4, rows // sub))] * 2,
+        compiler_params=params(56, collective_id=5, has_side_effects=True),
+        cost_estimate=cost(1e6, 1e6),
+        name="merge",
+    )(part, tok_full)
+
+
 def norm_back_kernel(
     n, sub, part_ref, cot_ref, resid_ref, stat_ref, out_ref, from_left, from_right, send, recv
 ):
@@ -642,79 +1038,156 @@
         scratch_shapes=[pltpu.VMEM((rows, width), BF16)] * 2
         + [pltpu.SemaphoreType.DMA((4, rows // sub))] * 2,
         compiler_params=params(56, collective_id=1, has_side_effects=True),
-        cost_estimate=cost(100e9, 12 * rows * width),
+        cost_estimate=cost(1e6, 1e6),
         name="norm_back",
     )(part, cot, resid, stat)
 
 
-def unproject_kernel(
-    heads, dq_ref, dk_ref, dv_ref, cos_ref, sin_ref, tok_ref, stat_ref, w_ref,
-    dproj_ref, part_ref, sums_ref,
-):
+def unrotate_kernel(heads, dq_ref, dk_ref, dv_ref, cos_ref, sin_ref, dproj_ref):
     cosine, sine = cos_ref[...], sin_ref[...]
     span = heads * HD
 
     def back(piece):
-        return piece * cosine - pltpu.roll(piece, HD // 2, 1) * sine
+        return (piece * cosine - pltpu.roll(piece, HD // 2, 1) * sine).astype(BF16)
 
     for h in range(heads):
         hs = slice(h * HD, (h + 1) * HD)
-        dproj_ref[:, hs] = back(dq_ref[:, hs]).astype(BF16)
-        dproj_ref[:, span + h * HD : span + (h + 1) * HD] = back(dk_ref[:, hs]).astype(BF16)
+        dproj_ref[:, hs] = back(dq_ref[:, hs])
+        dproj_ref[:, span + h * HD : span + (h + 1) * HD] = back(dk_ref[:, hs])
     dproj_ref[:, 2 * span :] = dv_ref[...].astype(BF16)
-    total = None
-    for part in range(3):
-        term = lax.dot_general(
-            dproj_ref[:, part * span : (part + 1) * span], w_ref[part], NT,
-            preferred_element_type=F32,
-        )
-        total = term if total is None else total + term
-    part_ref[...] = total.astype(BF16)
-    normed = (tok_ref[...].astype(F32) - stat_ref[:, 0:1]) * stat_ref[:, 1:2]
-    sums_ref[...] = jnp.concatenate(
-        [
-            jnp.sum(total, axis=1, keepdims=True),
-            jnp.sum(total * normed, axis=1, keepdims=True),
-        ],
-        axis=1,
-    )
-
-
-def unproject(dq, dk, dv, cosine, sine, tok_full, stat, weight, heads):
-    rows, width = tok_full.shape
-    span = heads * HD
+
+
+def unrotate(dq, dk, dv, cosine, sine, heads):
+    rows, span = dq.shape
     block = 256
     row = lambda n: pl.BlockSpec((block, n), lambda i: (i, 0))
     return pl.pallas_call(
-        functools.partial(unproject_kernel, heads),
+        functools.partial(unrotate_kernel, heads),
         grid=(rows // block,),
-        in_specs=[
-            row(span), row(span), row(span), row(HD), row(HD), row(width), row(2),
-            pl.BlockSpec((3, width, span), lambda i: (0, 0, 0)),
+        in_specs=[row(span), row(span), row(span), row(HD), row(HD)],
+        out_specs=row(3 * span),
+        out_shape=jax.ShapeDtypeStruct((rows, 3 * span), BF16),
+        compiler_params=params(56),
+        cost_estimate=cost(1e6, 18 * rows * span),
+        name="unrotate",
+    )(dq, dk, dv, cosine, sine)
+
+
+def unproject_kernel(
+    heads, n, dproj_ref, tok_ref, stat_ref, w_ref, branch_ref, out_ref,
+    part_ref, mine_ref, land_ref, sums_ref, far_ref, send, recv, ssend, srecv,
+):
+    rows, width = tok_ref.shape
+    shard = width // n
+    span = heads * HD
+    at = lax.axis_index("tp")
+    barrier = pltpu.get_barrier_semaphore()
+    for o in range(1, n):
+        pl.semaphore_signal(
+            barrier, inc=1, device_id={"tp": lax.rem(at + o, n)}, device_id_type=MESH
+        )
+    pl.semaphore_wait(barrier, n - 1)
+    block = 256
+    count = rows // block
+
+    def term(o, i):
+        target = lax.rem(at + o, n)
+        place = pl.ds(i * block, block)
+        return pltpu.make_async_remote_copy(
+            src_ref=part_ref.at[place, pl.ds(pl.multiple_of(target * shard, 128), shard)],
+            dst_ref=land_ref.at[o - 1, place],
+            send_sem=send.at[o - 1, i], recv_sem=recv.at[o - 1, i],
+            device_id={"tp": target}, device_id_type=MESH,
+        )
+
+    def sums(o):
+        return pltpu.make_async_remote_copy(
+            src_ref=sums_ref, dst_ref=far_ref.at[o - 1],
+            send_sem=ssend.at[o - 1], recv_sem=srecv.at[o - 1],
+            device_id={"tp": lax.rem(at + o, n)}, device_id_type=MESH,
+        )
+
+    own = pl.ds(pl.multiple_of(at * shard, 128), shard)
+    for i in range(count):
+        place = pl.ds(i * block, block)
+        total = None
+        for part in range(3):
+            piece = lax.dot_general(
+                dproj_ref[place, part * span : (part + 1) * span], w_ref[part], NT,
+                preferred_element_type=F32,
+            )
+            total = piece if total is None else total + piece
+        part_ref[place, :] = total.astype(BF16)
+        for o in range(1, n):
+            term(o, i).start()
+        normed = (tok_ref[place, :].astype(F32) - stat_ref[place, 0:1]) * stat_ref[place, 1:2]
+        first = jnp.sum(total, axis=1, keepdims=True)
+        second = jnp.sum(total * normed, axis=1, keepdims=True)
+        lane = lax.broadcasted_iota(jnp.int32, (block, HD), 1)
+        both = jnp.where(lane == 0, first, jnp.where(lane == 1, second, 0.0))
+        sums_ref[:, i * block : (i + 1) * block] = both.T[:8]
+    for o in range(1, n):
+        sums(o).start()
+    total = sums_ref[...]
+    for o in range(1, n):
+        sums(o).wait_recv()
+        total = total + far_ref[o - 1]
+    mine_ref[...] = total
+    for i in range(count):
+        place = pl.ds(i * block, block)
+        spread = jnp.concatenate(
+            [mine_ref[:, i * block : (i + 1) * block], jnp.zeros((HD - 8, block), F32)], axis=0
+        ).T / width
+        total = part_ref[place, own].astype(F32)
+        for o in range(1, n):
+            term(o, i).wait_recv()
+            total = total + land_ref[o - 1, place].astype(F32)
+        inverse = stat_ref[place, 1:2]
+        normed = (tok_ref[place, own].astype(F32) - stat_ref[place, 0:1]) * inverse
+        out_ref[place, :] = branch_ref[place, own].astype(F32) + inverse * (
+            total - spread[:, 0:1] - normed * spread[:, 1:2]
+        )
+    for o in range(1, n):
+        sums(o).wait_send()
+        for i in range(count):
+            term(o, i).wait_send()
+
+
+def unproject(dproj, tok_full, stat, weight, branch, heads, n):
+    rows, width = tok_full.shape
+    shard = width // n
+    vmem = pl.BlockSpec(memory_space=pltpu.VMEM)
+    return pl.pallas_call(
+        functools.partial(unproject_kernel, heads, n),
+        in_specs=[vmem] * 5,
+        out_specs=vmem,
+        out_shape=jax.ShapeDtypeStruct((rows, shard), F32),
+        scratch_shapes=[
+            pltpu.VMEM((rows, width), BF16),
+            pltpu.VMEM((8, rows), F32),
+            pltpu.VMEM((n - 1, rows, shard), BF16),
+            pltpu.VMEM((8, rows), F32),
+            pltpu.VMEM((n - 1, 8, rows), F32),
+            pltpu.SemaphoreType.DMA((n - 1, rows // 256)),
+            pltpu.SemaphoreType.DMA((n - 1, rows // 256)),
+            pltpu.SemaphoreType.DMA((n - 1,)),
+            pltpu.SemaphoreType.DMA((n - 1,)),
         ],
-        out_specs=[row(3 * span), row(width), row(2)],
-        out_shape=[
-            jax.ShapeDtypeStruct((rows, 3 * span), BF16),
-            jax.ShapeDtypeStruct((rows, width), BF16),
-            jax.ShapeDtypeStruct((rows, 2), F32),
-        ],
-        compiler_params=params(56),
-        cost_estimate=cost(6 * rows * width * span, 6 * width * span + 6 * rows * width),
+        compiler_params=params(56, collective_id=4, has_side_effects=True),
+        cost_estimate=cost(1e6, 1e6),
         name="unproject",
-    )(dq, dk, dv, cosine, sine, tok_full, stat, weight)
+    )(dproj, tok_full, stat, weight, branch)
 
 
 def per_device(tokens, segment_ids, in_weight, out_weight, gate_up_weight, down_weight, cotangent):
-    rows, shard = tokens.shape
+    rows = tokens.shape[0]
     width = in_weight.shape[0]
     span = in_weight.shape[2]
     heads = span // HD
     hidden_local = down_weight.shape[0]
     me = lax.axis_index("ctx")
-    tp_at = lax.axis_index("tp")
-
-    def own(whole):
-        return lax.dynamic_slice_in_dim(whole, tp_at * shard, shard, axis=1)
+    tp_size = lax.axis_size("tp")
+    cube = lax.axis_size("ctx") == CUBE
 
     def gather(local, axis=1):
         return lax.all_gather(local, "tp", axis=axis, tiled=True)
@@ -725,7 +1198,7 @@
     gu_w = jnp.transpose(
         gate_up_weight.reshape(width, 2, hidden_local // BLOCK, BLOCK), (0, 2, 1, 3)
     )
-    gu_w = lax.optimization_barrier(gu_w.reshape(width, 2 * hidden_local))
+    gu_w = gu_w.reshape(width, 2 * hidden_local)
 
     all_seg = lax.all_gather(segment_ids, "ctx", axis=0, tiled=True)
     count = all_seg.shape[0]
@@ -746,39 +1219,45 @@
     ).astype(jnp.int32)
     begin, all_begin = begin[None, :], all_begin[None, :]
 
-    tok_full = gather(tokens)
+    tok_full, gu_w = lax.optimization_barrier((gather(tokens), gu_w))
     inner1, stat1, query, pairs = project(tok_full, in_w, cosine, sine, heads)
-    all_pairs = lax.all_gather(pairs, "ctx", axis=0, tiled=True)
-    share = width // lax.axis_size("ctx")
-    out_full = gather(lax.dynamic_slice_in_dim(out_weight, me * share, share, axis=1), 0)
-    out_full = lax.all_gather(out_full, "ctx", axis=1, tiled=True)
+    if cube:
+        raw, mixed, lse, all_pairs, cot_full = attend_far(
+            query, pairs, begin, cotangent, heads, tp_size
+        )
+    else:
+        all_pairs = lax.all_gather(pairs, "ctx", axis=0, tiled=True)
+        cot_full = gather(cotangent)
+        raw, mixed, lse = attend(key_info, query, all_pairs, begin, heads)
+    out_part = jnp.dot(mixed, out_weight, preferred_element_type=F32).astype(BF16)
+    inner2, resid1, stat2 = merge(out_part, tok_full, tp_size)
     all_query = lax.all_gather(query, "ctx", axis=0, tiled=True)
-    cot_full = gather(cotangent)
-    raw, mixed, lse = attend(key_info, query, all_pairs, begin, heads)
-    resid1, stat2, inner2 = merge(gather(mixed), out_full, tok_full)
 
     hidden, grad_gu = feed(inner2, cot_full, gu_w, down_weight, BLOCK)
-    grad_part = lax.dot_general(grad_gu, gu_w, NT, preferred_element_type=F32).astype(BF16)
-    down_grad = lax.dot_general(hidden, cot_full, TN, preferred_element_type=F32)
-    gu_grad = lax.dot_general(inner2, grad_gu, TN, preferred_element_type=F32)
-    grad_part, down_grad, gu_grad = lax.optimization_barrier(
-        (grad_part, down_grad.astype(BF16), gu_grad.astype(BF16))
+    down_grad = lax.dot_general(hidden, cot_full, TN, preferred_element_type=F32).astype(BF16)
+    gu_grad = lax.dot_general(inner2, grad_gu, TN, preferred_element_type=F32).astype(BF16)
+    down_grad, gu_grad, all_query, grad_gu, hidden = lax.optimization_barrier(
+        (down_grad, gu_grad, all_query, grad_gu, hidden)
     )
     down_grad, gu_grad = lax.optimization_barrier(lax.psum((down_grad, gu_grad), "ctx"))
-    branch_grad = norm_back(grad_part, cot_full, resid1, stat2, lax.axis_size("tp"))
-
-    branch = jnp.dot(hidden, down_weight, preferred_element_type=F32).astype(BF16)
-    branch = lax.psum_scatter(branch, "tp", scatter_dimension=1, tiled=True)
-    layer_out = (own(resid1) + branch.astype(F32)).astype(BF16)
-
+
+    grad_part = lax.dot_general(grad_gu, gu_w, NT, preferred_element_type=F32).astype(BF16)
+    branch_grad = norm_back(grad_part, cot_full, resid1, stat2, tp_size)
     out_grad = lax.dot_general(mixed, branch_grad, TN, preferred_element_type=F32).astype(BF16)
     grad_mixed, delta = mixed_grad(branch_grad, out_weight, raw, lse, heads)
-    all_grad = lax.all_gather(grad_mixed, "ctx", axis=0, tiled=True)
-    dq = query_grad(key_info, query, grad_mixed, lse, delta, all_pairs, begin, heads)
-    dk, dv = key_grad(query_info, pairs, all_query, all_grad, all_begin, heads)
-    dproj, part, sums = unproject(dq, dk, dv, cosine, sine, tok_full, stat1, in_w, heads)
-    grad_normed1 = lax.psum_scatter(part, "tp", scatter_dimension=1, tiled=True).astype(F32)
-    sums = lax.psum(sums, "tp") / width
+    branch = (resid1 + jnp.dot(hidden, down_weight, preferred_element_type=F32)).astype(BF16)
+    if cube:
+        dq, dk, dv, layer_out = attend_back_far(
+            grad_mixed, all_query, all_pairs, blocks, branch, heads, tp_size
+        )
+    else:
+        branch = lax.psum_scatter(branch, "tp", scatter_dimension=1, tiled=True)
+        layer_out = branch
+        all_grad = lax.all_gather(grad_mixed, "ctx", axis=0, tiled=True)
+        dq = query_grad(key_info, query, grad_mixed, lse, delta, all_pairs, begin, heads)
+        dk, dv = key_grad(query_info, pairs, all_query, all_grad, all_begin, heads)
+
+    dproj = unrotate(dq, dk, dv, cosine, sine, heads)
     in_grad = jnp.stack(
         [
             lax.dot_general(
@@ -787,15 +1266,11 @@
             for i in range(3)
         ]
     )
-    in_grad, out_grad, down_grad, gu_grad = lax.optimization_barrier(
-        (in_grad, out_grad, down_grad, gu_grad)
+    in_grad, out_grad, dproj, down_grad, gu_grad = lax.optimization_barrier(
+        (in_grad, out_grad, dproj, down_grad, gu_grad)
     )
     in_grad, out_grad = lax.psum((in_grad, out_grad), "ctx")
-
-    normed1 = (tokens.astype(F32) - stat1[:, 0:1]) * stat1[:, 1:2]
-    tokens_grad = own(branch_grad).astype(F32) + stat1[:, 1:2] * (
-        grad_normed1 - sums[:, 0:1] - normed1 * sums[:, 1:2]
-    )
+    tokens_grad = unproject(dproj, tok_full, stat1, in_w, branch_grad, heads, tp_size)
     return (
         layer_out,
         tokens_grad,

time: 1120 us -> 874 us (0.78)
  waiting for transfers between devices: 653 us -> 125 us
  Pallas kernels: 268 us -> 581 us
  blocking collectives: 36.5 us -> 9.13 us
    pallas_call x5, Pallas kernels: 91.5 us -> 405 us  [the longest x1 111 us: merge(): pl.pallas_call(functools.partial(merge_kernel, n, sub), in_specs=[vmem] *...]
    all_gather x4 -> x1, waiting for transfers between devices: 196 us -> 37.4 us  [gather(): return lax.all_gather(local, 'tp', axis=axis, tiled=True)]
    all_gather x3 -> x0, waiting for transfers between devices: 134 us -> none  [the longest x1 58.9 us: per_device(): all_pairs = lax.all_gather(pairs, 'ctx', axis=0, tiled=True)]
    psum x1, waiting for transfers between devices: 160 us -> 71.7 us  [per_device(): lax.psum((down_grad, gu_grad), 'ctx')]
    reduce_scatter x2 -> x0, waiting for transfers between devices: 50.6 us -> none  [the longest x1 50.6 us: per_device(): lax.psum_scatter(part, 'tp', scatter_dimension=1, tiled=True).astype(F32)]
    all_gather x1, waiting for transfers between devices: 48.3 us -> 0.01 us  [per_device(): all_query = lax.all_gather(query, 'ctx', axis=0, tiled=True)]
    psum x1, waiting for transfers between devices: 61.8 us -> 15.5 us  [per_device(): in_grad, out_grad = lax.psum((in_grad, out_grad), 'ctx')]
    psum x1 -> x0, blocking collectives: 26.9 us -> none  [per_device(): sums = lax.psum(sums, 'tp') / width]
  transfers between devices with their start and end apart: 12 -> 4, of which waited for: 11 -> 3; matrix products, arithmetic and copies ran while one was open for 8% -> 14% of each run, Pallas kernels for 22% -> 66%
where the time goes in v3:
time: 874 us; the launch traced here: 869 us
  Pallas kernels  581 us (66%)
  waiting for transfers between devices  125 us (14%)
  matrix products  76.7 us (9%)
  local copies, waits for them, and re-layouts  31.9 us (4%)
  other arithmetic  30.1 us (3%)
  between operations  14.2 us (2%)
  blocking collectives  9.13 us (1%)
    pallas_call x1, Pallas kernels, merge(): pl.pallas_call(functools.partial(merge_kernel, n, sub), in_specs=[vmem] *...  111 us
    pallas_call x1, Pallas kernels, norm_back(): pl.pallas_call(functools.partial(norm_back_kernel, n, sub), in_specs=[vme...  111 us
    pallas_call x1, Pallas kernels, attend_back_far(): pl.pallas_call(functools.partial(attend_back_far_kernel, heads, n), in_sp...  102 us
    pallas_call x1, Pallas kernels, attend_far(): pl.pallas_call(functools.partial(attend_far_kernel, heads, n), in_specs=[...  102 us
    pallas_call x1, Pallas kernels, unproject(): pl.pallas_call(functools.partial(unproject_kernel, heads, n), in_specs=[v...  83.6 us
    psum x1, waiting for transfers between devices, per_device(): lax.psum((down_grad, gu_grad), 'ctx')  71.7 us
    all_gather x1, waiting for transfers between devices, gather(): return lax.all_gather(local, 'tp', axis=axis, tiled=True)  37.4 us
    reshape x1, local copies, waits for them, and re-layouts, per_device(): gu_w = gu_w.reshape(width, 2 * hidden_local)  27.8 us
  transfers between devices with their start and end apart: 4, of which 3 were waited for; matrix products, arithmetic and copies ran while one was open for 14% of the time, Pallas kernels for 66%

profile of v3, /device:TPU:0, one launch (start us, length us, event | category | flops | bytes accessed | tf_op | source)
XLA Modules:
  0.0 869.0 jit_solution(15897997236474642402)
XLA Ops:
  8.0 27.8 %reshape.57.w_ref = bf16[2048,4096]{1,0:T(8,128)(2,1)} reshape(bf16[2048,4,2,512]{3,2,1,0:T(2,128)(2,1)} %bitcast.36) | data formatting | bytes 33554432 | tf_op jit(solution)/shard_map/reshape | solution.py:1201
  35.8 1.4 fusion.6
  37.2 1.2 pad_maximum_fusion.1
  38.4 37.4 %all-gather.4.cloned.1.call-done.tok_ref = bf16[768,2048]{1,0:T(8,128)(2,1)} async-done(((bf16[768,512]{1,0:T(8,128)(2,1)}), bf16[768,2048]{1,0:T(8,128)(2,1)}) %all-gather.4.cloned.1.call-update) | async-done | bytes 3145744 | tf_op jit(solution)/shard_map/all_gather | solution.py:1193
  75.8 11.2 %project.1 = (bf16[768,2048]{1,0:T(8,128)(2,1)}, f32[768,2]{1,0:T(8,128)}, bf16[768,512]{1,0:T(8,128)(2,1)}, bf16[768,1024]{1,0:T(8,128)(2,1)}) custom-call(bf16[768,2048]{1,0:T(8,128)(2,1)} %all-gather.4.cloned.1.call-done.tok_ref, bf16[3,2048,512]{2,1,0:T(8,128)(2,1)} %bitcast.37, f32[768,128]{1,0:T(8,128)} %get-tuple-element.79.cos_ref, ...), custom_call_target="tpu_custom_call" | custom-call | flops 4831838208 | bytes 15728640 | tf_op jit(solution)/shard_map/project/pallas_call | solution.py:70
  87.1 9.1 %all-gather = s32[8,1,768]{2,1,0:T(1,128)S(1)} all-gather(s32[1,1,768]{2,1,0:T(1,128)S(1)} %reshape.62), channel_id=1, replica_groups=mesh['ctx'=8,'tp'=4] {'ctx'}, dimensions={0}, use_global_device_ids=true | all-gather | bytes 27648 | tf_op jit(solution)/shard_map/all_gather | solution.py:1203
  97.7 102.1 %attend_far.1 = (f32[768,512]{1,0:T(8,128)}, bf16[768,512]{1,0:T(8,128)(2,1)}, f32[4,768]{1,0:T(4,128)}, bf16[6144,1024]{1,0:T(8,128)(2,1)}, bf16[768,2048]{1,0:T(8,128)(2,1)}) custom-call(bf16[768,512]{1,0:T(8,128)(2,1)} %get-tuple-element.40.q_ref, bf16[768,1024]{1,0:T(8,128)(2,1)} %get-tuple-element.41.own_ref, s32[1,768]{1,0:T(1,128)} %broadcast_in_dim.10.begin_ref, ...), custom_call_target="tpu_custom_call" | custom-call | flops 1000000 | bytes 1000000 | tf_op jit(solution)/shard_map/attend_far/pallas_call | solution.py:411
  199.8 4.6 convolution_convert_fusion.3.part_ref
  204.4 111.1 %merge.1 = (bf16[768,2048]{1,0:T(8,128)(2,1)}, f32[768,2048]{1,0:T(8,128)}, f32[768,2]{1,0:T(8,128)}) custom-call(bf16[768,2048]{1,0:T(8,128)(2,1)} %convolution_convert_fusion.3.part_ref, bf16[768,2048]{1,0:T(8,128)(2,1)} %all-gather.4.cloned.1.call-done.tok_ref), custom_call_target="tpu_custom_call" | custom-call | flops 1000000 | bytes 1000000 | tf_op jit(solution)/shard_map/merge/pallas_call | solution.py:996
  315.6 27.1 %feed.1 = (bf16[768,2048]{1,0:T(8,128)(2,1)}, bf16[768,4096]{1,0:T(8,128)(2,1)}) custom-call(bf16[768,2048]{1,0:T(8,128)(2,1)} %get-tuple-element.43.inner_ref, bf16[768,2048]{1,0:T(8,128)(2,1)} %get-tuple-element.44.cot_ref, bf16[2048,4096]{1,0:T(8,128)(2,1)} %reshape.57.w_ref, bf16[2048,2048]{1,0:T(8,128)(2,1)} %down_ref.1), custom_call_target="tpu_custom_call" | custom-call | flops 19327352832 | bytes 31457280 | tf_op jit(solution)/shard_map/feed/pallas_call | solution.py:809
  342.7 11.0 %convolution_convert_fusion.1 = bf16[2048,2048]{1,0:T(8,128)(2,1)} fusion(bf16[768,2048]{1,0:T(8,128)(2,1)} %get-tuple-element.56, bf16[768,2048]{1,0:T(8,128)(2,1)S(1)} %copy-done.4), kind=kOutput, calls=%fused_computation.1 | convolution fusion | flops 6446645248 | bytes 14680064 | tf_op jit(solution)/shard_map/dot_general | solution.py:1237
  353.8 18.8 %convolution_convert_fusion = bf16[2048,4096]{1,0:T(8,128)(2,1)} fusion(bf16[768,2048]{1,0:T(8,128)(2,1)S(1)} %copy-done.9, bf16[768,4096]{1,0:T(8,128)(2,1)} %get-tuple-element.48), kind=kOutput, calls=%fused_computation | convolution fusion | flops 12893290496 | bytes 26214400 | tf_op jit(solution)/shard_map/dot_general | solution.py:1238
  373.7 19.9 %convolution_convert_fusion.2.part_ref = bf16[768,2048]{1,0:T(8,128)(2,1)} fusion(bf16[768,4096]{1,0:T(8,128)(2,1)} %get-tuple-element.48, bf16[2048,4096]{1,0:T(8,128)(2,1)} %reshape.57.w_ref), kind=kOutput, calls=%fused_computation.4 | convolution fusion | flops 12886474752 | bytes 26214400 | tf_op jit(solution)/shard_map/dot_general | solution.py:1244
  393.6 110.8 %norm_back.1.branch_ref = bf16[768,2048]{1,0:T(8,128)(2,1)} custom-call(bf16[768,2048]{1,0:T(8,128)(2,1)} %convolution_convert_fusion.2.part_ref, bf16[768,2048]{1,0:T(8,128)(2,1)} %get-tuple-element.44.cot_ref, f32[768,2048]{1,0:T(8,128)} %get-tuple-element.49.resid_ref, f32[768,2]{1,0:T(8,128)} %get-tuple-element.50.stat_ref), custom_call_target="tpu_custom_call" | custom-call | flops 1000000 | bytes 1000000 | tf_op jit(solution)/shard_map/norm_back/pallas_call | solution.py:1033
  504.4 6.7 mixed_grad.1
  511.1 12.3 %add_convert_fusion.part_ref = bf16[768,2048]{1,0:T(8,128)(2,1)} fusion(f32[768,2048]{1,0:T(8,128)S(1)} %bitcast.40, bf16[768,2048]{1,0:T(8,128)(2,1)} %get-tuple-element.56, bf16[2048,2048]{1,0:T(8,128)(2,1)} %down_ref.1), kind=kOutput, calls=%fused_computation.3 | convolution fusion | flops 6445596672 | bytes 20971520 | tf_op jit(solution)/shard_map/dot_general | solution.py:1248
  523.5 102.4 %attend_back_far.1 = (f32[768,512]{1,0:T(8,128)}, f32[768,512]{1,0:T(8,128)}, f32[768,512]{1,0:T(8,128)}, bf16[768,512]{1,0:T(8,128)(2,1)}) custom-call(bf16[768,640]{1,0:T(8,128)(2,1)} %get-tuple-element.53.g_ref, bf16[6144,512]{1,0:T(8,128)(2,1)} %all-gather.6.cloned.1.call-done.q_ref, bf16[6144,1024]{1,0:T(8,128)(2,1)} %get-tuple-element.55.pair_ref, ...), custom_call_target="tpu_custom_call" | custom-call | flops 1000000 | bytes 1000000 | tf_op jit(solution)/shard_map/attend_back_far/pallas_call | solution.py:555
  625.8 5.6 unrotate.1.dproj_ref
  631.5 3.1 fusion.2
  634.7 1.8 fusion.1
  636.5 1.8 fusion
  638.4 3.5 pad_maximum_fusion
  642.9 3.2 convolution_convert_fusion.4
  646.0 71.7 %all-reduce.7.cloned.1.call-done = (bf16[2048,2048]{1,0:T(8,128)(2,1)}, bf16[2048,4096]{1,0:T(8,128)(2,1)}) async-done(((bf16[2048,2048]{1,0:T(8,128)(2,1)}, bf16[2048,4096]{1,0:T(8,128)(2,1)}), (bf16[2048,2048]{1,0:T(8,128)(2,1)}, bf16[2048,4096]{1,0:T(8,128)(2,1)})) %all-reduce.7.cloned.1.call-update) | async-done | bytes 25165840 | tf_op jit(solution)/shard_map/psum | solution.py:1242
  717.7 83.6 %unproject.1 = f32[768,512]{1,0:T(8,128)} custom-call(bf16[768,1536]{1,0:T(8,128)(2,1)} %unrotate.1.dproj_ref, bf16[768,2048]{1,0:T(8,128)(2,1)} %all-gather.4.cloned.1.call-done.tok_ref, f32[768,2]{1,0:T(8,128)} %get-tuple-element.67.stat_ref, bf16[3,2048,512]{2,1,0:T(8,128)(2,1)} %bitcast.38, bf16[768,2048]{1,0:T(8,128)(2,1)} %norm_back.1.branch_ref), custom_call_target="tpu_custom_call" | custom-call | flops 1000000 | bytes 1000000 | tf_op jit(solution)/shard_map/unproject/pallas_call | solution.py:1160
  801.4 11.7 %convert_element_type.59 = f32[2048,2048]{1,0:T(8,128)} convert(bf16[2048,2048]{1,0:T(8,128)(2,1)} %get-tuple-element.71) | non-fusion elementwise | flops 4194304 | bytes 25165824 | tf_op jit(solution)/shard_map/convert_element_type | solution.py:1280
  813.1 20.8 %weave.1 = f32[2048,2,2048]{2,1,0:T(2,128)} custom-call(bf16[2048,4096]{1,0:T(8,128)(2,1)} %get-tuple-element.70.sum_ref), custom_call_target="tpu_custom_call" | custom-call | flops 8388608 | bytes 50331648 | tf_op jit(solution)/shard_map/weave/pallas_call | solution.py:843
  833.9 15.5 %all-reduce.5.cloned.1.call-done = (bf16[2048,3,512]{2,0,1:T(8,128)(2,1)}, bf16[512,2048]{1,0:T(8,128)(2,1)}) async-done(((bf16[2048,3,512]{2,0,1:T(8,128)(2,1)}, bf16[512,2048]{1,0:T(8,128)(2,1)}), (bf16[2048,3,512]{2,0,1:T(8,128)(2,1)}, bf16[512,2048]{1,0:T(8,128)(2,1)})) %all-reduce.5.cloned.1.call-update) | async-done | bytes 8388624 | tf_op jit(solution)/shard_map/psum | solution.py:1272
  849.4 4.3 convert_element_type.58
  853.7 6.6 convert_element_type.57
  860.3 0.9 copy.25
  861.2 1.1 copy.26
  (52 shorter events, 4.4 us)
Async XLA Ops:
  7.2 68.6 %all-gather.4.cloned.1.call-start = ((), (), s32[]{:S(2)}) async-start(), calls=%async_computation | async-start | bytes 3932160 | tf_op jit(solution)/shard_map/all_gather | solution.py:1193
  7.9 364.7 %all-gather.6.cloned.1.call-start = ((), (), s32[]{:S(2)}) async-start(), calls=%async_computation.1 | async-start | bytes 7077888 | tf_op jit(solution)/shard_map/all_gather | solution.py:1234
  75.8 11.3 %copy-start.8 = (s32[768]{0:T(1024)S(1)}, s32[768]{0:T(1024)}, u32[]{:S(2)}) copy-start(s32[768]{0:T(1024)} %param.8) | copy-start | bytes 9220
  87.0 112.8 %copy-start.5 = (bf16[512,2048]{1,0:T(8,128)(2,1)S(1)}, bf16[512,2048]{1,0:T(8,128)(2,1)}, u32[]{:S(2)}) copy-start(bf16[512,2048]{1,0:T(8,128)(2,1)} %w_ref.1) | copy-start | bytes 6291460
  87.0 630.7 %all-reduce.7.cloned.1.call-start = ((), (), s32[]{:S(2)}) async-start(), calls=%async_computation.3 | async-start | bytes 50331648 | tf_op jit(solution)/shard_map/psum | solution.py:1242
  315.6 27.2 %copy-start.4 = (bf16[768,2048]{1,0:T(8,128)(2,1)S(1)}, bf16[768,2048]{1,0:T(8,128)(2,1)}, u32[]{:S(2)}) copy-start(bf16[768,2048]{1,0:T(8,128)(2,1)} %get-tuple-element.44.cot_ref) | copy-start | bytes 9437188
  342.7 11.0 %copy-start.9 = (bf16[768,2048]{1,0:T(8,128)(2,1)S(1)}, bf16[768,2048]{1,0:T(8,128)(2,1)}, u32[]{:S(2)}) copy-start(bf16[768,2048]{1,0:T(8,128)(2,1)} %get-tuple-element.43.inner_ref) | copy-start | bytes 9437188
  372.6 138.5 %slice-start = ((s8[6291456]{0:T(1024)(128)(4,1)}), s8[2097152]{0:T(1024)(128)(4,1)S(1)}, s32[]{:S(2)}) async-start(s8[6291456]{0:T(1024)(128)(4,1)} %bitcast.39), calls=%async_computation.4 | async-start | bytes 4194304
  372.6 476.8 %all-reduce.5.cloned.1.call-start = ((), (), s32[]{:S(2)}) async-start(), calls=%async_computation.2 | async-start | bytes 16777216 | tf_op jit(solution)/shard_map/psum | solution.py:1272
  373.7 137.4 %slice-start.1 = ((s8[6291456]{0:T(1024)(128)(4,1)}), s8[4194304]{0:T(1024)(128)(4,1)S(1)}, s32[]{:S(2)}) async-start(s8[6291456]{0:T(1024)(128)(4,1)} %bitcast.39), calls=%async_computation.5 | async-start | bytes 8388608
  625.8 5.7 copy-start.10
  631.5 3.1 copy-start.1
  638.3 3.9 copy-start
  638.4 4.5 copy-start.7
  849.4 4.3 copy-start.3
  853.7 6.6 copy-start.6
  853.7 7.5 copy-start.2
Sparse Core Ops, SparseCore 0:
  9.6 66.1 all-gather.3
  87.2 65.9 all-gather.5
  372.8 344.9 all-reduce.6
  722.3 127.0 all-reduce.4

commit v4 on v3

--- a/solution.py
+++ b/solution.py
@@ -282,6 +282,121 @@
             self.copy(n).wait_send()
 
 
+SUM_SENDS = 11
+
+
+class CubeSum:
+    def __init__(self, own, out, land, send, recv):
+        me = lax.axis_index("ctx")
+        core, x, y = me % 2, (me // 2) % 2, me // 4
+        self.me, self.own, self.out, self.land = me, own, out, land
+        self.send, self.recv = send, recv
+        rows = own.shape[0]
+        self.half, self.quarter = rows // 2, rows // 4
+        self.eighth, self.last = rows // 8, rows // 16
+        mine = core * self.half
+        first, second = mine, mine + self.quarter
+        self.to = (1 - 2 * core, 2 - 4 * x, 4 - 8 * y)
+        self.mine, self.other = mine, (1 - core) * self.half
+        self.keep1 = (first + x * self.eighth, second + y * self.eighth)
+        self.give1 = (first + (1 - x) * self.eighth, second + (1 - y) * self.eighth)
+        self.keep2 = (self.keep1[0] + y * self.last, self.keep1[1] + x * self.last)
+        self.give2 = (self.keep1[0] + (1 - y) * self.last, self.keep1[1] + (1 - x) * self.last)
+
+    def place(self, ref, start, size):
+        return ref.at[pl.ds(pl.multiple_of(start, 16), size)]
+
+    def copy(self, n):
+        core, x, y = self.to
+        half, eighth, last, out, land = self.half, self.eighth, self.last, self.out, self.land
+        landing = (0, half, half + eighth, half + 2 * eighth, half + 2 * eighth + last)
+        mine = self.mine
+        source, start, size, target = (
+            (self.own, self.other, half, core),
+            (land, self.give1[0] - mine, eighth, x), (land, self.give1[1] - mine, eighth, y),
+            (land, self.give2[0] - mine, last, y), (land, self.give2[1] - mine, last, x),
+            (out, self.keep2[0], last, y), (out, self.keep2[1], last, x),
+            (out, self.keep1[0], eighth, x), (out, self.keep1[1], eighth, y),
+            (out, mine, self.quarter, core),
+            (out, mine + self.quarter, self.quarter, core),
+        )[n]
+        src = self.place(source, start, size)
+        dst = land.at[pl.ds(landing[n], size)] if n < 5 else src
+        return pltpu.make_async_remote_copy(
+            src_ref=src, dst_ref=dst, send_sem=self.send.at[n], recv_sem=self.recv.at[n],
+            device_id={"ctx": self.me + target}, device_id_type=MESH,
+        )
+
+    def add(self, target, to, source, at, landed, size):
+        step = size
+        while step * self.own.shape[1] > 256 * 1024 and step % 32 == 0:
+            step = step // 2
+
+        def part(i, carry):
+            rows = lambda begin: pl.ds(pl.multiple_of(begin + i * step, 16), step)
+            total = source[rows(at), :].astype(F32) + self.land[rows(landed), :].astype(F32)
+            target[rows(to), :] = total.astype(BF16)
+            return carry
+
+        lax.fori_loop(0, size // step, part, 0)
+
+    def step(self, k):
+        half, eighth, last, land, mine = self.half, self.eighth, self.last, self.land, self.mine
+        if k == 0:
+            self.copy(0).start()
+        if k == 1:
+            self.copy(0).wait_recv()
+            for i in range(2):
+                at = self.give1[i]
+                self.add(land, at - mine, self.own, at, at - mine, eighth)
+                self.copy(1 + i).start()
+            for i in range(2):
+                at = self.keep1[i]
+                self.add(land, at - mine, self.own, at, at - mine, eighth)
+        if k == 2:
+            for i in range(2):
+                self.copy(1 + i).wait_recv()
+                landed = half + i * eighth - self.keep1[i]
+                at = self.give2[i]
+                self.add(land, at - mine, land, at - mine, landed + at, last)
+                self.copy(3 + i).start()
+                at = self.keep2[i]
+                self.add(land, at - mine, land, at - mine, landed + at, last)
+        if k == 3:
+            for i in range(2):
+                self.copy(3 + i).wait_recv()
+                at = self.keep2[i]
+                self.add(self.out, at, land, at - mine, half + 2 * eighth + i * last, last)
+                self.copy(5 + i).start()
+        if k == 4:
+            for i in range(2):
+                self.copy(5 + i).wait_recv()
+                self.copy(7 + i).start()
+        if k == 5:
+            for i in range(2):
+                self.copy(7 + i).wait_recv()
+                self.copy(9 + i).start()
+        if k == 6:
+            for i in range(2):
+                self.copy(9 + i).wait_recv()
+            for n in range(SUM_SENDS):
+                self.copy(n).wait_send()
+
+    def signal(self, barrier):
+        for target in self.to:
+            pl.semaphore_signal(
+                barrier, inc=1, device_id={"ctx": self.me + target}, device_id_type=MESH
+            )
+
+
+def sum_scratch(shape):
+    return [
+        pltpu.VMEM((shape[0] // 2 + 3 * (shape[0] // 8), shape[1]), BF16),
+        pltpu.SemaphoreType.DMA((SUM_SENDS,)),
+        pltpu.SemaphoreType.DMA((SUM_SENDS,)),
+    ]
+
+
 def hidden_scores(scores, key_block, query_block, rows, begin):
     key_place = lax.broadcasted_iota(jnp.int32, scores.shape, 0) + key_block * rows
     query_place = lax.broadcasted_iota(jnp.int32, scores.shape, 1) + query_block * rows
@@ -901,10 +1016,6 @@
             edge = 0 if right else n - 1
             held = came(right)
 
-            @pl.when(at == edge)
-            def _():
-                first(right, c).start()
-
             @pl.when(((at < owner) if right else (at > owner)) & (at != edge))
             def _():
                 copy = onward(right, c)
@@ -942,6 +1053,15 @@
                 @pl.when(at != edge)
                 def _():
                     copy.start()
+
+    for c in range(chunks):
+        @pl.when(at == 0)
+        def _():
+            first(True, c).start()
+
+        @pl.when(at == n - 1)
+        def _():
+            first(False, c).start()
 
     for c in range(chunks + 4):
         if c < chunks:
@@ -991,7 +1111,7 @@
 
 def merge(part, tok_full, n):
     rows, width = part.shape
-    sub = 48
+    sub = 32
     vmem = pl.BlockSpec(memory_space=pltpu.VMEM)
     return pl.pallas_call(
         functools.partial(merge_kernel, n, sub),
@@ -1028,7 +1148,7 @@
 
 def norm_back(part, cot, resid, stat, n):
     rows, width = part.shape
-    sub = 48
+    sub = 32
     vmem = pl.BlockSpec(memory_space=pltpu.VMEM)
     return pl.pallas_call(
         functools.partial(norm_back_kernel, n, sub),
@@ -1073,10 +1193,19 @@
     )(dq, dk, dv, cosine, sine)
 
 
-def unproject_kernel(
-    heads, n, dproj_ref, tok_ref, stat_ref, w_ref, branch_ref, out_ref,
-    part_ref, mine_ref, land_ref, sums_ref, far_ref, send, recv, ssend, srecv,
-):
+def unproject_kernel(heads, n, cube, dproj_ref, tok_ref, stat_ref, w_ref, branch_ref, *refs):
+    sums = []
+    if cube:
+        in_ref, og_ref, out_ref, in_out, og_out = refs[:5]
+        part_ref, mine_ref, land_ref, sums_ref, far_ref, send, recv, ssend, srecv = refs[5:14]
+        sums = [CubeSum(in_ref, in_out, *refs[14:17]), CubeSum(og_ref, og_out, *refs[17:20])]
+    else:
+        out_ref, part_ref, mine_ref, land_ref, sums_ref, far_ref, send, recv, ssend, srecv = refs
+
+    def advance(k):
+        for item in sums:
+            item.step(k)
+
     rows, width = tok_ref.shape
     shard = width // n
     span = heads * HD
@@ -1086,7 +1215,10 @@
         pl.semaphore_signal(
             barrier, inc=1, device_id={"tp": lax.rem(at + o, n)}, device_id_type=MESH
         )
-    pl.semaphore_wait(barrier, n - 1)
+    if cube:
+        sums[0].signal(barrier)
+    pl.semaphore_wait(barrier, n - 1 + (3 if cube else 0))
+    advance(0)
     block = 256
     count = rows // block
 
@@ -1100,7 +1232,7 @@
             device_id={"tp": target}, device_id_type=MESH,
         )
 
-    def sums(o):
+    def totals(o):
         return pltpu.make_async_remote_copy(
             src_ref=sums_ref, dst_ref=far_ref.at[o - 1],
             send_sem=ssend.at[o - 1], recv_sem=srecv.at[o - 1],
@@ -1127,12 +1259,15 @@
         both = jnp.where(lane == 0, first, jnp.where(lane == 1, second, 0.0))
         sums_ref[:, i * block : (i + 1) * block] = both.T[:8]
     for o in range(1, n):
-        sums(o).start()
+        totals(o).start()
+    for k in range(1, 5):
+        advance(k)
     total = sums_ref[...]
     for o in range(1, n):
-        sums(o).wait_recv()
+        totals(o).wait_recv()
         total = total + far_ref[o - 1]
     mine_ref[...] = total
+    advance(5)
     for i in range(count):
         place = pl.ds(i * block, block)
         spread = jnp.concatenate(
@@ -1147,21 +1282,26 @@
         out_ref[place, :] = branch_ref[place, own].astype(F32) + inverse * (
             total - spread[:, 0:1] - normed * spread[:, 1:2]
         )
+    advance(6)
     for o in range(1, n):
-        sums(o).wait_send()
+        totals(o).wait_send()
         for i in range(count):
             term(o, i).wait_send()
 
 
-def unproject(dproj, tok_full, stat, weight, branch, heads, n):
+def unproject(dproj, tok_full, stat, weight, branch, heads, n, grads):
     rows, width = tok_full.shape
     shard = width // n
     vmem = pl.BlockSpec(memory_space=pltpu.VMEM)
-    return pl.pallas_call(
-        functools.partial(unproject_kernel, heads, n),
-        in_specs=[vmem] * 5,
-        out_specs=vmem,
-        out_shape=jax.ShapeDtypeStruct((rows, shard), F32),
+    extra = []
+    for grad in grads:
+        extra += sum_scratch(grad.shape)
+    result = pl.pallas_call(
+        functools.partial(unproject_kernel, heads, n, len(grads) > 0),
+        in_specs=[vmem] * (5 + len(grads)),
+        out_specs=[vmem] * (1 + len(grads)),
+        out_shape=[jax.ShapeDtypeStruct((rows, shard), F32)]
+        + [jax.ShapeDtypeStruct(grad.shape, BF16) for grad in grads],
         scratch_shapes=[
             pltpu.VMEM((rows, width), BF16),
             pltpu.VMEM((8, rows), F32),
@@ -1172,11 +1312,13 @@
             pltpu.SemaphoreType.DMA((n - 1, rows // 256)),
             pltpu.SemaphoreType.DMA((n - 1,)),
             pltpu.SemaphoreType.DMA((n - 1,)),
-        ],
-        compiler_params=params(56, collective_id=4, has_side_effects=True),
+        ]
+        + extra,
+        compiler_params=params(60, collective_id=4, has_side_effects=True),
         cost_estimate=cost(1e6, 1e6),
         name="unproject",
-    )(dproj, tok_full, stat, weight, branch)
+    )(dproj, tok_full, stat, weight, branch, *grads)
+    return result
 
 
 def per_device(tokens, segment_ids, in_weight, out_weight, gate_up_weight, down_weight, cotangent):
@@ -1205,8 +1347,11 @@
     every = jnp.arange(count, dtype=jnp.int32)
     opens = jnp.concatenate([jnp.ones((1,), jnp.bool_), all_seg[1:] != all_seg[:-1]])
     all_begin = lax.cummax(jnp.where(opens, every, 0))
-    begin = lax.dynamic_slice_in_dim(all_begin, me * rows, rows, 0)
     blocks = all_begin.reshape(count // rows, rows)
+
+    tok_full, gu_w, blocks, all_begin = lax.optimization_barrier(
+        (gather(tokens), gu_w, blocks, all_begin)
+    )
     key_info = jnp.stack(
         [me, blocks[me, 0] // rows, (blocks[me, rows - 1] + rows - 1) // rows]
     ).astype(jnp.int32)
@@ -1217,9 +1362,8 @@
             jnp.sum((blocks[:, rows - 1] <= me * rows).astype(jnp.int32)) - 1,
         ]
     ).astype(jnp.int32)
-    begin, all_begin = begin[None, :], all_begin[None, :]
-
-    tok_full, gu_w = lax.optimization_barrier((gather(tokens), gu_w))
+    begin = lax.dynamic_slice_in_dim(blocks, me, 1, 0)
+    all_begin = all_begin[None, :]
     inner1, stat1, query, pairs = project(tok_full, in_w, cosine, sine, heads)
     if cube:
         raw, mixed, lse, all_pairs, cot_full = attend_far(
@@ -1229,9 +1373,10 @@
         all_pairs = lax.all_gather(pairs, "ctx", axis=0, tiled=True)
         cot_full = gather(cotangent)
         raw, mixed, lse = attend(key_info, query, all_pairs, begin, heads)
+    late_query, mixed = lax.optimization_barrier((query, mixed))
+    all_query = lax.all_gather(late_query, "ctx", axis=0, tiled=True)
     out_part = jnp.dot(mixed, out_weight, preferred_element_type=F32).astype(BF16)
     inner2, resid1, stat2 = merge(out_part, tok_full, tp_size)
-    all_query = lax.all_gather(query, "ctx", axis=0, tiled=True)
 
     hidden, grad_gu = feed(inner2, cot_full, gu_w, down_weight, BLOCK)
     down_grad = lax.dot_general(hidden, cot_full, TN, preferred_element_type=F32).astype(BF16)
@@ -1266,11 +1411,20 @@
             for i in range(3)
         ]
     )
-    in_grad, out_grad, dproj, down_grad, gu_grad = lax.optimization_barrier(
-        (in_grad, out_grad, dproj, down_grad, gu_grad)
-    )
-    in_grad, out_grad = lax.psum((in_grad, out_grad), "ctx")
-    tokens_grad = unproject(dproj, tok_full, stat1, in_w, branch_grad, heads, tp_size)
+    if cube:
+        tokens_grad, in_grad, out_grad = unproject(
+            dproj, tok_full, stat1, in_w, branch_grad, heads, tp_size,
+            [in_grad.reshape(3 * width, span), out_grad],
+        )
+        in_grad = in_grad.reshape(3, width, span)
+    else:
+        in_grad, out_grad, down_grad, gu_grad = lax.optimization_barrier(
+            (in_grad, out_grad, down_grad, gu_grad)
+        )
+        in_grad, out_grad = lax.psum((in_grad, out_grad), "ctx")
+        (tokens_grad,) = unproject(
+            dproj, tok_full, stat1, in_w, branch_grad, heads, tp_size, []
+        )
     return (
         layer_out,
         tokens_grad,

time: 874 us -> 779 us (0.89)
  waiting for transfers between devices: 125 us -> 26 us
    pallas_call x1, Pallas kernels: 83.6 us -> 160 us  [unproject(): pl.pallas_call(functools.partial(unproject_kernel, heads, n, len(grads) >...]
    psum x1, waiting for transfers between devices: 71.7 us -> 0.01 us  [per_device(): lax.psum((down_grad, gu_grad), 'ctx')]
    pallas_call x1, Pallas kernels: 111 us -> 87 us  [norm_back(): pl.pallas_call(functools.partial(norm_back_kernel, n, sub), in_specs=[vme...]
    pallas_call x1, Pallas kernels: 102 us -> 80.1 us  [attend_far(): pl.pallas_call(functools.partial(attend_far_kernel, heads, n), in_specs=[...]
    pallas_call x1, Pallas kernels: 111 us -> 89.7 us  [merge(): pl.pallas_call(functools.partial(merge_kernel, n, sub), in_specs=[vmem] *...]
    psum x1 -> x0, waiting for transfers between devices: 15.5 us -> none  [per_device(): in_grad, out_grad = lax.psum((in_grad, out_grad), 'ctx')]
    all_gather x1, waiting for transfers between devices: 37.4 us -> 25.3 us  [gather(): return lax.all_gather(local, 'tp', axis=axis, tiled=True)]
    pallas_call x1, Pallas kernels: 102 us -> 92.6 us  [attend_back_far(): pl.pallas_call(functools.partial(attend_back_far_kernel, heads, n), in_sp...]
  transfers between devices with their start and end apart: 4 -> 3, of which waited for: 3 -> 1; matrix products, arithmetic and copies ran while one was open for 14% -> 16% of each run, Pallas kernels for 66% -> 61%
where the time goes in v4:
time: 779 us; the launch traced here: 770 us
  Pallas kernels  580 us (74%)
  matrix products  76.7 us (10%)
  local copies, waits for them, and re-layouts  32.5 us (4%)
  other arithmetic  29.5 us (4%)
  waiting for transfers between devices  26 us (3%)
  between operations  14.2 us (2%)
  blocking collectives  10.5 us (1%)
    pallas_call x1, Pallas kernels, unproject(): pl.pallas_call(functools.partial(unproject_kernel, heads, n, len(grads) >...  160 us
    pallas_call x1, Pallas kernels, attend_back_far(): pl.pallas_call(functools.partial(attend_back_far_kernel, heads, n), in_sp...  92.6 us
    pallas_call x1, Pallas kernels, merge(): pl.pallas_call(functools.partial(merge_kernel, n, sub), in_specs=[vmem] *...  89.7 us
    pallas_call x1, Pallas kernels, norm_back(): pl.pallas_call(functools.partial(norm_back_kernel, n, sub), in_specs=[vme...  87 us
    pallas_call x1, Pallas kernels, attend_far(): pl.pallas_call(functools.partial(attend_far_kernel, heads, n), in_specs=[...  80.1 us
    reshape x1, local copies, waits for them, and re-layouts, per_device(): gu_w = gu_w.reshape(width, 2 * hidden_local)  27.8 us
    pallas_call x1, Pallas kernels, feed(): pl.pallas_call(feed_kernel, grid=(units // block,), in_specs=[whole, whol...  27 us
    all_gather x1, waiting for transfers between devices, gather(): return lax.all_gather(local, 'tp', axis=axis, tiled=True)  25.3 us
  transfers between devices with their start and end apart: 3, of which 1 were waited for; matrix products, arithmetic and copies ran while one was open for 16% of the time, Pallas kernels for 61%

profile of v4, /device:TPU:0, one launch (start us, length us, event | category | flops | bytes accessed | tf_op | source)
XLA Modules:
  0.0 770.0 jit_solution(11133752662482124394)
XLA Ops:
  7.2 0.7 all-gather.4.cloned.1.call-update
  8.0 0.7 reshape.64
  8.6 10.5 %all-gather = s32[8,1,768]{2,1,0:T(1,128)S(1)} all-gather(s32[1,1,768]{2,1,0:T(1,128)S(1)} %reshape.64), channel_id=1, replica_groups=mesh['ctx'=8,'tp'=4] {'ctx'}, dimensions={0}, use_global_device_ids=true | all-gather | bytes 27648 | tf_op jit(solution)/shard_map/all_gather | solution.py:1345
  20.0 27.8 %reshape.58.w_ref = bf16[2048,4096]{1,0:T(8,128)(2,1)} reshape(bf16[2048,4,2,512]{3,2,1,0:T(2,128)(2,1)} %bitcast.38) | data formatting | bytes 33554432 | tf_op jit(solution)/shard_map/reshape | solution.py:1343
  47.8 1.4 fusion.6
  49.2 1.2 pad_maximum_fusion.1
  50.5 25.3 %all-gather.4.cloned.1.call-done.tok_ref = bf16[768,2048]{1,0:T(8,128)(2,1)} async-done(((bf16[768,512]{1,0:T(8,128)(2,1)}), bf16[768,2048]{1,0:T(8,128)(2,1)}) %all-gather.4.cloned.1.call-update) | async-done | bytes 3145744 | tf_op jit(solution)/shard_map/all_gather | solution.py:1335
  76.3 11.2 %project.1 = (bf16[768,2048]{1,0:T(8,128)(2,1)}, f32[768,2]{1,0:T(8,128)}, bf16[768,512]{1,0:T(8,128)(2,1)}, bf16[768,1024]{1,0:T(8,128)(2,1)}) custom-call(bf16[768,2048]{1,0:T(8,128)(2,1)} %all-gather.4.cloned.1.call-done.tok_ref, bf16[3,2048,512]{2,1,0:T(8,128)(2,1)} %bitcast.39, f32[768,128]{1,0:T(8,128)} %get-tuple-element.79.cos_ref, ...), custom_call_target="tpu_custom_call" | custom-call | flops 4831838208 | bytes 15728640 | tf_op jit(solution)/shard_map/project/pallas_call | solution.py:70
  87.6 80.1 %attend_far.1 = (f32[768,512]{1,0:T(8,128)}, bf16[768,512]{1,0:T(8,128)(2,1)}, f32[4,768]{1,0:T(4,128)}, bf16[6144,1024]{1,0:T(8,128)(2,1)}, bf16[768,2048]{1,0:T(8,128)(2,1)}) custom-call(bf16[768,512]{1,0:T(8,128)(2,1)} %get-tuple-element.51.q_ref, bf16[768,1024]{1,0:T(8,128)(2,1)} %get-tuple-element.42.own_ref, ...), custom_call_target="tpu_custom_call" | custom-call | flops 1000000 | bytes 1000000 | tf_op jit(solution)/shard_map/attend_far/pallas_call | solution.py:526
  168.0 4.6 convolution_convert_fusion.3.part_ref
  172.6 89.7 %merge.1 = (bf16[768,2048]{1,0:T(8,128)(2,1)}, f32[768,2048]{1,0:T(8,128)}, f32[768,2]{1,0:T(8,128)}) custom-call(bf16[768,2048]{1,0:T(8,128)(2,1)} %convolution_convert_fusion.3.part_ref, bf16[768,2048]{1,0:T(8,128)(2,1)} %all-gather.4.cloned.1.call-done.tok_ref), custom_call_target="tpu_custom_call" | custom-call | flops 1000000 | bytes 1000000 | tf_op jit(solution)/shard_map/merge/pallas_call | solution.py:1116
  262.3 27.0 %feed.1 = (bf16[768,2048]{1,0:T(8,128)(2,1)}, bf16[768,4096]{1,0:T(8,128)(2,1)}) custom-call(bf16[768,2048]{1,0:T(8,128)(2,1)} %get-tuple-element.46.inner_ref, bf16[768,2048]{1,0:T(8,128)(2,1)} %get-tuple-element.47.cot_ref, bf16[2048,4096]{1,0:T(8,128)(2,1)} %reshape.58.w_ref, bf16[2048,2048]{1,0:T(8,128)(2,1)} %down_ref.1), custom_call_target="tpu_custom_call" | custom-call | flops 19327352832 | bytes 31457280 | tf_op jit(solution)/shard_map/feed/pallas_call | solution.py:924
  289.3 11.1 %convolution_convert_fusion.1 = bf16[2048,2048]{1,0:T(8,128)(2,1)} fusion(bf16[768,2048]{1,0:T(8,128)(2,1)} %get-tuple-element.60, bf16[768,2048]{1,0:T(8,128)(2,1)S(1)} %copy-done.3), kind=kOutput, calls=%fused_computation.2 | convolution fusion | flops 6446645248 | bytes 14680064 | tf_op jit(solution)/shard_map/dot_general | solution.py:1382
  300.5 18.8 %convolution_convert_fusion = bf16[2048,4096]{1,0:T(8,128)(2,1)} fusion(bf16[768,2048]{1,0:T(8,128)(2,1)S(1)} %copy-done.9, bf16[768,4096]{1,0:T(8,128)(2,1)} %get-tuple-element.52), kind=kOutput, calls=%fused_computation | convolution fusion | flops 12893290496 | bytes 26214400 | tf_op jit(solution)/shard_map/dot_general | solution.py:1383
  319.3 20.1 %convolution_convert_fusion.2.part_ref = bf16[768,2048]{1,0:T(8,128)(2,1)} fusion(bf16[768,4096]{1,0:T(8,128)(2,1)} %get-tuple-element.52, bf16[2048,4096]{1,0:T(8,128)(2,1)} %reshape.58.w_ref), kind=kOutput, calls=%fused_computation.5 | convolution fusion | flops 12886474752 | bytes 26214400 | tf_op jit(solution)/shard_map/dot_general | solution.py:1389
  339.4 87.0 %norm_back.1.branch_ref = bf16[768,2048]{1,0:T(8,128)(2,1)} custom-call(bf16[768,2048]{1,0:T(8,128)(2,1)} %convolution_convert_fusion.2.part_ref, bf16[768,2048]{1,0:T(8,128)(2,1)} %get-tuple-element.47.cot_ref, f32[768,2048]{1,0:T(8,128)} %get-tuple-element.53.resid_ref, f32[768,2]{1,0:T(8,128)} %get-tuple-element.54.stat_ref), custom_call_target="tpu_custom_call" | custom-call | flops 1000000 | bytes 1000000 | tf_op jit(solution)/shard_map/norm_back/pallas_call | solution.py:1153
  426.5 6.7 mixed_grad.1
  433.2 12.1 %add_convert_fusion.part_ref = bf16[768,2048]{1,0:T(8,128)(2,1)} fusion(f32[768,2048]{1,0:T(8,128)S(1)} %bitcast.42, bf16[768,2048]{1,0:T(8,128)(2,1)} %get-tuple-element.60, bf16[2048,2048]{1,0:T(8,128)(2,1)} %down_ref.1), kind=kOutput, calls=%fused_computation.4 | convolution fusion | flops 6445596672 | bytes 20971520 | tf_op jit(solution)/shard_map/dot_general | solution.py:1393
  445.2 92.6 %attend_back_far.1 = (f32[768,512]{1,0:T(8,128)}, f32[768,512]{1,0:T(8,128)}, f32[768,512]{1,0:T(8,128)}, bf16[768,512]{1,0:T(8,128)(2,1)}) custom-call(bf16[768,640]{1,0:T(8,128)(2,1)} %get-tuple-element.57.g_ref, bf16[6144,512]{1,0:T(8,128)(2,1)} %all-gather.6.cloned.1.call-done.q_ref, bf16[6144,1024]{1,0:T(8,128)(2,1)} %get-tuple-element.59.pair_ref, ...), custom_call_target="tpu_custom_call" | custom-call | flops 1000000 | bytes 1000000 | tf_op jit(solution)/shard_map/attend_back_far/pallas_call | solution.py:670
  537.8 5.4 unrotate.1.dproj_ref
  543.3 3.1 fusion.2
  546.4 1.8 fusion.1
  548.3 1.8 fusion
  550.1 3.6 pad_maximum_fusion
  554.8 3.2 convolution_convert_fusion.4.refs_1_
  557.9 160.2 %unproject.1 = (f32[768,512]{1,0:T(8,128)}, bf16[6144,512]{1,0:T(8,128)(2,1)}, bf16[512,2048]{1,0:T(8,128)(2,1)}) custom-call(bf16[768,1536]{1,0:T(8,128)(2,1)} %unrotate.1.dproj_ref, bf16[768,2048]{1,0:T(8,128)(2,1)} %all-gather.4.cloned.1.call-done.tok_ref, f32[768,2]{1,0:T(8,128)} %get-tuple-element.65.stat_ref, bf16[3,2048,512]{2,1,0:T(8,128)(2,1)} %bitcast.40, ...), custom_call_target="tpu_custom_call" | custom-call | flops 1000000 | bytes 1000000 | tf_op jit(solution)/shard_map/unproject/pallas_call | solution.py:1299
  718.1 4.3 convert_element_type.62
  722.4 6.6 convert_bitcast_fusion
  729.0 20.4 %weave.1 = f32[2048,2,2048]{2,1,0:T(2,128)} custom-call(bf16[2048,4096]{1,0:T(8,128)(2,1)} %get-tuple-element.72.sum_ref), custom_call_target="tpu_custom_call" | custom-call | flops 8388608 | bytes 50331648 | tf_op jit(solution)/shard_map/weave/pallas_call | solution.py:958
  749.4 11.8 %convert_element_type.63 = f32[2048,2048]{1,0:T(8,128)} convert(bf16[2048,2048]{1,0:T(8,128)(2,1)} %get-tuple-element.73) | non-fusion elementwise | flops 4194304 | bytes 25165824 | tf_op jit(solution)/shard_map/convert_element_type | solution.py:1434
  761.2 0.9 copy.23
  762.1 1.1 copy.24
  (47 shorter events, 3.0 us)
Async XLA Ops:
  7.2 68.6 %all-gather.4.cloned.1.call-start = ((), (), s32[]{:S(2)}) async-start(), calls=%async_computation | async-start | bytes 3932160 | tf_op jit(solution)/shard_map/all_gather | solution.py:1335
  7.9 311.4 %all-gather.6.cloned.1.call-start = ((), (), s32[]{:S(2)}) async-start(), calls=%async_computation.1 | async-start | bytes 7077888 | tf_op jit(solution)/shard_map/all_gather | solution.py:1377
  50.5 37.1 %copy-start.8 = (s32[8,768]{1,0:T(8,128)}, s32[8,768]{1,0:T(8,128)S(1)}, u32[]{:S(2)}) copy-start(s32[8,768]{1,0:T(8,128)S(1)} %bitcast_maximum_fusion.begin_ref) | copy-start | bytes 73732
  87.6 80.4 %copy-start.4 = (bf16[512,2048]{1,0:T(8,128)(2,1)S(1)}, bf16[512,2048]{1,0:T(8,128)(2,1)}, u32[]{:S(2)}) copy-start(bf16[512,2048]{1,0:T(8,128)(2,1)} %w_ref.1) | copy-start | bytes 6291460
  167.8 561.2 %all-reduce.3.cloned.1.call-start = ((), (), s32[]{:S(2)}) async-start(), calls=%async_computation.2 | async-start | bytes 50331648 | tf_op jit(solution)/shard_map/psum | solution.py:1387
  262.3 27.1 %copy-start.3 = (bf16[768,2048]{1,0:T(8,128)(2,1)S(1)}, bf16[768,2048]{1,0:T(8,128)(2,1)}, u32[]{:S(2)}) copy-start(bf16[768,2048]{1,0:T(8,128)(2,1)} %get-tuple-element.47.cot_ref) | copy-start | bytes 9437188
  289.3 11.1 %copy-start.9 = (bf16[768,2048]{1,0:T(8,128)(2,1)S(1)}, bf16[768,2048]{1,0:T(8,128)(2,1)}, u32[]{:S(2)}) copy-start(bf16[768,2048]{1,0:T(8,128)(2,1)} %get-tuple-element.46.inner_ref) | copy-start | bytes 9437188
  319.3 113.9 %slice-start = ((s8[6291456]{0:T(1024)(128)(4,1)}), s8[2097152]{0:T(1024)(128)(4,1)S(1)}, s32[]{:S(2)}) async-start(s8[6291456]{0:T(1024)(128)(4,1)} %bitcast.41), calls=%async_computation.3 | async-start | bytes 4194304
  319.3 113.8 %slice-start.1 = ((s8[6291456]{0:T(1024)(128)(4,1)}), s8[4194304]{0:T(1024)(128)(4,1)S(1)}, s32[]{:S(2)}) async-start(s8[6291456]{0:T(1024)(128)(4,1)} %bitcast.41), calls=%async_computation.4 | async-start | bytes 8388608
  537.8 5.5 copy-start.10
  543.3 3.1 copy-start.1
  550.1 4.2 copy-start
  550.1 4.6 copy-start.7
  718.1 4.3 copy-start.2
  749.4 11.8 %copy-start.6 = (bf16[768,512]{1,0:T(8,128)(2,1)S(1)}, bf16[768,512]{1,0:T(8,128)(2,1)}, u32[]{:S(2)}) copy-start(bf16[768,512]{1,0:T(8,128)(2,1)} %get-tuple-element.87) | copy-start | bytes 2359300
  749.4 12.7 %copy-start.5 = (f32[768,512]{1,0:T(8,128)S(1)}, f32[768,512]{1,0:T(8,128)}, u32[]{:S(2)}) copy-start(f32[768,512]{1,0:T(8,128)} %get-tuple-element.88) | copy-start | bytes 4718596
Sparse Core Ops, SparseCore 0:
  9.6 66.1 all-gather.3
  167.9 53.5 all-gather.5
  319.5 402.7 all-reduce.2

commit v5 on v4

--- a/solution.py
+++ b/solution.py
@@ -18,7 +18,7 @@
 NT = (((1,), (1,)), ((), ()))
 TN = (((0,), (0,)), ((), ()))
 MESH = pl.DeviceIdType.MESH
-BLOCK = 512
+BLOCK = 256
 
 
 def params(mib, **more):
@@ -404,9 +404,9 @@
 
 
 def attend_far_kernel(
-    heads, n, q_ref, own_ref, begin_ref, cot_ref,
-    raw_ref, mixed_ref, lse_ref, pair_ref, full_ref,
-    high_ref, total_ref, acc_ref, s_ref, send, recv, zsend, zrecv,
+    heads, n, q_ref, own_ref, begin_ref, cot_ref, w_ref,
+    raw_ref, mixed_ref, lse_ref, keep_ref, full_ref, part_ref,
+    pair_ref, high_ref, total_ref, acc_ref, s_ref, send, recv, zsend, zrecv, keep_sem,
 ):
     rows = q_ref.shape[0]
     span = heads * HD
@@ -459,8 +459,13 @@
             def _():
                 pass_on(False, at + k, k).start()
 
+    def keep(step):
+        place = pl.ds(pl.multiple_of(cube.block(step) * rows, 16), rows)
+        return pltpu.make_async_copy(pair_ref.at[place], keep_ref.at[place], keep_sem.at[step])
+
     def turn(step, carry):
         cube.advance(step)
+        keep(step).start()
         for k in range(n):
             @pl.when(step == min(k * 2, CUBE - 1 - (n - 1 - k)) if n <= CUBE else k)
             def _():
@@ -507,7 +512,16 @@
         out = (acc_ref[h] / total_ref[h : h + 1, :]).T
         raw_ref[:, hs] = out
         mixed_ref[:, hs] = out.astype(BF16)
+    part_ref[...] = jnp.dot(
+        mixed_ref[...], w_ref[...], preferred_element_type=F32
+    ).astype(BF16)
     lse_ref[...] = high_ref[...] * C2 + jnp.log2(total_ref[...])
+
+    def kept(step, carry):
+        keep(step).wait()
+        return carry
+
+    lax.fori_loop(0, CUBE, kept, 0)
     cube.finish()
     for k in range(n):
         @pl.when((at >= k) & (at < n - 1))
@@ -519,22 +533,25 @@
             pass_on(False, at + k, k).wait_send()
 
 
-def attend_far(query, pairs, begin, cot, heads, n):
+def attend_far(query, pairs, begin, cot, weight, heads, n):
     rows = query.shape[0]
+    width = weight.shape[1]
     span = heads * HD
     vmem = pl.BlockSpec(memory_space=pltpu.VMEM)
     return pl.pallas_call(
         functools.partial(attend_far_kernel, heads, n),
-        in_specs=[vmem] * 4,
-        out_specs=[vmem] * 5,
+        in_specs=[vmem] * 5,
+        out_specs=[vmem] * 3 + [pl.BlockSpec(memory_space=pl.ANY)] + [vmem] * 2,
         out_shape=[
             jax.ShapeDtypeStruct((rows, span), F32),
             jax.ShapeDtypeStruct((rows, span), BF16),
             jax.ShapeDtypeStruct((heads, rows), F32),
             jax.ShapeDtypeStruct((CUBE * rows, 2 * span), BF16),
             jax.ShapeDtypeStruct((rows, n * cot.shape[1]), BF16),
+            jax.ShapeDtypeStruct((rows, width), BF16),
         ],
         scratch_shapes=[
+            pltpu.VMEM((CUBE * rows, 2 * span), BF16),
             pltpu.VMEM((heads, rows), F32),
             pltpu.VMEM((heads, rows), F32),
             pltpu.VMEM((heads, HD, rows), F32),
@@ -543,17 +560,19 @@
             pltpu.SemaphoreType.DMA((CUBE_SENDS,)),
             pltpu.SemaphoreType.DMA((2, n)),
             pltpu.SemaphoreType.DMA((2, n)),
+            pltpu.SemaphoreType.DMA((CUBE,)),
         ],
         compiler_params=params(58, collective_id=2, has_side_effects=True),
         cost_estimate=cost(1e6, 1e6),
         name="attend_far",
-    )(query, pairs, begin, cot)
+    )(query, pairs, begin, cot, weight)
 
 
 def attend_back_far_kernel(
-    heads, n, g_ref, q_ref, pair_ref, begin_ref, part_ref,
+    heads, n, g_ref, far_q_ref, far_pair_ref, begin_ref, part_ref,
     dq_ref, dk_ref, dv_ref, layer_ref,
-    all_ref, acc_ref, rows_ref, s_ref, p_ref, land_ref, send, recv, zsend, zrecv,
+    all_ref, acc_ref, rows_ref, s_ref, p_ref, land_ref, pair_ref, q_ref,
+    send, recv, zsend, zrecv, read_sem,
 ):
     rows = g_ref.shape[0]
     span = heads * HD
@@ -567,6 +586,28 @@
         pl.semaphore_signal(
             barrier, inc=1, device_id={"tp": lax.rem(at + o, n)}, device_id_type=MESH
         )
+
+    def read(step, keys):
+        place = pl.ds(pl.multiple_of(cube.block(step) * rows, 16), rows)
+        far, near = (far_pair_ref, pair_ref) if keys else (far_q_ref, q_ref)
+        return pltpu.make_async_copy(
+            far.at[place], near.at[place], read_sem.at[0 if keys else 1, step]
+        )
+
+    def read_all(step, carry):
+        block = cube.block(step)
+
+        @pl.when(block <= me)
+        def _():
+            read(step, True).start()
+
+        @pl.when(block >= me)
+        def _():
+            read(step, False).start()
+
+        return carry
+
+    lax.fori_loop(0, CUBE, read_all, 0)
     all_ref[pl.ds(pl.multiple_of(me * rows, 16), rows), :] = g_ref[...]
     acc_ref[...] = jnp.zeros_like(acc_ref)
     dk_ref[...] = jnp.zeros_like(dk_ref)
@@ -594,6 +635,14 @@
 
         block = cube.block(step)
         place = pl.ds(pl.multiple_of(block * rows, 16), rows)
+
+        @pl.when(block <= me)
+        def _():
+            read(step, True).wait()
+
+        @pl.when(block >= me)
+        def _():
+            read(step, False).wait()
 
         def scores(h, key_block, key_place, query_block, query_place):
             hs = slice(h * HD, (h + 1) * HD)
@@ -669,7 +718,7 @@
     wide = jax.ShapeDtypeStruct((rows, span), F32)
     return pl.pallas_call(
         functools.partial(attend_back_far_kernel, heads, n),
-        in_specs=[vmem] * 5,
+        in_specs=[vmem] + [pl.BlockSpec(memory_space=pl.ANY)] * 2 + [vmem] * 2,
         out_specs=[vmem] * 4,
         out_shape=[wide, wide, wide, jax.ShapeDtypeStruct((rows, shard), BF16)],
         scratch_shapes=[
@@ -679,10 +728,13 @@
             pltpu.VMEM((2, rows, rows), F32),
             pltpu.VMEM((2, rows, rows), F32),
             pltpu.VMEM((n - 1, rows, shard), BF16),
+            pltpu.VMEM((CUBE * rows, 2 * span), BF16),
+            pltpu.VMEM((CUBE * rows, span), BF16),
             pltpu.SemaphoreType.DMA((CUBE_SENDS,)),
             pltpu.SemaphoreType.DMA((CUBE_SENDS,)),
             pltpu.SemaphoreType.DMA((n - 1,)),
             pltpu.SemaphoreType.DMA((n - 1,)),
+            pltpu.SemaphoreType.DMA((2, CUBE)),
         ],
         compiler_params=params(60, collective_id=3, has_side_effects=True),
         cost_estimate=cost(1e6, 1e6),
@@ -905,7 +957,9 @@
     )(branch, weight, raw, lse)
 
 
-def feed_kernel(inner_ref, cot_ref, w_ref, down_ref, hidden_ref, dgu_ref):
+def feed_kernel(
+    inner_ref, cot_ref, w_ref, down_ref, hidden_ref, dgu_ref, down_grad_ref, gu_grad_ref
+):
     block = down_ref.shape[0]
     both = jnp.dot(inner_ref[...], w_ref[...], preferred_element_type=F32)
     grad = lax.dot_general(cot_ref[...], down_ref[...], NT, preferred_element_type=F32)
@@ -915,31 +969,34 @@
     hidden_ref[...] = (active * up).astype(BF16)
     dgu_ref[:, :block] = (grad * up * sigma * (1.0 + gate * (1.0 - sigma))).astype(BF16)
     dgu_ref[:, block:] = (grad * active).astype(BF16)
+    down_grad_ref[...] = lax.dot_general(
+        hidden_ref[...], cot_ref[...], TN, preferred_element_type=F32
+    ).astype(BF16)
+    gu_grad_ref[...] = lax.dot_general(
+        inner_ref[...], dgu_ref[...], TN, preferred_element_type=F32
+    ).astype(BF16)
 
 
 def feed(inner, cot, weight, down, block):
     rows, width = inner.shape
     units = down.shape[0]
     whole = pl.BlockSpec((rows, width), lambda j: (0, 0))
+    column = lambda high, wide: pl.BlockSpec((high, wide), lambda j: (0, j))
+    line = pl.BlockSpec((block, width), lambda j: (j, 0))
     return pl.pallas_call(
         feed_kernel,
         grid=(units // block,),
-        in_specs=[
-            whole, whole,
-            pl.BlockSpec((width, 2 * block), lambda j: (0, j)),
-            pl.BlockSpec((block, width), lambda j: (j, 0)),
-        ],
-        out_specs=[
-            pl.BlockSpec((rows, block), lambda j: (0, j)),
-            pl.BlockSpec((rows, 2 * block), lambda j: (0, j)),
-        ],
+        in_specs=[whole, whole, column(width, 2 * block), line],
+        out_specs=[column(rows, block), column(rows, 2 * block), line, column(width, 2 * block)],
         out_shape=[
             jax.ShapeDtypeStruct((rows, units), BF16),
             jax.ShapeDtypeStruct((rows, 2 * units), BF16),
+            jax.ShapeDtypeStruct((units, width), BF16),
+            jax.ShapeDtypeStruct((width, 2 * units), BF16),
         ],
-        compiler_params=params(56),
+        compiler_params=params(60),
         cost_estimate=cost(
-            6 * rows * width * units, 6 * width * units + 4 * rows * width, rows * units
+            12 * rows * width * units, 12 * width * units + 4 * rows * width, rows * units
         ),
         name="feed",
     )(inner, cot, weight, down)
@@ -954,7 +1011,7 @@
 
 def weave(summed, block):
     width, both = summed.shape
-    rows = 256
+    rows = 512
     return pl.pallas_call(
         functools.partial(weave_kernel, block),
         grid=(width // rows,),
@@ -964,6 +1021,25 @@
         compiler_params=params(56),
         cost_estimate=cost(width * both, 6 * width * both),
         name="weave",
+    )(summed)
+
+
+def widen_kernel(in_ref, out_ref):
+    out_ref[...] = in_ref[...].astype(F32)
+
+
+def widen(summed):
+    high, wide = summed.shape
+    block = pl.BlockSpec((512, wide), lambda i: (i, 0))
+    return pl.pallas_call(
+        widen_kernel,
+        grid=(high // 512,),
+        in_specs=[block],
+        out_specs=block,
+        out_shape=jax.ShapeDtypeStruct((high, wide), F32),
+        compiler_params=params(56),
+        cost_estimate=cost(high * wide, 6 * high * wide),
+        name="widen",
     )(summed)
 
 
@@ -1163,34 +1239,56 @@
     )(part, cot, resid, stat)
 
 
-def unrotate_kernel(heads, dq_ref, dk_ref, dv_ref, cos_ref, sin_ref, dproj_ref):
-    cosine, sine = cos_ref[...], sin_ref[...]
-    span = heads * HD
-
-    def back(piece):
-        return (piece * cosine - pltpu.roll(piece, HD // 2, 1) * sine).astype(BF16)
-
-    for h in range(heads):
-        hs = slice(h * HD, (h + 1) * HD)
-        dproj_ref[:, hs] = back(dq_ref[:, hs])
-        dproj_ref[:, span + h * HD : span + (h + 1) * HD] = back(dk_ref[:, hs])
-    dproj_ref[:, 2 * span :] = dv_ref[...].astype(BF16)
-
-
-def unrotate(dq, dk, dv, cosine, sine, heads):
+def unrotate_kernel(
+    heads, dq_ref, dk_ref, dv_ref, cos_ref, sin_ref, inner_ref, dproj_ref, grad_ref
+):
+    def back(ref):
+        for h in range(heads):
+            hs = slice(h * HD, (h + 1) * HD)
+            piece = ref[:, hs]
+            dproj_ref[:, hs] = (
+                piece * cos_ref[...] - pltpu.roll(piece, HD // 2, 1) * sin_ref[...]
+            ).astype(BF16)
+
+    part = pl.program_id(0)
+
+    @pl.when(part == 0)
+    def _():
+        back(dq_ref)
+
+    @pl.when(part == 1)
+    def _():
+        back(dk_ref)
+
+    @pl.when(part == 2)
+    def _():
+        dproj_ref[...] = dv_ref[...].astype(BF16)
+
+    grad_ref[...] = lax.dot_general(
+        inner_ref[...], dproj_ref[...], TN, preferred_element_type=F32
+    ).astype(BF16)
+
+
+def unrotate(dq, dk, dv, cosine, sine, inner, heads):
     rows, span = dq.shape
-    block = 256
-    row = lambda n: pl.BlockSpec((block, n), lambda i: (i, 0))
+    width = inner.shape[1]
+    whole = lambda n: pl.BlockSpec((rows, n), lambda i: (0, 0))
     return pl.pallas_call(
         functools.partial(unrotate_kernel, heads),
-        grid=(rows // block,),
-        in_specs=[row(span), row(span), row(span), row(HD), row(HD)],
-        out_specs=row(3 * span),
-        out_shape=jax.ShapeDtypeStruct((rows, 3 * span), BF16),
+        grid=(3,),
+        in_specs=[whole(span)] * 3 + [whole(HD)] * 2 + [whole(width)],
+        out_specs=[
+            pl.BlockSpec((rows, span), lambda i: (0, i)),
+            pl.BlockSpec((width, span), lambda i: (i, 0)),
+        ],
+        out_shape=[
+            jax.ShapeDtypeStruct((rows, 3 * span), BF16),
+            jax.ShapeDtypeStruct((3 * width, span), BF16),
+        ],
         compiler_params=params(56),
-        cost_estimate=cost(1e6, 18 * rows * span),
+        cost_estimate=cost(6 * rows * span * width, 12 * rows * span + 6 * width * span),
         name="unrotate",
-    )(dq, dk, dv, cosine, sine)
+    )(dq, dk, dv, cosine, sine, inner)
 
 
 def unproject_kernel(heads, n, cube, dproj_ref, tok_ref, stat_ref, w_ref, branch_ref, *refs):
@@ -1366,21 +1464,19 @@
     all_begin = all_begin[None, :]
     inner1, stat1, query, pairs = project(tok_full, in_w, cosine, sine, heads)
     if cube:
-        raw, mixed, lse, all_pairs, cot_full = attend_far(
-            query, pairs, begin, cotangent, heads, tp_size
+        raw, mixed, lse, all_pairs, cot_full, out_part = attend_far(
+            query, pairs, begin, cotangent, out_weight, heads, tp_size
         )
     else:
         all_pairs = lax.all_gather(pairs, "ctx", axis=0, tiled=True)
         cot_full = gather(cotangent)
         raw, mixed, lse = attend(key_info, query, all_pairs, begin, heads)
+        out_part = jnp.dot(mixed, out_weight, preferred_element_type=F32).astype(BF16)
     late_query, mixed = lax.optimization_barrier((query, mixed))
     all_query = lax.all_gather(late_query, "ctx", axis=0, tiled=True)
-    out_part = jnp.dot(mixed, out_weight, preferred_element_type=F32).astype(BF16)
     inner2, resid1, stat2 = merge(out_part, tok_full, tp_size)
 
-    hidden, grad_gu = feed(inner2, cot_full, gu_w, down_weight, BLOCK)
-    down_grad = lax.dot_general(hidden, cot_full, TN, preferred_element_type=F32).astype(BF16)
-    gu_grad = lax.dot_general(inner2, grad_gu, TN, preferred_element_type=F32).astype(BF16)
+    hidden, grad_gu, down_grad, gu_grad = feed(inner2, cot_full, gu_w, down_weight, BLOCK)
     down_grad, gu_grad, all_query, grad_gu, hidden = lax.optimization_barrier(
         (down_grad, gu_grad, all_query, grad_gu, hidden)
     )
@@ -1402,21 +1498,12 @@
         dq = query_grad(key_info, query, grad_mixed, lse, delta, all_pairs, begin, heads)
         dk, dv = key_grad(query_info, pairs, all_query, all_grad, all_begin, heads)
 
-    dproj = unrotate(dq, dk, dv, cosine, sine, heads)
-    in_grad = jnp.stack(
-        [
-            lax.dot_general(
-                inner1, dproj[:, i * span : (i + 1) * span], TN, preferred_element_type=F32
-            ).astype(BF16)
-            for i in range(3)
-        ]
-    )
+    dproj, in_grad = unrotate(dq, dk, dv, cosine, sine, inner1, heads)
     if cube:
         tokens_grad, in_grad, out_grad = unproject(
             dproj, tok_full, stat1, in_w, branch_grad, heads, tp_size,
-            [in_grad.reshape(3 * width, span), out_grad],
+            [in_grad, out_grad],
         )
-        in_grad = in_grad.reshape(3, width, span)
     else:
         in_grad, out_grad, down_grad, gu_grad = lax.optimization_barrier(
             (in_grad, out_grad, down_grad, gu_grad)
@@ -1428,10 +1515,10 @@
     return (
         layer_out,
         tokens_grad,
-        jnp.transpose(in_grad, (1, 0, 2)).astype(F32),
+        jnp.transpose(widen(in_grad).reshape(3, width, span), (1, 0, 2)),
         out_grad.astype(F32),
         weave(gu_grad, BLOCK),
-        down_grad.astype(F32),
+        widen(down_grad),
     )
 
 

time: 779 us -> 767 us (0.985)
  Pallas kernels: 580 us -> 632 us
  matrix products: 76.7 us -> 35 us
  other arithmetic: 29.5 us -> 7.37 us
    dot_general x6 -> x0, matrix products: 41.3 us -> none  [the longest x1 18.8 us: per_device(): lax.dot_general(inner2, grad_gu, TN, preferred_element_type=F32)]
    pallas_call x1 -> x3, Pallas kernels: 5.44 us -> 31.9 us  [the longest x2 20 us: widen(): pl.pallas_call(widen_kernel, grid=(high // 512,), in_specs=[block], out_s...]
    pallas_call x1, Pallas kernels: 27 us -> 47.1 us  [feed(): pl.pallas_call(feed_kernel, grid=(units // block,), in_specs=[whole, whol...]
    convert_element_type x2 -> x0, other arithmetic: 18.4 us -> none  [the longest x1 11.8 us: per_device(): down_grad.astype(F32)]
  transfers between devices with their start and end apart: 3 -> 3, of which waited for: 1 -> 1; matrix products, arithmetic and copies ran while one was open for 16% -> 9% of each run, Pallas kernels for 61% -> 67%
where the time goes in v5:
time: 767 us; the launch traced here: 757 us
  Pallas kernels  632 us (82%)
  matrix products  35 us (5%)
  local copies, waits for them, and re-layouts  31.4 us (4%)
  waiting for transfers between devices  26 us (3%)
  between operations  14.1 us (2%)
  blocking collectives  10.5 us (1%)
    pallas_call x1, Pallas kernels, unproject(): pl.pallas_call(functools.partial(unproject_kernel, heads, n, len(grads) >...  161 us
    pallas_call x1, Pallas kernels, attend_back_far(): pl.pallas_call(functools.partial(attend_back_far_kernel, heads, n), in_sp...  92.9 us
    pallas_call x1, Pallas kernels, merge(): pl.pallas_call(functools.partial(merge_kernel, n, sub), in_specs=[vmem] *...  90.1 us
    pallas_call x1, Pallas kernels, norm_back(): pl.pallas_call(functools.partial(norm_back_kernel, n, sub), in_specs=[vme...  87.3 us
    pallas_call x1, Pallas kernels, attend_far(): pl.pallas_call(functools.partial(attend_far_kernel, heads, n), in_specs=[...  79.6 us
    pallas_call x1, Pallas kernels, feed(): pl.pallas_call(feed_kernel, grid=(units // block,), in_specs=[whole, whol...  47.1 us
    reshape x1, local copies, waits for them, and re-layouts, per_device(): gu_w = gu_w.reshape(width, 2 * hidden_local)  27.8 us
    all_gather x1, waiting for transfers between devices, gather(): return lax.all_gather(local, 'tp', axis=axis, tiled=True)  25.3 us
  transfers between devices with their start and end apart: 3, of which 1 were waited for; matrix products, arithmetic and copies ran while one was open for 9% of the time, Pallas kernels for 67%

profile of v5, /device:TPU:0, one launch (start us, length us, event | category | flops | bytes accessed | tf_op | source)
XLA Modules:
  0.0 756.9 jit_solution(7448780344559976824)
XLA Ops:
  7.2 0.7 all-gather.4.cloned.1.call-update
  8.0 0.7 reshape.60
  8.6 10.5 %all-gather = s32[8,1,768]{2,1,0:T(1,128)S(1)} all-gather(s32[1,1,768]{2,1,0:T(1,128)S(1)} %reshape.60), channel_id=1, replica_groups=mesh['ctx'=8,'tp'=4] {'ctx'}, dimensions={0}, use_global_device_ids=true | all-gather | bytes 27648 | tf_op jit(solution)/shard_map/all_gather | solution.py:1443
  19.1 0.1 slice_compare_fusion
  19.2 0.1 add_select_fusion
  19.3 0.3 reduce-window.9
  19.7 0.1 slice_reduce_fusion
  19.8 0.1 reshape.57
  19.9 0.1 copy.18
  20.0 27.8 %reshape.55.w_ref = bf16[2048,4096]{1,0:T(8,128)(2,1)} reshape(bf16[2048,8,2,256]{3,2,1,0:T(2,128)(2,1)} %bitcast.20) | data formatting | bytes 33554432 | tf_op jit(solution)/shard_map/reshape | solution.py:1441
  47.8 1.4 fusion
  49.2 1.2 pad_maximum_fusion
  50.5 25.3 %all-gather.4.cloned.1.call-done.tok_ref = bf16[768,2048]{1,0:T(8,128)(2,1)} async-done(((bf16[768,512]{1,0:T(8,128)(2,1)}), bf16[768,2048]{1,0:T(8,128)(2,1)}) %all-gather.4.cloned.1.call-update) | async-done | bytes 3145744 | tf_op jit(solution)/shard_map/all_gather | solution.py:1433
  75.8 0.6 constant_dynamic-slice_fusion.begin_ref
  76.3 11.2 %project.1 = (bf16[768,2048]{1,0:T(8,128)(2,1)}, f32[768,2]{1,0:T(8,128)}, bf16[768,512]{1,0:T(8,128)(2,1)}, bf16[768,1024]{1,0:T(8,128)(2,1)}) custom-call(bf16[768,2048]{1,0:T(8,128)(2,1)} %all-gather.4.cloned.1.call-done.tok_ref, bf16[3,2048,512]{2,1,0:T(8,128)(2,1)} %bitcast.22, f32[768,128]{1,0:T(8,128)} %get-tuple-element.89.cos_ref, ...), custom_call_target="tpu_custom_call" | custom-call | flops 4831838208 | bytes 15728640 | tf_op jit(solution)/shard_map/project/pallas_call | solution.py:70
  87.6 79.6 %attend_far.1 = (f32[768,512]{1,0:T(8,128)}, bf16[768,512]{1,0:T(8,128)(2,1)}, f32[4,768]{1,0:T(4,128)}, bf16[6144,1024]{1,0:T(8,128)(2,1)}, bf16[768,2048]{1,0:T(8,128)(2,1)}, /*index=5*/bf16[768,2048]{1,0:T(8,128)(2,1)}) custom-call(bf16[768,512]{1,0:T(8,128)(2,1)} %get-tuple-element.56.q_ref, bf16[768,1024]{1,0:T(8,128)(2,1)} %get-tuple-element.47.own_ref, ...), custom_call_target="tpu_custom_call" | custom-call | flops 1000000 | bytes 1000000 | tf_op jit(solution)/shard_map/attend_far/pallas_call | solution.py:541
  167.2 90.1 %merge.1 = (bf16[768,2048]{1,0:T(8,128)(2,1)}, f32[768,2048]{1,0:T(8,128)}, f32[768,2]{1,0:T(8,128)}) custom-call(bf16[768,2048]{1,0:T(8,128)(2,1)} %get-tuple-element.49.part_ref, bf16[768,2048]{1,0:T(8,128)(2,1)} %all-gather.4.cloned.1.call-done.tok_ref), custom_call_target="tpu_custom_call" | custom-call | flops 1000000 | bytes 1000000 | tf_op jit(solution)/shard_map/merge/pallas_call | solution.py:1192
  257.4 47.1 %feed.1 = (bf16[768,2048]{1,0:T(8,128)(2,1)}, bf16[768,4096]{1,0:T(8,128)(2,1)}, bf16[2048,2048]{1,0:T(8,128)(2,1)}, bf16[2048,4096]{1,0:T(8,128)(2,1)}) custom-call(bf16[768,2048]{1,0:T(8,128)(2,1)} %get-tuple-element.50.inner_ref, bf16[768,2048]{1,0:T(8,128)(2,1)} %get-tuple-element.51.cot_ref, bf16[2048,4096]{1,0:T(8,128)(2,1)} %reshape.55.w_ref, ...), custom_call_target="tpu_custom_call" | custom-call | flops 38654705664 | bytes 56623104 | tf_op jit(solution)/shard_map/feed/pallas_call | solution.py:986
  304.5 19.7 %convolution_convert_fusion.part_ref = bf16[768,2048]{1,0:T(8,128)(2,1)} fusion(bf16[768,4096]{1,0:T(8,128)(2,1)} %get-tuple-element.59, bf16[2048,4096]{1,0:T(8,128)(2,1)} %reshape.55.w_ref), kind=kOutput, calls=%fused_computation.1 | convolution fusion | flops 12886474752 | bytes 26214400 | tf_op jit(solution)/shard_map/dot_general | solution.py:1485
  324.2 87.3 %norm_back.1.branch_ref = bf16[768,2048]{1,0:T(8,128)(2,1)} custom-call(bf16[768,2048]{1,0:T(8,128)(2,1)} %convolution_convert_fusion.part_ref, bf16[768,2048]{1,0:T(8,128)(2,1)} %get-tuple-element.51.cot_ref, f32[768,2048]{1,0:T(8,128)} %get-tuple-element.60.resid_ref, f32[768,2]{1,0:T(8,128)} %get-tuple-element.61.stat_ref), custom_call_target="tpu_custom_call" | custom-call | flops 1000000 | bytes 1000000 | tf_op jit(solution)/shard_map/norm_back/pallas_call | solution.py:1229
  411.5 6.7 mixed_grad.1
  418.2 12.1 %add_convert_fusion.part_ref = bf16[768,2048]{1,0:T(8,128)(2,1)} fusion(f32[768,2048]{1,0:T(8,128)S(1)} %bitcast.25, bf16[768,2048]{1,0:T(8,128)(2,1)} %get-tuple-element.67, bf16[2048,2048]{1,0:T(8,128)(2,1)} %down_ref.1), kind=kOutput, calls=%fused_computation | convolution fusion | flops 6445596672 | bytes 20971520 | tf_op jit(solution)/shard_map/dot_general | solution.py:1489
  430.3 92.9 %attend_back_far.1 = (f32[768,512]{1,0:T(8,128)}, f32[768,512]{1,0:T(8,128)}, f32[768,512]{1,0:T(8,128)}, bf16[768,512]{1,0:T(8,128)(2,1)}) custom-call(bf16[768,640]{1,0:T(8,128)(2,1)} %get-tuple-element.64.g_ref, bf16[6144,512]{1,0:T(8,128)(2,1)} %all-gather.6.cloned.1.call-done.far_q_ref, bf16[6144,1024]{1,0:T(8,128)(2,1)} %get-tuple-element.66.far_pair_ref, ...), custom_call_target="tpu_custom_call" | custom-call | flops 1000000 | bytes 1000000 | tf_op jit(solution)/shard_map/attend_back_far/pallas_call | solution.py:719
  523.2 11.9 %unrotate.1 = (bf16[768,1536]{1,0:T(8,128)(2,1)}, bf16[6144,512]{1,0:T(8,128)(2,1)}) custom-call(f32[768,512]{1,0:T(8,128)} %get-tuple-element.69.dq_ref, f32[768,512]{1,0:T(8,128)} %get-tuple-element.70.dk_ref, f32[768,512]{1,0:T(8,128)} %get-tuple-element.71.dv_ref, f32[768,128]{1,0:T(8,128)} %get-tuple-element.89.cos_ref, ...), custom_call_target="tpu_custom_call" | custom-call | flops 4831838208 | bytes 11010048 | tf_op jit(solution)/shard_map/unrotate/pallas_call | solution.py:1276
  535.1 3.1 convolution_convert_fusion.1.refs_1_
  538.2 161.0 %unproject.1 = (f32[768,512]{1,0:T(8,128)}, bf16[6144,512]{1,0:T(8,128)(2,1)}, bf16[512,2048]{1,0:T(8,128)(2,1)}) custom-call(bf16[768,1536]{1,0:T(8,128)(2,1)} %get-tuple-element.73.dproj_ref, bf16[768,2048]{1,0:T(8,128)(2,1)} %all-gather.4.cloned.1.call-done.tok_ref, f32[768,2]{1,0:T(8,128)} %get-tuple-element.74.stat_ref, bf16[3,2048,512]{2,1,0:T(8,128)(2,1)} %bitcast.23, ...), custom_call_target="tpu_custom_call" | custom-call | flops 1000000 | bytes 1000000 | tf_op jit(solution)/shard_map/unproject/pallas_call | solution.py:1397
  699.3 4.1 convert_element_type.23
  703.4 10.3 %widen.2 = f32[6144,512]{1,0:T(8,128)} custom-call(bf16[6144,512]{1,0:T(8,128)(2,1)} %get-tuple-element.78.in_ref), custom_call_target="tpu_custom_call" | custom-call | flops 3145728 | bytes 18874368 | tf_op jit(solution)/shard_map/widen/pallas_call | solution.py:1034
  713.8 24.7 %weave.1 = f32[2048,2,2048]{2,1,0:T(2,128)} custom-call(bf16[2048,4096]{1,0:T(8,128)(2,1)} %get-tuple-element.82.sum_ref), custom_call_target="tpu_custom_call" | custom-call | flops 8388608 | bytes 50331648 | tf_op jit(solution)/shard_map/weave/pallas_call | solution.py:1015
  738.4 9.7 %widen.3 = f32[2048,2048]{1,0:T(8,128)} custom-call(bf16[2048,2048]{1,0:T(8,128)(2,1)} %get-tuple-element.83.in_ref), custom_call_target="tpu_custom_call" | custom-call | flops 4194304 | bytes 25165824 | tf_op jit(solution)/shard_map/widen/pallas_call | solution.py:1034
  748.1 0.9 copy.23
  749.0 1.1 copy.24
  (28 shorter events, 0.4 us)
Async XLA Ops:
  7.2 68.6 %all-gather.4.cloned.1.call-start = ((), (), s32[]{:S(2)}) async-start(), calls=%async_computation | async-start | bytes 3932160 | tf_op jit(solution)/shard_map/all_gather | solution.py:1433
  7.9 296.5 %all-gather.6.cloned.1.call-start = ((), (), s32[]{:S(2)}) async-start(), calls=%async_computation.1 | async-start | bytes 7077888 | tf_op jit(solution)/shard_map/all_gather | solution.py:1476
  50.5 37.1 %copy-start.4 = (s32[8,768]{1,0:T(8,128)}, s32[8,768]{1,0:T(8,128)S(1)}, u32[]{:S(2)}) copy-start(s32[8,768]{1,0:T(8,128)S(1)} %bitcast_maximum_fusion.begin_ref) | copy-start | bytes 73732
  167.2 546.6 %all-reduce.3.cloned.1.call-start = ((), (), s32[]{:S(2)}) async-start(), calls=%async_computation.2 | async-start | bytes 50331648 | tf_op jit(solution)/shard_map/psum | solution.py:1483
  324.2 94.0 %slice-start = ((s8[6291456]{0:T(1024)(128)(4,1)}), s8[4194304]{0:T(1024)(128)(4,1)S(1)}, s32[]{:S(2)}) async-start(s8[6291456]{0:T(1024)(128)(4,1)} %bitcast.24), calls=%async_computation.3 | async-start | bytes 8388608
  324.2 94.0 %slice-start.1 = ((s8[6291456]{0:T(1024)(128)(4,1)}), s8[2097152]{0:T(1024)(128)(4,1)S(1)}, s32[]{:S(2)}) async-start(s8[6291456]{0:T(1024)(128)(4,1)} %bitcast.24), calls=%async_computation.4 | async-start | bytes 4194304
  523.2 11.9 %copy-start = (bf16[768,2048]{1,0:T(8,128)(2,1)S(1)}, bf16[768,2048]{1,0:T(8,128)(2,1)}, u32[]{:S(2)}) copy-start(bf16[768,2048]{1,0:T(8,128)(2,1)} %norm_back.1.branch_ref) | copy-start | bytes 9437188
  523.2 11.9 %copy-start.3 = (bf16[768,512]{1,0:T(8,128)(2,1)S(1)}, bf16[768,512]{1,0:T(8,128)(2,1)}, u32[]{:S(2)}) copy-start(bf16[768,512]{1,0:T(8,128)(2,1)} %get-tuple-element.76) | copy-start | bytes 2359300
  738.4 9.7 %copy-start.2 = (bf16[768,512]{1,0:T(8,128)(2,1)S(1)}, bf16[768,512]{1,0:T(8,128)(2,1)}, u32[]{:S(2)}) copy-start(bf16[768,512]{1,0:T(8,128)(2,1)} %get-tuple-element.97) | copy-start | bytes 2359300
  738.4 10.6 %copy-start.1 = (f32[768,512]{1,0:T(8,128)S(1)}, f32[768,512]{1,0:T(8,128)}, u32[]{:S(2)}) copy-start(f32[768,512]{1,0:T(8,128)} %get-tuple-element.98) | copy-start | bytes 4718596
Sparse Core Ops, SparseCore 0:
  9.6 66.1 all-gather.3
  167.3 53.4 all-gather.5
  304.6 406.2 all-reduce.2

commit v6 on v5

--- a/solution.py
+++ b/solution.py
@@ -286,12 +286,11 @@
 
 
 class CubeSum:
-    def __init__(self, own, out, land, send, recv):
+    def __init__(self, rows, send, recv, own=None, land=None, out=None, shard=None, local=None):
         me = lax.axis_index("ctx")
         core, x, y = me % 2, (me // 2) % 2, me // 4
         self.me, self.own, self.out, self.land = me, own, out, land
-        self.send, self.recv = send, recv
-        rows = own.shape[0]
+        self.send, self.recv, self.shard, self.local = send, recv, shard, local
         self.half, self.quarter = rows // 2, rows // 4
         self.eighth, self.last = rows // 8, rows // 16
         mine = core * self.half
@@ -304,24 +303,33 @@
         self.give2 = (self.keep1[0] + (1 - y) * self.last, self.keep1[1] + (1 - x) * self.last)
 
     def place(self, ref, start, size):
-        return ref.at[pl.ds(pl.multiple_of(start, 16), size)]
+        return ref.at[pl.ds(start if isinstance(start, int) else pl.multiple_of(start, 16), size)]
+
+    def final(self, i):
+        if self.shard is not None:
+            return self.shard, i * self.last
+        return self.out, self.keep2[i]
 
     def copy(self, n):
         core, x, y = self.to
         half, eighth, last, out, land = self.half, self.eighth, self.last, self.out, self.land
-        landing = (0, half, half + eighth, half + 2 * eighth, half + 2 * eighth + last)
         mine = self.mine
-        source, start, size, target = (
-            (self.own, self.other, half, core),
-            (land, self.give1[0] - mine, eighth, x), (land, self.give1[1] - mine, eighth, y),
-            (land, self.give2[0] - mine, last, y), (land, self.give2[1] - mine, last, x),
-            (out, self.keep2[0], last, y), (out, self.keep2[1], last, x),
-            (out, self.keep1[0], eighth, x), (out, self.keep1[1], eighth, y),
-            (out, mine, self.quarter, core),
-            (out, mine + self.quarter, self.quarter, core),
-        )[n]
-        src = self.place(source, start, size)
-        dst = land.at[pl.ds(landing[n], size)] if n < 5 else src
+        if n < 5:
+            source, start, size, target = (
+                (self.own, self.other, half, core),
+                (land, self.give1[0] - mine, eighth, x), (land, self.give1[1] - mine, eighth, y),
+                (land, self.give2[0] - mine, last, y), (land, self.give2[1] - mine, last, x),
+            )[n]
+            landing = (0, half, half + eighth, half + 2 * eighth, half + 2 * eighth + last)[n]
+            src, dst = self.place(source, start, size), self.place(land, landing, size)
+        else:
+            start, size, target = (
+                (self.keep2[0], last, y), (self.keep2[1], last, x),
+                (self.keep1[0], eighth, x), (self.keep1[1], eighth, y),
+                (mine, self.quarter, core), (mine + self.quarter, self.quarter, core),
+            )[n - 5]
+            dst = self.place(out, start, size)
+            src = self.place(*self.final(n - 5), size) if n < 7 else dst
         return pltpu.make_async_remote_copy(
             src_ref=src, dst_ref=dst, send_sem=self.send.at[n], recv_sem=self.recv.at[n],
             device_id={"ctx": self.me + target}, device_id_type=MESH,
@@ -333,54 +341,71 @@
             step = step // 2
 
         def part(i, carry):
-            rows = lambda begin: pl.ds(pl.multiple_of(begin + i * step, 16), step)
+            def rows(begin):
+                return pl.ds(pl.multiple_of(begin + i * step, 16), step)
+
             total = source[rows(at), :].astype(F32) + self.land[rows(landed), :].astype(F32)
             target[rows(to), :] = total.astype(BF16)
             return carry
 
         lax.fori_loop(0, size // step, part, 0)
 
-    def step(self, k):
+    def begin(self):
+        self.copy(0).start()
+
+    def reduce(self, k):
         half, eighth, last, land, mine = self.half, self.eighth, self.last, self.land, self.mine
+        i = k % 2
         if k == 0:
-            self.copy(0).start()
-        if k == 1:
             self.copy(0).wait_recv()
-            for i in range(2):
-                at = self.give1[i]
-                self.add(land, at - mine, self.own, at, at - mine, eighth)
-                self.copy(1 + i).start()
-            for i in range(2):
-                at = self.keep1[i]
-                self.add(land, at - mine, self.own, at, at - mine, eighth)
-        if k == 2:
-            for i in range(2):
-                self.copy(1 + i).wait_recv()
-                landed = half + i * eighth - self.keep1[i]
-                at = self.give2[i]
-                self.add(land, at - mine, land, at - mine, landed + at, last)
-                self.copy(3 + i).start()
-                at = self.keep2[i]
-                self.add(land, at - mine, land, at - mine, landed + at, last)
-        if k == 3:
-            for i in range(2):
-                self.copy(3 + i).wait_recv()
-                at = self.keep2[i]
-                self.add(self.out, at, land, at - mine, half + 2 * eighth + i * last, last)
+        if k < 2:
+            at = self.give1[i]
+            self.add(land, at - mine, self.own, at, at - mine, eighth)
+            self.copy(1 + i).start()
+        elif k < 4:
+            at = self.keep1[i]
+            self.add(land, at - mine, self.own, at, at - mine, eighth)
+        elif k < 6:
+            self.copy(1 + i).wait_recv()
+            landed = half + i * eighth - self.keep1[i]
+            at = self.give2[i]
+            self.add(land, at - mine, land, at - mine, landed + at, last)
+            self.copy(3 + i).start()
+            at = self.keep2[i]
+            self.add(land, at - mine, land, at - mine, landed + at, last)
+        else:
+            self.copy(3 + i).wait_recv()
+            target, to = self.final(i)
+            at = self.keep2[i]
+            self.add(target, to, land, at - mine, half + 2 * eighth + i * last, last)
+
+    def keep(self, i):
+        return pltpu.make_async_copy(
+            self.place(self.shard, i * self.last, self.last),
+            self.place(self.out, self.keep2[i], self.last),
+            self.local.at[i],
+        )
+
+    def gather(self, k):
+        for i in range(2):
+            if k == 0:
                 self.copy(5 + i).start()
-        if k == 4:
-            for i in range(2):
+                if self.shard is not None:
+                    self.keep(i).start()
+            if k == 1:
                 self.copy(5 + i).wait_recv()
+                if self.shard is not None:
+                    self.keep(i).wait()
                 self.copy(7 + i).start()
-        if k == 5:
-            for i in range(2):
+            if k == 2:
                 self.copy(7 + i).wait_recv()
                 self.copy(9 + i).start()
-        if k == 6:
-            for i in range(2):
+            if k == 3:
                 self.copy(9 + i).wait_recv()
-            for n in range(SUM_SENDS):
-                self.copy(n).wait_send()
+
+    def finish(self):
+        for n in range(0 if self.own is not None else 5, SUM_SENDS if self.out is not None else 5):
+            self.copy(n).wait_send()
 
     def signal(self, barrier):
         for target in self.to:
@@ -1011,7 +1036,7 @@
 
 def weave(summed, block):
     width, both = summed.shape
-    rows = 512
+    rows = 256
     return pl.pallas_call(
         functools.partial(weave_kernel, block),
         grid=(width // rows,),
@@ -1043,8 +1068,10 @@
     )(summed)
 
 
-def line_barrier(at, n):
+def line_barrier(at, n, cube=None):
     barrier = pltpu.get_barrier_semaphore()
+    if cube is not None:
+        cube.signal(barrier)
 
     @pl.when(at > 0)
     def _():
@@ -1054,10 +1081,11 @@
     def _():
         pl.semaphore_signal(barrier, inc=1, device_id={"tp": at + 1}, device_id_type=MESH)
 
-    pl.semaphore_wait(barrier, jnp.where((at > 0) & (at < n - 1), 2, 1))
-
-
-def sum_rows(n, sub, part_ref, out_ref, row_fn, from_left, from_right, send, recv):
+    near = jnp.where((at > 0) & (at < n - 1), 2, 1)
+    pl.semaphore_wait(barrier, near + (0 if cube is None else 3))
+
+
+def sum_rows(n, sub, part_ref, out_ref, row_fn, from_left, from_right, send, recv, aside={}):
     at = lax.axis_index("tp")
     chunks = part_ref.shape[0] // sub
     middle = (n // 2 - 1, n // 2)
@@ -1140,6 +1168,8 @@
             first(False, c).start()
 
     for c in range(chunks + 4):
+        for piece in aside.get(c, ()):
+            piece()
         if c < chunks:
             reduce_step(c)
         if 2 <= c < chunks + 2:
@@ -1206,37 +1236,55 @@
     )(part, tok_full)
 
 
-def norm_back_kernel(
-    n, sub, part_ref, cot_ref, resid_ref, stat_ref, out_ref, from_left, from_right, send, recv
-):
-    line_barrier(lax.axis_index("tp"), n)
-
-    def row_fn(total, rows):
+def norm_back_kernel(n, sub, cube, part_ref, cot_ref, resid_ref, stat_ref, *refs):
+    total = None
+    if cube:
+        own_ref, out_ref, shard_ref, from_left, from_right, send, recv, land, csend, crecv = refs
+        total = CubeSum(own_ref.shape[0], csend, crecv, own=own_ref, land=land, shard=shard_ref)
+    else:
+        out_ref, from_left, from_right, send, recv = refs
+    line_barrier(lax.axis_index("tp"), n, total)
+    aside = {}
+    if cube:
+        total.begin()
+        for k, c in enumerate((7, 8, 9, 10, 19, 20)):
+            aside[c] = (functools.partial(total.reduce, k),)
+
+    def row_fn(summed, rows):
         inverse = stat_ref[rows, 1:2]
         normed = (resid_ref[rows, :] - stat_ref[rows, 0:1]) * inverse
-        mean = jnp.mean(total, axis=1, keepdims=True)
-        inner = jnp.mean(total * normed, axis=1, keepdims=True)
-        out = cot_ref[rows, :].astype(F32) + inverse * (total - mean - normed * inner)
+        mean = jnp.mean(summed, axis=1, keepdims=True)
+        inner = jnp.mean(summed * normed, axis=1, keepdims=True)
+        out = cot_ref[rows, :].astype(F32) + inverse * (summed - mean - normed * inner)
         out_ref[rows, :] = out.astype(BF16)
 
-    sum_rows(n, sub, part_ref, out_ref, row_fn, from_left, from_right, send, recv)
-
-
-def norm_back(part, cot, resid, stat, n):
+    sum_rows(n, sub, part_ref, out_ref, row_fn, from_left, from_right, send, recv, aside)
+    if cube:
+        total.reduce(6)
+        total.reduce(7)
+        total.finish()
+
+
+def norm_back(part, cot, resid, stat, n, grads):
     rows, width = part.shape
     sub = 32
     vmem = pl.BlockSpec(memory_space=pltpu.VMEM)
+    extra = []
+    for grad in grads:
+        extra += sum_scratch(grad.shape)
     return pl.pallas_call(
-        functools.partial(norm_back_kernel, n, sub),
-        in_specs=[vmem] * 4,
-        out_specs=vmem,
-        out_shape=jax.ShapeDtypeStruct((rows, width), BF16),
+        functools.partial(norm_back_kernel, n, sub, len(grads) > 0),
+        in_specs=[vmem] * (4 + len(grads)),
+        out_specs=[vmem] * (1 + len(grads)),
+        out_shape=[jax.ShapeDtypeStruct((rows, width), BF16)]
+        + [jax.ShapeDtypeStruct((grad.shape[0] // 8, grad.shape[1]), BF16) for grad in grads],
         scratch_shapes=[pltpu.VMEM((rows, width), BF16)] * 2
-        + [pltpu.SemaphoreType.DMA((4, rows // sub))] * 2,
+        + [pltpu.SemaphoreType.DMA((4, rows // sub))] * 2
+        + extra,
         compiler_params=params(56, collective_id=1, has_side_effects=True),
         cost_estimate=cost(1e6, 1e6),
         name="norm_back",
-    )(part, cot, resid, stat)
+    )(part, cot, resid, stat, *grads)
 
 
 def unrotate_kernel(
@@ -1292,17 +1340,31 @@
 
 
 def unproject_kernel(heads, n, cube, dproj_ref, tok_ref, stat_ref, w_ref, branch_ref, *refs):
-    sums = []
+    sums, rest = [], None
     if cube:
-        in_ref, og_ref, out_ref, in_out, og_out = refs[:5]
-        part_ref, mine_ref, land_ref, sums_ref, far_ref, send, recv, ssend, srecv = refs[5:14]
-        sums = [CubeSum(in_ref, in_out, *refs[14:17]), CubeSum(og_ref, og_out, *refs[17:20])]
+        in_ref, og_ref, shard_ref, out_ref, in_out, og_out, down_out = refs[:7]
+        part_ref, mine_ref, land_ref, sums_ref, far_ref, send, recv, ssend, srecv = refs[7:16]
+        for own, out, at in ((in_ref, in_out, 16), (og_ref, og_out, 19)):
+            land, csend, crecv = refs[at : at + 3]
+            sums.append(CubeSum(own.shape[0], csend, crecv, own=own, land=land, out=out))
+        rest = CubeSum(
+            down_out.shape[0], refs[22], refs[23], out=down_out, shard=shard_ref, local=refs[24]
+        )
     else:
         out_ref, part_ref, mine_ref, land_ref, sums_ref, far_ref, send, recv, ssend, srecv = refs
 
-    def advance(k):
+    def reduce(*pieces):
+        for k in pieces:
+            for item in sums:
+                item.reduce(k)
+
+    def gather(k):
         for item in sums:
-            item.step(k)
+            item.gather(k)
+
+    def rest_gather(k):
+        if rest is not None:
+            rest.gather(k)
 
     rows, width = tok_ref.shape
     shard = width // n
@@ -1316,7 +1378,9 @@
     if cube:
         sums[0].signal(barrier)
     pl.semaphore_wait(barrier, n - 1 + (3 if cube else 0))
-    advance(0)
+    for item in sums:
+        item.begin()
+    rest_gather(0)
     block = 256
     count = rows // block
 
@@ -1358,14 +1422,19 @@
         sums_ref[:, i * block : (i + 1) * block] = both.T[:8]
     for o in range(1, n):
         totals(o).start()
-    for k in range(1, 5):
-        advance(k)
+    reduce(0, 1, 2, 3)
+    rest_gather(1)
+    reduce(4, 5)
+    rest_gather(2)
+    reduce(6, 7)
+    gather(0)
+    gather(1)
     total = sums_ref[...]
     for o in range(1, n):
         totals(o).wait_recv()
         total = total + far_ref[o - 1]
     mine_ref[...] = total
-    advance(5)
+    gather(2)
     for i in range(count):
         place = pl.ds(i * block, block)
         spread = jnp.concatenate(
@@ -1380,26 +1449,32 @@
         out_ref[place, :] = branch_ref[place, own].astype(F32) + inverse * (
             total - spread[:, 0:1] - normed * spread[:, 1:2]
         )
-    advance(6)
+    rest_gather(3)
+    gather(3)
+    for item in sums + ([rest] if cube else []):
+        item.finish()
     for o in range(1, n):
         totals(o).wait_send()
         for i in range(count):
             term(o, i).wait_send()
 
 
-def unproject(dproj, tok_full, stat, weight, branch, heads, n, grads):
+def unproject(dproj, tok_full, stat, weight, branch, heads, n, grads, shards):
     rows, width = tok_full.shape
     shard = width // n
     vmem = pl.BlockSpec(memory_space=pltpu.VMEM)
     extra = []
     for grad in grads:
         extra += sum_scratch(grad.shape)
-    result = pl.pallas_call(
+    for _ in shards:
+        extra += [pltpu.SemaphoreType.DMA((SUM_SENDS,))] * 2 + [pltpu.SemaphoreType.DMA((2,))]
+    return pl.pallas_call(
         functools.partial(unproject_kernel, heads, n, len(grads) > 0),
-        in_specs=[vmem] * (5 + len(grads)),
-        out_specs=[vmem] * (1 + len(grads)),
+        in_specs=[vmem] * (5 + len(grads) + len(shards)),
+        out_specs=[vmem] * (1 + len(grads)) + [pl.BlockSpec(memory_space=pl.ANY)] * len(shards),
         out_shape=[jax.ShapeDtypeStruct((rows, shard), F32)]
-        + [jax.ShapeDtypeStruct(grad.shape, BF16) for grad in grads],
+        + [jax.ShapeDtypeStruct(grad.shape, BF16) for grad in grads]
+        + [jax.ShapeDtypeStruct((8 * piece.shape[0], piece.shape[1]), BF16) for piece in shards],
         scratch_shapes=[
             pltpu.VMEM((rows, width), BF16),
             pltpu.VMEM((8, rows), F32),
@@ -1415,8 +1490,7 @@
         compiler_params=params(60, collective_id=4, has_side_effects=True),
         cost_estimate=cost(1e6, 1e6),
         name="unproject",
-    )(dproj, tok_full, stat, weight, branch, *grads)
-    return result
+    )(dproj, tok_full, stat, weight, branch, *grads, *shards)
 
 
 def per_device(tokens, segment_ids, in_weight, out_weight, gate_up_weight, down_weight, cotangent):
@@ -1480,10 +1554,14 @@
     down_grad, gu_grad, all_query, grad_gu, hidden = lax.optimization_barrier(
         (down_grad, gu_grad, all_query, grad_gu, hidden)
     )
-    down_grad, gu_grad = lax.optimization_barrier(lax.psum((down_grad, gu_grad), "ctx"))
+    if not cube:
+        down_grad = lax.psum(down_grad, "ctx")
+    gu_grad = lax.optimization_barrier(lax.psum(gu_grad, "ctx"))
 
     grad_part = lax.dot_general(grad_gu, gu_w, NT, preferred_element_type=F32).astype(BF16)
-    branch_grad = norm_back(grad_part, cot_full, resid1, stat2, tp_size)
+    branch_grad, *shards = norm_back(
+        grad_part, cot_full, resid1, stat2, tp_size, [down_grad] if cube else []
+    )
     out_grad = lax.dot_general(mixed, branch_grad, TN, preferred_element_type=F32).astype(BF16)
     grad_mixed, delta = mixed_grad(branch_grad, out_weight, raw, lse, heads)
     branch = (resid1 + jnp.dot(hidden, down_weight, preferred_element_type=F32)).astype(BF16)
@@ -1500,9 +1578,9 @@
 
     dproj, in_grad = unrotate(dq, dk, dv, cosine, sine, inner1, heads)
     if cube:
-        tokens_grad, in_grad, out_grad = unproject(
+        tokens_grad, in_grad, out_grad, down_grad = unproject(
             dproj, tok_full, stat1, in_w, branch_grad, heads, tp_size,
-            [in_grad, out_grad],
+            [in_grad, out_grad], shards,
         )
     else:
         in_grad, out_grad, down_grad, gu_grad = lax.optimization_barrier(
@@ -1510,7 +1588,7 @@
         )
         in_grad, out_grad = lax.psum((in_grad, out_grad), "ctx")
         (tokens_grad,) = unproject(
-            dproj, tok_full, stat1, in_w, branch_grad, heads, tp_size, []
+            dproj, tok_full, stat1, in_w, branch_grad, heads, tp_size, [], []
         )
     return (
         layer_out,

time: 767 us -> 755 us (0.984)
  Pallas kernels: 632 us -> 621 us
    pallas_call x1, Pallas kernels: 87.3 us -> 114 us  [norm_back(): pl.pallas_call(functools.partial(norm_back_kernel, n, sub, len(grads) > 0...]
    pallas_call x1, Pallas kernels: 161 us -> 135 us  [unproject(): pl.pallas_call(functools.partial(unproject_kernel, heads, n, len(grads) >...]
    pallas_call x1, Pallas kernels: 92.9 us -> 80.4 us  [attend_back_far(): pl.pallas_call(functools.partial(attend_back_far_kernel, heads, n), in_sp...]
  transfers between devices with their start and end apart: 3 -> 3, of which waited for: 1 -> 1; matrix products, arithmetic and copies ran while one was open for 9% -> 10% of each run, Pallas kernels for 67% -> 68%
where the time goes in v6:
time: 755 us; the launch traced here: 746 us
  Pallas kernels  621 us (82%)
  matrix products  34.9 us (5%)
  local copies, waits for them, and re-layouts  31.4 us (4%)
  waiting for transfers between devices  26 us (3%)
  between operations  14 us (2%)
  blocking collectives  10.5 us (1%)
    pallas_call x1, Pallas kernels, unproject(): pl.pallas_call(functools.partial(unproject_kernel, heads, n, len(grads) >...  135 us
    pallas_call x1, Pallas kernels, norm_back(): pl.pallas_call(functools.partial(norm_back_kernel, n, sub, len(grads) > 0...  114 us
    pallas_call x1, Pallas kernels, merge(): pl.pallas_call(functools.partial(merge_kernel, n, sub), in_specs=[vmem] *...  89.9 us
    pallas_call x1, Pallas kernels, attend_back_far(): pl.pallas_call(functools.partial(attend_back_far_kernel, heads, n), in_sp...  80.4 us
    pallas_call x1, Pallas kernels, attend_far(): pl.pallas_call(functools.partial(attend_far_kernel, heads, n), in_specs=[...  79.6 us
    pallas_call x1, Pallas kernels, feed(): pl.pallas_call(feed_kernel, grid=(units // block,), in_specs=[whole, whol...  47.1 us
    reshape x1, local copies, waits for them, and re-layouts, per_device(): gu_w = gu_w.reshape(width, 2 * hidden_local)  27.8 us
    all_gather x1, waiting for transfers between devices, gather(): return lax.all_gather(local, 'tp', axis=axis, tiled=True)  25.3 us
  transfers between devices with their start and end apart: 3, of which 1 were waited for; matrix products, arithmetic and copies ran while one was open for 10% of the time, Pallas kernels for 68%

profile of v6, /device:TPU:0, one launch (start us, length us, event | category | flops | bytes accessed | tf_op | source)
XLA Modules:
  0.0 745.6 jit_solution(3757387646367015838)
XLA Ops:
  7.2 0.7 all-gather.4.cloned.1.call-update
  8.0 0.7 reshape.60
  8.6 10.5 %all-gather = s32[8,1,768]{2,1,0:T(1,128)S(1)} all-gather(s32[1,1,768]{2,1,0:T(1,128)S(1)} %reshape.60), channel_id=1, replica_groups=mesh['ctx'=8,'tp'=4] {'ctx'}, dimensions={0}, use_global_device_ids=true | all-gather | bytes 27648 | tf_op jit(solution)/shard_map/all_gather | solution.py:1517
  19.1 0.1 slice_compare_fusion
  19.2 0.1 add_select_fusion
  19.3 0.3 reduce-window.9
  19.7 0.1 slice_reduce_fusion
  19.8 0.1 reshape.57
  19.9 0.1 copy.18
  20.0 27.8 %reshape.55.w_ref = bf16[2048,4096]{1,0:T(8,128)(2,1)} reshape(bf16[2048,8,2,256]{3,2,1,0:T(2,128)(2,1)} %bitcast.20) | data formatting | bytes 33554432 | tf_op jit(solution)/shard_map/reshape | solution.py:1515
  47.8 1.4 fusion
  49.2 1.2 pad_maximum_fusion
  50.5 25.3 %all-gather.4.cloned.1.call-done.tok_ref = bf16[768,2048]{1,0:T(8,128)(2,1)} async-done(((bf16[768,512]{1,0:T(8,128)(2,1)}), bf16[768,2048]{1,0:T(8,128)(2,1)}) %all-gather.4.cloned.1.call-update) | async-done | bytes 3145744 | tf_op jit(solution)/shard_map/all_gather | solution.py:1507
  75.8 0.6 constant_dynamic-slice_fusion.begin_ref
  76.3 11.2 %project.1 = (bf16[768,2048]{1,0:T(8,128)(2,1)}, f32[768,2]{1,0:T(8,128)}, bf16[768,512]{1,0:T(8,128)(2,1)}, bf16[768,1024]{1,0:T(8,128)(2,1)}) custom-call(bf16[768,2048]{1,0:T(8,128)(2,1)} %all-gather.4.cloned.1.call-done.tok_ref, bf16[3,2048,512]{2,1,0:T(8,128)(2,1)} %bitcast.22, f32[768,128]{1,0:T(8,128)} %get-tuple-element.89.cos_ref, ...), custom_call_target="tpu_custom_call" | custom-call | flops 4831838208 | bytes 15728640 | tf_op jit(solution)/shard_map/project/pallas_call | solution.py:70
  87.6 79.6 %attend_far.1 = (f32[768,512]{1,0:T(8,128)}, bf16[768,512]{1,0:T(8,128)(2,1)}, f32[4,768]{1,0:T(4,128)}, bf16[6144,1024]{1,0:T(8,128)(2,1)}, bf16[768,2048]{1,0:T(8,128)(2,1)}, /*index=5*/bf16[768,2048]{1,0:T(8,128)(2,1)}) custom-call(bf16[768,512]{1,0:T(8,128)(2,1)} %get-tuple-element.57.q_ref, bf16[768,1024]{1,0:T(8,128)(2,1)} %get-tuple-element.48.own_ref, ...), custom_call_target="tpu_custom_call" | custom-call | flops 1000000 | bytes 1000000 | tf_op jit(solution)/shard_map/attend_far/pallas_call | solution.py:566
  167.3 89.9 %merge.1 = (bf16[768,2048]{1,0:T(8,128)(2,1)}, f32[768,2048]{1,0:T(8,128)}, f32[768,2]{1,0:T(8,128)}) custom-call(bf16[768,2048]{1,0:T(8,128)(2,1)} %get-tuple-element.50.part_ref, bf16[768,2048]{1,0:T(8,128)(2,1)} %all-gather.4.cloned.1.call-done.tok_ref), custom_call_target="tpu_custom_call" | custom-call | flops 1000000 | bytes 1000000 | tf_op jit(solution)/shard_map/merge/pallas_call | solution.py:1222
  257.2 47.1 %feed.1 = (bf16[768,2048]{1,0:T(8,128)(2,1)}, bf16[768,4096]{1,0:T(8,128)(2,1)}, bf16[2048,2048]{1,0:T(8,128)(2,1)}, bf16[2048,4096]{1,0:T(8,128)(2,1)}) custom-call(bf16[768,2048]{1,0:T(8,128)(2,1)} %get-tuple-element.51.inner_ref, bf16[768,2048]{1,0:T(8,128)(2,1)} %get-tuple-element.52.cot_ref, bf16[2048,4096]{1,0:T(8,128)(2,1)} %reshape.55.w_ref, ...), custom_call_target="tpu_custom_call" | custom-call | flops 38654705664 | bytes 56623104 | tf_op jit(solution)/shard_map/feed/pallas_call | solution.py:1011
  304.4 19.8 %convolution_convert_fusion.part_ref = bf16[768,2048]{1,0:T(8,128)(2,1)} fusion(bf16[768,4096]{1,0:T(8,128)(2,1)} %get-tuple-element.60, bf16[2048,4096]{1,0:T(8,128)(2,1)} %reshape.55.w_ref), kind=kOutput, calls=%fused_computation.1 | convolution fusion | flops 12886474752 | bytes 26214400 | tf_op jit(solution)/shard_map/dot_general | solution.py:1561
  324.2 113.8 %norm_back.1 = (bf16[768,2048]{1,0:T(8,128)(2,1)}, bf16[256,2048]{1,0:T(8,128)(2,1)}) custom-call(bf16[768,2048]{1,0:T(8,128)(2,1)} %convolution_convert_fusion.part_ref, bf16[768,2048]{1,0:T(8,128)(2,1)} %get-tuple-element.52.cot_ref, f32[768,2048]{1,0:T(8,128)} %get-tuple-element.61.resid_ref, f32[768,2]{1,0:T(8,128)} %get-tuple-element.62.stat_ref, ...), custom_call_target="tpu_custom_call" | custom-call | flops 1000000 | bytes 1000000 | tf_op jit(solution)/shard_map/norm_back/pallas_call | solution.py:1275
  438.0 6.6 mixed_grad.1
  444.6 12.0 %add_convert_fusion.part_ref = bf16[768,2048]{1,0:T(8,128)(2,1)} fusion(f32[768,2048]{1,0:T(8,128)S(1)} %bitcast.25, bf16[768,2048]{1,0:T(8,128)(2,1)} %get-tuple-element.70, bf16[2048,2048]{1,0:T(8,128)(2,1)} %down_ref.1), kind=kOutput, calls=%fused_computation | convolution fusion | flops 6445596672 | bytes 20971520 | tf_op jit(solution)/shard_map/dot_general | solution.py:1567
  456.6 80.4 %attend_back_far.1 = (f32[768,512]{1,0:T(8,128)}, f32[768,512]{1,0:T(8,128)}, f32[768,512]{1,0:T(8,128)}, bf16[768,512]{1,0:T(8,128)(2,1)}) custom-call(bf16[768,640]{1,0:T(8,128)(2,1)} %get-tuple-element.67.g_ref, bf16[6144,512]{1,0:T(8,128)(2,1)} %all-gather.6.cloned.1.call-done.far_q_ref, bf16[6144,1024]{1,0:T(8,128)(2,1)} %get-tuple-element.69.far_pair_ref, ...), custom_call_target="tpu_custom_call" | custom-call | flops 1000000 | bytes 1000000 | tf_op jit(solution)/shard_map/attend_back_far/pallas_call | solution.py:744
  537.0 12.4 %unrotate.1 = (bf16[768,1536]{1,0:T(8,128)(2,1)}, bf16[6144,512]{1,0:T(8,128)(2,1)}) custom-call(f32[768,512]{1,0:T(8,128)} %get-tuple-element.72.dq_ref, f32[768,512]{1,0:T(8,128)} %get-tuple-element.73.dk_ref, f32[768,512]{1,0:T(8,128)} %get-tuple-element.74.dv_ref, f32[768,128]{1,0:T(8,128)} %get-tuple-element.89.cos_ref, ...), custom_call_target="tpu_custom_call" | custom-call | flops 4831838208 | bytes 11010048 | tf_op jit(solution)/shard_map/unrotate/pallas_call | solution.py:1324
  549.4 3.1 convolution_convert_fusion.1.refs_1_
  552.6 135.3 %unproject.1 = (f32[768,512]{1,0:T(8,128)}, bf16[6144,512]{1,0:T(8,128)(2,1)}, bf16[512,2048]{1,0:T(8,128)(2,1)}, bf16[2048,2048]{1,0:T(8,128)(2,1)}) custom-call(bf16[768,1536]{1,0:T(8,128)(2,1)} %get-tuple-element.76.dproj_ref, bf16[768,2048]{1,0:T(8,128)(2,1)} %all-gather.4.cloned.1.call-done.tok_ref, f32[768,2]{1,0:T(8,128)} %get-tuple-element.77.stat_ref, ...), custom_call_target="tpu_custom_call" | custom-call | flops 1000000 | bytes 1000000 | tf_op jit(solution)/shard_map/unproject/pallas_call | solution.py:1471
  687.9 4.1 convert_element_type.23
  692.0 10.3 %widen.2 = f32[6144,512]{1,0:T(8,128)} custom-call(bf16[6144,512]{1,0:T(8,128)(2,1)} %get-tuple-element.82.in_ref), custom_call_target="tpu_custom_call" | custom-call | flops 3145728 | bytes 18874368 | tf_op jit(solution)/shard_map/widen/pallas_call | solution.py:1059
  702.4 9.5 %widen.3 = f32[2048,2048]{1,0:T(8,128)} custom-call(bf16[2048,2048]{1,0:T(8,128)(2,1)} %get-tuple-element.85.in_ref), custom_call_target="tpu_custom_call" | custom-call | flops 4194304 | bytes 25165824 | tf_op jit(solution)/shard_map/widen/pallas_call | solution.py:1059
  711.9 25.0 %weave.1 = f32[2048,2,2048]{2,1,0:T(2,128)} custom-call(bf16[2048,4096]{1,0:T(8,128)(2,1)} %all-reduce.2.cloned.1.call-done.sum_ref), custom_call_target="tpu_custom_call" | custom-call | flops 8388608 | bytes 50331648 | tf_op jit(solution)/shard_map/weave/pallas_call | solution.py:1040
  736.9 0.9 copy.22
  737.8 1.1 copy.23
  (28 shorter events, 0.4 us)
Async XLA Ops:
  7.2 68.6 %all-gather.4.cloned.1.call-start = ((), (), s32[]{:S(2)}) async-start(), calls=%async_computation | async-start | bytes 3932160 | tf_op jit(solution)/shard_map/all_gather | solution.py:1507
  7.9 296.4 %all-gather.6.cloned.1.call-start = ((), (), s32[]{:S(2)}) async-start(), calls=%async_computation.1 | async-start | bytes 7077888 | tf_op jit(solution)/shard_map/all_gather | solution.py:1550
  50.5 37.1 %copy-start.4 = (s32[8,768]{1,0:T(8,128)}, s32[8,768]{1,0:T(8,128)S(1)}, u32[]{:S(2)}) copy-start(s32[8,768]{1,0:T(8,128)S(1)} %bitcast_maximum_fusion.begin_ref) | copy-start | bytes 73732
  167.2 544.7 %all-reduce.2.cloned.1.call-start = ((), (), s32[]{:S(2)}) async-start(), calls=%async_computation.2 | async-start | bytes 33554432 | tf_op jit(solution)/shard_map/psum | solution.py:1559
  324.2 120.5 %slice-start = ((s8[6291456]{0:T(1024)(128)(4,1)}), s8[4194304]{0:T(1024)(128)(4,1)S(1)}, s32[]{:S(2)}) async-start(s8[6291456]{0:T(1024)(128)(4,1)} %bitcast.24), calls=%async_computation.3 | async-start | bytes 8388608
  324.2 120.5 %slice-start.1 = ((s8[6291456]{0:T(1024)(128)(4,1)}), s8[2097152]{0:T(1024)(128)(4,1)S(1)}, s32[]{:S(2)}) async-start(s8[6291456]{0:T(1024)(128)(4,1)} %bitcast.24), calls=%async_computation.4 | async-start | bytes 4194304
  537.0 12.4 %copy-start = (bf16[768,2048]{1,0:T(8,128)(2,1)S(1)}, bf16[768,2048]{1,0:T(8,128)(2,1)}, u32[]{:S(2)}) copy-start(bf16[768,2048]{1,0:T(8,128)(2,1)} %get-tuple-element.64.branch_ref) | copy-start | bytes 9437188
  537.0 12.4 %copy-start.3 = (bf16[768,512]{1,0:T(8,128)(2,1)S(1)}, bf16[768,512]{1,0:T(8,128)(2,1)}, u32[]{:S(2)}) copy-start(bf16[768,512]{1,0:T(8,128)(2,1)} %get-tuple-element.79) | copy-start | bytes 2359300
  711.9 25.0 %copy-start.2 = (bf16[768,512]{1,0:T(8,128)(2,1)S(1)}, bf16[768,512]{1,0:T(8,128)(2,1)}, u32[]{:S(2)}) copy-start(bf16[768,512]{1,0:T(8,128)(2,1)} %get-tuple-element.97) | copy-start | bytes 2359300
  711.9 25.9 %copy-start.1 = (f32[768,512]{1,0:T(8,128)S(1)}, f32[768,512]{1,0:T(8,128)}, u32[]{:S(2)}) copy-start(f32[768,512]{1,0:T(8,128)} %get-tuple-element.98) | copy-start | bytes 4718596
Sparse Core Ops, SparseCore 0:
  9.6 66.1 all-gather.3
  167.3 53.3 all-gather.5
  304.5 286.9 all-reduce.1

commit v7 on v6

--- a/solution.py
+++ b/solution.py
@@ -18,7 +18,7 @@
 NT = (((1,), (1,)), ((), ()))
 TN = (((0,), (0,)), ((), ()))
 MESH = pl.DeviceIdType.MESH
-BLOCK = 256
+BLOCK = 512
 
 
 def params(mib, **more):
@@ -282,54 +282,41 @@
             self.copy(n).wait_send()
 
 
-SUM_SENDS = 11
+SUM_SENDS = 9
 
 
 class CubeSum:
-    def __init__(self, rows, send, recv, own=None, land=None, out=None, shard=None, local=None):
+    def __init__(self, own, land, send, recv, out=None, mid=None):
         me = lax.axis_index("ctx")
         core, x, y = me % 2, (me // 2) % 2, me // 4
-        self.me, self.own, self.out, self.land = me, own, out, land
-        self.send, self.recv, self.shard, self.local = send, recv, shard, local
-        self.half, self.quarter = rows // 2, rows // 4
-        self.eighth, self.last = rows // 8, rows // 16
-        mine = core * self.half
-        first, second = mine, mine + self.quarter
+        self.me, self.own, self.out, self.land, self.mid = me, own, out, land, mid
+        self.send, self.recv = send, recv
+        rows = own.shape[0]
+        self.half, self.eighth, self.last = rows // 2, rows // 8, rows // 16
+        second = rows // 4
         self.to = (1 - 2 * core, 2 - 4 * x, 4 - 8 * y)
-        self.mine, self.other = mine, (1 - core) * self.half
-        self.keep1 = (first + x * self.eighth, second + y * self.eighth)
-        self.give1 = (first + (1 - x) * self.eighth, second + (1 - y) * self.eighth)
+        self.mine, self.other = core * self.half, (1 - core) * self.half
+        self.keep1 = (x * self.eighth, second + y * self.eighth)
+        self.give1 = ((1 - x) * self.eighth, second + (1 - y) * self.eighth)
         self.keep2 = (self.keep1[0] + y * self.last, self.keep1[1] + x * self.last)
         self.give2 = (self.keep1[0] + (1 - y) * self.last, self.keep1[1] + (1 - x) * self.last)
-
-    def place(self, ref, start, size):
-        return ref.at[pl.ds(start if isinstance(start, int) else pl.multiple_of(start, 16), size)]
-
-    def final(self, i):
-        if self.shard is not None:
-            return self.shard, i * self.last
-        return self.out, self.keep2[i]
 
     def copy(self, n):
         core, x, y = self.to
         half, eighth, last, out, land = self.half, self.eighth, self.last, self.out, self.land
-        mine = self.mine
+        source, start, size, target = (
+            (self.own, self.other, half, core),
+            (land, self.give1[0], eighth, x), (land, self.give1[1], eighth, y),
+            (land, self.give2[0], last, y), (land, self.give2[1], last, x),
+            (out, self.keep2[0], last, y), (out, self.keep2[1], last, x),
+            (out, self.keep1[0], eighth, x), (out, self.keep1[1], eighth, y),
+        )[n]
+        src = source.at[pl.ds(pl.multiple_of(start, 16), size)]
         if n < 5:
-            source, start, size, target = (
-                (self.own, self.other, half, core),
-                (land, self.give1[0] - mine, eighth, x), (land, self.give1[1] - mine, eighth, y),
-                (land, self.give2[0] - mine, last, y), (land, self.give2[1] - mine, last, x),
-            )[n]
             landing = (0, half, half + eighth, half + 2 * eighth, half + 2 * eighth + last)[n]
-            src, dst = self.place(source, start, size), self.place(land, landing, size)
+            dst = land.at[pl.ds(landing, size)]
         else:
-            start, size, target = (
-                (self.keep2[0], last, y), (self.keep2[1], last, x),
-                (self.keep1[0], eighth, x), (self.keep1[1], eighth, y),
-                (mine, self.quarter, core), (mine + self.quarter, self.quarter, core),
-            )[n - 5]
-            dst = self.place(out, start, size)
-            src = self.place(*self.final(n - 5), size) if n < 7 else dst
+            dst = src
         return pltpu.make_async_remote_copy(
             src_ref=src, dst_ref=dst, send_sem=self.send.at[n], recv_sem=self.recv.at[n],
             device_id={"ctx": self.me + target}, device_id_type=MESH,
@@ -354,57 +341,46 @@
         self.copy(0).start()
 
     def reduce(self, k):
-        half, eighth, last, land, mine = self.half, self.eighth, self.last, self.land, self.mine
+        half, eighth, last, land = self.half, self.eighth, self.last, self.land
         i = k % 2
         if k == 0:
             self.copy(0).wait_recv()
         if k < 2:
             at = self.give1[i]
-            self.add(land, at - mine, self.own, at, at - mine, eighth)
+            self.add(land, at, self.own, self.mine + at, at, eighth)
             self.copy(1 + i).start()
         elif k < 4:
             at = self.keep1[i]
-            self.add(land, at - mine, self.own, at, at - mine, eighth)
+            self.add(land, at, self.own, self.mine + at, at, eighth)
         elif k < 6:
             self.copy(1 + i).wait_recv()
             landed = half + i * eighth - self.keep1[i]
+            if self.out is None:
+                at = self.keep1[i]
+                self.add(self.mid, i * eighth, land, at, landed + at, eighth)
+                return
             at = self.give2[i]
-            self.add(land, at - mine, land, at - mine, landed + at, last)
+            self.add(land, at, land, at, landed + at, last)
             self.copy(3 + i).start()
             at = self.keep2[i]
-            self.add(land, at - mine, land, at - mine, landed + at, last)
+            self.add(land, at, land, at, landed + at, last)
         else:
             self.copy(3 + i).wait_recv()
-            target, to = self.final(i)
             at = self.keep2[i]
-            self.add(target, to, land, at - mine, half + 2 * eighth + i * last, last)
-
-    def keep(self, i):
-        return pltpu.make_async_copy(
-            self.place(self.shard, i * self.last, self.last),
-            self.place(self.out, self.keep2[i], self.last),
-            self.local.at[i],
-        )
+            self.add(self.out, at, land, at, half + 2 * eighth + i * last, last)
 
     def gather(self, k):
         for i in range(2):
             if k == 0:
                 self.copy(5 + i).start()
-                if self.shard is not None:
-                    self.keep(i).start()
             if k == 1:
                 self.copy(5 + i).wait_recv()
-                if self.shard is not None:
-                    self.keep(i).wait()
                 self.copy(7 + i).start()
             if k == 2:
                 self.copy(7 + i).wait_recv()
-                self.copy(9 + i).start()
-            if k == 3:
-                self.copy(9 + i).wait_recv()
 
     def finish(self):
-        for n in range(0 if self.own is not None else 5, SUM_SENDS if self.out is not None else 5):
+        for n in range(3 if self.out is None else SUM_SENDS):
             self.copy(n).wait_send()
 
     def signal(self, barrier):
@@ -412,6 +388,87 @@
             pl.semaphore_signal(
                 barrier, inc=1, device_id={"ctx": self.me + target}, device_id_type=MESH
             )
+
+
+class MidSum:
+    def __init__(self, mid, land, out, send, recv):
+        me = lax.axis_index("ctx")
+        x, y = (me // 2) % 2, me // 4
+        self.me, self.mid, self.land, self.out, self.send, self.recv = me, mid, land, out, send, recv
+        self.eighth, self.last = mid.shape[0] // 2, mid.shape[0] // 4
+        self.bit = (y, x)
+        self.to = (4 - 8 * y, 2 - 4 * x)
+
+    def copy(self, n):
+        i = n % 2
+        keep = i * self.eighth + self.bit[i] * self.last
+        give = i * self.eighth + (1 - self.bit[i]) * self.last
+        if n < 2:
+            src = self.mid.at[pl.ds(pl.multiple_of(give, 16), self.last)]
+            dst = self.land.at[pl.ds(i * self.last, self.last)]
+        else:
+            src = dst = self.out.at[pl.ds(pl.multiple_of(keep, 16), self.last)]
+        return pltpu.make_async_remote_copy(
+            src_ref=src, dst_ref=dst, send_sem=self.send.at[n], recv_sem=self.recv.at[n],
+            device_id={"ctx": self.me + self.to[i]}, device_id_type=MESH,
+        )
+
+    def begin(self):
+        for i in range(2):
+            self.copy(i).start()
+
+    def turn(self):
+        for i in range(2):
+            self.copy(i).wait_recv()
+            keep = i * self.eighth + self.bit[i] * self.last
+            rows = pl.ds(pl.multiple_of(keep, 16), self.last)
+            landed = self.land[i * self.last : (i + 1) * self.last, :]
+            self.out[rows, :] = (
+                self.mid[rows, :].astype(F32) + landed.astype(F32)
+            ).astype(BF16)
+            self.copy(2 + i).start()
+
+    def finish(self):
+        for i in range(2):
+            self.copy(2 + i).wait_recv()
+        for n in range(4):
+            self.copy(n).wait_send()
+
+
+class LastGather:
+    def __init__(self, mid, out, send, recv, local):
+        me = lax.axis_index("ctx")
+        x, y = (me // 2) % 2, me // 4
+        self.me, self.mid, self.out = me, mid, out
+        self.send, self.recv, self.local = send, recv, local
+        self.eighth = mid.shape[0] // 2
+        self.start_at = (x * self.eighth, (2 + y) * self.eighth)
+        self.to = (2 - 4 * x, 4 - 8 * y)
+
+    def ends(self, i):
+        src = self.mid.at[pl.ds(i * self.eighth, self.eighth)]
+        return src, self.out.at[pl.ds(pl.multiple_of(self.start_at[i], 16), self.eighth)]
+
+    def copy(self, i):
+        src, dst = self.ends(i)
+        return pltpu.make_async_remote_copy(
+            src_ref=src, dst_ref=dst, send_sem=self.send.at[i], recv_sem=self.recv.at[i],
+            device_id={"ctx": self.me + self.to[i]}, device_id_type=MESH,
+        )
+
+    def keep(self, i):
+        src, dst = self.ends(i)
+        return pltpu.make_async_copy(src, dst, self.local.at[i])
+
+    def begin(self):
+        for i in range(2):
+            self.copy(i).start()
+            self.keep(i).start()
+
+    def finish(self):
+        for i in range(2):
+            self.copy(i).wait()
+            self.keep(i).wait()
 
 
 def sum_scratch(shape):
@@ -420,6 +477,42 @@
         pltpu.SemaphoreType.DMA((SUM_SENDS,)),
         pltpu.SemaphoreType.DMA((SUM_SENDS,)),
     ]
+
+
+def join_kernel(core_ref, own_ref, far_ref, out_ref):
+    @pl.when(pl.program_id(0) == 0)
+    def _():
+        out_ref[...] = own_ref[...].astype(F32)
+
+    @pl.when(pl.program_id(0) == 1)
+    def _():
+        out_ref[...] = far_ref[...].astype(F32)
+
+
+def join(core, own, far):
+    high, wide = own.shape
+    rows = high
+    while rows * wide > 1024 * 1024:
+        rows = rows // 2
+    count = high // rows
+    return pl.pallas_call(
+        join_kernel,
+        grid_spec=pltpu.PrefetchScalarGridSpec(
+            num_scalar_prefetch=1,
+            grid=(2, count),
+            in_specs=[
+                pl.BlockSpec((rows, wide), lambda h, b, s: (jnp.where(h == 0, b, count - 1), 0)),
+                pl.BlockSpec((rows, wide), lambda h, b, s: (jnp.where(h == 0, 0, b), 0)),
+            ],
+            out_specs=pl.BlockSpec(
+                (rows, wide), lambda h, b, s: (jnp.where(h == 0, s[0], 1 - s[0]) * count + b, 0)
+            ),
+        ),
+        out_shape=jax.ShapeDtypeStruct((2 * high, wide), F32),
+        compiler_params=params(56),
+        cost_estimate=cost(2 * high * wide, 12 * high * wide),
+        name="join",
+    )(core, own, far)
 
 
 def hidden_scores(scores, key_block, query_block, rows, begin):
@@ -594,16 +687,17 @@
 
 
 def attend_back_far_kernel(
-    heads, n, g_ref, far_q_ref, far_pair_ref, begin_ref, part_ref,
-    dq_ref, dk_ref, dv_ref, layer_ref,
+    heads, n, g_ref, far_q_ref, far_pair_ref, begin_ref, part_ref, mid_ref,
+    dq_ref, dk_ref, dv_ref, layer_ref, next_ref,
     all_ref, acc_ref, rows_ref, s_ref, p_ref, land_ref, pair_ref, q_ref,
-    send, recv, zsend, zrecv, read_sem,
+    send, recv, zsend, zrecv, read_sem, mid_land, msend, mrecv,
 ):
     rows = g_ref.shape[0]
     span = heads * HD
     shard = layer_ref.shape[1]
     at = lax.axis_index("tp")
     cube = Cube(all_ref, send, recv)
+    middle = MidSum(mid_ref, mid_land, next_ref, msend, mrecv)
     me = cube.me
     barrier = pltpu.get_barrier_semaphore()
     cube.signal(barrier)
@@ -657,6 +751,11 @@
         def _():
             for o in range(1, n):
                 term(o).start()
+            middle.begin()
+
+        @pl.when(step == 3)
+        def _():
+            middle.turn()
 
         block = cube.block(step)
         place = pl.ds(pl.multiple_of(block * rows, 16), rows)
@@ -730,12 +829,13 @@
         term(o).wait_recv()
         total = total + land_ref[o - 1].astype(F32)
     layer_ref[...] = total.astype(BF16)
+    middle.finish()
     cube.finish()
     for o in range(1, n):
         term(o).wait_send()
 
 
-def attend_back_far(grad, all_query, all_pairs, all_begin, part, heads, n):
+def attend_back_far(grad, all_query, all_pairs, all_begin, part, mid, heads, n):
     rows = grad.shape[0]
     span = heads * HD
     shard = part.shape[1] // n
@@ -743,9 +843,10 @@
     wide = jax.ShapeDtypeStruct((rows, span), F32)
     return pl.pallas_call(
         functools.partial(attend_back_far_kernel, heads, n),
-        in_specs=[vmem] + [pl.BlockSpec(memory_space=pl.ANY)] * 2 + [vmem] * 2,
-        out_specs=[vmem] * 4,
-        out_shape=[wide, wide, wide, jax.ShapeDtypeStruct((rows, shard), BF16)],
+        in_specs=[vmem] + [pl.BlockSpec(memory_space=pl.ANY)] * 2 + [vmem] * 3,
+        out_specs=[vmem] * 5,
+        out_shape=[wide, wide, wide, jax.ShapeDtypeStruct((rows, shard), BF16)]
+        + [jax.ShapeDtypeStruct(mid.shape, BF16)],
         scratch_shapes=[
             pltpu.VMEM((CUBE * rows, span + HD), BF16),
             pltpu.VMEM((heads, HD, rows), F32),
@@ -760,11 +861,14 @@
             pltpu.SemaphoreType.DMA((n - 1,)),
             pltpu.SemaphoreType.DMA((n - 1,)),
             pltpu.SemaphoreType.DMA((2, CUBE)),
+            pltpu.VMEM((mid.shape[0] // 2, mid.shape[1]), BF16),
+            pltpu.SemaphoreType.DMA((4,)),
+            pltpu.SemaphoreType.DMA((4,)),
         ],
-        compiler_params=params(60, collective_id=3, has_side_effects=True),
+        compiler_params=params(62, collective_id=3, has_side_effects=True),
         cost_estimate=cost(1e6, 1e6),
         name="attend_back_far",
-    )(grad, all_query, all_pairs, all_begin, part)
+    )(grad, all_query, all_pairs, all_begin, part, mid)
 
 
 def query_grad_kernel(
@@ -983,11 +1087,11 @@
 
 
 def feed_kernel(
-    inner_ref, cot_ref, w_ref, down_ref, hidden_ref, dgu_ref, down_grad_ref, gu_grad_ref
+    inner_ref, cot_ref, w_ref, grad_ref, hidden_ref, dgu_ref, down_grad_ref, gu_grad_ref
 ):
-    block = down_ref.shape[0]
+    block = grad_ref.shape[1]
     both = jnp.dot(inner_ref[...], w_ref[...], preferred_element_type=F32)
-    grad = lax.dot_general(cot_ref[...], down_ref[...], NT, preferred_element_type=F32)
+    grad = grad_ref[...].astype(F32)
     gate, up = both[:, :block], both[:, block:]
     sigma = 1.0 / (1.0 + jnp.exp(-gate))
     active = gate * sigma
@@ -1002,16 +1106,16 @@
     ).astype(BF16)
 
 
-def feed(inner, cot, weight, down, block):
+def feed(inner, cot, weight, grad, block):
     rows, width = inner.shape
-    units = down.shape[0]
+    units = grad.shape[1]
     whole = pl.BlockSpec((rows, width), lambda j: (0, 0))
     column = lambda high, wide: pl.BlockSpec((high, wide), lambda j: (0, j))
     line = pl.BlockSpec((block, width), lambda j: (j, 0))
     return pl.pallas_call(
         feed_kernel,
         grid=(units // block,),
-        in_specs=[whole, whole, column(width, 2 * block), line],
+        in_specs=[whole, whole, column(width, 2 * block), column(rows, block)],
         out_specs=[column(rows, block), column(rows, 2 * block), line, column(width, 2 * block)],
         out_shape=[
             jax.ShapeDtypeStruct((rows, units), BF16),
@@ -1024,7 +1128,7 @@
             12 * rows * width * units, 12 * width * units + 4 * rows * width, rows * units
         ),
         name="feed",
-    )(inner, cot, weight, down)
+    )(inner, cot, weight, grad)
 
 
 def weave_kernel(block, sum_ref, out_ref):
@@ -1197,7 +1301,8 @@
 
 
 def merge_kernel(
-    n, sub, part_ref, tok_ref, inner_ref, resid_ref, stat_ref, from_left, from_right, send, recv
+    n, sub, part_ref, tok_ref, cot_ref, down_ref, inner_ref, resid_ref, stat_ref, hidden_ref,
+    from_left, from_right, send, recv,
 ):
     line_barrier(lax.axis_index("tp"), n)
     resid_ref[...] = jnp.zeros_like(resid_ref)
@@ -1212,42 +1317,63 @@
         stat_ref[rows, :] = jnp.concatenate([mean, inverse], axis=1)
         inner_ref[rows, :] = (center * inverse).astype(BF16)
 
-    sum_rows(n, sub, part_ref, inner_ref, row_fn, from_left, from_right, send, recv)
-
-
-def merge(part, tok_full, n):
+    def piece(at):
+        hidden_ref[:, at : at + 256] = lax.dot_general(
+            cot_ref[...], down_ref[at : at + 256, :], NT, preferred_element_type=F32
+        ).astype(BF16)
+
+    aside = {}
+    for k in range(down_ref.shape[0] // 256):
+        aside[1 + 2 * k] = (functools.partial(piece, k * 256),)
+    sum_rows(n, sub, part_ref, inner_ref, row_fn, from_left, from_right, send, recv, aside)
+
+
+def merge(part, tok_full, cot_full, down, n):
     rows, width = part.shape
     sub = 32
     vmem = pl.BlockSpec(memory_space=pltpu.VMEM)
     return pl.pallas_call(
         functools.partial(merge_kernel, n, sub),
-        in_specs=[vmem] * 2,
-        out_specs=[vmem] * 3,
+        in_specs=[vmem] * 4,
+        out_specs=[vmem] * 4,
         out_shape=[
             jax.ShapeDtypeStruct((rows, width), BF16),
             jax.ShapeDtypeStruct((rows, width), F32),
             jax.ShapeDtypeStruct((rows, 2), F32),
+            jax.ShapeDtypeStruct((rows, down.shape[0]), BF16),
         ],
         scratch_shapes=[pltpu.VMEM((rows, width), BF16)] * 2
         + [pltpu.SemaphoreType.DMA((4, rows // sub))] * 2,
         compiler_params=params(56, collective_id=5, has_side_effects=True),
         cost_estimate=cost(1e6, 1e6),
         name="merge",
-    )(part, tok_full)
-
-
-def norm_back_kernel(n, sub, cube, part_ref, cot_ref, resid_ref, stat_ref, *refs):
+    )(part, tok_full, cot_full, down)
+
+
+def norm_back_kernel(
+    n, sub, cube, part_ref, cot_ref, resid_ref, stat_ref, hidden_ref, down_ref, *refs
+):
     total = None
     if cube:
-        own_ref, out_ref, shard_ref, from_left, from_right, send, recv, land, csend, crecv = refs
-        total = CubeSum(own_ref.shape[0], csend, crecv, own=own_ref, land=land, shard=shard_ref)
+        own, out_ref, layer_ref, mid, from_left, from_right, send, recv, land, csend, crecv = refs
+        total = CubeSum(own, land, csend, crecv, mid=mid)
     else:
-        out_ref, from_left, from_right, send, recv = refs
+        out_ref, layer_ref, from_left, from_right, send, recv = refs
     line_barrier(lax.axis_index("tp"), n, total)
     aside = {}
+
+    def piece(at):
+        cols = slice(at, at + 256)
+        layer_ref[:, cols] = (
+            resid_ref[:, cols]
+            + jnp.dot(hidden_ref[...], down_ref[:, cols], preferred_element_type=F32)
+        ).astype(BF16)
+
+    for k in range(down_ref.shape[1] // 256):
+        aside[1 + 2 * k] = (functools.partial(piece, k * 256),)
     if cube:
         total.begin()
-        for k, c in enumerate((7, 8, 9, 10, 19, 20)):
+        for k, c in enumerate((6, 8, 10, 12)):
             aside[c] = (functools.partial(total.reduce, k),)
 
     def row_fn(summed, rows):
@@ -1260,12 +1386,12 @@
 
     sum_rows(n, sub, part_ref, out_ref, row_fn, from_left, from_right, send, recv, aside)
     if cube:
-        total.reduce(6)
-        total.reduce(7)
+        total.reduce(4)
+        total.reduce(5)
         total.finish()
 
 
-def norm_back(part, cot, resid, stat, n, grads):
+def norm_back(part, cot, resid, stat, hidden, down, n, grads):
     rows, width = part.shape
     sub = 32
     vmem = pl.BlockSpec(memory_space=pltpu.VMEM)
@@ -1274,17 +1400,17 @@
         extra += sum_scratch(grad.shape)
     return pl.pallas_call(
         functools.partial(norm_back_kernel, n, sub, len(grads) > 0),
-        in_specs=[vmem] * (4 + len(grads)),
-        out_specs=[vmem] * (1 + len(grads)),
-        out_shape=[jax.ShapeDtypeStruct((rows, width), BF16)]
-        + [jax.ShapeDtypeStruct((grad.shape[0] // 8, grad.shape[1]), BF16) for grad in grads],
+        in_specs=[vmem] * (6 + len(grads)),
+        out_specs=[vmem] * (2 + len(grads)),
+        out_shape=[jax.ShapeDtypeStruct((rows, width), BF16)] * 2
+        + [jax.ShapeDtypeStruct((grad.shape[0] // 4, grad.shape[1]), BF16) for grad in grads],
         scratch_shapes=[pltpu.VMEM((rows, width), BF16)] * 2
         + [pltpu.SemaphoreType.DMA((4, rows // sub))] * 2
         + extra,
-        compiler_params=params(56, collective_id=1, has_side_effects=True),
+        compiler_params=params(60, collective_id=1, has_side_effects=True),
         cost_estimate=cost(1e6, 1e6),
         name="norm_back",
-    )(part, cot, resid, stat, *grads)
+    )(part, cot, resid, stat, hidden, down, *grads)
 
 
 def unrotate_kernel(
@@ -1342,14 +1468,12 @@
 def unproject_kernel(heads, n, cube, dproj_ref, tok_ref, stat_ref, w_ref, branch_ref, *refs):
     sums, rest = [], None
     if cube:
-        in_ref, og_ref, shard_ref, out_ref, in_out, og_out, down_out = refs[:7]
+        in_ref, og_ref, mid_ref, out_ref, in_out, og_out, down_out = refs[:7]
         part_ref, mine_ref, land_ref, sums_ref, far_ref, send, recv, ssend, srecv = refs[7:16]
         for own, out, at in ((in_ref, in_out, 16), (og_ref, og_out, 19)):
             land, csend, crecv = refs[at : at + 3]
-            sums.append(CubeSum(own.shape[0], csend, crecv, own=own, land=land, out=out))
-        rest = CubeSum(
-            down_out.shape[0], refs[22], refs[23], out=down_out, shard=shard_ref, local=refs[24]
-        )
+            sums.append(CubeSum(own, land, csend, crecv, out=out))
+        rest = LastGather(mid_ref, down_out, *refs[22:25])
     else:
         out_ref, part_ref, mine_ref, land_ref, sums_ref, far_ref, send, recv, ssend, srecv = refs
 
@@ -1361,10 +1485,6 @@
     def gather(k):
         for item in sums:
             item.gather(k)
-
-    def rest_gather(k):
-        if rest is not None:
-            rest.gather(k)
 
     rows, width = tok_ref.shape
     shard = width // n
@@ -1380,7 +1500,8 @@
     pl.semaphore_wait(barrier, n - 1 + (3 if cube else 0))
     for item in sums:
         item.begin()
-    rest_gather(0)
+    if cube:
+        rest.begin()
     block = 256
     count = rows // block
 
@@ -1422,11 +1543,7 @@
         sums_ref[:, i * block : (i + 1) * block] = both.T[:8]
     for o in range(1, n):
         totals(o).start()
-    reduce(0, 1, 2, 3)
-    rest_gather(1)
-    reduce(4, 5)
-    rest_gather(2)
-    reduce(6, 7)
+    reduce(0, 1, 2, 3, 4, 5, 6, 7)
     gather(0)
     gather(1)
     total = sums_ref[...]
@@ -1434,7 +1551,6 @@
         totals(o).wait_recv()
         total = total + far_ref[o - 1]
     mine_ref[...] = total
-    gather(2)
     for i in range(count):
         place = pl.ds(i * block, block)
         spread = jnp.concatenate(
@@ -1449,8 +1565,7 @@
         out_ref[place, :] = branch_ref[place, own].astype(F32) + inverse * (
             total - spread[:, 0:1] - normed * spread[:, 1:2]
         )
-    rest_gather(3)
-    gather(3)
+    gather(2)
     for item in sums + ([rest] if cube else []):
         item.finish()
     for o in range(1, n):
@@ -1459,22 +1574,22 @@
             term(o, i).wait_send()
 
 
-def unproject(dproj, tok_full, stat, weight, branch, heads, n, grads, shards):
+def unproject(dproj, tok_full, stat, weight, branch, heads, n, grads, mids):
     rows, width = tok_full.shape
     shard = width // n
     vmem = pl.BlockSpec(memory_space=pltpu.VMEM)
     extra = []
     for grad in grads:
         extra += sum_scratch(grad.shape)
-    for _ in shards:
-        extra += [pltpu.SemaphoreType.DMA((SUM_SENDS,))] * 2 + [pltpu.SemaphoreType.DMA((2,))]
+    for _ in mids:
+        extra += [pltpu.SemaphoreType.DMA((2,))] * 3
     return pl.pallas_call(
         functools.partial(unproject_kernel, heads, n, len(grads) > 0),
-        in_specs=[vmem] * (5 + len(grads) + len(shards)),
-        out_specs=[vmem] * (1 + len(grads)) + [pl.BlockSpec(memory_space=pl.ANY)] * len(shards),
+        in_specs=[vmem] * (5 + len(grads) + len(mids)),
+        out_specs=[vmem] * (1 + len(grads)) + [pl.BlockSpec(memory_space=pl.ANY)] * len(mids),
         out_shape=[jax.ShapeDtypeStruct((rows, shard), F32)]
-        + [jax.ShapeDtypeStruct(grad.shape, BF16) for grad in grads]
-        + [jax.ShapeDtypeStruct((8 * piece.shape[0], piece.shape[1]), BF16) for piece in shards],
+        + [jax.ShapeDtypeStruct((grad.shape[0] // 2, grad.shape[1]), BF16) for grad in grads]
+        + [jax.ShapeDtypeStruct((2 * mid.shape[0], mid.shape[1]), BF16) for mid in mids],
         scratch_shapes=[
             pltpu.VMEM((rows, width), BF16),
             pltpu.VMEM((8, rows), F32),
@@ -1490,7 +1605,7 @@
         compiler_params=params(60, collective_id=4, has_side_effects=True),
         cost_estimate=cost(1e6, 1e6),
         name="unproject",
-    )(dproj, tok_full, stat, weight, branch, *grads, *shards)
+    )(dproj, tok_full, stat, weight, branch, *grads, *mids)
 
 
 def per_device(tokens, segment_ids, in_weight, out_weight, gate_up_weight, down_weight, cotangent):
@@ -1548,9 +1663,11 @@
         out_part = jnp.dot(mixed, out_weight, preferred_element_type=F32).astype(BF16)
     late_query, mixed = lax.optimization_barrier((query, mixed))
     all_query = lax.all_gather(late_query, "ctx", axis=0, tiled=True)
-    inner2, resid1, stat2 = merge(out_part, tok_full, tp_size)
-
-    hidden, grad_gu, down_grad, gu_grad = feed(inner2, cot_full, gu_w, down_weight, BLOCK)
+    inner2, resid1, stat2, grad_hidden = merge(
+        out_part, tok_full, cot_full, down_weight, tp_size
+    )
+
+    hidden, grad_gu, down_grad, gu_grad = feed(inner2, cot_full, gu_w, grad_hidden, BLOCK)
     down_grad, gu_grad, all_query, grad_gu, hidden = lax.optimization_barrier(
         (down_grad, gu_grad, all_query, grad_gu, hidden)
     )
@@ -1559,15 +1676,15 @@
     gu_grad = lax.optimization_barrier(lax.psum(gu_grad, "ctx"))
 
     grad_part = lax.dot_general(grad_gu, gu_w, NT, preferred_element_type=F32).astype(BF16)
-    branch_grad, *shards = norm_back(
-        grad_part, cot_full, resid1, stat2, tp_size, [down_grad] if cube else []
+    branch_grad, branch, *mids = norm_back(
+        grad_part, cot_full, resid1, stat2, hidden, down_weight, tp_size,
+        [down_grad] if cube else [],
     )
     out_grad = lax.dot_general(mixed, branch_grad, TN, preferred_element_type=F32).astype(BF16)
     grad_mixed, delta = mixed_grad(branch_grad, out_weight, raw, lse, heads)
-    branch = (resid1 + jnp.dot(hidden, down_weight, preferred_element_type=F32)).astype(BF16)
     if cube:
-        dq, dk, dv, layer_out = attend_back_far(
-            grad_mixed, all_query, all_pairs, blocks, branch, heads, tp_size
+        dq, dk, dv, layer_out, mid = attend_back_far(
+            grad_mixed, all_query, all_pairs, blocks, branch, mids[0], heads, tp_size
         )
     else:
         branch = lax.psum_scatter(branch, "tp", scatter_dimension=1, tiled=True)
@@ -1578,10 +1695,14 @@
 
     dproj, in_grad = unrotate(dq, dk, dv, cosine, sine, inner1, heads)
     if cube:
-        tokens_grad, in_grad, out_grad, down_grad = unproject(
-            dproj, tok_full, stat1, in_w, branch_grad, heads, tp_size,
-            [in_grad, out_grad], shards,
+        tokens_grad, *halves = unproject(
+            dproj, tok_full, stat1, in_w, branch_grad, heads, tp_size, [in_grad, out_grad], [mid]
         )
+        swap = [(i, i + 1 - 2 * (i % 2)) for i in range(CUBE)]
+        core = (me % 2)[None]
+        far = [lax.ppermute(half, "ctx", swap) for half in halves]
+        *far, gu_grad = lax.optimization_barrier((*far, weave(gu_grad, BLOCK)))
+        in_grad, out_grad, down_grad = [join(core, *both) for both in zip(halves, far)]
     else:
         in_grad, out_grad, down_grad, gu_grad = lax.optimization_barrier(
             (in_grad, out_grad, down_grad, gu_grad)
@@ -1590,13 +1711,15 @@
         (tokens_grad,) = unproject(
             dproj, tok_full, stat1, in_w, branch_grad, heads, tp_size, [], []
         )
+        in_grad, out_grad, down_grad = widen(in_grad), out_grad.astype(F32), widen(down_grad)
+        gu_grad = weave(gu_grad, BLOCK)
     return (
         layer_out,
         tokens_grad,
-        jnp.transpose(widen(in_grad).reshape(3, width, span), (1, 0, 2)),
-        out_grad.astype(F32),
-        weave(gu_grad, BLOCK),
-        widen(down_grad),
+        jnp.transpose(in_grad.reshape(3, width, span), (1, 0, 2)),
+        out_grad,
+        gu_grad,
+        down_grad,
     )
 
 

time: 755 us -> 749 us (level)
  matrix products: 34.9 us -> 23.2 us
  Pallas kernels: 621 us -> 630 us
    pallas_call x1, Pallas kernels: 80.4 us -> 110 us  [attend_back_far(): pl.pallas_call(functools.partial(attend_back_far_kernel, heads, n), in_sp...]
    pallas_call x1, Pallas kernels: 135 us -> 123 us  [unproject(): pl.pallas_call(functools.partial(unproject_kernel, heads, n, len(grads) >...]
    dot_general x1 -> x0, matrix products: 12 us -> none  [per_device(): jnp.dot(hidden, down_weight, preferred_element_type=F32)]
    pallas_call x2 -> x3, Pallas kernels: 19.9 us -> 23 us  [join(): pl.pallas_call(join_kernel, grid_spec=pltpu.PrefetchScalarGridSpec(num_sc...]
  transfers between devices with their start and end apart: 3 -> 6, of which waited for: 1 -> 1; matrix products, arithmetic and copies ran while one was open for 10% -> 7% of each run, Pallas kernels for 68% -> 70%
where the time goes in v7:
time: 749 us; the launch traced here: 739 us
  Pallas kernels  630 us (84%)
  local copies, waits for them, and re-layouts  31.4 us (4%)
  waiting for transfers between devices  26 us (3%)
  matrix products  23.2 us (3%)
  between operations  14.3 us (2%)
  blocking collectives  10.5 us (1%)
    pallas_call x1, Pallas kernels, unproject(): pl.pallas_call(functools.partial(unproject_kernel, heads, n, len(grads) >...  123 us
    pallas_call x1, Pallas kernels, attend_back_far(): pl.pallas_call(functools.partial(attend_back_far_kernel, heads, n), in_sp...  110 us
    pallas_call x1, Pallas kernels, norm_back(): pl.pallas_call(functools.partial(norm_back_kernel, n, sub, len(grads) > 0...  109 us
    pallas_call x1, Pallas kernels, merge(): pl.pallas_call(functools.partial(merge_kernel, n, sub), in_specs=[vmem] *...  94.3 us
    pallas_call x1, Pallas kernels, attend_far(): pl.pallas_call(functools.partial(attend_far_kernel, heads, n), in_specs=[...  79.5 us
    pallas_call x1, Pallas kernels, feed(): pl.pallas_call(feed_kernel, grid=(units // block,), in_specs=[whole, whol...  41.2 us
    reshape x1, local copies, waits for them, and re-layouts, per_device(): gu_w = gu_w.reshape(width, 2 * hidden_local)  27.8 us
    all_gather x1, waiting for transfers between devices, gather(): return lax.all_gather(local, 'tp', axis=axis, tiled=True)  25.3 us
  transfers between devices with their start and end apart: 6, of which 1 were waited for; matrix products, arithmetic and copies ran while one was open for 7% of the time, Pallas kernels for 70%

profile of v7, /device:TPU:0, one launch (start us, length us, event | category | flops | bytes accessed | tf_op | source)
XLA Modules:
  0.0 739.3 jit_solution(11691704486610449707)
XLA Ops:
  7.2 0.7 all-gather.4.cloned.1.call-update
  8.0 0.7 reshape.60
  8.6 10.5 %all-gather = s32[8,1,768]{2,1,0:T(1,128)S(1)} all-gather(s32[1,1,768]{2,1,0:T(1,128)S(1)} %reshape.60), channel_id=1, replica_groups=mesh['ctx'=8,'tp'=4] {'ctx'}, dimensions={0}, use_global_device_ids=true | all-gather | bytes 27648 | tf_op jit(solution)/shard_map/all_gather | solution.py:1632
  19.1 0.1 slice_compare_fusion
  19.2 0.1 add_select_fusion
  19.3 0.3 reduce-window.9
  19.7 0.1 slice_reduce_fusion
  19.9 0.1 copy.18
  20.0 27.8 %reshape.55.w_ref = bf16[2048,4096]{1,0:T(8,128)(2,1)} reshape(bf16[2048,4,2,512]{3,2,1,0:T(2,128)(2,1)} %bitcast.19) | data formatting | bytes 33554432 | tf_op jit(solution)/shard_map/reshape | solution.py:1630
  47.8 1.4 fusion
  49.2 1.2 pad_maximum_fusion
  50.5 25.3 %all-gather.4.cloned.1.call-done.tok_ref = bf16[768,2048]{1,0:T(8,128)(2,1)} async-done(((bf16[768,512]{1,0:T(8,128)(2,1)}), bf16[768,2048]{1,0:T(8,128)(2,1)}) %all-gather.4.cloned.1.call-update) | async-done | bytes 3145744 | tf_op jit(solution)/shard_map/all_gather | solution.py:1622
  75.8 0.6 constant_dynamic-slice_fusion.begin_ref
  76.3 11.2 %project.1 = (bf16[768,2048]{1,0:T(8,128)(2,1)}, f32[768,2]{1,0:T(8,128)}, bf16[768,512]{1,0:T(8,128)(2,1)}, bf16[768,1024]{1,0:T(8,128)(2,1)}) custom-call(bf16[768,2048]{1,0:T(8,128)(2,1)} %all-gather.4.cloned.1.call-done.tok_ref, bf16[3,2048,512]{2,1,0:T(8,128)(2,1)} %bitcast.21, f32[768,128]{1,0:T(8,128)} %get-tuple-element.103.cos_ref, ...), custom_call_target="tpu_custom_call" | custom-call | flops 4831838208 | bytes 15728640 | tf_op jit(solution)/shard_map/project/pallas_call | solution.py:70
  87.6 79.5 %attend_far.1 = (f32[768,512]{1,0:T(8,128)}, bf16[768,512]{1,0:T(8,128)(2,1)}, f32[4,768]{1,0:T(4,128)}, bf16[6144,1024]{1,0:T(8,128)(2,1)}, bf16[768,2048]{1,0:T(8,128)(2,1)}, /*index=5*/bf16[768,2048]{1,0:T(8,128)(2,1)}) custom-call(bf16[768,512]{1,0:T(8,128)(2,1)} %get-tuple-element.65.q_ref, bf16[768,1024]{1,0:T(8,128)(2,1)} %get-tuple-element.55.own_ref, ...), custom_call_target="tpu_custom_call" | custom-call | flops 1000000 | bytes 1000000 | tf_op jit(solution)/shard_map/attend_far/pallas_call | solution.py:659
  167.2 94.3 %merge.1 = (bf16[768,2048]{1,0:T(8,128)(2,1)}, f32[768,2048]{1,0:T(8,128)}, f32[768,2]{1,0:T(8,128)}, bf16[768,2048]{1,0:T(8,128)(2,1)}) custom-call(bf16[768,2048]{1,0:T(8,128)(2,1)} %get-tuple-element.57.part_ref, bf16[768,2048]{1,0:T(8,128)(2,1)} %all-gather.4.cloned.1.call-done.tok_ref, bf16[768,2048]{1,0:T(8,128)(2,1)} %get-tuple-element.58.cot_ref, ...), custom_call_target="tpu_custom_call" | custom-call | flops 1000000 | bytes 1000000 | tf_op jit(solution)/shard_map/merge/pallas_call | solution.py:1335
  261.5 41.2 %feed.1 = (bf16[768,2048]{1,0:T(8,128)(2,1)}, bf16[768,4096]{1,0:T(8,128)(2,1)}, bf16[2048,2048]{1,0:T(8,128)(2,1)}, bf16[2048,4096]{1,0:T(8,128)(2,1)}) custom-call(bf16[768,2048]{1,0:T(8,128)(2,1)} %get-tuple-element.59.inner_ref, bf16[768,2048]{1,0:T(8,128)(2,1)} %get-tuple-element.58.cot_ref, bf16[2048,4096]{1,0:T(8,128)(2,1)} %reshape.55.w_ref, ...), custom_call_target="tpu_custom_call" | custom-call | flops 38654705664 | bytes 56623104 | tf_op jit(solution)/shard_map/feed/pallas_call | solution.py:1115
  302.8 20.0 %convolution_convert_fusion.part_ref = bf16[768,2048]{1,0:T(8,128)(2,1)} fusion(bf16[768,4096]{1,0:T(8,128)(2,1)} %get-tuple-element.68, bf16[2048,4096]{1,0:T(8,128)(2,1)} %reshape.55.w_ref), kind=kOutput, calls=%fused_computation | convolution fusion | flops 12886474752 | bytes 26214400 | tf_op jit(solution)/shard_map/dot_general | solution.py:1678
  322.8 109.0 %norm_back.1 = (bf16[768,2048]{1,0:T(8,128)(2,1)}, bf16[768,2048]{1,0:T(8,128)(2,1)}, bf16[512,2048]{1,0:T(8,128)(2,1)}) custom-call(bf16[768,2048]{1,0:T(8,128)(2,1)} %convolution_convert_fusion.part_ref, bf16[768,2048]{1,0:T(8,128)(2,1)} %get-tuple-element.58.cot_ref, f32[768,2048]{1,0:T(8,128)} %get-tuple-element.69.resid_ref, ...), custom_call_target="tpu_custom_call" | custom-call | flops 1000000 | bytes 1000000 | tf_op jit(solution)/shard_map/norm_back/pallas_call | solution.py:1401
  431.8 6.7 mixed_grad.1
  438.5 109.8 %attend_back_far.1 = (f32[768,512]{1,0:T(8,128)}, f32[768,512]{1,0:T(8,128)}, f32[768,512]{1,0:T(8,128)}, bf16[768,512]{1,0:T(8,128)(2,1)}, bf16[512,2048]{1,0:T(8,128)(2,1)}) custom-call(bf16[768,640]{1,0:T(8,128)(2,1)} %get-tuple-element.76.g_ref, bf16[6144,512]{1,0:T(8,128)(2,1)} %all-gather.6.cloned.1.call-done.far_q_ref, ...), custom_call_target="tpu_custom_call" | custom-call | flops 1000000 | bytes 1000000 | tf_op jit(solution)/shard_map/attend_back_far/pallas_call | solution.py:844
  548.3 12.1 %unrotate.1 = (bf16[768,1536]{1,0:T(8,128)(2,1)}, bf16[6144,512]{1,0:T(8,128)(2,1)}) custom-call(f32[768,512]{1,0:T(8,128)} %get-tuple-element.82.dq_ref, f32[768,512]{1,0:T(8,128)} %get-tuple-element.83.dk_ref, f32[768,512]{1,0:T(8,128)} %get-tuple-element.84.dv_ref, f32[768,128]{1,0:T(8,128)} %get-tuple-element.103.cos_ref, ...), custom_call_target="tpu_custom_call" | custom-call | flops 4831838208 | bytes 11010048 | tf_op jit(solution)/shard_map/unrotate/pallas_call | solution.py:1450
  560.5 3.1 convolution_convert_fusion.1.refs_1_
  563.6 122.5 %unproject.1 = (f32[768,512]{1,0:T(8,128)}, bf16[3072,512]{1,0:T(8,128)(2,1)}, bf16[256,2048]{1,0:T(8,128)(2,1)}, bf16[1024,2048]{1,0:T(8,128)(2,1)}) custom-call(bf16[768,1536]{1,0:T(8,128)(2,1)} %get-tuple-element.86.dproj_ref, bf16[768,2048]{1,0:T(8,128)(2,1)} %all-gather.4.cloned.1.call-done.tok_ref, f32[768,2]{1,0:T(8,128)} %get-tuple-element.87.stat_ref, ...), custom_call_target="tpu_custom_call" | custom-call | flops 1000000 | bytes 1000000 | tf_op jit(solution)/shard_map/unproject/pallas_call | solution.py:1586
  686.2 0.5 collective-permute-start
  686.7 0.1 collective-permute-start.1
  686.8 20.4 %weave.1 = f32[2048,2,2048]{2,1,0:T(2,128)} custom-call(bf16[2048,4096]{1,0:T(8,128)(2,1)} %all-reduce.2.cloned.1.call-done.sum_ref), custom_call_target="tpu_custom_call" | custom-call | flops 8388608 | bytes 50331648 | tf_op jit(solution)/shard_map/weave/pallas_call | solution.py:1144
  707.2 11.0 %join.5 = f32[2048,2048]{1,0:T(8,128)} custom-call(s32[1]{0:T(128)} %bitcast.6.core_ref, bf16[1024,2048]{1,0:T(8,128)(2,1)} %get-tuple-element.94.own_ref, bf16[1024,2048]{1,0:T(8,128)(2,1)} %collective-permute-done.2.far_ref), custom_call_target="tpu_custom_call" | custom-call | flops 4194304 | bytes 25165824 | tf_op jit(solution)/shard_map/join/pallas_call | solution.py:498
  718.2 3.7 join.4
  721.9 8.3 %join.3 = f32[6144,512]{1,0:T(8,128)} custom-call(s32[1]{0:T(128)} %bitcast.6.core_ref, bf16[3072,512]{1,0:T(8,128)(2,1)} %get-tuple-element.92.own_ref, bf16[3072,512]{1,0:T(8,128)(2,1)} %copy-done.1), custom_call_target="tpu_custom_call" | custom-call | flops 3145728 | bytes 18874368 | tf_op jit(solution)/shard_map/join/pallas_call | solution.py:498
  730.3 0.9 copy.22
  731.1 1.1 copy.23
  (30 shorter events, 0.6 us)
Async XLA Ops:
  7.2 68.6 %all-gather.4.cloned.1.call-start = ((), (), s32[]{:S(2)}) async-start(), calls=%async_computation | async-start | bytes 3932160 | tf_op jit(solution)/shard_map/all_gather | solution.py:1622
  7.9 294.8 %all-gather.6.cloned.1.call-start = ((), (), s32[]{:S(2)}) async-start(), calls=%async_computation.1 | async-start | bytes 7077888 | tf_op jit(solution)/shard_map/all_gather | solution.py:1665
  50.5 37.1 %copy-start.5 = (s32[8,768]{1,0:T(8,128)}, s32[8,768]{1,0:T(8,128)S(1)}, u32[]{:S(2)}) copy-start(s32[8,768]{1,0:T(8,128)S(1)} %bitcast_maximum_fusion.begin_ref) | copy-start | bytes 73732
  167.1 519.7 %all-reduce.2.cloned.1.call-start = ((), (), s32[]{:S(2)}) async-start(), calls=%async_computation.2 | async-start | bytes 33554432 | tf_op jit(solution)/shard_map/psum | solution.py:1676
  548.3 12.2 %copy-start = (bf16[768,2048]{1,0:T(8,128)(2,1)S(1)}, bf16[768,2048]{1,0:T(8,128)(2,1)}, u32[]{:S(2)}) copy-start(bf16[768,2048]{1,0:T(8,128)(2,1)} %get-tuple-element.73.branch_ref) | copy-start | bytes 9437188
  548.3 12.1 %copy-start.4 = (bf16[768,512]{1,0:T(8,128)(2,1)S(1)}, bf16[768,512]{1,0:T(8,128)(2,1)}, u32[]{:S(2)}) copy-start(bf16[768,512]{1,0:T(8,128)(2,1)} %get-tuple-element.89) | copy-start | bytes 2359300
  686.2 21.0 %collective-permute-start.2 = (bf16[1024,2048]{1,0:T(8,128)(2,1)}, bf16[1024,2048]{1,0:T(8,128)(2,1)}, u32[]{:S(2)}, u32[]{:S(2)}) collective-permute-start(bf16[1024,2048]{1,0:T(8,128)(2,1)} %get-tuple-element.94.own_ref), channel_id=1, source_target_pairs={{0,4},{4,0},{8,12},{12,8},{16,20},{20,16},{24,28},{28,24},{1,5},{5... | collective-permute-start | bytes 12582920 | tf_op jit(solution)/shard_map/ppermute | solution.py:1703
  686.2 20.9 %collective-permute-start = (bf16[3072,512]{1,0:T(8,128)(2,1)}, bf16[3072,512]{1,0:T(8,128)(2,1)S(1)}, u32[]{:S(2)}, u32[]{:S(2)}) collective-permute-start(bf16[3072,512]{1,0:T(8,128)(2,1)} %get-tuple-element.92.own_ref), channel_id=1, source_target_pairs={{0,4},{4,0},{8,12},{12,8},{16,20},{20,16},{24,28},{28,24},{1,5},{5... | collective-permute-start | bytes 9437192 | tf_op jit(solution)/shard_map/ppermute | solution.py:1703
  686.7 20.4 %collective-permute-start.1 = (bf16[256,2048]{1,0:T(8,128)(2,1)}, bf16[256,2048]{1,0:T(8,128)(2,1)}, u32[]{:S(2)}, u32[]{:S(2)}) collective-permute-start(bf16[256,2048]{1,0:T(8,128)(2,1)} %get-tuple-element.93.own_ref), channel_id=1, source_target_pairs={{0,4},{4,0},{8,12},{12,8},{16,20},{20,16},{24,28},{28,24},{1,5},{5... | collective-permute-start | bytes 3145736 | tf_op jit(solution)/shard_map/ppermute | solution.py:1703
  707.2 11.0 %copy-start.1 = (bf16[3072,512]{1,0:T(8,128)(2,1)}, bf16[3072,512]{1,0:T(8,128)(2,1)S(1)}, u32[]{:S(2)}) copy-start(bf16[3072,512]{1,0:T(8,128)(2,1)S(1)} %collective-permute-done.far_ref) | copy-start | bytes 9437188
  721.9 8.3 %copy-start.3 = (bf16[768,512]{1,0:T(8,128)(2,1)S(1)}, bf16[768,512]{1,0:T(8,128)(2,1)}, u32[]{:S(2)}) copy-start(bf16[768,512]{1,0:T(8,128)(2,1)} %get-tuple-element.111) | copy-start | bytes 2359300
  721.9 9.2 %copy-start.2 = (f32[768,512]{1,0:T(8,128)S(1)}, f32[768,512]{1,0:T(8,128)}, u32[]{:S(2)}) copy-start(f32[768,512]{1,0:T(8,128)} %get-tuple-element.112) | copy-start | bytes 4718596
Sparse Core Ops, SparseCore 0:
  9.6 66.1 all-gather.3
  167.3 53.3 all-gather.5
  302.9 302.4 all-reduce.1

commit v8 on v7

--- a/solution.py
+++ b/solution.py
@@ -19,6 +19,7 @@
 TN = (((0,), (0,)), ((), ()))
 MESH = pl.DeviceIdType.MESH
 BLOCK = 512
+SUB = 32
 
 
 def params(mib, **more):
@@ -286,11 +287,11 @@
 
 
 class CubeSum:
-    def __init__(self, own, land, send, recv, out=None, mid=None):
+    def __init__(self, own, near, land, send, recv, local, out=None, mid=None):
         me = lax.axis_index("ctx")
         core, x, y = me % 2, (me // 2) % 2, me // 4
         self.me, self.own, self.out, self.land, self.mid = me, own, out, land, mid
-        self.send, self.recv = send, recv
+        self.near, self.send, self.recv, self.local = near, send, recv, local
         rows = own.shape[0]
         self.half, self.eighth, self.last = rows // 2, rows // 8, rows // 16
         second = rows // 4
@@ -337,21 +338,27 @@
 
         lax.fori_loop(0, size // step, part, 0)
 
+    def read(self):
+        rows = pl.ds(pl.multiple_of(self.mine, 16), self.half)
+        return pltpu.make_async_copy(self.own.at[rows], self.near, self.local.at[0])
+
     def begin(self):
         self.copy(0).start()
+        self.read().start()
 
     def reduce(self, k):
         half, eighth, last, land = self.half, self.eighth, self.last, self.land
         i = k % 2
         if k == 0:
+            self.read().wait()
             self.copy(0).wait_recv()
         if k < 2:
             at = self.give1[i]
-            self.add(land, at, self.own, self.mine + at, at, eighth)
+            self.add(land, at, self.near, at, at, eighth)
             self.copy(1 + i).start()
         elif k < 4:
             at = self.keep1[i]
-            self.add(land, at, self.own, self.mine + at, at, eighth)
+            self.add(land, at, self.near, at, at, eighth)
         elif k < 6:
             self.copy(1 + i).wait_recv()
             landed = half + i * eighth - self.keep1[i]
@@ -473,46 +480,47 @@
 
 def sum_scratch(shape):
     return [
+        pltpu.VMEM((shape[0] // 2, shape[1]), BF16),
         pltpu.VMEM((shape[0] // 2 + 3 * (shape[0] // 8), shape[1]), BF16),
         pltpu.SemaphoreType.DMA((SUM_SENDS,)),
         pltpu.SemaphoreType.DMA((SUM_SENDS,)),
+        pltpu.SemaphoreType.DMA((1,)),
     ]
 
 
-def join_kernel(core_ref, own_ref, far_ref, out_ref):
-    @pl.when(pl.program_id(0) == 0)
-    def _():
-        out_ref[...] = own_ref[...].astype(F32)
-
-    @pl.when(pl.program_id(0) == 1)
-    def _():
-        out_ref[...] = far_ref[...].astype(F32)
+def join_kernel(count, core_ref, *refs):
+    for own_ref, far_ref, out_ref in zip(refs[:count], refs[count : 2 * count], refs[2 * count :]):
+        @pl.when(pl.program_id(0) == 0)
+        def _():
+            out_ref[...] = own_ref[...].astype(F32)
+
+        @pl.when(pl.program_id(0) == 1)
+        def _():
+            out_ref[...] = far_ref[...].astype(F32)
 
 
 def join(core, own, far):
-    high, wide = own.shape
-    rows = high
-    while rows * wide > 1024 * 1024:
-        rows = rows // 2
-    count = high // rows
+    steps = 4
+    block = lambda half, at: pl.BlockSpec((half.shape[0] // steps, half.shape[1]), at)
+    first = lambda h, b, s: (jnp.where(h == 0, b, steps - 1), 0)
+    second = lambda h, b, s: (jnp.where(h == 0, 0, b), 0)
+    target = lambda h, b, s: (jnp.where(h == 0, s[0], 1 - s[0]) * steps + b, 0)
+    size = sum(half.shape[0] * half.shape[1] for half in own)
     return pl.pallas_call(
-        join_kernel,
+        functools.partial(join_kernel, len(own)),
         grid_spec=pltpu.PrefetchScalarGridSpec(
             num_scalar_prefetch=1,
-            grid=(2, count),
-            in_specs=[
-                pl.BlockSpec((rows, wide), lambda h, b, s: (jnp.where(h == 0, b, count - 1), 0)),
-                pl.BlockSpec((rows, wide), lambda h, b, s: (jnp.where(h == 0, 0, b), 0)),
-            ],
-            out_specs=pl.BlockSpec(
-                (rows, wide), lambda h, b, s: (jnp.where(h == 0, s[0], 1 - s[0]) * count + b, 0)
-            ),
+            grid=(2, steps),
+            in_specs=[block(half, first) for half in own] + [block(half, second) for half in own],
+            out_specs=[block(half, target) for half in own],
         ),
-        out_shape=jax.ShapeDtypeStruct((2 * high, wide), F32),
+        out_shape=[
+            jax.ShapeDtypeStruct((2 * half.shape[0], half.shape[1]), F32) for half in own
+        ],
         compiler_params=params(56),
-        cost_estimate=cost(2 * high * wide, 12 * high * wide),
+        cost_estimate=cost(2 * size, 12 * size),
         name="join",
-    )(core, own, far)
+    )(core, *own, *far)
 
 
 def hidden_scores(scores, key_block, query_block, rows, begin):
@@ -1301,23 +1309,40 @@
 
 
 def merge_kernel(
-    n, sub, part_ref, tok_ref, cot_ref, down_ref, inner_ref, resid_ref, stat_ref, hidden_ref,
-    from_left, from_right, send, recv,
+    n, sub, part_ref, tok_ref, far_cot, far_down, inner_ref, resid_out, stat_ref, hidden_ref,
+    from_left, from_right, send, recv, cot_ref, down_ref, resid_ref, read_sem, keep_sem,
 ):
+    reads = (
+        pltpu.make_async_copy(far_cot, cot_ref, read_sem.at[0]),
+        pltpu.make_async_copy(far_down, down_ref, read_sem.at[1]),
+    )
+    for read in reads:
+        read.start()
     line_barrier(lax.axis_index("tp"), n)
-    resid_ref[...] = jnp.zeros_like(resid_ref)
     stat_ref[...] = jnp.zeros_like(stat_ref)
+
+    def keep(rows):
+        slot = rows.start // (2 * sub)
+        held = resid_ref.at[pl.ds(slot * sub, sub)]
+        return pltpu.make_async_copy(
+            held, resid_out.at[pl.ds(rows.start, sub)], keep_sem.at[slot]
+        )
 
     def row_fn(total, rows):
         x = tok_ref[rows, :].astype(F32) + total
         mean = jnp.mean(x, axis=1, keepdims=True)
         center = x - mean
         inverse = lax.rsqrt(jnp.mean(center * center, axis=1, keepdims=True) + EPS)
-        resid_ref[rows, :] = x
+        slot = rows.start // (2 * sub)
+        resid_ref[slot * sub : (slot + 1) * sub, :] = x
+        keep(rows).start()
         stat_ref[rows, :] = jnp.concatenate([mean, inverse], axis=1)
         inner_ref[rows, :] = (center * inverse).astype(BF16)
 
     def piece(at):
+        if at == 0:
+            for read in reads:
+                read.wait()
         hidden_ref[:, at : at + 256] = lax.dot_general(
             cot_ref[...], down_ref[at : at + 256, :], NT, preferred_element_type=F32
         ).astype(BF16)
@@ -1326,16 +1351,21 @@
     for k in range(down_ref.shape[0] // 256):
         aside[1 + 2 * k] = (functools.partial(piece, k * 256),)
     sum_rows(n, sub, part_ref, inner_ref, row_fn, from_left, from_right, send, recv, aside)
+    for c in range(part_ref.shape[0] // sub):
+        @pl.when(lax.axis_index("tp") == n // 2 - 1 + c % 2)
+        def _():
+            keep(slice(c * sub, (c + 1) * sub)).wait()
 
 
 def merge(part, tok_full, cot_full, down, n):
     rows, width = part.shape
-    sub = 32
+    sub = SUB
     vmem = pl.BlockSpec(memory_space=pltpu.VMEM)
+    far = pl.BlockSpec(memory_space=pl.ANY)
     return pl.pallas_call(
         functools.partial(merge_kernel, n, sub),
-        in_specs=[vmem] * 4,
-        out_specs=[vmem] * 4,
+        in_specs=[vmem, vmem, far, far],
+        out_specs=[vmem, far, vmem, vmem],
         out_shape=[
             jax.ShapeDtypeStruct((rows, width), BF16),
             jax.ShapeDtypeStruct((rows, width), F32),
@@ -1343,7 +1373,14 @@
             jax.ShapeDtypeStruct((rows, down.shape[0]), BF16),
         ],
         scratch_shapes=[pltpu.VMEM((rows, width), BF16)] * 2
-        + [pltpu.SemaphoreType.DMA((4, rows // sub))] * 2,
+        + [pltpu.SemaphoreType.DMA((4, rows // sub))] * 2
+        + [
+            pltpu.VMEM((rows, width), BF16),
+            pltpu.VMEM(down.shape, BF16),
+            pltpu.VMEM((rows // 2, width), F32),
+            pltpu.SemaphoreType.DMA((2,)),
+            pltpu.SemaphoreType.DMA((rows // (2 * sub),)),
+        ],
         compiler_params=params(56, collective_id=5, has_side_effects=True),
         cost_estimate=cost(1e6, 1e6),
         name="merge",
@@ -1351,21 +1388,36 @@
 
 
 def norm_back_kernel(
-    n, sub, cube, part_ref, cot_ref, resid_ref, stat_ref, hidden_ref, down_ref, *refs
+    n, sub, cube, part_ref, cot_ref, stat_ref, *refs
 ):
     total = None
+    far, refs = refs[:3], refs[3:]
     if cube:
-        own, out_ref, layer_ref, mid, from_left, from_right, send, recv, land, csend, crecv = refs
-        total = CubeSum(own, land, csend, crecv, mid=mid)
+        own, out_ref, layer_ref, mid, from_left, from_right, send, recv = refs[:8]
+        resid_ref, hidden_ref, down_ref, read_sem = refs[8:12]
+        total = CubeSum(own, *refs[12:17], mid=mid)
     else:
-        out_ref, layer_ref, from_left, from_right, send, recv = refs
+        out_ref, layer_ref, from_left, from_right, send, recv = refs[:6]
+        resid_ref, hidden_ref, down_ref, read_sem = refs[6:10]
+    reads = [
+        pltpu.make_async_copy(source, held, read_sem.at[k])
+        for k, (source, held) in enumerate(zip(far, (resid_ref, hidden_ref, down_ref)))
+    ]
+    for read in reads:
+        read.start()
+    at = lax.axis_index("tp")
     line_barrier(lax.axis_index("tp"), n, total)
     aside = {}
 
-    def piece(at):
-        cols = slice(at, at + 256)
+    def piece(start):
+        if start == 0:
+            for read in reads:
+                read.wait()
+        cols = slice(start, start + 256)
+        row = lax.broadcasted_iota(jnp.int32, (part_ref.shape[0], 256), 0)
+        owned = (row // sub) % 2 == at - (n // 2 - 1)
         layer_ref[:, cols] = (
-            resid_ref[:, cols]
+            jnp.where(owned, resid_ref[:, cols], 0.0)
             + jnp.dot(hidden_ref[...], down_ref[:, cols], preferred_element_type=F32)
         ).astype(BF16)
 
@@ -1393,24 +1445,31 @@
 
 def norm_back(part, cot, resid, stat, hidden, down, n, grads):
     rows, width = part.shape
-    sub = 32
+    sub = SUB
     vmem = pl.BlockSpec(memory_space=pltpu.VMEM)
+    far = pl.BlockSpec(memory_space=pl.ANY)
     extra = []
     for grad in grads:
         extra += sum_scratch(grad.shape)
     return pl.pallas_call(
         functools.partial(norm_back_kernel, n, sub, len(grads) > 0),
-        in_specs=[vmem] * (6 + len(grads)),
+        in_specs=[vmem] * 3 + [far] * (3 + len(grads)),
         out_specs=[vmem] * (2 + len(grads)),
         out_shape=[jax.ShapeDtypeStruct((rows, width), BF16)] * 2
         + [jax.ShapeDtypeStruct((grad.shape[0] // 4, grad.shape[1]), BF16) for grad in grads],
         scratch_shapes=[pltpu.VMEM((rows, width), BF16)] * 2
         + [pltpu.SemaphoreType.DMA((4, rows // sub))] * 2
+        + [
+            pltpu.VMEM(resid.shape, F32),
+            pltpu.VMEM(hidden.shape, BF16),
+            pltpu.VMEM(down.shape, BF16),
+            pltpu.SemaphoreType.DMA((3,)),
+        ]
         + extra,
         compiler_params=params(60, collective_id=1, has_side_effects=True),
         cost_estimate=cost(1e6, 1e6),
         name="norm_back",
-    )(part, cot, resid, stat, hidden, down, *grads)
+    )(part, cot, stat, resid, hidden, down, *grads)
 
 
 def unrotate_kernel(
@@ -1470,12 +1529,13 @@
     if cube:
         in_ref, og_ref, mid_ref, out_ref, in_out, og_out, down_out = refs[:7]
         part_ref, mine_ref, land_ref, sums_ref, far_ref, send, recv, ssend, srecv = refs[7:16]
-        for own, out, at in ((in_ref, in_out, 16), (og_ref, og_out, 19)):
-            land, csend, crecv = refs[at : at + 3]
-            sums.append(CubeSum(own, land, csend, crecv, out=out))
-        rest = LastGather(mid_ref, down_out, *refs[22:25])
+        for own, out, at in ((in_ref, in_out, 18), (og_ref, og_out, 23)):
+            sums.append(CubeSum(own, *refs[at : at + 5], out=out))
+        rest = LastGather(mid_ref, down_out, *refs[28:31])
+        mine_branch, branch_sem = refs[16:18]
     else:
-        out_ref, part_ref, mine_ref, land_ref, sums_ref, far_ref, send, recv, ssend, srecv = refs
+        out_ref, part_ref, mine_ref, land_ref, sums_ref, far_ref = refs[:6]
+        send, recv, ssend, srecv, mine_branch, branch_sem = refs[6:12]
 
     def reduce(*pieces):
         for k in pieces:
@@ -1523,6 +1583,8 @@
         )
 
     own = pl.ds(pl.multiple_of(at * shard, 128), shard)
+    branch_read = pltpu.make_async_copy(branch_ref.at[:, own], mine_branch, branch_sem.at[0])
+    branch_read.start()
     for i in range(count):
         place = pl.ds(i * block, block)
         total = None
@@ -1551,6 +1613,7 @@
         totals(o).wait_recv()
         total = total + far_ref[o - 1]
     mine_ref[...] = total
+    branch_read.wait()
     for i in range(count):
         place = pl.ds(i * block, block)
         spread = jnp.concatenate(
@@ -1562,7 +1625,7 @@
             total = total + land_ref[o - 1, place].astype(F32)
         inverse = stat_ref[place, 1:2]
         normed = (tok_ref[place, own].astype(F32) - stat_ref[place, 0:1]) * inverse
-        out_ref[place, :] = branch_ref[place, own].astype(F32) + inverse * (
+        out_ref[place, :] = mine_branch[place, :].astype(F32) + inverse * (
             total - spread[:, 0:1] - normed * spread[:, 1:2]
         )
     gather(2)
@@ -1585,7 +1648,9 @@
         extra += [pltpu.SemaphoreType.DMA((2,))] * 3
     return pl.pallas_call(
         functools.partial(unproject_kernel, heads, n, len(grads) > 0),
-        in_specs=[vmem] * (5 + len(grads) + len(mids)),
+        in_specs=[vmem] * 4
+        + [pl.BlockSpec(memory_space=pl.ANY)] * (1 + len(grads))
+        + [vmem] * len(mids),
         out_specs=[vmem] * (1 + len(grads)) + [pl.BlockSpec(memory_space=pl.ANY)] * len(mids),
         out_shape=[jax.ShapeDtypeStruct((rows, shard), F32)]
         + [jax.ShapeDtypeStruct((grad.shape[0] // 2, grad.shape[1]), BF16) for grad in grads]
@@ -1600,6 +1665,8 @@
             pltpu.SemaphoreType.DMA((n - 1, rows // 256)),
             pltpu.SemaphoreType.DMA((n - 1,)),
             pltpu.SemaphoreType.DMA((n - 1,)),
+            pltpu.VMEM((rows, shard), BF16),
+            pltpu.SemaphoreType.DMA((1,)),
         ]
         + extra,
         compiler_params=params(60, collective_id=4, has_side_effects=True),
@@ -1702,7 +1769,7 @@
         core = (me % 2)[None]
         far = [lax.ppermute(half, "ctx", swap) for half in halves]
         *far, gu_grad = lax.optimization_barrier((*far, weave(gu_grad, BLOCK)))
-        in_grad, out_grad, down_grad = [join(core, *both) for both in zip(halves, far)]
+        in_grad, out_grad, down_grad = join(core, halves, far)
     else:
         in_grad, out_grad, down_grad, gu_grad = lax.optimization_barrier(
             (in_grad, out_grad, down_grad, gu_grad)

time: 749 us -> 732 us (0.977)
  Pallas kernels: 630 us -> 611 us
    pallas_call x1, Pallas kernels: 123 us -> 136 us  [unproject(): pl.pallas_call(functools.partial(unproject_kernel, heads, n, len(grads) >...]
    pallas_call x1, Pallas kernels: 110 us -> 99 us  [attend_back_far(): pl.pallas_call(functools.partial(attend_back_far_kernel, heads, n), in_sp...]
    pallas_call x1, Pallas kernels: 109 us -> 98.4 us  [norm_back(): pl.pallas_call(functools.partial(norm_back_kernel, n, sub, len(grads) > 0...]
    pallas_call x4 -> x2, Pallas kernels: 117 us -> 107 us  [the longest x1 88.9 us: merge(): pl.pallas_call(functools.partial(merge_kernel, n, sub), in_specs=[vmem, v...]
  transfers between devices with their start and end apart: 6 -> 6, of which waited for: 1 -> 1; matrix products, arithmetic and copies ran while one was open for 7% -> 8% of each run, Pallas kernels for 70% -> 70%
where the time goes in v8:
time: 732 us; the launch traced here: 722 us
  Pallas kernels  611 us (83%)
  local copies, waits for them, and re-layouts  33 us (5%)
  waiting for transfers between devices  26 us (4%)
  matrix products  23.1 us (3%)
  between operations  14.3 us (2%)
  blocking collectives  10.5 us (1%)
    pallas_call x1, Pallas kernels, unproject(): pl.pallas_call(functools.partial(unproject_kernel, heads, n, len(grads) >...  136 us
    pallas_call x1, Pallas kernels, attend_back_far(): pl.pallas_call(functools.partial(attend_back_far_kernel, heads, n), in_sp...  99 us
    pallas_call x1, Pallas kernels, norm_back(): pl.pallas_call(functools.partial(norm_back_kernel, n, sub, len(grads) > 0...  98.4 us
    pallas_call x1, Pallas kernels, merge(): pl.pallas_call(functools.partial(merge_kernel, n, sub), in_specs=[vmem, v...  88.9 us
    pallas_call x1, Pallas kernels, attend_far(): pl.pallas_call(functools.partial(attend_far_kernel, heads, n), in_specs=[...  79.6 us
    pallas_call x1, Pallas kernels, feed(): pl.pallas_call(feed_kernel, grid=(units // block,), in_specs=[whole, whol...  41.1 us
    reshape x1, local copies, waits for them, and re-layouts, per_device(): gu_w = gu_w.reshape(width, 2 * hidden_local)  27.8 us
    all_gather x1, waiting for transfers between devices, gather(): return lax.all_gather(local, 'tp', axis=axis, tiled=True)  25.3 us
  transfers between devices with their start and end apart: 6, of which 1 were waited for; matrix products, arithmetic and copies ran while one was open for 8% of the time, Pallas kernels for 70%

profile of v8, /device:TPU:0, one launch (start us, length us, event | category | flops | bytes accessed | tf_op | source)
XLA Modules:
  0.0 722.0 jit_solution(3868821410554893397)
XLA Ops:
  7.2 0.7 all-gather.4.cloned.1.call-update
  8.0 0.7 reshape.60
  8.6 10.5 %all-gather = s32[8,1,768]{2,1,0:T(1,128)S(1)} all-gather(s32[1,1,768]{2,1,0:T(1,128)S(1)} %reshape.60), channel_id=1, replica_groups=mesh['ctx'=8,'tp'=4] {'ctx'}, dimensions={0}, use_global_device_ids=true | all-gather | bytes 27648 | tf_op jit(solution)/shard_map/all_gather | solution.py:1699
  19.1 0.1 slice_compare_fusion
  19.2 0.1 add_select_fusion
  19.3 0.3 reduce-window.9
  19.7 0.1 slice_reduce_fusion
  19.8 0.1 reshape.57
  19.9 0.1 copy.18
  20.0 27.8 %reshape.55.w_ref = bf16[2048,4096]{1,0:T(8,128)(2,1)} reshape(bf16[2048,4,2,512]{3,2,1,0:T(2,128)(2,1)} %bitcast.19) | data formatting | bytes 33554432 | tf_op jit(solution)/shard_map/reshape | solution.py:1697
  47.8 1.4 fusion
  49.2 1.2 pad_maximum_fusion
  50.5 25.3 %all-gather.4.cloned.1.call-done.tok_ref = bf16[768,2048]{1,0:T(8,128)(2,1)} async-done(((bf16[768,512]{1,0:T(8,128)(2,1)}), bf16[768,2048]{1,0:T(8,128)(2,1)}) %all-gather.4.cloned.1.call-update) | async-done | bytes 3145744 | tf_op jit(solution)/shard_map/all_gather | solution.py:1689
  75.8 0.6 constant_dynamic-slice_fusion.begin_ref
  76.3 11.2 %project.1 = (bf16[768,2048]{1,0:T(8,128)(2,1)}, f32[768,2]{1,0:T(8,128)}, bf16[768,512]{1,0:T(8,128)(2,1)}, bf16[768,1024]{1,0:T(8,128)(2,1)}) custom-call(bf16[768,2048]{1,0:T(8,128)(2,1)} %all-gather.4.cloned.1.call-done.tok_ref, bf16[3,2048,512]{2,1,0:T(8,128)(2,1)} %bitcast.20, f32[768,128]{1,0:T(8,128)} %get-tuple-element.109.cos_ref, ...), custom_call_target="tpu_custom_call" | custom-call | flops 4831838208 | bytes 15728640 | tf_op jit(solution)/shard_map/project/pallas_call | solution.py:71
  87.6 79.6 %attend_far.1 = (f32[768,512]{1,0:T(8,128)}, bf16[768,512]{1,0:T(8,128)(2,1)}, f32[4,768]{1,0:T(4,128)}, bf16[6144,1024]{1,0:T(8,128)(2,1)}, bf16[768,2048]{1,0:T(8,128)(2,1)}, /*index=5*/bf16[768,2048]{1,0:T(8,128)(2,1)}) custom-call(bf16[768,512]{1,0:T(8,128)(2,1)} %get-tuple-element.68.q_ref, bf16[768,1024]{1,0:T(8,128)(2,1)} %get-tuple-element.58.own_ref, ...), custom_call_target="tpu_custom_call" | custom-call | flops 1000000 | bytes 1000000 | tf_op jit(solution)/shard_map/attend_far/pallas_call | solution.py:667
  167.2 88.9 %merge.1 = (bf16[768,2048]{1,0:T(8,128)(2,1)}, f32[768,2048]{1,0:T(8,128)}, f32[768,2]{1,0:T(8,128)}, bf16[768,2048]{1,0:T(8,128)(2,1)}) custom-call(bf16[768,2048]{1,0:T(8,128)(2,1)} %get-tuple-element.60.part_ref, bf16[768,2048]{1,0:T(8,128)(2,1)} %all-gather.4.cloned.1.call-done.tok_ref, bf16[768,2048]{1,0:T(8,128)(2,1)} %get-tuple-element.61.far_cot.cot_ref, ...), custom_call_target="tpu_custom_call" | custom-call | flops 1000000 | bytes 1000000 | tf_op jit(solution)/shard_map/merge/pallas_call | solution.py:1365
  256.2 41.1 %feed.1 = (bf16[768,2048]{1,0:T(8,128)(2,1)}, bf16[768,4096]{1,0:T(8,128)(2,1)}, bf16[2048,2048]{1,0:T(8,128)(2,1)}, bf16[2048,4096]{1,0:T(8,128)(2,1)}) custom-call(bf16[768,2048]{1,0:T(8,128)(2,1)} %get-tuple-element.62.inner_ref, bf16[768,2048]{1,0:T(8,128)(2,1)} %get-tuple-element.61.far_cot.cot_ref, bf16[2048,4096]{1,0:T(8,128)(2,1)} %reshape.55.w_ref, ...), custom_call_target="tpu_custom_call" | custom-call | flops 38654705664 | bytes 56623104 | tf_op jit(solution)/shard_map/feed/pallas_call | solution.py:1123
  297.3 20.0 %convolution_convert_fusion.part_ref = bf16[768,2048]{1,0:T(8,128)(2,1)} fusion(bf16[768,4096]{1,0:T(8,128)(2,1)} %get-tuple-element.71, bf16[2048,4096]{1,0:T(8,128)(2,1)} %reshape.55.w_ref), kind=kOutput, calls=%fused_computation | convolution fusion | flops 12886474752 | bytes 26214400 | tf_op jit(solution)/shard_map/dot_general | solution.py:1745
  317.3 98.4 %norm_back.1 = (bf16[768,2048]{1,0:T(8,128)(2,1)}, bf16[768,2048]{1,0:T(8,128)(2,1)}, bf16[512,2048]{1,0:T(8,128)(2,1)}) custom-call(bf16[768,2048]{1,0:T(8,128)(2,1)} %convolution_convert_fusion.part_ref, bf16[768,2048]{1,0:T(8,128)(2,1)} %get-tuple-element.61.far_cot.cot_ref, f32[768,2]{1,0:T(8,128)} %get-tuple-element.72.stat_ref, ...), custom_call_target="tpu_custom_call" | custom-call | flops 1000000 | bytes 1000000 | tf_op jit(solution)/shard_map/norm_back/pallas_call | solution.py:1454
  415.7 6.6 mixed_grad.1
  422.3 99.0 %attend_back_far.1 = (f32[768,512]{1,0:T(8,128)}, f32[768,512]{1,0:T(8,128)}, f32[768,512]{1,0:T(8,128)}, bf16[768,512]{1,0:T(8,128)(2,1)}, bf16[512,2048]{1,0:T(8,128)(2,1)}) custom-call(bf16[768,640]{1,0:T(8,128)(2,1)} %get-tuple-element.79.g_ref, bf16[6144,512]{1,0:T(8,128)(2,1)} %all-gather.6.cloned.1.call-done.far_q_ref, ...), custom_call_target="tpu_custom_call" | custom-call | flops 1000000 | bytes 1000000 | tf_op jit(solution)/shard_map/attend_back_far/pallas_call | solution.py:852
  521.4 12.1 %unrotate.1 = (bf16[768,1536]{1,0:T(8,128)(2,1)}, bf16[6144,512]{1,0:T(8,128)(2,1)}) custom-call(f32[768,512]{1,0:T(8,128)} %get-tuple-element.85.dq_ref, f32[768,512]{1,0:T(8,128)} %get-tuple-element.86.dk_ref, f32[768,512]{1,0:T(8,128)} %get-tuple-element.87.dv_ref, f32[768,128]{1,0:T(8,128)} %get-tuple-element.109.cos_ref, ...), custom_call_target="tpu_custom_call" | custom-call | flops 4831838208 | bytes 11010048 | tf_op jit(solution)/shard_map/unrotate/pallas_call | solution.py:1509
  533.5 3.1 convolution_convert_fusion.1.refs_1_
  536.7 135.6 %unproject.1 = (f32[768,512]{1,0:T(8,128)}, bf16[3072,512]{1,0:T(8,128)(2,1)}, bf16[256,2048]{1,0:T(8,128)(2,1)}, bf16[1024,2048]{1,0:T(8,128)(2,1)}) custom-call(bf16[768,1536]{1,0:T(8,128)(2,1)} %get-tuple-element.89.dproj_ref, bf16[768,2048]{1,0:T(8,128)(2,1)} %all-gather.4.cloned.1.call-done.tok_ref, f32[768,2]{1,0:T(8,128)} %get-tuple-element.90.stat_ref, ...), custom_call_target="tpu_custom_call" | custom-call | flops 1000000 | bytes 1000000 | tf_op jit(solution)/shard_map/unproject/pallas_call | solution.py:1649
  672.4 0.5 collective-permute-start
  672.9 0.1 collective-permute-start.1
  673.0 20.4 %weave.1 = f32[2048,2,2048]{2,1,0:T(2,128)} custom-call(bf16[2048,4096]{1,0:T(8,128)(2,1)} %all-reduce.2.cloned.1.call-done.sum_ref), custom_call_target="tpu_custom_call" | custom-call | flops 8388608 | bytes 50331648 | tf_op jit(solution)/shard_map/weave/pallas_call | solution.py:1152
  693.4 1.6 copy-done.1
  695.0 18.0 %join.1 = (f32[6144,512]{1,0:T(8,128)}, f32[512,2048]{1,0:T(8,128)}, f32[2048,2048]{1,0:T(8,128)}) custom-call(s32[1]{0:T(128)} %bitcast.6.core_ref, bf16[3072,512]{1,0:T(8,128)(2,1)} %get-tuple-element.95.refs_0_, bf16[256,2048]{1,0:T(8,128)(2,1)} %get-tuple-element.96.refs_1_, bf16[1024,2048]{1,0:T(8,128)(2,1)} %get-tuple-element.97.refs_2_, ...), custom_call_target="tpu_custom_call" | custom-call | flops 8388608 | bytes 50331648 | tf_op jit(solution)/shard_map/join/pallas_call | solution.py:509
  713.0 0.9 copy.22
  713.9 1.1 copy.23
  (28 shorter events, 0.5 us)
Async XLA Ops:
  7.2 68.6 %all-gather.4.cloned.1.call-start = ((), (), s32[]{:S(2)}) async-start(), calls=%async_computation | async-start | bytes 3932160 | tf_op jit(solution)/shard_map/all_gather | solution.py:1689
  7.9 289.4 %all-gather.6.cloned.1.call-start = ((), (), s32[]{:S(2)}) async-start(), calls=%async_computation.1 | async-start | bytes 7077888 | tf_op jit(solution)/shard_map/all_gather | solution.py:1732
  50.5 37.1 %copy-start.5 = (s32[8,768]{1,0:T(8,128)}, s32[8,768]{1,0:T(8,128)S(1)}, u32[]{:S(2)}) copy-start(s32[8,768]{1,0:T(8,128)S(1)} %bitcast_maximum_fusion.begin_ref) | copy-start | bytes 73732
  167.2 505.8 %all-reduce.2.cloned.1.call-start = ((), (), s32[]{:S(2)}) async-start(), calls=%async_computation.2 | async-start | bytes 33554432 | tf_op jit(solution)/shard_map/psum | solution.py:1743
  521.4 12.1 %copy-start = (bf16[768,2048]{1,0:T(8,128)(2,1)S(1)}, bf16[768,2048]{1,0:T(8,128)(2,1)}, u32[]{:S(2)}) copy-start(bf16[768,2048]{1,0:T(8,128)(2,1)} %get-tuple-element.76.branch_ref) | copy-start | bytes 9437188
  521.4 12.1 %copy-start.4 = (bf16[768,512]{1,0:T(8,128)(2,1)S(1)}, bf16[768,512]{1,0:T(8,128)(2,1)}, u32[]{:S(2)}) copy-start(bf16[768,512]{1,0:T(8,128)(2,1)} %get-tuple-element.92) | copy-start | bytes 2359300
  672.3 21.0 %collective-permute-start.2 = (bf16[1024,2048]{1,0:T(8,128)(2,1)}, bf16[1024,2048]{1,0:T(8,128)(2,1)}, u32[]{:S(2)}, u32[]{:S(2)}) collective-permute-start(bf16[1024,2048]{1,0:T(8,128)(2,1)} %get-tuple-element.97.refs_2_), channel_id=1, source_target_pairs={{0,4},{4,0},{8,12},{12,8},{16,20},{20,16},{24,28},{28,24},{1,5},{5... | collective-permute-start | bytes 12582920 | tf_op jit(solution)/shard_map/ppermute | solution.py:1770
  672.4 20.9 %collective-permute-start = (bf16[3072,512]{1,0:T(8,128)(2,1)}, bf16[3072,512]{1,0:T(8,128)(2,1)S(1)}, u32[]{:S(2)}, u32[]{:S(2)}) collective-permute-start(bf16[3072,512]{1,0:T(8,128)(2,1)} %get-tuple-element.95.refs_0_), channel_id=1, source_target_pairs={{0,4},{4,0},{8,12},{12,8},{16,20},{20,16},{24,28},{28,24},{1,5},{5... | collective-permute-start | bytes 9437192 | tf_op jit(solution)/shard_map/ppermute | solution.py:1770
  672.9 20.4 %collective-permute-start.1 = (bf16[256,2048]{1,0:T(8,128)(2,1)}, bf16[256,2048]{1,0:T(8,128)(2,1)}, u32[]{:S(2)}, u32[]{:S(2)}) collective-permute-start(bf16[256,2048]{1,0:T(8,128)(2,1)} %get-tuple-element.96.refs_1_), channel_id=1, source_target_pairs={{0,4},{4,0},{8,12},{12,8},{16,20},{20,16},{24,28},{28,24},{1,5},{5... | collective-permute-start | bytes 3145736 | tf_op jit(solution)/shard_map/ppermute | solution.py:1770
  693.3 1.6 copy-start.1
  695.0 18.0 %copy-start.3 = (bf16[768,512]{1,0:T(8,128)(2,1)S(1)}, bf16[768,512]{1,0:T(8,128)(2,1)}, u32[]{:S(2)}) copy-start(bf16[768,512]{1,0:T(8,128)(2,1)} %get-tuple-element.117) | copy-start | bytes 2359300
  695.0 18.9 %copy-start.2 = (f32[768,512]{1,0:T(8,128)S(1)}, f32[768,512]{1,0:T(8,128)}, u32[]{:S(2)}) copy-start(f32[768,512]{1,0:T(8,128)} %get-tuple-element.118) | copy-start | bytes 4718596
Sparse Core Ops, SparseCore 0:
  9.6 66.1 all-gather.3
  167.3 53.3 all-gather.5
  297.4 312.6 all-reduce.1

commit v9 on v8

--- a/solution.py
+++ b/solution.py
@@ -238,10 +238,6 @@
         return self.me + on(1, 4, 5, 7) * core + on(2, 4, 6, 7) * x + on(3, 5, 6, 7) * y
 
     def advance(self, step):
-        @pl.when(step == 0)
-        def _():
-            self.start(0, 1, 3, 2, 4)
-
         @pl.when(step == 1)
         def _():
             self.arrived(0)
@@ -297,6 +293,7 @@
         second = rows // 4
         self.to = (1 - 2 * core, 2 - 4 * x, 4 - 8 * y)
         self.mine, self.other = core * self.half, (1 - core) * self.half
+        self.offset = 0 if local is not None else self.mine
         self.keep1 = (x * self.eighth, second + y * self.eighth)
         self.give1 = ((1 - x) * self.eighth, second + (1 - y) * self.eighth)
         self.keep2 = (self.keep1[0] + y * self.last, self.keep1[1] + x * self.last)
@@ -344,21 +341,23 @@
 
     def begin(self):
         self.copy(0).start()
-        self.read().start()
+        if self.local is not None:
+            self.read().start()
 
     def reduce(self, k):
         half, eighth, last, land = self.half, self.eighth, self.last, self.land
         i = k % 2
         if k == 0:
-            self.read().wait()
+            if self.local is not None:
+                self.read().wait()
             self.copy(0).wait_recv()
         if k < 2:
             at = self.give1[i]
-            self.add(land, at, self.near, at, at, eighth)
+            self.add(land, at, self.near, self.offset + at, at, eighth)
             self.copy(1 + i).start()
         elif k < 4:
             at = self.keep1[i]
-            self.add(land, at, self.near, at, at, eighth)
+            self.add(land, at, self.near, self.offset + at, at, eighth)
         elif k < 6:
             self.copy(1 + i).wait_recv()
             landed = half + i * eighth - self.keep1[i]
@@ -530,8 +529,8 @@
 
 
 def attend_far_kernel(
-    heads, n, q_ref, own_ref, begin_ref, cot_ref, w_ref,
-    raw_ref, mixed_ref, lse_ref, keep_ref, full_ref, part_ref,
+    heads, n, tok_ref, in_ref, cos_ref, sin_ref, begin_ref, cot_ref, w_ref,
+    inner_ref, stat_ref, q_ref, raw_ref, mixed_ref, lse_ref, keep_ref, full_ref, part_ref,
     pair_ref, high_ref, total_ref, acc_ref, s_ref, send, recv, zsend, zrecv, keep_sem,
 ):
     rows = q_ref.shape[0]
@@ -551,12 +550,40 @@
     def _():
         pl.semaphore_signal(barrier, inc=1, device_id={"tp": at + 1}, device_id_type=MESH)
 
-    pair_ref[pl.ds(pl.multiple_of(me * rows, 16), rows), :] = own_ref[...]
+    def project(rows_at, part):
+        out = jnp.dot(inner_ref[rows_at, :], in_ref[part], preferred_element_type=F32)
+        if part == 2:
+            return out.astype(BF16)
+        cosine, sine = cos_ref[rows_at, :], sin_ref[rows_at, :]
+        pieces = []
+        for h in range(heads):
+            piece = out[:, h * HD : (h + 1) * HD]
+            pieces.append((piece * cosine + pltpu.roll(piece, HD // 2, 1) * sine).astype(BF16))
+        return jnp.concatenate(pieces, axis=1)
+
+    def own_pairs(part):
+        half = rows // 2
+        here = slice(part * half, (part + 1) * half)
+        x = tok_ref[here, :].astype(F32)
+        mean = jnp.mean(x, axis=1, keepdims=True)
+        center = x - mean
+        inverse = lax.rsqrt(jnp.mean(center * center, axis=1, keepdims=True) + EPS)
+        stat_ref[here, :] = jnp.concatenate([mean, inverse], axis=1)
+        inner_ref[here, :] = (center * inverse).astype(BF16)
+        place = pl.ds(pl.multiple_of(me * rows + part * half, 16), half)
+        pair_ref[place, :span] = project(here, 1)
+        pair_ref[place, span:] = project(here, 2)
+
+    own_pairs(0)
     full_ref[:, pl.ds(pl.multiple_of(at * shard, 128), shard)] = cot_ref[...]
     high_ref[...] = jnp.full_like(high_ref, NEG)
     total_ref[...] = jnp.zeros_like(total_ref)
     acc_ref[...] = jnp.zeros_like(acc_ref)
     pl.semaphore_wait(barrier, jnp.where((at > 0) & (at < n - 1), 5, 4))
+    cube.start(1, 4)
+    own_pairs(1)
+    cube.start(3, 2, 0)
+    q_ref[...] = project(slice(0, rows), 0)
 
     def pass_on(right, s, k):
         place = full_ref.at[:, pl.ds(pl.multiple_of(s * shard, 128), shard)]
@@ -659,16 +686,18 @@
             pass_on(False, at + k, k).wait_send()
 
 
-def attend_far(query, pairs, begin, cot, weight, heads, n):
-    rows = query.shape[0]
-    width = weight.shape[1]
+def attend_far(tok_full, in_weight, cosine, sine, begin, cot, weight, heads, n):
+    rows, width = tok_full.shape
     span = heads * HD
     vmem = pl.BlockSpec(memory_space=pltpu.VMEM)
     return pl.pallas_call(
         functools.partial(attend_far_kernel, heads, n),
-        in_specs=[vmem] * 5,
-        out_specs=[vmem] * 3 + [pl.BlockSpec(memory_space=pl.ANY)] + [vmem] * 2,
+        in_specs=[vmem] * 7,
+        out_specs=[vmem] * 6 + [pl.BlockSpec(memory_space=pl.ANY)] + [vmem] * 2,
         out_shape=[
+            jax.ShapeDtypeStruct((rows, width), BF16),
+            jax.ShapeDtypeStruct((rows, 2), F32),
+            jax.ShapeDtypeStruct((rows, span), BF16),
             jax.ShapeDtypeStruct((rows, span), F32),
             jax.ShapeDtypeStruct((rows, span), BF16),
             jax.ShapeDtypeStruct((heads, rows), F32),
@@ -691,7 +720,7 @@
         compiler_params=params(58, collective_id=2, has_side_effects=True),
         cost_estimate=cost(1e6, 1e6),
         name="attend_far",
-    )(query, pairs, begin, cot, weight)
+    )(tok_full, in_weight, cosine, sine, begin, cot, weight)
 
 
 def attend_back_far_kernel(
@@ -751,6 +780,8 @@
         )
 
     own = pl.ds(pl.multiple_of(me * rows, 16), rows)
+
+    cube.start(0, 1, 3, 2, 4)
 
     def turn(step, carry):
         cube.advance(step)
@@ -1524,18 +1555,19 @@
     )(dq, dk, dv, cosine, sine, inner)
 
 
-def unproject_kernel(heads, n, cube, dproj_ref, tok_ref, stat_ref, w_ref, branch_ref, *refs):
+def unproject_kernel(heads, n, cube, *refs):
     sums, rest = [], None
     if cube:
-        in_ref, og_ref, mid_ref, out_ref, in_out, og_out, down_out = refs[:7]
-        part_ref, mine_ref, land_ref, sums_ref, far_ref, send, recv, ssend, srecv = refs[7:16]
-        for own, out, at in ((in_ref, in_out, 18), (og_ref, og_out, 23)):
-            sums.append(CubeSum(own, *refs[at : at + 5], out=out))
-        rest = LastGather(mid_ref, down_out, *refs[28:31])
-        mine_branch, branch_sem = refs[16:18]
+        dq_ref, dk_ref, dv_ref, cos_ref, sin_ref, inner_ref, mixed_ref = refs[:7]
+        branch_ref, mid_ref, tok_ref, stat_ref, w_ref = refs[7:12]
+        out_ref, in_out, og_out, down_out, dproj_ref, in_ref, og_ref = refs[12:19]
+        part_ref, mine_ref, land_ref, sums_ref, far_ref, send, recv, ssend, srecv = refs[19:28]
+        for own, out, at in ((in_ref, in_out, 28), (og_ref, og_out, 31)):
+            sums.append(CubeSum(own, own, *refs[at : at + 3], None, out=out))
+        rest = LastGather(mid_ref, down_out, *refs[34:37])
     else:
-        out_ref, part_ref, mine_ref, land_ref, sums_ref, far_ref = refs[:6]
-        send, recv, ssend, srecv, mine_branch, branch_sem = refs[6:12]
+        dproj_ref, branch_ref, tok_ref, stat_ref, w_ref, out_ref = refs[:6]
+        part_ref, mine_ref, land_ref, sums_ref, far_ref, send, recv, ssend, srecv = refs[6:15]
 
     def reduce(*pieces):
         for k in pieces:
@@ -1558,10 +1590,26 @@
     if cube:
         sums[0].signal(barrier)
     pl.semaphore_wait(barrier, n - 1 + (3 if cube else 0))
-    for item in sums:
-        item.begin()
     if cube:
         rest.begin()
+        og_ref[...] = lax.dot_general(
+            mixed_ref[...], branch_ref[...], TN, preferred_element_type=F32
+        ).astype(BF16)
+        sums[1].begin()
+        for part, ref in enumerate((dq_ref, dk_ref, dv_ref)):
+            for h in range(heads):
+                piece = ref[:, h * HD : (h + 1) * HD]
+                if part < 2:
+                    piece = (
+                        piece * cos_ref[...] - pltpu.roll(piece, HD // 2, 1) * sin_ref[...]
+                    )
+                at_column = part * span + h * HD
+                dproj_ref[:, at_column : at_column + HD] = piece.astype(BF16)
+            in_ref[part * width : (part + 1) * width, :] = lax.dot_general(
+                inner_ref[...], dproj_ref[:, part * span : (part + 1) * span], TN,
+                preferred_element_type=F32,
+            ).astype(BF16)
+        sums[0].begin()
     block = 256
     count = rows // block
 
@@ -1583,8 +1631,6 @@
         )
 
     own = pl.ds(pl.multiple_of(at * shard, 128), shard)
-    branch_read = pltpu.make_async_copy(branch_ref.at[:, own], mine_branch, branch_sem.at[0])
-    branch_read.start()
     for i in range(count):
         place = pl.ds(i * block, block)
         total = None
@@ -1613,7 +1659,6 @@
         totals(o).wait_recv()
         total = total + far_ref[o - 1]
     mine_ref[...] = total
-    branch_read.wait()
     for i in range(count):
         place = pl.ds(i * block, block)
         spread = jnp.concatenate(
@@ -1625,7 +1670,7 @@
             total = total + land_ref[o - 1, place].astype(F32)
         inverse = stat_ref[place, 1:2]
         normed = (tok_ref[place, own].astype(F32) - stat_ref[place, 0:1]) * inverse
-        out_ref[place, :] = mine_branch[place, :].astype(F32) + inverse * (
+        out_ref[place, :] = branch_ref[place, own].astype(F32) + inverse * (
             total - spread[:, 0:1] - normed * spread[:, 1:2]
         )
     gather(2)
@@ -1637,25 +1682,28 @@
             term(o, i).wait_send()
 
 
-def unproject(dproj, tok_full, stat, weight, branch, heads, n, grads, mids):
+def unproject(cube, operands, tok_full, stat, weight, heads, n):
     rows, width = tok_full.shape
     shard = width // n
+    span = heads * HD
     vmem = pl.BlockSpec(memory_space=pltpu.VMEM)
-    extra = []
-    for grad in grads:
-        extra += sum_scratch(grad.shape)
-    for _ in mids:
+    shapes = [(3 * width, span), (span, width)] if cube else []
+    more_out, early, extra = [], [], []
+    if cube:
+        mid = operands[-1]
+        more_out = [jax.ShapeDtypeStruct((high // 2, wide), BF16) for high, wide in shapes]
+        more_out.append(jax.ShapeDtypeStruct((2 * mid.shape[0], mid.shape[1]), BF16))
+        early = [pltpu.VMEM(shape, BF16) for shape in [(rows, 3 * span)] + shapes]
+        for shape in shapes:
+            extra += sum_scratch(shape)[1:4]
         extra += [pltpu.SemaphoreType.DMA((2,))] * 3
     return pl.pallas_call(
-        functools.partial(unproject_kernel, heads, n, len(grads) > 0),
-        in_specs=[vmem] * 4
-        + [pl.BlockSpec(memory_space=pl.ANY)] * (1 + len(grads))
-        + [vmem] * len(mids),
-        out_specs=[vmem] * (1 + len(grads)) + [pl.BlockSpec(memory_space=pl.ANY)] * len(mids),
-        out_shape=[jax.ShapeDtypeStruct((rows, shard), F32)]
-        + [jax.ShapeDtypeStruct((grad.shape[0] // 2, grad.shape[1]), BF16) for grad in grads]
-        + [jax.ShapeDtypeStruct((2 * mid.shape[0], mid.shape[1]), BF16) for mid in mids],
-        scratch_shapes=[
+        functools.partial(unproject_kernel, heads, n, cube),
+        in_specs=[vmem] * (len(operands) + 3),
+        out_specs=[vmem] * (1 + len(shapes)) + [pl.BlockSpec(memory_space=pl.ANY)] * int(cube),
+        out_shape=[jax.ShapeDtypeStruct((rows, shard), F32)] + more_out,
+        scratch_shapes=early
+        + [
             pltpu.VMEM((rows, width), BF16),
             pltpu.VMEM((8, rows), F32),
             pltpu.VMEM((n - 1, rows, shard), BF16),
@@ -1665,14 +1713,12 @@
             pltpu.SemaphoreType.DMA((n - 1, rows // 256)),
             pltpu.SemaphoreType.DMA((n - 1,)),
             pltpu.SemaphoreType.DMA((n - 1,)),
-            pltpu.VMEM((rows, shard), BF16),
-            pltpu.SemaphoreType.DMA((1,)),
         ]
         + extra,
-        compiler_params=params(60, collective_id=4, has_side_effects=True),
+        compiler_params=params(61, collective_id=4, has_side_effects=True),
         cost_estimate=cost(1e6, 1e6),
         name="unproject",
-    )(dproj, tok_full, stat, weight, branch, *grads, *mids)
+    )(*operands, tok_full, stat, weight)
 
 
 def per_device(tokens, segment_ids, in_weight, out_weight, gate_up_weight, down_weight, cotangent):
@@ -1718,12 +1764,12 @@
     ).astype(jnp.int32)
     begin = lax.dynamic_slice_in_dim(blocks, me, 1, 0)
     all_begin = all_begin[None, :]
-    inner1, stat1, query, pairs = project(tok_full, in_w, cosine, sine, heads)
     if cube:
-        raw, mixed, lse, all_pairs, cot_full, out_part = attend_far(
-            query, pairs, begin, cotangent, out_weight, heads, tp_size
+        inner1, stat1, query, raw, mixed, lse, all_pairs, cot_full, out_part = attend_far(
+            tok_full, in_w, cosine, sine, begin, cotangent, out_weight, heads, tp_size
         )
     else:
+        inner1, stat1, query, pairs = project(tok_full, in_w, cosine, sine, heads)
         all_pairs = lax.all_gather(pairs, "ctx", axis=0, tiled=True)
         cot_full = gather(cotangent)
         raw, mixed, lse = attend(key_info, query, all_pairs, begin, heads)
@@ -1747,7 +1793,6 @@
         grad_part, cot_full, resid1, stat2, hidden, down_weight, tp_size,
         [down_grad] if cube else [],
     )
-    out_grad = lax.dot_general(mixed, branch_grad, TN, preferred_element_type=F32).astype(BF16)
     grad_mixed, delta = mixed_grad(branch_grad, out_weight, raw, lse, heads)
     if cube:
         dq, dk, dv, layer_out, mid = attend_back_far(
@@ -1760,10 +1805,10 @@
         dq = query_grad(key_info, query, grad_mixed, lse, delta, all_pairs, begin, heads)
         dk, dv = key_grad(query_info, pairs, all_query, all_grad, all_begin, heads)
 
-    dproj, in_grad = unrotate(dq, dk, dv, cosine, sine, inner1, heads)
     if cube:
         tokens_grad, *halves = unproject(
-            dproj, tok_full, stat1, in_w, branch_grad, heads, tp_size, [in_grad, out_grad], [mid]
+            True, [dq, dk, dv, cosine, sine, inner1, mixed, branch_grad, mid],
+            tok_full, stat1, in_w, heads, tp_size,
         )
         swap = [(i, i + 1 - 2 * (i % 2)) for i in range(CUBE)]
         core = (me % 2)[None]
@@ -1771,12 +1816,16 @@
         *far, gu_grad = lax.optimization_barrier((*far, weave(gu_grad, BLOCK)))
         in_grad, out_grad, down_grad = join(core, halves, far)
     else:
+        out_grad = lax.dot_general(
+            mixed, branch_grad, TN, preferred_element_type=F32
+        ).astype(BF16)
+        dproj, in_grad = unrotate(dq, dk, dv, cosine, sine, inner1, heads)
         in_grad, out_grad, down_grad, gu_grad = lax.optimization_barrier(
             (in_grad, out_grad, down_grad, gu_grad)
         )
         in_grad, out_grad = lax.psum((in_grad, out_grad), "ctx")
         (tokens_grad,) = unproject(
-            dproj, tok_full, stat1, in_w, branch_grad, heads, tp_size, [], []
+            False, [dproj, branch_grad], tok_full, stat1, in_w, heads, tp_size
         )
         in_grad, out_grad, down_grad = widen(in_grad), out_grad.astype(F32), widen(down_grad)
         gu_grad = weave(gu_grad, BLOCK)

time: 732 us -> 721 us (0.985)
    pallas_call x3 -> x1, Pallas kernels: 159 us -> 153 us  [unproject(): pl.pallas_call(functools.partial(unproject_kernel, heads, n, cube), in_sp...]
  transfers between devices with their start and end apart: 6 -> 6, of which waited for: 1 -> 1; matrix products, arithmetic and copies ran while one was open for 8% -> 7% of each run, Pallas kernels for 70% -> 71%
where the time goes in v9:
time: 721 us; the launch traced here: 718 us
  Pallas kernels  610 us (85%)
  local copies, waits for them, and re-layouts  33 us (5%)
  waiting for transfers between devices  26 us (4%)
  matrix products  20.1 us (3%)
  between operations  14 us (2%)
  blocking collectives  10.5 us (1%)
    pallas_call x1, Pallas kernels, unproject(): pl.pallas_call(functools.partial(unproject_kernel, heads, n, cube), in_sp...  153 us
    pallas_call x1, Pallas kernels, norm_back(): pl.pallas_call(functools.partial(norm_back_kernel, n, sub, len(grads) > 0...  101 us
    pallas_call x1, Pallas kernels, attend_back_far(): pl.pallas_call(functools.partial(attend_back_far_kernel, heads, n), in_sp...  94.8 us
    pallas_call x1, Pallas kernels, merge(): pl.pallas_call(functools.partial(merge_kernel, n, sub), in_specs=[vmem, v...  89.8 us
    pallas_call x1, Pallas kernels, attend_far(): pl.pallas_call(functools.partial(attend_far_kernel, heads, n), in_specs=[...  84.9 us
    pallas_call x1, Pallas kernels, feed(): pl.pallas_call(feed_kernel, grid=(units // block,), in_specs=[whole, whol...  41.1 us
    reshape x1, local copies, waits for them, and re-layouts, per_device(): gu_w = gu_w.reshape(width, 2 * hidden_local)  27.8 us
    all_gather x1, waiting for transfers between devices, gather(): return lax.all_gather(local, 'tp', axis=axis, tiled=True)  25.3 us
  transfers between devices with their start and end apart: 6, of which 1 were waited for; matrix products, arithmetic and copies ran while one was open for 7% of the time, Pallas kernels for 71%

profile of v9, /device:TPU:0, one launch (start us, length us, event | category | flops | bytes accessed | tf_op | source)
XLA Modules:
  0.0 717.6 jit_solution(230701761447167801)
XLA Ops:
  7.2 0.7 all-gather.4.cloned.1.call-update
  7.9 0.7 reshape.60
  8.6 10.5 %all-gather = s32[8,1,768]{2,1,0:T(1,128)S(1)} all-gather(s32[1,1,768]{2,1,0:T(1,128)S(1)} %reshape.60), channel_id=1, replica_groups=mesh['ctx'=8,'tp'=4] {'ctx'}, dimensions={0}, use_global_device_ids=true | all-gather | bytes 27648 | tf_op jit(solution)/shard_map/all_gather | solution.py:1745
  19.1 0.1 slice_compare_fusion
  19.2 0.1 add_select_fusion
  19.3 0.3 reduce-window.9
  19.6 0.1 slice.19
  19.6 0.1 reduce-window.12
  19.7 0.1 slice_reduce_fusion
  19.8 0.1 reshape.57
  19.9 0.1 copy.18
  20.0 27.8 %reshape.55.w_ref = bf16[2048,4096]{1,0:T(8,128)(2,1)} reshape(bf16[2048,4,2,512]{3,2,1,0:T(2,128)(2,1)} %bitcast.19) | data formatting | bytes 33554432 | tf_op jit(solution)/shard_map/reshape | solution.py:1743
  47.8 1.4 fusion
  49.2 1.1 pad_maximum_fusion
  50.4 0.1 bitcast_maximum_fusion.begin_ref
  50.4 25.3 %all-gather.4.cloned.1.call-done.tok_ref.refs_9_ = bf16[768,2048]{1,0:T(8,128)(2,1)} async-done(((bf16[768,512]{1,0:T(8,128)(2,1)}), bf16[768,2048]{1,0:T(8,128)(2,1)}) %all-gather.4.cloned.1.call-update) | async-done | bytes 3145744 | tf_op jit(solution)/shard_map/all_gather | solution.py:1735
  75.8 0.6 constant_dynamic-slice_fusion.begin_ref
  76.3 84.9 %attend_far.1 = (bf16[768,2048]{1,0:T(8,128)(2,1)}, f32[768,2]{1,0:T(8,128)}, bf16[768,512]{1,0:T(8,128)(2,1)}, f32[768,512]{1,0:T(8,128)}, bf16[768,512]{1,0:T(...) custom-call(bf16[768,2048]{1,0:T(8,128)(2,1)} %all-gather.4.cloned.1, ...), custom_call_target="tpu_custom_call" | custom-call | flops 1000000 | bytes 1000000 | tf_op jit(solution)/shard_map/attend_far/pallas_call | solution.py:693
  161.3 89.8 %merge.1 = (bf16[768,2048]{1,0:T(8,128)(2,1)}, f32[768,2048]{1,0:T(8,128)}, f32[768,2]{1,0:T(8,128)}, bf16[768,2048]{1,0:T(8,128)(2,1)}) custom-call(bf16[768,2048]{1,0:T(8,128)(2,1)} %get-tuple-element.55.part_ref, bf16[768,2048]{1,0:T(8,128)(2,1)} %all-gather.4.cloned.1.call-done.tok_ref.refs_9_, bf16[768,2048]{1,0:T(8,128)(2,1)} %get-tuple-element.56.far_cot.cot_ref, ...), custom_call_target="tpu_custom_call" | custom-call | flops 1000000 | bytes 1000000 | tf_op jit(solution)/shard_map/merge/pallas_call | solution.py:1396
  251.1 41.1 %feed.1 = (bf16[768,2048]{1,0:T(8,128)(2,1)}, bf16[768,4096]{1,0:T(8,128)(2,1)}, bf16[2048,2048]{1,0:T(8,128)(2,1)}, bf16[2048,4096]{1,0:T(8,128)(2,1)}) custom-call(bf16[768,2048]{1,0:T(8,128)(2,1)} %get-tuple-element.57.inner_ref, bf16[768,2048]{1,0:T(8,128)(2,1)} %get-tuple-element.56.far_cot.cot_ref, bf16[2048,4096]{1,0:T(8,128)(2,1)} %reshape.55.w_ref, ...), custom_call_target="tpu_custom_call" | custom-call | flops 38654705664 | bytes 56623104 | tf_op jit(solution)/shard_map/feed/pallas_call | solution.py:1154
  292.3 20.1 %convolution_convert_fusion.part_ref = bf16[768,2048]{1,0:T(8,128)(2,1)} fusion(bf16[768,4096]{1,0:T(8,128)(2,1)} %get-tuple-element.67, bf16[2048,4096]{1,0:T(8,128)(2,1)} %reshape.55.w_ref), kind=kOutput, calls=%fused_computation | convolution fusion | flops 12886474752 | bytes 26214400 | tf_op jit(solution)/shard_map/dot_general | solution.py:1791
  312.4 101.1 %norm_back.1 = (bf16[768,2048]{1,0:T(8,128)(2,1)}, bf16[768,2048]{1,0:T(8,128)(2,1)}, bf16[512,2048]{1,0:T(8,128)(2,1)}) custom-call(bf16[768,2048]{1,0:T(8,128)(2,1)} %convolution_convert_fusion.part_ref, bf16[768,2048]{1,0:T(8,128)(2,1)} %get-tuple-element.56.far_cot.cot_ref, f32[768,2]{1,0:T(8,128)} %get-tuple-element.68.stat_ref, ...), custom_call_target="tpu_custom_call" | custom-call | flops 1000000 | bytes 1000000 | tf_op jit(solution)/shard_map/norm_back/pallas_call | solution.py:1485
  413.6 6.8 mixed_grad.1
  420.4 94.8 %attend_back_far.1 = (f32[768,512]{1,0:T(8,128)}, f32[768,512]{1,0:T(8,128)}, f32[768,512]{1,0:T(8,128)}, bf16[768,512]{1,0:T(8,128)(2,1)}, bf16[512,2048]{1,0:T(8,128)(2,1)}) custom-call(bf16[768,640]{1,0:T(8,128)(2,1)} %get-tuple-element.75.g_ref, bf16[6144,512]{1,0:T(8,128)(2,1)} %all-gather.6.cloned.1.call-done.far_q_ref, ...), custom_call_target="tpu_custom_call" | custom-call | flops 1000000 | bytes 1000000 | tf_op jit(solution)/shard_map/attend_back_far/pallas_call | solution.py:883
  515.1 153.0 %unproject.1 = (f32[768,512]{1,0:T(8,128)}, bf16[3072,512]{1,0:T(8,128)(2,1)}, bf16[256,2048]{1,0:T(8,128)(2,1)}, bf16[1024,2048]{1,0:T(8,128)(2,1)}) custom-call(f32[768,512]{1,0:T(8,128)} %get-tuple-element.81.refs_0_, f32[768,512]{1,0:T(8,128)} %get-tuple-element.82.refs_1_, f32[768,512]{1,0:T(8,128)} %get-tuple-element.83.refs_2_, ...), custom_call_target="tpu_custom_call" | custom-call | flops 1000000 | bytes 1000000 | tf_op jit(solution)/shard_map/unproject/pallas_call | solution.py:1700
  668.2 0.5 collective-permute-start
  668.7 0.1 collective-permute-start.1
  668.8 20.4 %weave.1 = f32[2048,2,2048]{2,1,0:T(2,128)} custom-call(bf16[2048,4096]{1,0:T(8,128)(2,1)} %all-reduce.2.cloned.1.call-done.sum_ref), custom_call_target="tpu_custom_call" | custom-call | flops 8388608 | bytes 50331648 | tf_op jit(solution)/shard_map/weave/pallas_call | solution.py:1183
  689.2 1.6 copy-done
  690.8 18.0 %join.1 = (f32[6144,512]{1,0:T(8,128)}, f32[512,2048]{1,0:T(8,128)}, f32[2048,2048]{1,0:T(8,128)}) custom-call(s32[1]{0:T(128)} %bitcast.6.core_ref, bf16[3072,512]{1,0:T(8,128)(2,1)} %get-tuple-element.89.refs_0_, bf16[256,2048]{1,0:T(8,128)(2,1)} %get-tuple-element.90.refs_1_, bf16[1024,2048]{1,0:T(8,128)(2,1)} %get-tuple-element.91.refs_2_, ...), custom_call_target="tpu_custom_call" | custom-call | flops 8388608 | bytes 50331648 | tf_op jit(solution)/shard_map/join/pallas_call | solution.py:508
  708.8 0.9 copy.22
  709.7 1.1 copy.23
  (21 shorter events, 0.3 us)
Async XLA Ops:
  7.2 68.6 %all-gather.4.cloned.1.call-start = ((), (), s32[]{:S(2)}) async-start(), calls=%async_computation | async-start | bytes 3932160 | tf_op jit(solution)/shard_map/all_gather | solution.py:1735
  7.9 284.4 %all-gather.6.cloned.1.call-start = ((), (), s32[]{:S(2)}) async-start(), calls=%async_computation.1 | async-start | bytes 7077888 | tf_op jit(solution)/shard_map/all_gather | solution.py:1778
  50.4 110.8 %copy-start.3 = (s32[8,768]{1,0:T(8,128)}, s32[8,768]{1,0:T(8,128)S(1)}, u32[]{:S(2)}) copy-start(s32[8,768]{1,0:T(8,128)S(1)} %bitcast_maximum_fusion.begin_ref) | copy-start | bytes 73732
  161.3 507.5 %all-reduce.2.cloned.1.call-start = ((), (), s32[]{:S(2)}) async-start(), calls=%async_computation.2 | async-start | bytes 33554432 | tf_op jit(solution)/shard_map/psum | solution.py:1789
  668.1 21.0 %collective-permute-start.2 = (bf16[1024,2048]{1,0:T(8,128)(2,1)}, bf16[1024,2048]{1,0:T(8,128)(2,1)}, u32[]{:S(2)}, u32[]{:S(2)}) collective-permute-start(bf16[1024,2048]{1,0:T(8,128)(2,1)} %get-tuple-element.91.refs_2_), channel_id=1, source_target_pairs={{0,4},{4,0},{8,12},{12,8},{16,20},{20,16},{24,28},{28,24},{1,5},{5... | collective-permute-start | bytes 12582920 | tf_op jit(solution)/shard_map/ppermute | solution.py:1815
  668.2 20.9 %collective-permute-start = (bf16[3072,512]{1,0:T(8,128)(2,1)}, bf16[3072,512]{1,0:T(8,128)(2,1)S(1)}, u32[]{:S(2)}, u32[]{:S(2)}) collective-permute-start(bf16[3072,512]{1,0:T(8,128)(2,1)} %get-tuple-element.89.refs_0_), channel_id=1, source_target_pairs={{0,4},{4,0},{8,12},{12,8},{16,20},{20,16},{24,28},{28,24},{1,5},{5... | collective-permute-start | bytes 9437192 | tf_op jit(solution)/shard_map/ppermute | solution.py:1815
  668.7 20.4 %collective-permute-start.1 = (bf16[256,2048]{1,0:T(8,128)(2,1)}, bf16[256,2048]{1,0:T(8,128)(2,1)}, u32[]{:S(2)}, u32[]{:S(2)}) collective-permute-start(bf16[256,2048]{1,0:T(8,128)(2,1)} %get-tuple-element.90.refs_1_), channel_id=1, source_target_pairs={{0,4},{4,0},{8,12},{12,8},{16,20},{20,16},{24,28},{28,24},{1,5},{5... | collective-permute-start | bytes 3145736 | tf_op jit(solution)/shard_map/ppermute | solution.py:1815
  689.1 1.6 copy-start
  690.8 18.0 %copy-start.2 = (bf16[768,512]{1,0:T(8,128)(2,1)S(1)}, bf16[768,512]{1,0:T(8,128)(2,1)}, u32[]{:S(2)}) copy-start(bf16[768,512]{1,0:T(8,128)(2,1)} %get-tuple-element.111) | copy-start | bytes 2359300
  690.8 18.9 %copy-start.1 = (f32[768,512]{1,0:T(8,128)S(1)}, f32[768,512]{1,0:T(8,128)}, u32[]{:S(2)}) copy-start(f32[768,512]{1,0:T(8,128)} %get-tuple-element.112) | copy-start | bytes 4718596
Sparse Core Ops, SparseCore 0:
  9.6 66.1 all-gather.3
  161.4 53.7 all-gather.5
  292.4 327.2 all-reduce.1

commit v10 on v9

--- a/solution.py
+++ b/solution.py
@@ -528,19 +528,29 @@
     return jnp.where((key_place <= query_place) & (key_place >= begin), scores, NEG)
 
 
+FAR_STEPS = 8
+FAR_SENDS = 17
+
+
 def attend_far_kernel(
     heads, n, tok_ref, in_ref, cos_ref, sin_ref, begin_ref, cot_ref, w_ref,
-    inner_ref, stat_ref, q_ref, raw_ref, mixed_ref, lse_ref, keep_ref, full_ref, part_ref,
-    pair_ref, high_ref, total_ref, acc_ref, s_ref, send, recv, zsend, zrecv, keep_sem,
+    inner_ref, stat_ref, raw_ref, mixed_ref, lse_ref, keep_ref, full_ref, part_ref,
+    pair_ref, q_ref, high_ref, total_ref, acc_ref, s_ref,
+    guest_ref, guest_high, guest_total, guest_acc, guest_out, guest_stat, back_out, back_stat,
+    send, recv, zsend, zrecv,
 ):
     rows = q_ref.shape[0]
+    half = rows // 2
     span = heads * HD
     shard = cot_ref.shape[1]
     at = lax.axis_index("tp")
-    cube = Cube(pair_ref, send, recv)
-    me = cube.me
+    me = lax.axis_index("ctx")
+    core, x, y = me % 2, (me // 2) % 2, me // 4
+    to_core, to_x, to_y = 1 - 2 * core, 2 - 4 * x, 4 - 8 * y
+    diagonal = me + to_x + to_y
     barrier = pltpu.get_barrier_semaphore()
-    cube.signal(barrier)
+    for target in (me + to_core, me + to_x, me + to_y, diagonal):
+        pl.semaphore_signal(barrier, inc=1, device_id={"ctx": target}, device_id_type=MESH)
 
     @pl.when(at > 0)
     def _():
@@ -549,6 +559,35 @@
     @pl.when(at < n - 1)
     def _():
         pl.semaphore_signal(barrier, inc=1, device_id={"tp": at + 1}, device_id_type=MESH)
+
+    def block_rows(block):
+        return pl.ds(pl.multiple_of(block * rows, 16), rows)
+
+    def copy(k):
+        if k < 14:
+            block, part, parts, target = (
+                (me, 0, 1, to_core),
+                (me, 0, 2, to_x), (me, 1, 2, to_x),
+                (me, 0, 4, to_y), (me, 1, 4, to_y), (me, 2, 4, to_y), (me, 3, 4, to_y),
+                (me + to_x, 0, 1, to_core), (me + to_y, 0, 1, to_core),
+                (me + to_y, 0, 4, to_x), (me + to_y, 1, 4, to_x),
+                (me + to_y, 2, 4, to_x), (me + to_y, 3, 4, to_x),
+                (diagonal, 0, 1, to_core),
+            )[k]
+            size = rows // parts
+            src = dst = pair_ref.at[pl.ds(pl.multiple_of(block * rows + part * size, 16), size)]
+        else:
+            src, dst = (
+                (q_ref, guest_ref), (guest_out, back_out), (guest_stat, back_stat)
+            )[k - 14]
+            target = to_x + to_y
+        return pltpu.make_async_remote_copy(
+            src_ref=src, dst_ref=dst, send_sem=send.at[k], recv_sem=recv.at[k],
+            device_id={"ctx": me + target}, device_id_type=MESH,
+        )
+
+    def on_chip(*which):
+        return sum((me // 2 == chip).astype(jnp.int32) for chip in which) > 0
 
     def project(rows_at, part):
         out = jnp.dot(inner_ref[rows_at, :], in_ref[part], preferred_element_type=F32)
@@ -562,11 +601,10 @@
         return jnp.concatenate(pieces, axis=1)
 
     def own_pairs(part):
-        half = rows // 2
         here = slice(part * half, (part + 1) * half)
-        x = tok_ref[here, :].astype(F32)
-        mean = jnp.mean(x, axis=1, keepdims=True)
-        center = x - mean
+        value = tok_ref[here, :].astype(F32)
+        mean = jnp.mean(value, axis=1, keepdims=True)
+        center = value - mean
         inverse = lax.rsqrt(jnp.mean(center * center, axis=1, keepdims=True) + EPS)
         stat_ref[here, :] = jnp.concatenate([mean, inverse], axis=1)
         inner_ref[here, :] = (center * inverse).astype(BF16)
@@ -576,14 +614,37 @@
 
     own_pairs(0)
     full_ref[:, pl.ds(pl.multiple_of(at * shard, 128), shard)] = cot_ref[...]
-    high_ref[...] = jnp.full_like(high_ref, NEG)
-    total_ref[...] = jnp.zeros_like(total_ref)
-    acc_ref[...] = jnp.zeros_like(acc_ref)
-    pl.semaphore_wait(barrier, jnp.where((at > 0) & (at < n - 1), 5, 4))
-    cube.start(1, 4)
+    pl.semaphore_wait(barrier, jnp.where((at > 0) & (at < n - 1), 6, 5))
+
+    @pl.when(y == 0)
+    def _():
+        copy(3).start()
+        copy(4).start()
+
+    @pl.when(x == 0)
+    def _():
+        copy(1).start()
+
     own_pairs(1)
-    cube.start(3, 2, 0)
+
+    @pl.when(y == 0)
+    def _():
+        copy(5).start()
+        copy(6).start()
+
+    @pl.when(x == 0)
+    def _():
+        copy(2).start()
+
+    copy(0).start()
     q_ref[...] = project(slice(0, rows), 0)
+
+    @pl.when(on_chip(3))
+    def _():
+        copy(14).start()
+
+    keep_ref[:, : 2 * span] = pair_ref[block_rows(me), :]
+    keep_ref[:, 2 * span :] = q_ref[...]
 
     def pass_on(right, s, k):
         place = full_ref.at[:, pl.ds(pl.multiple_of(s * shard, 128), shard)]
@@ -612,54 +673,145 @@
             def _():
                 pass_on(False, at + k, k).start()
 
-    def keep(step):
-        place = pl.ds(pl.multiple_of(cube.block(step) * rows, 16), rows)
-        return pltpu.make_async_copy(pair_ref.at[place], keep_ref.at[place], keep_sem.at[step])
+    def clear(high, total, acc):
+        high[...] = jnp.full_like(high, NEG)
+        total[...] = jnp.zeros_like(total)
+        acc[...] = jnp.zeros_like(acc)
+
+    def attend_block(key_block, queries, query_block, high, total, acc):
+        place = block_rows(key_block)
+        begin = begin_ref[pl.ds(query_block, 1), :]
+
+        def score(h):
+            hs = slice(h * HD, (h + 1) * HD)
+            s = lax.dot_general(
+                pair_ref[place, hs], queries[:, hs], NT, preferred_element_type=F32
+            )
+            s_ref[h % 2] = hidden_scores(s, key_block, query_block, rows, begin)
+
+        def spread(h):
+            s = s_ref[h % 2]
+            old = high[h : h + 1, :]
+            new = jnp.maximum(old, jnp.max(s, axis=0, keepdims=True))
+            high[h : h + 1, :] = new
+            p = jnp.exp2(s * C2 - new * C2)
+            decay = jnp.exp2((old - new) * C2)
+            total[h : h + 1, :] = total[h : h + 1, :] * decay + jnp.sum(p, axis=0, keepdims=True)
+            acc[h] = acc[h] * decay + lax.dot_general(
+                pair_ref[place, span + h * HD : span + (h + 1) * HD], p.astype(BF16), TN,
+                preferred_element_type=F32,
+            )
+
+        score(0)
+        for h in range(heads):
+            if h + 1 < heads:
+                score(h + 1)
+            spread(h)
+
+    def guest():
+        clear(guest_high, guest_total, guest_acc)
+        copy(14).wait_recv()
+
+        def turn(k, carry):
+            attend_block(
+                me + k * to_core, guest_ref, diagonal, guest_high, guest_total, guest_acc
+            )
+            return carry
+
+        lax.fori_loop(0, 2, turn, 0)
+        for h in range(heads):
+            guest_out[h * HD : (h + 1) * HD, :] = (
+                guest_acc[h] / guest_total[h : h + 1, :]
+            ).astype(BF16)
+        guest_stat[:heads, :] = guest_high[...]
+        guest_stat[heads:, :] = guest_total[...]
+        copy(15).start()
+        copy(16).start()
+
+    clear(high_ref, total_ref, acc_ref)
 
     def turn(step, carry):
-        cube.advance(step)
-        keep(step).start()
         for k in range(n):
-            @pl.when(step == min(k * 2, CUBE - 1 - (n - 1 - k)) if n <= CUBE else k)
+            @pl.when(step == (min(k * 2, FAR_STEPS - n + k) if n <= FAR_STEPS else k))
             def _():
                 line_step(k)
-        block = cube.block(step)
-
-        @pl.when(block <= me)
-        def _():
-            place = pl.ds(pl.multiple_of(block * rows, 16), rows)
-
-            def score(h):
-                hs = slice(h * HD, (h + 1) * HD)
-                s = lax.dot_general(
-                    pair_ref[place, hs], q_ref[:, hs], NT, preferred_element_type=F32
-                )
-                s_ref[h % 2] = hidden_scores(s, block, me, rows, begin_ref[...])
-
-            def spread(h):
-                s = s_ref[h % 2]
-                old = high_ref[h : h + 1, :]
-                new = jnp.maximum(old, jnp.max(s, axis=0, keepdims=True))
-                high_ref[h : h + 1, :] = new
-                p = jnp.exp2(s * C2 - new * C2)
-                decay = jnp.exp2((old - new) * C2)
-                total_ref[h : h + 1, :] = total_ref[h : h + 1, :] * decay + jnp.sum(
-                    p, axis=0, keepdims=True
-                )
-                acc_ref[h] = acc_ref[h] * decay + lax.dot_general(
-                    pair_ref[place, span + h * HD : span + (h + 1) * HD], p.astype(BF16), TN,
-                    preferred_element_type=F32,
-                )
-
-            score(0)
-            for h in range(heads):
-                if h + 1 < heads:
-                    score(h + 1)
-                spread(h)
+
+        @pl.when(step == 1)
+        def _():
+            copy(0).wait_recv()
+
+        @pl.when((step == 2) & on_chip(0))
+        def _():
+            guest()
+
+        @pl.when((step == 2) & on_chip(3))
+        def _():
+            for k in range(4):
+                copy(3 + k).wait_recv()
+                copy(9 + k).start()
+
+        @pl.when((step == 2) & (x == 1))
+        def _():
+            copy(1).wait_recv()
+            copy(2).wait_recv()
+            copy(7).start()
+
+        @pl.when((step == 3) & on_chip(2))
+        def _():
+            for k in range(4):
+                copy(3 + k).wait_recv()
+
+        @pl.when((step == 3) & (y == 1))
+        def _():
+            copy(8).start()
+
+        @pl.when((step == 4) & (x == 1))
+        def _():
+            copy(7).wait_recv()
+
+        @pl.when((step == 5) & (y == 1))
+        def _():
+            copy(8).wait_recv()
+
+        @pl.when((step == 6) & on_chip(2))
+        def _():
+            for k in range(4):
+                copy(9 + k).wait_recv()
+            copy(13).start()
+
+        @pl.when((step == 7) & on_chip(2))
+        def _():
+            copy(13).wait_recv()
+
+        on = lambda *steps: sum((step == k).astype(jnp.int32) for k in steps)
+        block = (
+            me + on(1, 4, 5, 7) * to_core + on(2, 4, 6, 7) * to_x + on(3, 5, 6, 7) * to_y
+        )
+        here = on(0, 1) + on(2, 4) * x + on(3, 5) * y + on(6, 7) * y * (1 - x)
+
+        @pl.when((block <= me) & (here > 0))
+        def _():
+            attend_block(block, q_ref, me, high_ref, total_ref, acc_ref)
 
         return carry
 
-    lax.fori_loop(0, CUBE, turn, 0)
+    lax.fori_loop(0, FAR_STEPS, turn, 0)
+
+    @pl.when(on_chip(3))
+    def _():
+        copy(15).wait_recv()
+        copy(16).wait_recv()
+        for h in range(heads):
+            old, other = high_ref[h : h + 1, :], back_stat[h : h + 1, :]
+            new = jnp.maximum(old, other)
+            high_ref[h : h + 1, :] = new
+            decay = jnp.exp2((old - new) * C2)
+            weight = jnp.exp2((other - new) * C2) * back_stat[heads + h : heads + h + 1, :]
+            total_ref[h : h + 1, :] = total_ref[h : h + 1, :] * decay + weight
+            acc_ref[h] = acc_ref[h] * decay + weight * back_out[
+                h * HD : (h + 1) * HD, :
+            ].astype(F32)
+
     for h in range(heads):
         hs = slice(h * HD, (h + 1) * HD)
         out = (acc_ref[h] / total_ref[h : h + 1, :]).T
@@ -669,13 +821,15 @@
         mixed_ref[...], w_ref[...], preferred_element_type=F32
     ).astype(BF16)
     lse_ref[...] = high_ref[...] * C2 + jnp.log2(total_ref[...])
-
-    def kept(step, carry):
-        keep(step).wait()
-        return carry
-
-    lax.fori_loop(0, CUBE, kept, 0)
-    cube.finish()
+    for senders, which in (
+        (me >= 0, (0,)), (x == 0, (1, 2)), (y == 0, (3, 4, 5, 6)), (x == 1, (7,)), (y == 1, (8,)),
+        (on_chip(3), (9, 10, 11, 12, 14)), (on_chip(2), (13,)), (on_chip(0), (15, 16)),
+    ):
+        @pl.when(senders)
+        def _():
+            for k in which:
+                copy(k).wait_send()
+
     for k in range(n):
         @pl.when((at >= k) & (at < n - 1))
         def _():
@@ -690,41 +844,48 @@
     rows, width = tok_full.shape
     span = heads * HD
     vmem = pl.BlockSpec(memory_space=pltpu.VMEM)
+    state = [
+        pltpu.VMEM((heads, rows), F32),
+        pltpu.VMEM((heads, rows), F32),
+        pltpu.VMEM((heads, HD, rows), F32),
+    ]
+    answer = [pltpu.VMEM((span, rows), BF16), pltpu.VMEM((2 * heads, rows), F32)]
     return pl.pallas_call(
         functools.partial(attend_far_kernel, heads, n),
         in_specs=[vmem] * 7,
-        out_specs=[vmem] * 6 + [pl.BlockSpec(memory_space=pl.ANY)] + [vmem] * 2,
+        out_specs=[vmem] * 8,
         out_shape=[
             jax.ShapeDtypeStruct((rows, width), BF16),
             jax.ShapeDtypeStruct((rows, 2), F32),
-            jax.ShapeDtypeStruct((rows, span), BF16),
             jax.ShapeDtypeStruct((rows, span), F32),
             jax.ShapeDtypeStruct((rows, span), BF16),
             jax.ShapeDtypeStruct((heads, rows), F32),
-            jax.ShapeDtypeStruct((CUBE * rows, 2 * span), BF16),
+            jax.ShapeDtypeStruct((rows, 3 * span), BF16),
             jax.ShapeDtypeStruct((rows, n * cot.shape[1]), BF16),
             jax.ShapeDtypeStruct((rows, width), BF16),
         ],
         scratch_shapes=[
             pltpu.VMEM((CUBE * rows, 2 * span), BF16),
-            pltpu.VMEM((heads, rows), F32),
-            pltpu.VMEM((heads, rows), F32),
-            pltpu.VMEM((heads, HD, rows), F32),
+            pltpu.VMEM((rows, span), BF16),
+            *state,
             pltpu.VMEM((2, rows, rows), F32),
-            pltpu.SemaphoreType.DMA((CUBE_SENDS,)),
-            pltpu.SemaphoreType.DMA((CUBE_SENDS,)),
+            pltpu.VMEM((rows, span), BF16),
+            *state,
+            *answer,
+            *answer,
+            pltpu.SemaphoreType.DMA((FAR_SENDS,)),
+            pltpu.SemaphoreType.DMA((FAR_SENDS,)),
             pltpu.SemaphoreType.DMA((2, n)),
             pltpu.SemaphoreType.DMA((2, n)),
-            pltpu.SemaphoreType.DMA((CUBE,)),
         ],
-        compiler_params=params(58, collective_id=2, has_side_effects=True),
+        compiler_params=params(60, collective_id=2, has_side_effects=True),
         cost_estimate=cost(1e6, 1e6),
         name="attend_far",
     )(tok_full, in_weight, cosine, sine, begin, cot, weight)
 
 
 def attend_back_far_kernel(
-    heads, n, g_ref, far_q_ref, far_pair_ref, begin_ref, part_ref, mid_ref,
+    heads, n, g_ref, kept_ref, begin_ref, part_ref, mid_ref,
     dq_ref, dk_ref, dv_ref, layer_ref, next_ref,
     all_ref, acc_ref, rows_ref, s_ref, p_ref, land_ref, pair_ref, q_ref,
     send, recv, zsend, zrecv, read_sem, mid_land, msend, mrecv,
@@ -745,9 +906,10 @@
 
     def read(step, keys):
         place = pl.ds(pl.multiple_of(cube.block(step) * rows, 16), rows)
-        far, near = (far_pair_ref, pair_ref) if keys else (far_q_ref, q_ref)
+        near, columns = (pair_ref, (0, 2 * span)) if keys else (q_ref, (2 * span, span))
         return pltpu.make_async_copy(
-            far.at[place], near.at[place], read_sem.at[0 if keys else 1, step]
+            kept_ref.at[place, pl.ds(*columns)], near.at[place],
+            read_sem.at[0 if keys else 1, step],
         )
 
     def read_all(step, carry):
@@ -874,7 +1036,7 @@
         term(o).wait_send()
 
 
-def attend_back_far(grad, all_query, all_pairs, all_begin, part, mid, heads, n):
+def attend_back_far(grad, kept, all_begin, part, mid, heads, n):
     rows = grad.shape[0]
     span = heads * HD
     shard = part.shape[1] // n
@@ -882,7 +1044,7 @@
     wide = jax.ShapeDtypeStruct((rows, span), F32)
     return pl.pallas_call(
         functools.partial(attend_back_far_kernel, heads, n),
-        in_specs=[vmem] + [pl.BlockSpec(memory_space=pl.ANY)] * 2 + [vmem] * 3,
+        in_specs=[vmem, pl.BlockSpec(memory_space=pl.ANY)] + [vmem] * 3,
         out_specs=[vmem] * 5,
         out_shape=[wide, wide, wide, jax.ShapeDtypeStruct((rows, shard), BF16)]
         + [jax.ShapeDtypeStruct(mid.shape, BF16)],
@@ -907,7 +1069,7 @@
         compiler_params=params(62, collective_id=3, has_side_effects=True),
         cost_estimate=cost(1e6, 1e6),
         name="attend_back_far",
-    )(grad, all_query, all_pairs, all_begin, part, mid)
+    )(grad, kept, all_begin, part, mid)
 
 
 def query_grad_kernel(
@@ -1765,24 +1927,25 @@
     begin = lax.dynamic_slice_in_dim(blocks, me, 1, 0)
     all_begin = all_begin[None, :]
     if cube:
-        inner1, stat1, query, raw, mixed, lse, all_pairs, cot_full, out_part = attend_far(
-            tok_full, in_w, cosine, sine, begin, cotangent, out_weight, heads, tp_size
+        inner1, stat1, raw, mixed, lse, kept, cot_full, out_part = attend_far(
+            tok_full, in_w, cosine, sine, blocks, cotangent, out_weight, heads, tp_size
         )
+        kept = lax.all_gather(kept, "ctx", axis=0, tiled=True)
     else:
         inner1, stat1, query, pairs = project(tok_full, in_w, cosine, sine, heads)
         all_pairs = lax.all_gather(pairs, "ctx", axis=0, tiled=True)
         cot_full = gather(cotangent)
         raw, mixed, lse = attend(key_info, query, all_pairs, begin, heads)
         out_part = jnp.dot(mixed, out_weight, preferred_element_type=F32).astype(BF16)
-    late_query, mixed = lax.optimization_barrier((query, mixed))
-    all_query = lax.all_gather(late_query, "ctx", axis=0, tiled=True)
+        late_query, mixed = lax.optimization_barrier((query, mixed))
+        kept = lax.all_gather(late_query, "ctx", axis=0, tiled=True)
     inner2, resid1, stat2, grad_hidden = merge(
         out_part, tok_full, cot_full, down_weight, tp_size
     )
 
     hidden, grad_gu, down_grad, gu_grad = feed(inner2, cot_full, gu_w, grad_hidden, BLOCK)
-    down_grad, gu_grad, all_query, grad_gu, hidden = lax.optimization_barrier(
-        (down_grad, gu_grad, all_query, grad_gu, hidden)
+    down_grad, gu_grad, kept, grad_gu, hidden = lax.optimization_barrier(
+        (down_grad, gu_grad, kept, grad_gu, hidden)
     )
     if not cube:
         down_grad = lax.psum(down_grad, "ctx")
@@ -1796,14 +1959,14 @@
     grad_mixed, delta = mixed_grad(branch_grad, out_weight, raw, lse, heads)
     if cube:
         dq, dk, dv, layer_out, mid = attend_back_far(
-            grad_mixed, all_query, all_pairs, blocks, branch, mids[0], heads, tp_size
+            grad_mixed, kept, blocks, branch, mids[0], heads, tp_size
         )
     else:
         branch = lax.psum_scatter(branch, "tp", scatter_dimension=1, tiled=True)
         layer_out = branch
         all_grad = lax.all_gather(grad_mixed, "ctx", axis=0, tiled=True)
         dq = query_grad(key_info, query, grad_mixed, lse, delta, all_pairs, begin, heads)
-        dk, dv = key_grad(query_info, pairs, all_query, all_grad, all_begin, heads)
+        dk, dv = key_grad(query_info, pairs, kept, all_grad, all_begin, heads)
 
     if cube:
         tokens_grad, *halves = unproject(

time: 721 us -> 713 us (0.989)
  Pallas kernels: 610 us -> 598 us
    pallas_call x1, Pallas kernels: 84.9 us -> 73.6 us  [attend_far(): pl.pallas_call(functools.partial(attend_far_kernel, heads, n), in_specs=[...]
  transfers between devices with their start and end apart: 6 -> 6, of which waited for: 1 -> 1; matrix products, arithmetic and copies ran while one was open for 7% -> 7% of each run, Pallas kernels for 71% -> 72%
where the time goes in v10:
time: 713 us; the launch traced here: 705 us
  Pallas kernels  598 us (84%)
  local copies, waits for them, and re-layouts  32.5 us (5%)
  waiting for transfers between devices  25.4 us (4%)
  matrix products  20 us (3%)
  between operations  14.3 us (2%)
  blocking collectives  10.5 us (1%)
    pallas_call x1, Pallas kernels, unproject(): pl.pallas_call(functools.partial(unproject_kernel, heads, n, cube), in_sp...  153 us
    pallas_call x1, Pallas kernels, norm_back(): pl.pallas_call(functools.partial(norm_back_kernel, n, sub, len(grads) > 0...  100 us
    pallas_call x1, Pallas kernels, attend_back_far(): pl.pallas_call(functools.partial(attend_back_far_kernel, heads, n), in_sp...  94.5 us
    pallas_call x1, Pallas kernels, merge(): pl.pallas_call(functools.partial(merge_kernel, n, sub), in_specs=[vmem, v...  89.9 us
    pallas_call x1, Pallas kernels, attend_far(): pl.pallas_call(functools.partial(attend_far_kernel, heads, n), in_specs=[...  73.6 us
    pallas_call x1, Pallas kernels, feed(): pl.pallas_call(feed_kernel, grid=(units // block,), in_specs=[whole, whol...  41.4 us
    reshape x1, local copies, waits for them, and re-layouts, per_device(): gu_w = gu_w.reshape(width, 2 * hidden_local)  27.8 us
    all_gather x1, waiting for transfers between devices, gather(): return lax.all_gather(local, 'tp', axis=axis, tiled=True)  24.7 us
  transfers between devices with their start and end apart: 6, of which 1 were waited for; matrix products, arithmetic and copies ran while one was open for 7% of the time, Pallas kernels for 72%

profile of v10, /device:TPU:0, one launch (start us, length us, event | category | flops | bytes accessed | tf_op | source)
XLA Modules:
  0.0 705.2 jit_solution(5864573773268038903)
XLA Ops:
  7.2 0.7 all-gather.4.cloned.1.call-update
  8.0 0.7 reshape.60
  8.6 10.5 %all-gather = s32[8,1,768]{2,1,0:T(1,128)S(1)} all-gather(s32[1,1,768]{2,1,0:T(1,128)S(1)} %reshape.60), channel_id=1, replica_groups=mesh['ctx'=8,'tp'=4] {'ctx'}, dimensions={0}, use_global_device_ids=true | all-gather | bytes 27648 | tf_op jit(solution)/shard_map/all_gather | solution.py:1907
  19.1 0.1 slice_compare_fusion
  19.2 0.1 add_select_fusion
  19.3 0.3 reduce-window.9
  19.6 0.1 slice.19
  19.6 0.1 reduce-window.12
  19.7 0.1 slice_reduce_fusion
  19.8 0.1 reshape.57
  19.9 0.1 copy.18
  20.0 27.8 %reshape.55.w_ref = bf16[2048,4096]{1,0:T(8,128)(2,1)} reshape(bf16[2048,4,2,512]{3,2,1,0:T(2,128)(2,1)} %bitcast.19) | data formatting | bytes 33554432 | tf_op jit(solution)/shard_map/reshape | solution.py:1905
  47.8 1.4 fusion
  49.2 1.2 pad_maximum_fusion
  50.4 0.7 bitcast_maximum_fusion.begin_ref
  51.1 24.7 %all-gather.4.cloned.1.call-done.tok_ref.refs_9_ = bf16[768,2048]{1,0:T(8,128)(2,1)} async-done(((bf16[768,512]{1,0:T(8,128)(2,1)}), bf16[768,2048]{1,0:T(8,128)(2,1)}) %all-gather.4.cloned.1.call-update) | async-done | bytes 3145744 | tf_op jit(solution)/shard_map/all_gather | solution.py:1897
  75.8 73.6 %attend_far.1 = (bf16[768,2048]{1,0:T(8,128)(2,1)}, f32[768,2]{1,0:T(8,128)}, f32[768,512]{1,0:T(8,128)}, bf16[768,512]{1,0:T(8,128)(2,1)}, f32[4,768]{1,0:T(4,1...) custom-call(bf16[768,2048]{1,0:T(8,128)(2,1)} %all-gather.4.cloned.1.call-done.tok_ref.refs_9_,, ...), custom_call_target="tpu_custom_call" | custom-call | flops 1000000 | bytes 1000000 | tf_op jit(solution)/shard_map/attend_far/pallas_call | solution.py:853
  149.5 89.9 %merge.1 = (bf16[768,2048]{1,0:T(8,128)(2,1)}, f32[768,2048]{1,0:T(8,128)}, f32[768,2]{1,0:T(8,128)}, bf16[768,2048]{1,0:T(8,128)(2,1)}) custom-call(bf16[768,2048]{1,0:T(8,128)(2,1)} %get-tuple-element.52.part_ref, bf16[768,2048]{1,0:T(8,128)(2,1)} %all-gather.4.cloned.1.call-done.tok_ref.refs_9_, bf16[768,2048]{1,0:T(8,128)(2,1)} %get-tuple-element.53.far_cot.cot_ref, ...), custom_call_target="tpu_custom_call" | custom-call | flops 1000000 | bytes 1000000 | tf_op jit(solution)/shard_map/merge/pallas_call | solution.py:1558
  239.3 41.4 %feed.1 = (bf16[768,2048]{1,0:T(8,128)(2,1)}, bf16[768,4096]{1,0:T(8,128)(2,1)}, bf16[2048,2048]{1,0:T(8,128)(2,1)}, bf16[2048,4096]{1,0:T(8,128)(2,1)}) custom-call(bf16[768,2048]{1,0:T(8,128)(2,1)} %get-tuple-element.54.inner_ref, bf16[768,2048]{1,0:T(8,128)(2,1)} %get-tuple-element.53.far_cot.cot_ref, bf16[2048,4096]{1,0:T(8,128)(2,1)} %reshape.55.w_ref, ...), custom_call_target="tpu_custom_call" | custom-call | flops 38654705664 | bytes 56623104 | tf_op jit(solution)/shard_map/feed/pallas_call | solution.py:1316
  280.8 20.0 %convolution_convert_fusion.part_ref = bf16[768,2048]{1,0:T(8,128)(2,1)} fusion(bf16[768,4096]{1,0:T(8,128)(2,1)} %get-tuple-element.62, bf16[2048,4096]{1,0:T(8,128)(2,1)} %reshape.55.w_ref), kind=kOutput, calls=%fused_computation | convolution fusion | flops 12886474752 | bytes 26214400 | tf_op jit(solution)/shard_map/dot_general | solution.py:1954
  300.8 100.4 %norm_back.1 = (bf16[768,2048]{1,0:T(8,128)(2,1)}, bf16[768,2048]{1,0:T(8,128)(2,1)}, bf16[512,2048]{1,0:T(8,128)(2,1)}) custom-call(bf16[768,2048]{1,0:T(8,128)(2,1)} %convolution_convert_fusion.part_ref, bf16[768,2048]{1,0:T(8,128)(2,1)} %get-tuple-element.53.far_cot.cot_ref, f32[768,2]{1,0:T(8,128)} %get-tuple-element.63.stat_ref, ...), custom_call_target="tpu_custom_call" | custom-call | flops 1000000 | bytes 1000000 | tf_op jit(solution)/shard_map/norm_back/pallas_call | solution.py:1647
  401.2 6.7 mixed_grad.1
  407.9 94.5 %attend_back_far.1 = (f32[768,512]{1,0:T(8,128)}, f32[768,512]{1,0:T(8,128)}, f32[768,512]{1,0:T(8,128)}, bf16[768,512]{1,0:T(8,128)(2,1)}, bf16[512,2048]{1,0:T(8,128)(2,1)}) custom-call(bf16[768,640]{1,0:T(8,128)(2,1)} %get-tuple-element.70.g_ref, bf16[6144,1536]{1,0:T(8,128)(2,1)} %all-gather.6.cloned.1.call-done.kept_ref, ...), custom_call_target="tpu_custom_call" | custom-call | flops 1000000 | bytes 1000000 | tf_op jit(solution)/shard_map/attend_back_far/pallas_call | solution.py:1045
  502.4 153.1 %unproject.1 = (f32[768,512]{1,0:T(8,128)}, bf16[3072,512]{1,0:T(8,128)(2,1)}, bf16[256,2048]{1,0:T(8,128)(2,1)}, bf16[1024,2048]{1,0:T(8,128)(2,1)}) custom-call(f32[768,512]{1,0:T(8,128)} %get-tuple-element.75.refs_0_, f32[768,512]{1,0:T(8,128)} %get-tuple-element.76.refs_1_, f32[768,512]{1,0:T(8,128)} %get-tuple-element.77.refs_2_, ...), custom_call_target="tpu_custom_call" | custom-call | flops 1000000 | bytes 1000000 | tf_op jit(solution)/shard_map/unproject/pallas_call | solution.py:1862
  655.5 0.1 collective-permute-start.2
  655.5 0.5 collective-permute-start
  656.0 0.1 collective-permute-start.1
  656.1 20.4 %weave.1 = f32[2048,2,2048]{2,1,0:T(2,128)} custom-call(bf16[2048,4096]{1,0:T(8,128)(2,1)} %all-reduce.2.cloned.1.call-done.sum_ref), custom_call_target="tpu_custom_call" | custom-call | flops 8388608 | bytes 50331648 | tf_op jit(solution)/shard_map/weave/pallas_call | solution.py:1345
  676.5 1.7 copy-done
  678.2 18.0 %join.1 = (f32[6144,512]{1,0:T(8,128)}, f32[512,2048]{1,0:T(8,128)}, f32[2048,2048]{1,0:T(8,128)}) custom-call(s32[1]{0:T(128)} %bitcast.6.core_ref, bf16[3072,512]{1,0:T(8,128)(2,1)} %get-tuple-element.83.refs_0_, bf16[256,2048]{1,0:T(8,128)(2,1)} %get-tuple-element.84.refs_1_, bf16[1024,2048]{1,0:T(8,128)(2,1)} %get-tuple-element.85.refs_2_, ...), custom_call_target="tpu_custom_call" | custom-call | flops 8388608 | bytes 50331648 | tf_op jit(solution)/shard_map/join/pallas_call | solution.py:508
  696.2 0.9 copy.22
  697.1 1.1 copy.23
  (18 shorter events, 0.2 us)
Async XLA Ops:
  7.2 68.6 %all-gather.4.cloned.1.call-start = ((), (), s32[]{:S(2)}) async-start(), calls=%async_computation | async-start | bytes 3932160 | tf_op jit(solution)/shard_map/all_gather | solution.py:1897
  7.9 272.9 %all-gather.6.cloned.1.call-start = ((), (), s32[]{:S(2)}) async-start(), calls=%async_computation.1 | async-start | bytes 21233664 | tf_op jit(solution)/shard_map/all_gather | solution.py:1933
  149.4 506.7 %all-reduce.2.cloned.1.call-start = ((), (), s32[]{:S(2)}) async-start(), calls=%async_computation.2 | async-start | bytes 33554432 | tf_op jit(solution)/shard_map/psum | solution.py:1952
  655.5 21.0 %collective-permute-start.2 = (bf16[1024,2048]{1,0:T(8,128)(2,1)}, bf16[1024,2048]{1,0:T(8,128)(2,1)}, u32[]{:S(2)}, u32[]{:S(2)}) collective-permute-start(bf16[1024,2048]{1,0:T(8,128)(2,1)} %get-tuple-element.85.refs_2_), channel_id=1, source_target_pairs={{0,4},{4,0},{8,12},{12,8},{16,20},{20,16},{24,28},{28,24},{1,5},{5... | collective-permute-start | bytes 12582920 | tf_op jit(solution)/shard_map/ppermute | solution.py:1978
  655.5 20.9 %collective-permute-start = (bf16[3072,512]{1,0:T(8,128)(2,1)}, bf16[3072,512]{1,0:T(8,128)(2,1)S(1)}, u32[]{:S(2)}, u32[]{:S(2)}) collective-permute-start(bf16[3072,512]{1,0:T(8,128)(2,1)} %get-tuple-element.83.refs_0_), channel_id=1, source_target_pairs={{0,4},{4,0},{8,12},{12,8},{16,20},{20,16},{24,28},{28,24},{1,5},{5... | collective-permute-start | bytes 9437192 | tf_op jit(solution)/shard_map/ppermute | solution.py:1978
  656.0 20.4 %collective-permute-start.1 = (bf16[256,2048]{1,0:T(8,128)(2,1)}, bf16[256,2048]{1,0:T(8,128)(2,1)}, u32[]{:S(2)}, u32[]{:S(2)}) collective-permute-start(bf16[256,2048]{1,0:T(8,128)(2,1)} %get-tuple-element.84.refs_1_), channel_id=1, source_target_pairs={{0,4},{4,0},{8,12},{12,8},{16,20},{20,16},{24,28},{28,24},{1,5},{5... | collective-permute-start | bytes 3145736 | tf_op jit(solution)/shard_map/ppermute | solution.py:1978
  676.5 1.7 copy-start
  678.2 18.0 %copy-start.2 = (bf16[768,512]{1,0:T(8,128)(2,1)S(1)}, bf16[768,512]{1,0:T(8,128)(2,1)}, u32[]{:S(2)}) copy-start(bf16[768,512]{1,0:T(8,128)(2,1)} %get-tuple-element.105) | copy-start | bytes 2359300
  678.2 18.9 %copy-start.1 = (f32[768,512]{1,0:T(8,128)S(1)}, f32[768,512]{1,0:T(8,128)}, u32[]{:S(2)}) copy-start(f32[768,512]{1,0:T(8,128)} %get-tuple-element.106) | copy-start | bytes 4718596
Sparse Core Ops, SparseCore 0:
  9.6 66.1 all-gather.3
  149.5 106.5 all-gather.5
  280.9 326.3 all-reduce.1

commit v11 on v10

--- a/solution.py
+++ b/solution.py
@@ -1618,7 +1618,7 @@
         aside[1 + 2 * k] = (functools.partial(piece, k * 256),)
     if cube:
         total.begin()
-        for k, c in enumerate((6, 8, 10, 12)):
+        for k, c in enumerate((14, 16, 18, 20)):
             aside[c] = (functools.partial(total.reduce, k),)
 
     def row_fn(summed, rows):
@@ -1753,7 +1753,6 @@
         sums[0].signal(barrier)
     pl.semaphore_wait(barrier, n - 1 + (3 if cube else 0))
     if cube:
-        rest.begin()
         og_ref[...] = lax.dot_general(
             mixed_ref[...], branch_ref[...], TN, preferred_element_type=F32
         ).astype(BF16)
@@ -1813,7 +1812,10 @@
         sums_ref[:, i * block : (i + 1) * block] = both.T[:8]
     for o in range(1, n):
         totals(o).start()
-    reduce(0, 1, 2, 3, 4, 5, 6, 7)
+    reduce(0, 1, 2, 3, 4, 5)
+    if cube:
+        rest.begin()
+    reduce(6, 7)
     gather(0)
     gather(1)
     total = sums_ref[...]

time: 713 us -> 710 us (level)
    pallas_call x1, Pallas kernels: 153 us -> 141 us  [unproject(): pl.pallas_call(functools.partial(unproject_kernel, heads, n, cube), in_sp...]
    pallas_call x1, Pallas kernels: 94.5 us -> 104 us  [attend_back_far(): pl.pallas_call(functools.partial(attend_back_far_kernel, heads, n), in_sp...]
where the time goes in v11:
time: 710 us; the launch traced here: 702 us
  Pallas kernels  595 us (84%)
  local copies, waits for them, and re-layouts  32.5 us (5%)
  waiting for transfers between devices  25.4 us (4%)
  matrix products  20 us (3%)
  between operations  14.3 us (2%)
  blocking collectives  10.5 us (1%)
    pallas_call x1, Pallas kernels, unproject(): pl.pallas_call(functools.partial(unproject_kernel, heads, n, cube), in_sp...  141 us
    pallas_call x1, Pallas kernels, attend_back_far(): pl.pallas_call(functools.partial(attend_back_far_kernel, heads, n), in_sp...  104 us
    pallas_call x1, Pallas kernels, norm_back(): pl.pallas_call(functools.partial(norm_back_kernel, n, sub, len(grads) > 0...  100 us
    pallas_call x1, Pallas kernels, merge(): pl.pallas_call(functools.partial(merge_kernel, n, sub), in_specs=[vmem, v...  89.9 us
    pallas_call x1, Pallas kernels, attend_far(): pl.pallas_call(functools.partial(attend_far_kernel, heads, n), in_specs=[...  73.6 us
    pallas_call x1, Pallas kernels, feed(): pl.pallas_call(feed_kernel, grid=(units // block,), in_specs=[whole, whol...  41.4 us
    reshape x1, local copies, waits for them, and re-layouts, per_device(): gu_w = gu_w.reshape(width, 2 * hidden_local)  27.8 us
    all_gather x1, waiting for transfers between devices, gather(): return lax.all_gather(local, 'tp', axis=axis, tiled=True)  24.7 us
  transfers between devices with their start and end apart: 6, of which 1 were waited for; matrix products, arithmetic and copies ran while one was open for 7% of the time, Pallas kernels for 72%

profile of v11, /device:TPU:0, one launch (start us, length us, event | category | flops | bytes accessed | tf_op | source)
XLA Modules:
  0.0 702.3 jit_solution(9393023343350833533)
XLA Ops:
  7.2 0.7 all-gather.4.cloned.1.call-update
  8.0 0.7 reshape.60
  8.6 10.5 %all-gather = s32[8,1,768]{2,1,0:T(1,128)S(1)} all-gather(s32[1,1,768]{2,1,0:T(1,128)S(1)} %reshape.60), channel_id=1, replica_groups=mesh['ctx'=8,'tp'=4] {'ctx'}, dimensions={0}, use_global_device_ids=true | all-gather | bytes 27648 | tf_op jit(solution)/shard_map/all_gather | solution.py:1909
  19.1 0.1 slice_compare_fusion
  19.2 0.1 add_select_fusion
  19.3 0.3 reduce-window.9
  19.6 0.1 slice.19
  19.6 0.1 reduce-window.12
  19.7 0.1 slice_reduce_fusion
  19.8 0.1 reshape.57
  19.9 0.1 copy.18
  20.0 27.8 %reshape.55.w_ref = bf16[2048,4096]{1,0:T(8,128)(2,1)} reshape(bf16[2048,4,2,512]{3,2,1,0:T(2,128)(2,1)} %bitcast.19) | data formatting | bytes 33554432 | tf_op jit(solution)/shard_map/reshape | solution.py:1907
  47.8 1.4 fusion
  49.2 1.2 pad_maximum_fusion
  50.4 0.7 bitcast_maximum_fusion.begin_ref
  51.1 24.7 %all-gather.4.cloned.1.call-done.tok_ref.refs_9_ = bf16[768,2048]{1,0:T(8,128)(2,1)} async-done(((bf16[768,512]{1,0:T(8,128)(2,1)}), bf16[768,2048]{1,0:T(8,128)(2,1)}) %all-gather.4.cloned.1.call-update) | async-done | bytes 3145744 | tf_op jit(solution)/shard_map/all_gather | solution.py:1899
  75.8 73.6 %attend_far.1 = (bf16[768,2048]{1,0:T(8,128)(2,1)}, f32[768,2]{1,0:T(8,128)}, f32[768,512]{1,0:T(8,128)}, bf16[768,512]{1,0:T(8,128)(2,1)}, f32[4,768]{1,0:T(4,1...) custom-call(bf16[768,2048]{1,0:T(8,128)(2,1)} %all-gather.4.cloned.1.call-done.tok_ref.refs_9_,, ...), custom_call_target="tpu_custom_call" | custom-call | flops 1000000 | bytes 1000000 | tf_op jit(solution)/shard_map/attend_far/pallas_call | solution.py:853
  149.5 89.9 %merge.1 = (bf16[768,2048]{1,0:T(8,128)(2,1)}, f32[768,2048]{1,0:T(8,128)}, f32[768,2]{1,0:T(8,128)}, bf16[768,2048]{1,0:T(8,128)(2,1)}) custom-call(bf16[768,2048]{1,0:T(8,128)(2,1)} %get-tuple-element.52.part_ref, bf16[768,2048]{1,0:T(8,128)(2,1)} %all-gather.4.cloned.1.call-done.tok_ref.refs_9_, bf16[768,2048]{1,0:T(8,128)(2,1)} %get-tuple-element.53.far_cot.cot_ref, ...), custom_call_target="tpu_custom_call" | custom-call | flops 1000000 | bytes 1000000 | tf_op jit(solution)/shard_map/merge/pallas_call | solution.py:1558
  239.3 41.4 %feed.1 = (bf16[768,2048]{1,0:T(8,128)(2,1)}, bf16[768,4096]{1,0:T(8,128)(2,1)}, bf16[2048,2048]{1,0:T(8,128)(2,1)}, bf16[2048,4096]{1,0:T(8,128)(2,1)}) custom-call(bf16[768,2048]{1,0:T(8,128)(2,1)} %get-tuple-element.54.inner_ref, bf16[768,2048]{1,0:T(8,128)(2,1)} %get-tuple-element.53.far_cot.cot_ref, bf16[2048,4096]{1,0:T(8,128)(2,1)} %reshape.55.w_ref, ...), custom_call_target="tpu_custom_call" | custom-call | flops 38654705664 | bytes 56623104 | tf_op jit(solution)/shard_map/feed/pallas_call | solution.py:1316
  280.8 20.0 %convolution_convert_fusion.part_ref = bf16[768,2048]{1,0:T(8,128)(2,1)} fusion(bf16[768,4096]{1,0:T(8,128)(2,1)} %get-tuple-element.62, bf16[2048,4096]{1,0:T(8,128)(2,1)} %reshape.55.w_ref), kind=kOutput, calls=%fused_computation | convolution fusion | flops 12886474752 | bytes 26214400 | tf_op jit(solution)/shard_map/dot_general | solution.py:1956
  300.8 100.4 %norm_back.1 = (bf16[768,2048]{1,0:T(8,128)(2,1)}, bf16[768,2048]{1,0:T(8,128)(2,1)}, bf16[512,2048]{1,0:T(8,128)(2,1)}) custom-call(bf16[768,2048]{1,0:T(8,128)(2,1)} %convolution_convert_fusion.part_ref, bf16[768,2048]{1,0:T(8,128)(2,1)} %get-tuple-element.53.far_cot.cot_ref, f32[768,2]{1,0:T(8,128)} %get-tuple-element.63.stat_ref, ...), custom_call_target="tpu_custom_call" | custom-call | flops 1000000 | bytes 1000000 | tf_op jit(solution)/shard_map/norm_back/pallas_call | solution.py:1647
  401.2 6.7 mixed_grad.1
  407.9 103.9 %attend_back_far.1 = (f32[768,512]{1,0:T(8,128)}, f32[768,512]{1,0:T(8,128)}, f32[768,512]{1,0:T(8,128)}, bf16[768,512]{1,0:T(8,128)(2,1)}, bf16[512,2048]{1,0:T(8,128)(2,1)}) custom-call(bf16[768,640]{1,0:T(8,128)(2,1)} %get-tuple-element.70.g_ref, bf16[6144,1536]{1,0:T(8,128)(2,1)} %all-gather.6.cloned.1.call-done.kept_ref, ...), custom_call_target="tpu_custom_call" | custom-call | flops 1000000 | bytes 1000000 | tf_op jit(solution)/shard_map/attend_back_far/pallas_call | solution.py:1045
  511.8 140.7 %unproject.1 = (f32[768,512]{1,0:T(8,128)}, bf16[3072,512]{1,0:T(8,128)(2,1)}, bf16[256,2048]{1,0:T(8,128)(2,1)}, bf16[1024,2048]{1,0:T(8,128)(2,1)}) custom-call(f32[768,512]{1,0:T(8,128)} %get-tuple-element.75.refs_0_, f32[768,512]{1,0:T(8,128)} %get-tuple-element.76.refs_1_, f32[768,512]{1,0:T(8,128)} %get-tuple-element.77.refs_2_, ...), custom_call_target="tpu_custom_call" | custom-call | flops 1000000 | bytes 1000000 | tf_op jit(solution)/shard_map/unproject/pallas_call | solution.py:1864
  652.5 0.1 collective-permute-start.2
  652.6 0.5 collective-permute-start
  653.1 0.1 collective-permute-start.1
  653.1 20.4 %weave.1 = f32[2048,2,2048]{2,1,0:T(2,128)} custom-call(bf16[2048,4096]{1,0:T(8,128)(2,1)} %all-reduce.2.cloned.1.call-done.sum_ref), custom_call_target="tpu_custom_call" | custom-call | flops 8388608 | bytes 50331648 | tf_op jit(solution)/shard_map/weave/pallas_call | solution.py:1345
  673.5 1.7 copy-done
  675.2 18.0 %join.1 = (f32[6144,512]{1,0:T(8,128)}, f32[512,2048]{1,0:T(8,128)}, f32[2048,2048]{1,0:T(8,128)}) custom-call(s32[1]{0:T(128)} %bitcast.6.core_ref, bf16[3072,512]{1,0:T(8,128)(2,1)} %get-tuple-element.83.refs_0_, bf16[256,2048]{1,0:T(8,128)(2,1)} %get-tuple-element.84.refs_1_, bf16[1024,2048]{1,0:T(8,128)(2,1)} %get-tuple-element.85.refs_2_, ...), custom_call_target="tpu_custom_call" | custom-call | flops 8388608 | bytes 50331648 | tf_op jit(solution)/shard_map/join/pallas_call | solution.py:508
  693.3 0.9 copy.22
  694.1 1.1 copy.23
  (18 shorter events, 0.2 us)
Async XLA Ops:
  7.2 68.6 %all-gather.4.cloned.1.call-start = ((), (), s32[]{:S(2)}) async-start(), calls=%async_computation | async-start | bytes 3932160 | tf_op jit(solution)/shard_map/all_gather | solution.py:1899
  7.9 272.9 %all-gather.6.cloned.1.call-start = ((), (), s32[]{:S(2)}) async-start(), calls=%async_computation.1 | async-start | bytes 21233664 | tf_op jit(solution)/shard_map/all_gather | solution.py:1935
  149.4 503.7 %all-reduce.2.cloned.1.call-start = ((), (), s32[]{:S(2)}) async-start(), calls=%async_computation.2 | async-start | bytes 33554432 | tf_op jit(solution)/shard_map/psum | solution.py:1954
  652.5 21.0 %collective-permute-start.2 = (bf16[1024,2048]{1,0:T(8,128)(2,1)}, bf16[1024,2048]{1,0:T(8,128)(2,1)}, u32[]{:S(2)}, u32[]{:S(2)}) collective-permute-start(bf16[1024,2048]{1,0:T(8,128)(2,1)} %get-tuple-element.85.refs_2_), channel_id=1, source_target_pairs={{0,4},{4,0},{8,12},{12,8},{16,20},{20,16},{24,28},{28,24},{1,5},{5... | collective-permute-start | bytes 12582920 | tf_op jit(solution)/shard_map/ppermute | solution.py:1980
  652.6 20.9 %collective-permute-start = (bf16[3072,512]{1,0:T(8,128)(2,1)}, bf16[3072,512]{1,0:T(8,128)(2,1)S(1)}, u32[]{:S(2)}, u32[]{:S(2)}) collective-permute-start(bf16[3072,512]{1,0:T(8,128)(2,1)} %get-tuple-element.83.refs_0_), channel_id=1, source_target_pairs={{0,4},{4,0},{8,12},{12,8},{16,20},{20,16},{24,28},{28,24},{1,5},{5... | collective-permute-start | bytes 9437192 | tf_op jit(solution)/shard_map/ppermute | solution.py:1980
  653.1 20.4 %collective-permute-start.1 = (bf16[256,2048]{1,0:T(8,128)(2,1)}, bf16[256,2048]{1,0:T(8,128)(2,1)}, u32[]{:S(2)}, u32[]{:S(2)}) collective-permute-start(bf16[256,2048]{1,0:T(8,128)(2,1)} %get-tuple-element.84.refs_1_), channel_id=1, source_target_pairs={{0,4},{4,0},{8,12},{12,8},{16,20},{20,16},{24,28},{28,24},{1,5},{5... | collective-permute-start | bytes 3145736 | tf_op jit(solution)/shard_map/ppermute | solution.py:1980
  673.5 1.7 copy-start
  675.2 18.0 %copy-start.2 = (bf16[768,512]{1,0:T(8,128)(2,1)S(1)}, bf16[768,512]{1,0:T(8,128)(2,1)}, u32[]{:S(2)}) copy-start(bf16[768,512]{1,0:T(8,128)(2,1)} %get-tuple-element.105) | copy-start | bytes 2359300
  675.2 18.9 %copy-start.1 = (f32[768,512]{1,0:T(8,128)S(1)}, f32[768,512]{1,0:T(8,128)}, u32[]{:S(2)}) copy-start(f32[768,512]{1,0:T(8,128)} %get-tuple-element.106) | copy-start | bytes 4718596
Sparse Core Ops, SparseCore 0:
  9.6 66.1 all-gather.3
  149.5 106.5 all-gather.5
  280.9 297.6 all-reduce.1

commit v12 on v11

--- a/solution.py
+++ b/solution.py
@@ -1721,15 +1721,23 @@
     sums, rest = [], None
     if cube:
         dq_ref, dk_ref, dv_ref, cos_ref, sin_ref, inner_ref, mixed_ref = refs[:7]
-        branch_ref, mid_ref, tok_ref, stat_ref, w_ref = refs[7:12]
+        branch_ref, mid_ref, far_tok, stat_ref, far_w = refs[7:12]
         out_ref, in_out, og_out, down_out, dproj_ref, in_ref, og_ref = refs[12:19]
         part_ref, mine_ref, land_ref, sums_ref, far_ref, send, recv, ssend, srecv = refs[19:28]
         for own, out, at in ((in_ref, in_out, 28), (og_ref, og_out, 31)):
             sums.append(CubeSum(own, own, *refs[at : at + 3], None, out=out))
         rest = LastGather(mid_ref, down_out, *refs[34:37])
     else:
-        dproj_ref, branch_ref, tok_ref, stat_ref, w_ref, out_ref = refs[:6]
+        dproj_ref, branch_ref, far_tok, stat_ref, far_w, out_ref = refs[:6]
         part_ref, mine_ref, land_ref, sums_ref, far_ref, send, recv, ssend, srecv = refs[6:15]
+
+    tok_ref, w_ref, read_sem = refs[-3:]
+    reads = (
+        pltpu.make_async_copy(far_tok, tok_ref, read_sem.at[0]),
+        pltpu.make_async_copy(far_w, w_ref, read_sem.at[1]),
+    )
+    for read in reads:
+        read.start()
 
     def reduce(*pieces):
         for k in pieces:
@@ -1792,6 +1800,8 @@
         )
 
     own = pl.ds(pl.multiple_of(at * shard, 128), shard)
+    for read in reads:
+        read.wait()
     for i in range(count):
         place = pl.ds(i * block, block)
         total = None
@@ -1850,6 +1860,7 @@
     rows, width = tok_full.shape
     shard = width // n
     span = heads * HD
+    far = pl.BlockSpec(memory_space=pl.ANY)
     vmem = pl.BlockSpec(memory_space=pltpu.VMEM)
     shapes = [(3 * width, span), (span, width)] if cube else []
     more_out, early, extra = [], [], []
@@ -1863,7 +1874,7 @@
         extra += [pltpu.SemaphoreType.DMA((2,))] * 3
     return pl.pallas_call(
         functools.partial(unproject_kernel, heads, n, cube),
-        in_specs=[vmem] * (len(operands) + 3),
+        in_specs=[vmem] * (len(operands) - int(cube)) + [far] * int(cube) + [far, vmem, far],
         out_specs=[vmem] * (1 + len(shapes)) + [pl.BlockSpec(memory_space=pl.ANY)] * int(cube),
         out_shape=[jax.ShapeDtypeStruct((rows, shard), F32)] + more_out,
         scratch_shapes=early
@@ -1878,7 +1889,12 @@
             pltpu.SemaphoreType.DMA((n - 1,)),
             pltpu.SemaphoreType.DMA((n - 1,)),
         ]
-        + extra,
+        + extra
+        + [
+            pltpu.VMEM((rows, width), BF16),
+            pltpu.VMEM(weight.shape, BF16),
+            pltpu.SemaphoreType.DMA((2,)),
+        ],
         compiler_params=params(61, collective_id=4, has_side_effects=True),
         cost_estimate=cost(1e6, 1e6),
         name="unproject",

time: 710 us -> 709 us (level)
  no operation moved by 1% of the time
where the time goes in v12:
time: 709 us; the launch traced here: 702 us
  Pallas kernels  594 us (84%)
  local copies, waits for them, and re-layouts  32.5 us (5%)
  waiting for transfers between devices  25.4 us (4%)
  matrix products  20 us (3%)
  between operations  14.3 us (2%)
  blocking collectives  10.5 us (1%)
    pallas_call x1, Pallas kernels, unproject(): pl.pallas_call(functools.partial(unproject_kernel, heads, n, cube), in_sp...  140 us
    pallas_call x1, Pallas kernels, attend_back_far(): pl.pallas_call(functools.partial(attend_back_far_kernel, heads, n), in_sp...  104 us
    pallas_call x1, Pallas kernels, norm_back(): pl.pallas_call(functools.partial(norm_back_kernel, n, sub, len(grads) > 0...  100 us
    pallas_call x1, Pallas kernels, merge(): pl.pallas_call(functools.partial(merge_kernel, n, sub), in_specs=[vmem, v...  89.9 us
    pallas_call x1, Pallas kernels, attend_far(): pl.pallas_call(functools.partial(attend_far_kernel, heads, n), in_specs=[...  73.6 us
    pallas_call x1, Pallas kernels, feed(): pl.pallas_call(feed_kernel, grid=(units // block,), in_specs=[whole, whol...  41.4 us
    reshape x1, local copies, waits for them, and re-layouts, per_device(): gu_w = gu_w.reshape(width, 2 * hidden_local)  27.8 us
    all_gather x1, waiting for transfers between devices, gather(): return lax.all_gather(local, 'tp', axis=axis, tiled=True)  24.7 us
  transfers between devices with their start and end apart: 6, of which 1 were waited for; matrix products, arithmetic and copies ran while one was open for 7% of the time, Pallas kernels for 72%

profile of v12, /device:TPU:0, one launch (start us, length us, event | category | flops | bytes accessed | tf_op | source)
XLA Modules:
  0.0 701.7 jit_solution(14101475036360399556)
XLA Ops:
  7.2 0.7 all-gather.4.cloned.1.call-update
  8.0 0.7 reshape.60
  8.6 10.5 %all-gather = s32[8,1,768]{2,1,0:T(1,128)S(1)} all-gather(s32[1,1,768]{2,1,0:T(1,128)S(1)} %reshape.60), channel_id=1, replica_groups=mesh['ctx'=8,'tp'=4] {'ctx'}, dimensions={0}, use_global_device_ids=true | all-gather | bytes 27648 | tf_op jit(solution)/shard_map/all_gather | solution.py:1925
  19.1 0.1 slice_compare_fusion
  19.2 0.1 add_select_fusion
  19.3 0.3 reduce-window.9
  19.6 0.1 slice.19
  19.6 0.1 reduce-window.12
  19.7 0.1 slice_reduce_fusion
  19.8 0.1 reshape.57
  19.9 0.1 copy.18
  20.0 27.8 %reshape.55.w_ref = bf16[2048,4096]{1,0:T(8,128)(2,1)} reshape(bf16[2048,4,2,512]{3,2,1,0:T(2,128)(2,1)} %bitcast.19) | data formatting | bytes 33554432 | tf_op jit(solution)/shard_map/reshape | solution.py:1923
  47.8 1.4 fusion
  49.2 1.2 pad_maximum_fusion
  50.4 0.7 bitcast_maximum_fusion.begin_ref
  51.1 24.7 %all-gather.4.cloned.1.call-done.tok_ref.refs_9_ = bf16[768,2048]{1,0:T(8,128)(2,1)} async-done(((bf16[768,512]{1,0:T(8,128)(2,1)}), bf16[768,2048]{1,0:T(8,128)(2,1)}) %all-gather.4.cloned.1.call-update) | async-done | bytes 3145744 | tf_op jit(solution)/shard_map/all_gather | solution.py:1915
  75.8 73.6 %attend_far.1 = (bf16[768,2048]{1,0:T(8,128)(2,1)}, f32[768,2]{1,0:T(8,128)}, f32[768,512]{1,0:T(8,128)}, bf16[768,512]{1,0:T(8,128)(2,1)}, f32[4,768]{1,0:T(4,1...) custom-call(bf16[768,2048]{1,0:T(8,128)(2,1)} %all-gather.4.cloned.1.call-done.tok_ref.refs_9_,, ...), custom_call_target="tpu_custom_call" | custom-call | flops 1000000 | bytes 1000000 | tf_op jit(solution)/shard_map/attend_far/pallas_call | solution.py:853
  149.5 89.9 %merge.1 = (bf16[768,2048]{1,0:T(8,128)(2,1)}, f32[768,2048]{1,0:T(8,128)}, f32[768,2]{1,0:T(8,128)}, bf16[768,2048]{1,0:T(8,128)(2,1)}) custom-call(bf16[768,2048]{1,0:T(8,128)(2,1)} %get-tuple-element.52.part_ref, bf16[768,2048]{1,0:T(8,128)(2,1)} %all-gather.4.cloned.1.call-done.tok_ref.refs_9_, bf16[768,2048]{1,0:T(8,128)(2,1)} %get-tuple-element.53.far_cot.cot_ref, ...), custom_call_target="tpu_custom_call" | custom-call | flops 1000000 | bytes 1000000 | tf_op jit(solution)/shard_map/merge/pallas_call | solution.py:1558
  239.3 41.4 %feed.1 = (bf16[768,2048]{1,0:T(8,128)(2,1)}, bf16[768,4096]{1,0:T(8,128)(2,1)}, bf16[2048,2048]{1,0:T(8,128)(2,1)}, bf16[2048,4096]{1,0:T(8,128)(2,1)}) custom-call(bf16[768,2048]{1,0:T(8,128)(2,1)} %get-tuple-element.54.inner_ref, bf16[768,2048]{1,0:T(8,128)(2,1)} %get-tuple-element.53.far_cot.cot_ref, bf16[2048,4096]{1,0:T(8,128)(2,1)} %reshape.55.w_ref, ...), custom_call_target="tpu_custom_call" | custom-call | flops 38654705664 | bytes 56623104 | tf_op jit(solution)/shard_map/feed/pallas_call | solution.py:1316
  280.8 20.0 %convolution_convert_fusion.part_ref = bf16[768,2048]{1,0:T(8,128)(2,1)} fusion(bf16[768,4096]{1,0:T(8,128)(2,1)} %get-tuple-element.62, bf16[2048,4096]{1,0:T(8,128)(2,1)} %reshape.55.w_ref), kind=kOutput, calls=%fused_computation | convolution fusion | flops 12886474752 | bytes 26214400 | tf_op jit(solution)/shard_map/dot_general | solution.py:1972
  300.8 100.4 %norm_back.1 = (bf16[768,2048]{1,0:T(8,128)(2,1)}, bf16[768,2048]{1,0:T(8,128)(2,1)}, bf16[512,2048]{1,0:T(8,128)(2,1)}) custom-call(bf16[768,2048]{1,0:T(8,128)(2,1)} %convolution_convert_fusion.part_ref, bf16[768,2048]{1,0:T(8,128)(2,1)} %get-tuple-element.53.far_cot.cot_ref, f32[768,2]{1,0:T(8,128)} %get-tuple-element.63.stat_ref, ...), custom_call_target="tpu_custom_call" | custom-call | flops 1000000 | bytes 1000000 | tf_op jit(solution)/shard_map/norm_back/pallas_call | solution.py:1647
  401.2 6.7 mixed_grad.1
  407.9 103.9 %attend_back_far.1 = (f32[768,512]{1,0:T(8,128)}, f32[768,512]{1,0:T(8,128)}, f32[768,512]{1,0:T(8,128)}, bf16[768,512]{1,0:T(8,128)(2,1)}, bf16[512,2048]{1,0:T(8,128)(2,1)}) custom-call(bf16[768,640]{1,0:T(8,128)(2,1)} %get-tuple-element.70.g_ref, bf16[6144,1536]{1,0:T(8,128)(2,1)} %all-gather.6.cloned.1.call-done.kept_ref, ...), custom_call_target="tpu_custom_call" | custom-call | flops 1000000 | bytes 1000000 | tf_op jit(solution)/shard_map/attend_back_far/pallas_call | solution.py:1045
  511.8 140.1 %unproject.1 = (f32[768,512]{1,0:T(8,128)}, bf16[3072,512]{1,0:T(8,128)(2,1)}, bf16[256,2048]{1,0:T(8,128)(2,1)}, bf16[1024,2048]{1,0:T(8,128)(2,1)}) custom-call(f32[768,512]{1,0:T(8,128)} %get-tuple-element.75.refs_0_, f32[768,512]{1,0:T(8,128)} %get-tuple-element.76.refs_1_, f32[768,512]{1,0:T(8,128)} %get-tuple-element.77.refs_2_, ...), custom_call_target="tpu_custom_call" | custom-call | flops 1000000 | bytes 1000000 | tf_op jit(solution)/shard_map/unproject/pallas_call | solution.py:1875
  651.9 0.1 collective-permute-start.2
  652.0 0.5 collective-permute-start
  652.5 0.1 collective-permute-start.1
  652.6 20.4 %weave.1 = f32[2048,2,2048]{2,1,0:T(2,128)} custom-call(bf16[2048,4096]{1,0:T(8,128)(2,1)} %all-reduce.2.cloned.1.call-done.sum_ref), custom_call_target="tpu_custom_call" | custom-call | flops 8388608 | bytes 50331648 | tf_op jit(solution)/shard_map/weave/pallas_call | solution.py:1345
  672.9 1.7 copy-done
  674.6 18.0 %join.1 = (f32[6144,512]{1,0:T(8,128)}, f32[512,2048]{1,0:T(8,128)}, f32[2048,2048]{1,0:T(8,128)}) custom-call(s32[1]{0:T(128)} %bitcast.6.core_ref, bf16[3072,512]{1,0:T(8,128)(2,1)} %get-tuple-element.83.refs_0_, bf16[256,2048]{1,0:T(8,128)(2,1)} %get-tuple-element.84.refs_1_, bf16[1024,2048]{1,0:T(8,128)(2,1)} %get-tuple-element.85.refs_2_, ...), custom_call_target="tpu_custom_call" | custom-call | flops 8388608 | bytes 50331648 | tf_op jit(solution)/shard_map/join/pallas_call | solution.py:508
  692.7 0.9 copy.22
  693.6 1.1 copy.23
  (18 shorter events, 0.2 us)
Async XLA Ops:
  7.2 68.6 %all-gather.4.cloned.1.call-start = ((), (), s32[]{:S(2)}) async-start(), calls=%async_computation | async-start | bytes 3932160 | tf_op jit(solution)/shard_map/all_gather | solution.py:1915
  7.9 272.9 %all-gather.6.cloned.1.call-start = ((), (), s32[]{:S(2)}) async-start(), calls=%async_computation.1 | async-start | bytes 21233664 | tf_op jit(solution)/shard_map/all_gather | solution.py:1951
  149.4 503.1 %all-reduce.2.cloned.1.call-start = ((), (), s32[]{:S(2)}) async-start(), calls=%async_computation.2 | async-start | bytes 33554432 | tf_op jit(solution)/shard_map/psum | solution.py:1970
  651.9 21.0 %collective-permute-start.2 = (bf16[1024,2048]{1,0:T(8,128)(2,1)}, bf16[1024,2048]{1,0:T(8,128)(2,1)}, u32[]{:S(2)}, u32[]{:S(2)}) collective-permute-start(bf16[1024,2048]{1,0:T(8,128)(2,1)} %get-tuple-element.85.refs_2_), channel_id=1, source_target_pairs={{0,4},{4,0},{8,12},{12,8},{16,20},{20,16},{24,28},{28,24},{1,5},{5... | collective-permute-start | bytes 12582920 | tf_op jit(solution)/shard_map/ppermute | solution.py:1996
  652.0 20.9 %collective-permute-start = (bf16[3072,512]{1,0:T(8,128)(2,1)}, bf16[3072,512]{1,0:T(8,128)(2,1)S(1)}, u32[]{:S(2)}, u32[]{:S(2)}) collective-permute-start(bf16[3072,512]{1,0:T(8,128)(2,1)} %get-tuple-element.83.refs_0_), channel_id=1, source_target_pairs={{0,4},{4,0},{8,12},{12,8},{16,20},{20,16},{24,28},{28,24},{1,5},{5... | collective-permute-start | bytes 9437192 | tf_op jit(solution)/shard_map/ppermute | solution.py:1996
  652.5 20.4 %collective-permute-start.1 = (bf16[256,2048]{1,0:T(8,128)(2,1)}, bf16[256,2048]{1,0:T(8,128)(2,1)}, u32[]{:S(2)}, u32[]{:S(2)}) collective-permute-start(bf16[256,2048]{1,0:T(8,128)(2,1)} %get-tuple-element.84.refs_1_), channel_id=1, source_target_pairs={{0,4},{4,0},{8,12},{12,8},{16,20},{20,16},{24,28},{28,24},{1,5},{5... | collective-permute-start | bytes 3145736 | tf_op jit(solution)/shard_map/ppermute | solution.py:1996
  672.9 1.7 copy-start
  674.6 18.0 %copy-start.2 = (bf16[768,512]{1,0:T(8,128)(2,1)S(1)}, bf16[768,512]{1,0:T(8,128)(2,1)}, u32[]{:S(2)}) copy-start(bf16[768,512]{1,0:T(8,128)(2,1)} %get-tuple-element.105) | copy-start | bytes 2359300
  674.6 18.9 %copy-start.1 = (f32[768,512]{1,0:T(8,128)S(1)}, f32[768,512]{1,0:T(8,128)}, u32[]{:S(2)}) copy-start(f32[768,512]{1,0:T(8,128)} %get-tuple-element.106) | copy-start | bytes 4718596
Sparse Core Ops, SparseCore 0:
  9.6 66.1 all-gather.3
  149.5 106.5 all-gather.5
  280.9 301.2 all-reduce.1
